TPU v7x, 32 devices: a whole 2x2x4 slice. The times are simulated.
32 devices in a mesh: row: 4 (over x, core), col: 8 (over z, y).
Axes of the slice: x: 2, y: 2, z: 4, core: 2. Of those that a mesh axis runs over, the one named last changes fastest.
Arguments:
- hidden: bfloat16 [2048, 8192], P('row', 'col'), may hold values from -600 to 600
- norm_gain: float32 [8192], replicated, may hold values from 0.5 to 2
- wq: bfloat16 [8192, 8192], P('row', 'col'), may hold values from -1 to 1
- wk: bfloat16 [8192, 1024], P('row', 'col'), may hold values from -1 to 1
- wv: bfloat16 [8192, 1024], P('row', 'col'), may hold values from -0.0625 to 0.0625
- wo: bfloat16 [8192, 8192], P('row', 'col'), may hold values from -0.25 to 0.25
Outputs:
- attn_out: bfloat16 [2048, 8192], P('row', 'col')
All inputs are finite; a program needn't handle non-finite values.
Results may differ from a plain program's by a relative error of at most 0.011.
Values may be sent and summed in bfloat16 or wider, within the bound.
No kernel may reach another device: no remote copies, remote signals or barrier semaphores. Data moves between devices by JAX's collectives and lax.ppermute only.
A program may use at most 128 MiB of HBM per device.

v0:
```python
import jax
import jax.numpy as jnp
from jax import lax
from jax.sharding import PartitionSpec as P

HD = 128


def as_sent(array):
    return jax.tree.map(lambda a: a.astype(jnp.bfloat16) if a.dtype == jnp.float32 else a, array)


def partner(array, axis, distance):
    return lax.ppermute(array, axis, [(i, i ^ 1 << distance) for i in range(lax.axis_size(axis))])


def rotary(field, positions):
    half = field.shape[-1] // 2
    steps = jnp.arange(half).astype(jnp.float32)
    freqs = 10000.0 ** (-steps / half)
    angles = positions.astype(jnp.float32)[:, None] * freqs[None, :]
    cosine = jnp.cos(angles)[:, None, :]
    sine = jnp.sin(angles)[:, None, :]
    first = field[..., :half]
    second = field[..., half:]
    return jnp.concatenate(
        [first * cosine - second * sine, second * cosine + first * sine], axis=-1
    )


def order_pair(mine, other, col_index, bit, axis_dim):
    upper = col_index // 2**bit % 2 == 1
    lower_part = jnp.where(upper, other, mine)
    upper_part = jnp.where(upper, mine, other)
    return jnp.concatenate([lower_part, upper_part], axis=axis_dim)


def per_device(hidden, norm_gain, wq, wk, wv, wo):
    tok_rows = hidden.shape[0]
    panel = lax.all_gather(hidden, "col", axis=1, tiled=True)
    values_in = panel.astype(jnp.float32)
    meansq = jnp.mean(values_in * values_in, axis=1, keepdims=True)
    normed = (values_in * lax.rsqrt(meansq + 1e-05) * norm_gain).astype(jnp.bfloat16)
    kv_cols = wk.shape[1]
    group = max(1, HD // kv_cols)
    bits = group.bit_length() - 1
    col_index = lax.axis_index("col")
    stacked = jnp.stack((wk, wv), axis=1)
    for bit in range(bits):
        other = partner(as_sent(stacked), "col", bit).astype(stacked.dtype)
        stacked = order_pair(stacked, other, col_index, bit, 2)
    columns = normed
    query_part = jnp.dot(
        columns, lax.all_gather(wq, "row", axis=0, tiled=True), preferred_element_type=jnp.float32
    )
    pair_part = jnp.einsum(
        "ho,omr->hmr",
        columns,
        lax.all_gather(stacked, "row", axis=0, tiled=True),
        preferred_element_type=jnp.float32,
    )
    heads_here = wq.shape[1] // HD
    kv_here = pair_part.shape[2] // HD
    per_kv = heads_here // kv_here
    positions = lax.axis_index("row") * tok_rows + jnp.arange(tok_rows)
    queries = rotary(query_part.reshape(tok_rows, heads_here, HD), positions).astype(jnp.bfloat16)
    queries = queries.reshape(tok_rows, kv_here, per_kv, HD)
    keys = rotary(pair_part[:, 0].reshape(tok_rows, kv_here, HD), positions).astype(jnp.bfloat16)
    values = pair_part[:, 1].reshape(tok_rows, kv_here, HD).astype(jnp.bfloat16)
    scale = HD ** (-0.5)
    best = jnp.full((kv_here, per_kv, tok_rows), -1e30, jnp.float32)
    key_piece = lax.all_gather(keys, "row", axis=0, tiled=True)
    value_piece = lax.all_gather(values, "row", axis=0, tiled=True)
    count = key_piece.shape[0]
    scores = (
        jnp.einsum("tagd,nad->agtn", queries, key_piece, preferred_element_type=jnp.float32) * scale
    )
    key_pos = jnp.arange(count)
    visible = positions[:, None] >= key_pos[None, :]
    scores = jnp.where(visible, scores, -jnp.inf)
    fresh = jnp.maximum(best, jnp.max(scores, axis=3))
    probs = jnp.exp(scores - fresh[..., None])
    total = jnp.sum(probs, axis=3)
    update = jnp.einsum(
        "agtn,nad->agtd",
        probs.astype(jnp.bfloat16),
        value_piece,
        preferred_element_type=jnp.float32,
    )
    numer = update
    best, total, numer = (fresh, total, numer)
    heads = (
        (numer / total[..., None])
        .transpose(2, 0, 1, 3)
        .reshape(tok_rows, heads_here * HD)
        .astype(jnp.bfloat16)
    )
    head_panel = lax.all_gather(heads, "col", axis=1, tiled=True)
    columns = head_panel
    result = jnp.dot(
        columns, lax.all_gather(wo, "row", axis=0, tiled=True), preferred_element_type=jnp.float32
    )
    return result.astype(jnp.bfloat16)


def solution(mesh):
    in_specs = (
        P("row", "col"),
        P(),
        P("row", "col"),
        P("row", "col"),
        P("row", "col"),
        P("row", "col"),
    )
    out_specs = P("row", "col")
    return jax.shard_map(
        per_device, mesh=mesh, in_specs=in_specs, out_specs=out_specs, check_vma=False
    )
```

profile of v0, /device:TPU:2, one launch (start us, length us, event | category | flops | bytes accessed | tf_op | source)
XLA Modules:
  0.0 536.8 jit_solution(12718820526983394018)
XLA Ops:
  6.5 0.7 all-gather.6.cloned.1.call-update
  7.3 0.0 all-gather.8.cloned.1.call-start
  7.3 1.2 copy.7
  8.6 1.2 copy.8
  9.8 1.1 pad_maximum_fusion
  10.9 0.0 all-gather.8.cloned.1.call-update
  10.9 0.0 all-gather.10.cloned.1.call-start
  11.0 0.7 all-gather.10.cloned.1.call-update
  11.6 0.0 all-gather.14.cloned.1.call-start
  11.7 0.5 all-gather.14.cloned.1.call-update
  12.2 0.0 all-gather.12.cloned.1.call-start
  12.3 1.0 multiply_cosine_fusion
  13.3 0.8 iota_compare_fusion
  14.1 121.6 %all-gather.6.cloned.1.call-done = bf16[512,8192]{1,0:T(8,128)(2,1)} async-done(((bf16[512,1024]{1,0:T(8,128)(2,1)}), bf16[512,8192]{1,0:T(8,128)(2,1)}) %all-gather.6.cloned.1.call-update) | async-done | bytes 8388624 | tf_op jit(solution)/shard_map/all_gather | solution.py:40
  135.7 5.1 fusion.3
  140.8 28.0 %all-gather.8.cloned.1.call-done = bf16[8192,2,128]{0,2,1:T(8,128)(2,1)} async-done(((bf16[2048,2,128]{0,2,1:T(8,128)(2,1)}), bf16[8192,2,128]{0,2,1:T(8,128)(2,1)}) %all-gather.8.cloned.1.call-update) | async-done | bytes 4194320 | tf_op jit(solution)/shard_map/all_gather | solution.py:59
  168.8 7.0 %fusion.12 = f32[512,256]{0,1:S(1)} fusion(bf16[8192,256]{0,1:T(8,128)(2,1)} %bitcast.53, bf16[512,8192]{1,0:T(8,128)(2,1)} %all-gather.6.cloned.1.call-done, f32[8192]{0:T(1024)S(1)} %copy-done, f32[512]{0:T(512)S(1)} %add_rsqrt_fusion), kind=kOutput, calls=%fused_computation.15 | convolution fusion | flops 2164260864 | bytes 13142016
  175.9 0.6 fusion.30
  176.5 7.4 %all_gather.23 = bf16[2048,1,128]{0,2,1:T(8,128)(2,1)S(1)} all-gather(bf16[512,1,128]{0,2,1:T(8,128)(2,1)S(1)} %pad_maximum_fusion.1), channel_id=1, replica_groups=mesh['row'=4,'col'=8] {'row'}, dimensions={0}, use_global_device_ids=true | all-gather | bytes 655360 | tf_op jit(solution)/shard_map/all_gather | solution.py:72
  183.9 10.6 %all_gather.25 = bf16[2048,1,128]{0,2,1:T(8,128)(2,1)S(1)} all-gather(bf16[512,1,128]{0,2,1:T(8,128)(2,1)S(1)} %slice.34), channel_id=1, replica_groups=mesh['row'=4,'col'=8] {'row'}, dimensions={0}, use_global_device_ids=true | all-gather | bytes 655360 | tf_op jit(solution)/shard_map/all_gather | solution.py:73
  194.5 84.7 %all-gather.10.cloned.1.call-done = bf16[8192,1024]{1,0:T(8,128)(2,1)} async-done(((bf16[2048,1024]{1,0:T(8,128)(2,1)}), bf16[8192,1024]{1,0:T(8,128)(2,1)}) %all-gather.10.cloned.1.call-update) | async-done | bytes 16777232 | tf_op jit(solution)/shard_map/all_gather | solution.py:54
  279.2 14.9 %fusion.14 = f32[64,8,8,128]{3,1,2,0:T(8,128)S(1)} fusion(bf16[8192,1024]{1,0:T(8,128)(2,1)} %all-gather.10.cloned.1.call-done, bf16[512,8192]{1,0:T(8,128)(2,1)} %all-gather.6.cloned.1.call-done, f32[8192]{0:T(1024)S(1)} %copy-done, f32[512]{0:T(512)S(1)} %add_rsqrt_fusion), kind=kOutput, calls=%fused_computation.19 | convolution fusion | flops 8606711808 | bytes 27297792 | tf_op jit(solution)/shard_map/dot_general | solution.py:53
  294.1 0.5 copy.18
  294.6 0.7 fusion.37
  295.2 0.8 subtract_convert_fusion
  296.0 14.2 %fusion.2 = (f32[8,512]{1,0:T(8,128)S(1)}, f32[2048,512,8]{1,0,2:T(8,128)}) fusion(pred[512,2048]{0,1:T(8,128)(4,1)S(1)} %iota_compare_fusion, bf16[512,8,64]{2,0,1:T(8,128)(2,1)S(1)} %get-tuple-element.6, bf16[512,8,64]{2,0,1:T(8,128)(2,1)S(1)} %get-tuple-element.5, bf16[2048,1,128]{0,2,1:T(8,128)(2,1)S(1)} %all_gather.23), kind=kOutput, calls=%fused_computation.4 | convolution fusion | flops 2174742528 | bytes 36192256 | tf_op jit(solution)/shard_map/tagd,nad->agtn/dot_general | solution.py:76
  310.2 14.4 %fusion = f32[8,512]{1,0:T(8,128)S(1)} fusion(f32[2048,512,8]{1,0,2:T(8,128)} %get-tuple-element.14, f32[8,512]{1,0:T(8,128)S(1)} %broadcast_maximum_fusion, pred[512,2048]{0,1:T(8,128)(4,1)S(1)} %iota_compare_fusion), kind=kLoop, calls=%fused_computation.2 | loop fusion | flops 33550336 | bytes 34635776 | tf_op jit(solution)/shard_map/reduce_sum | solution.py:83
  324.7 16.6 %divide_convert_fusion = bf16[8,512,128]{1,2,0:T(8,128)(2,1)} fusion(f32[8,512]{1,0:T(8,128)S(1)} %fusion, f32[2048,512,8]{1,0,2:T(8,128)} %get-tuple-element.14, f32[8,512]{1,0:T(8,128)S(1)} %broadcast_maximum_fusion, pred[512,2048]{0,1:T(8,128)(4,1)S(1)} %iota_compare_fusion, bf16[2048,1,128]{0,2,1:T(8,128)(2,1)S(1)} %all_gather.25), kind=kOutput, calls=%fused_computation.16 | convolution fusion | flops 2182086656 | bytes 36208640 | tf_op jit(solution)/shard_map/agtn,nad->agtd/dot_general | solution.py:84
  341.2 0.0 all-gather.12.cloned.1.call-update
  341.2 45.3 %all-gather.14.cloned.1.call-done = bf16[8192,1024]{1,0:T(8,128)(2,1)} async-done(((bf16[2048,1024]{1,0:T(8,128)(2,1)}), bf16[8192,1024]{1,0:T(8,128)(2,1)}) %all-gather.14.cloned.1.call-update) | async-done | bytes 16777232 | tf_op jit(solution)/shard_map/all_gather | solution.py:101
  386.5 128.1 %all-gather.12.cloned.1.call-done = bf16[512,8192]{0,1:T(8,128)(2,1)} async-done(((bf16[512,1024]{0,1:T(8,128)(2,1)}), bf16[512,8192]{0,1:T(8,128)(2,1)}) %all-gather.12.cloned.1.call-update) | async-done | bytes 8388624 | tf_op jit(solution)/shard_map/all_gather | solution.py:98
  514.6 15.6 %convolution_convert_fusion = bf16[512,1024]{1,0:T(8,128)(2,1)} fusion(bf16[512,8192]{0,1:T(8,128)(2,1)} %all-gather.12.cloned.1.call-done, bf16[8192,1024]{1,0:T(8,128)(2,1)} %all-gather.14.cloned.1.call-done), kind=kOutput, calls=%fused_computation.20 | convolution fusion | flops 8590458880 | bytes 26214400 | tf_op jit(solution)/shard_map/dot_general | solution.py:100
  (10 shorter events, 0.1 us)
Async XLA Ops:
  6.5 129.2 %all-gather.6.cloned.1.call-start = ((), (), s32[]{:S(2)}) async-start(), calls=%async_computation | async-start | bytes 9437184 | tf_op jit(solution)/shard_map/all_gather | solution.py:40
  7.3 161.6 %all-gather.8.cloned.1.call-start = ((), (), s32[]{:S(2)}) async-start(), calls=%async_computation.1 | async-start | bytes 5242880 | tf_op jit(solution)/shard_map/all_gather | solution.py:59
  10.9 157.9 %copy-start = (f32[8192]{0:T(1024)S(1)}, f32[8192]{0:T(1024)}, u32[]{:S(2)}) copy-start(f32[8192]{0:T(1024)} %param.7) | copy-start | bytes 98308
  10.9 268.2 %all-gather.10.cloned.1.call-start = ((), (), s32[]{:S(2)}) async-start(), calls=%async_computation.2 | async-start | bytes 20971520 | tf_op jit(solution)/shard_map/all_gather | solution.py:54
  11.6 374.9 %all-gather.14.cloned.1.call-start = ((), (), s32[]{:S(2)}) async-start(), calls=%async_computation.4 | async-start | bytes 20971520 | tf_op jit(solution)/shard_map/all_gather | solution.py:101
  12.2 502.4 %all-gather.12.cloned.1.call-start = ((), (), s32[]{:S(2)}) async-start(), calls=%async_computation.3 | async-start | bytes 9437184 | tf_op jit(solution)/shard_map/all_gather | solution.py:98
Sparse Core Ops, SparseCore 0:
  9.5 126.1 all-gather.5
  137.3 31.4 all-gather.7
  170.4 108.7 all-gather.9
  280.6 105.9 all-gather.13
  388.5 126.0 all-gather.11
where the time goes:
time: 539 us; the launch traced here: 537 us
  waiting for transfers between devices  410 us (76%)
  matrix products  68.2 us (13%)
  other arithmetic  23.8 us (4%)
  blocking collectives  18 us (3%)
  between operations  13.3 us (2%)
    all_gather x1, waiting for transfers between devices, per_device(): head_panel = lax.all_gather(heads, 'col', axis=1, tiled=True)  128 us
    all_gather x1, waiting for transfers between devices, per_device(): panel = lax.all_gather(hidden, 'col', axis=1, tiled=True)  122 us
    all_gather x1, waiting for transfers between devices, per_device(): lax.all_gather(wq, 'row', axis=0, tiled=True)  84.7 us
    all_gather x1, waiting for transfers between devices, per_device(): lax.all_gather(wo, 'row', axis=0, tiled=True)  45.3 us
    all_gather x1, waiting for transfers between devices, per_device(): lax.all_gather(stacked, 'row', axis=0, tiled=True)  28 us
    dot_general x1, matrix products, per_device(): jnp.einsum('agtn,nad->agtd', probs.astype(jnp.bfloat16), value_piece, pre...  16.6 us
    dot_general x1, matrix products, per_device(): jnp.dot(columns, lax.all_gather(wo, 'row', axis=0, tiled=True), preferred...  15.6 us
    dot_general x1, matrix products, per_device(): jnp.dot(columns, lax.all_gather(wq, 'row', axis=0, tiled=True), preferred...  14.9 us
  transfers between devices with their start and end apart: 5, of which 5 were waited for; matrix products, arithmetic and copies ran while one was open for 15% of the time, Pallas kernels for 0%

commit v1 on v0

v1 whole, which is shorter than its diff:
```python
import functools
import math

import jax
import jax.numpy as jnp
from jax import lax
from jax.experimental import pallas as pl
from jax.experimental.pallas import tpu as pltpu
from jax.sharding import PartitionSpec as P

HD = 128
CHUNKS = 2
MIB = 1 << 20


def after(array, *earlier):
    return lax.optimization_barrier((array, *earlier))[0]


def swap(array, axis, mask):
    return lax.ppermute(array, axis, [(i, i ^ mask) for i in range(lax.axis_size(axis))])


def row_bits():
    return [1 << b for b in reversed(range((lax.axis_size("row")).bit_length() - 1))]


def gather_row(array):
    pieces = {0: array}
    for bit in row_bits():
        pieces.update({j ^ bit: swap(p, "row", bit) for j, p in list(pieces.items())})
    return [pieces[j] for j in range(len(pieces))]


def order_pair(mine, other, col_index, bit, axis_dim):
    upper = col_index // 2**bit % 2 == 1
    lower_part = jnp.where(upper, other, mine)
    upper_part = jnp.where(upper, mine, other)
    return jnp.concatenate([lower_part, upper_part], axis=axis_dim)


def ring_order(n):
    return list(range(0, n, 2)) + list(range(1, n, 2))[::-1]


def ring_source(c, hops, n):
    at = jnp.where(c % 2 == 0, c // 2, n - 1 - c // 2)
    at = (at - hops) % n
    return jnp.where(at < n // 2, 2 * at, 2 * (n - 1 - at) + 1)


def ring_gather(block):
    n = lax.axis_size("col")
    c = lax.axis_index("col")
    order = ring_order(n)
    up = [(order[i], order[(i + 1) % n]) for i in range(n)]
    down = [(b, a) for a, b in up]
    rows = block.shape[0] // 2
    halves = [block[:rows], block[rows:]]
    found = [(c, 0, halves[0]), (c, 1, halves[1])]
    chains = [[halves[0], halves[1]], [halves[0], halves[1]]]
    for hop in range(1, n // 2 + 1):
        for half in (0, 1):
            for way, perm in ((0, up), (1, down)):
                if hop == n // 2 and way != half:
                    continue
                got = lax.ppermute(chains[way][half], "col", perm)
                chains[way][half] = got
                found.append((ring_source(c, hop if way == 0 else -hop, n), half, got))
    return found


def project_kernel(parts, heads, tiles, a_ref, *refs):
    weights = refs[:parts]
    scale_ref, cos_ref, sin_ref, o_ref, acc = refs[parts:]
    step = pl.program_id(0)

    @pl.when(step == 0)
    def _():
        acc[...] = jnp.zeros_like(acc)

    for p in range(parts):

        @pl.when(step // tiles == p)
        def _():
            acc[...] += jnp.dot(a_ref[...], weights[p][...], preferred_element_type=jnp.float32)

    @pl.when(step == parts * tiles - 1)
    def _():
        for h in range(acc.shape[1] // HD):
            at = pl.ds(h * HD, HD)
            x = acc[:, at] * scale_ref[...]
            if h < heads:
                x = x * cos_ref[...] + pltpu.roll(x, HD // 2, 1) * sin_ref[...]
            o_ref[:, at] = x.astype(o_ref.dtype)


def project(panel, weights, scale, cos, sin, heads):
    tok, depth = panel.shape
    parts = len(weights)
    rows, cols = weights[0].shape
    tile = min(1024, rows)
    tiles = rows // tile
    full = lambda a: pl.BlockSpec(a.shape, lambda k: (0, 0))
    part = lambda p: pl.BlockSpec((tile, cols), lambda k: (jnp.clip(k - p * tiles, 0, tiles - 1), 0))
    return pl.pallas_call(
        functools.partial(project_kernel, parts, heads, tiles),
        grid=(parts * tiles,),
        in_specs=[pl.BlockSpec((tok, tile), lambda k: (0, k))]
        + [part(p) for p in range(parts)]
        + [full(scale), full(cos), full(sin)],
        out_specs=pl.BlockSpec((tok, cols), lambda k: (0, 0)),
        out_shape=jax.ShapeDtypeStruct((tok, cols), jnp.bfloat16),
        scratch_shapes=[pltpu.VMEM((tok, cols), jnp.float32)],
        compiler_params=pltpu.CompilerParams(
            dimension_semantics=("arbitrary",), vmem_limit_bytes=40 * MIB
        ),
        cost_estimate=pl.CostEstimate(
            flops=2 * tok * depth * cols,
            bytes_accessed=2 * (tok * depth + depth * cols + tok * cols),
            transcendentals=0,
        ),
    )(panel, *weights, scale, cos, sin)


def attend_kernel(parts, r_ref, q_ref, *refs):
    pieces = refs[:parts]
    o_ref, top, total, acc = refs[parts:]
    r = r_ref[0]
    q = q_ref[...]
    tok = q.shape[0]
    dims = (((1,), (1,)), ((), ()))

    s = lax.dot_general(q, pieces[0][:, :HD], dims, preferred_element_type=jnp.float32)
    row = lax.broadcasted_iota(jnp.int32, (tok, tok), 0)
    col = lax.broadcasted_iota(jnp.int32, (tok, tok), 1)
    s = jnp.where(row >= col, s, -jnp.inf)
    m = jnp.max(s, axis=1, keepdims=True)
    p = jnp.exp2(s - m)
    top[...] = m
    total[...] = jnp.sum(p, axis=1, keepdims=True)
    acc[...] = jnp.dot(p.astype(jnp.bfloat16), pieces[0][:, HD:], preferred_element_type=jnp.float32)
    for j in range(1, parts):

        @pl.when(jnp.bitwise_xor(r, j) < r)
        def _():
            s = lax.dot_general(q, pieces[j][:, :HD], dims, preferred_element_type=jnp.float32)
            m = jnp.maximum(top[...], jnp.max(s, axis=1, keepdims=True))
            keep = jnp.exp2(top[...] - m)
            p = jnp.exp2(s - m)
            top[...] = m
            total[...] = total[...] * keep + jnp.sum(p, axis=1, keepdims=True)
            acc[...] = acc[...] * keep + jnp.dot(
                p.astype(jnp.bfloat16), pieces[j][:, HD:], preferred_element_type=jnp.float32
            )

    o_ref[...] = (acc[...] / total[...]).astype(o_ref.dtype)


def attend(r, queries, pieces):
    tok, cols = queries.shape
    heads = cols // HD
    parts = len(pieces)
    return pl.pallas_call(
        functools.partial(attend_kernel, parts),
        grid_spec=pltpu.PrefetchScalarGridSpec(
            num_scalar_prefetch=1,
            grid=(heads,),
            in_specs=[pl.BlockSpec((tok, HD), lambda h, r: (0, h))]
            + [pl.BlockSpec((tok, 2 * HD), lambda h, r: (0, 0)) for _ in pieces],
            out_specs=pl.BlockSpec((tok, HD), lambda h, r: (0, h)),
            scratch_shapes=[
                pltpu.VMEM((tok, 1), jnp.float32),
                pltpu.VMEM((tok, 1), jnp.float32),
                pltpu.VMEM((tok, HD), jnp.float32),
            ],
        ),
        out_shape=jax.ShapeDtypeStruct((tok, cols), jnp.bfloat16),
        compiler_params=pltpu.CompilerParams(
            dimension_semantics=("arbitrary",), vmem_limit_bytes=32 * MIB
        ),
        cost_estimate=pl.CostEstimate(
            flops=4 * heads * tok * tok * parts * HD,
            bytes_accessed=4 * tok * cols + parts * 4 * tok * HD,
            transcendentals=heads * tok * tok * parts,
        ),
    )(r.reshape(1), queries, *pieces)


def finish_kernel(parts, chunks, *refs):
    panels = refs[:chunks]
    weights = refs[chunks : chunks + parts]
    o_ref, acc = refs[chunks + parts :]
    step = pl.program_id(0)
    steps = pl.num_programs(0)

    @pl.when(step == 0)
    def _():
        acc[...] = jnp.zeros_like(acc)

    for j in range(chunks):
        for p in range(parts):

            @pl.when(step // (steps // (chunks * parts)) == j * parts + p)
            def _():
                acc[...] += jnp.dot(
                    panels[j][...], weights[p][...], preferred_element_type=jnp.float32
                )

    @pl.when(step == steps - 1)
    def _():
        o_ref[...] = acc[...].astype(o_ref.dtype)


def finish(panels, weights, width):
    chunks, parts = len(panels), len(weights)
    tok, depth = panels[0].shape
    rows, cols = weights[0].shape
    per = rows // (width * chunks)
    span = per * parts

    def panel_spec(j):
        return pl.BlockSpec((tok, width), lambda k: (0, jnp.clip(k - j * span, 0, span - 1)))

    def weight_spec(p):
        def index(k):
            j, rest = k // span, k % span
            s = jnp.clip(rest - p * per, 0, per - 1)
            return (s * chunks + j, 0)

        return pl.BlockSpec((width, cols), index)

    return pl.pallas_call(
        functools.partial(finish_kernel, parts, chunks),
        grid=(chunks * span,),
        in_specs=[panel_spec(j) for j in range(chunks)] + [weight_spec(p) for p in range(parts)],
        out_specs=pl.BlockSpec((tok, cols), lambda k: (0, 0)),
        out_shape=jax.ShapeDtypeStruct((tok, cols), jnp.bfloat16),
        scratch_shapes=[pltpu.VMEM((tok, cols), jnp.float32)],
        compiler_params=pltpu.CompilerParams(
            dimension_semantics=("arbitrary",), vmem_limit_bytes=40 * MIB
        ),
        cost_estimate=pl.CostEstimate(
            flops=2 * tok * depth * chunks * cols,
            bytes_accessed=2 * (tok * depth * chunks + rows * parts * cols + tok * cols),
            transcendentals=0,
        ),
    )(*panels, *weights)


def per_device(hidden, norm_gain, wq, wk, wv, wo):
    tok, feat = hidden.shape
    n_row, n_col = lax.axis_size("row"), lax.axis_size("col")
    r, c = lax.axis_index("row"), lax.axis_index("col")
    depth = feat * n_col
    rows = wq.shape[0]
    cols = wq.shape[1]

    kv_cols = wk.shape[1]
    group = max(1, HD // kv_cols)
    stacked = jnp.stack((wk, wv), axis=1)
    for bit in range(group.bit_length() - 1):
        other = swap(stacked, "col", 1 << bit)
        stacked = order_pair(stacked, other, c, bit, 2)
    stacked = stacked.reshape(rows, 2 * HD)

    kv_weights = gather_row(stacked)
    wide = cols // CHUNKS
    q_weights = []
    last = kv_weights
    for j in range(CHUNKS):
        mine = wq[:, j * wide : (j + 1) * wide]
        if j > 0:
            mine = after(mine, *last)
        last = gather_row(mine)
        q_weights.append(last)
    o_weights = gather_row(after(wo, *last))

    panel = jnp.zeros((tok, depth), jnp.bfloat16)
    squares = [jnp.zeros((tok // 2, 1), jnp.float32) for _ in range(2)]
    for source, half, piece in ring_gather(hidden):
        wider = piece.astype(jnp.float32)
        squares[half] += jnp.sum(wider * wider, axis=1, keepdims=True)
        gain = lax.dynamic_slice(norm_gain, (source * feat,), (feat,))
        scaled = (wider * gain).astype(jnp.bfloat16)
        at = source * feat
        at = (at // rows ^ r) * rows + at % rows
        panel = lax.dynamic_update_slice(panel, scaled, (half * (tok // 2), at))
    meansq = jnp.concatenate(squares, axis=0) / depth
    scale = lax.rsqrt(meansq + 1e-05)

    half = HD // 2
    positions = r * tok + jnp.arange(tok)
    freqs = 10000.0 ** (-jnp.arange(half).astype(jnp.float32) / half)
    angles = positions.astype(jnp.float32)[:, None] * freqs[None, :]
    cosine, sine = jnp.cos(angles), jnp.sin(angles)
    cosine = jnp.concatenate([cosine, cosine], axis=1)
    sine = jnp.concatenate([-sine, sine], axis=1)
    factor = HD ** (-0.5) * math.log2(math.e)

    kv = project(panel, kv_weights, scale, cosine, sine, 1)
    kv_pieces = gather_row(kv)
    panels = []
    for j in range(CHUNKS):
        queries = project(panel, q_weights[j], scale, cosine * factor, sine * factor, wide // HD)
        heads = attend(r, queries, kv_pieces)
        gathered = jnp.zeros((tok, wide * n_col), jnp.bfloat16)
        for source, half, piece in ring_gather(heads):
            at = source * cols
            at = ((at // rows ^ r) * rows + at % rows) // CHUNKS
            gathered = lax.dynamic_update_slice(gathered, piece, (half * (tok // 2), at))
        panels.append(gathered)
    return finish(panels, o_weights, wide)


def solution(mesh):
    in_specs = (
        P("row", "col"),
        P(),
        P("row", "col"),
        P("row", "col"),
        P("row", "col"),
        P("row", "col"),
    )
    out_specs = P("row", "col")
    return jax.shard_map(
        per_device, mesh=mesh, in_specs=in_specs, out_specs=out_specs, check_vma=False
    )
```

time: 539 us -> 568 us (1.054)
  the two profiles are of different devices: /device:TPU:2 before, /device:TPU:3 now
where the time goes in v1:
time: 568 us; the launch traced here: 558 us
  waiting for transfers between devices  232 us (41%)
  local copies, waits for them, and re-layouts  157 us (28%)
  Pallas kernels  88.5 us (16%)
  starting transfers between devices  49.3 us (9%)
  other arithmetic  30.2 us (5%)
    ppermute x15, waiting for transfers between devices, swap(): lax.ppermute(array, axis, [(i, i ^ mask) for i in range(lax.axis_size(axi...  154 us
    dynamic_update_slice x32, local copies, waits for them, and re-layouts, per_device(): lax.dynamic_update_slice(gathered, piece, (half * (tok // 2), at))  129 us
    ppermute x42, waiting for transfers between devices, ring_gather(): got = lax.ppermute(chains[way][half], 'col', perm)  77.8 us
    pallas_call x2, Pallas kernels, attend(): pl.pallas_call(functools.partial(attend_kernel, parts), grid_spec=pltpu.P...  38 us
    ppermute x42, starting transfers between devices, ring_gather(): got = lax.ppermute(chains[way][half], 'col', perm)  33.2 us
    pallas_call x3, Pallas kernels, project(): pl.pallas_call(functools.partial(project_kernel, parts, heads, tiles), gr...  30.2 us
    pallas_call x1, Pallas kernels, finish(): pl.pallas_call(functools.partial(finish_kernel, parts, chunks), grid=(chu...  20.3 us
    dynamic_update_slice x15, other arithmetic, per_device(): panel = lax.dynamic_update_slice(panel, scaled, (half * (tok // 2), at))  19.5 us
  transfers between devices with their start and end apart: 57, of which 30 were waited for; matrix products, arithmetic and copies ran while one was open for 31% of the time, Pallas kernels for 12%

profile of v1, /device:TPU:3, one launch (start us, length us, event | category | flops | bytes accessed | tf_op | source)
XLA Modules:
  0.0 558.3 jit_solution(7550849235246615296)
XLA Ops:
  4.6 44.5 %collective-permute-done.15.refs_2_ = bf16[2048,512]{1,0:T(8,128)(2,1)S(1)} collective-permute-done((bf16[2048,512]{1,0:T(8,128)(2,1)S(1)}, bf16[2048,512]{1,0:T(8,128)(2,1)S(1)}, u32[]{:S(2)}, u32[]{:S(2)}) %collective-permute-start.15) | collective-permute-done | bytes 2097184 | tf_op jit(solution)/shard_map/ppermute | solution.py:21
  68.3 34.5 %collective-permute-done.38.refs_2_ = bf16[2048,512]{1,0:T(8,128)(2,1)} collective-permute-done((bf16[2048,512]{1,0:T(8,128)(2,1)S(1)}, bf16[2048,512]{1,0:T(8,128)(2,1)}, u32[]{:S(2)}, u32[]{:S(2)}) %collective-permute-start.38) | collective-permute-done | bytes 2097184 | tf_op jit(solution)/shard_map/ppermute | solution.py:21
  114.4 5.8 %collective-permute-done.2 = bf16[256,1024]{1,0:T(8,128)(2,1)S(1)} collective-permute-done((bf16[256,1024]{1,0:T(8,128)(2,1)}, bf16[256,1024]{1,0:T(8,128)(2,1)S(1)}, u32[]{:S(2)}, u32[]{:S(2)}) %collective-permute-start.2) | collective-permute-done | bytes 524320 | tf_op jit(solution)/shard_map/ppermute | solution.py:67
  125.8 5.6 %collective-permute-done.4 = bf16[256,1024]{1,0:T(8,128)(2,1)S(1)} collective-permute-done((bf16[256,1024]{1,0:T(8,128)(2,1)}, bf16[256,1024]{1,0:T(8,128)(2,1)S(1)}, u32[]{:S(2)}, u32[]{:S(2)}) %collective-permute-start.4) | collective-permute-done | bytes 524320 | tf_op jit(solution)/shard_map/ppermute | solution.py:67
  138.2 6.1 %collective-permute-done.6 = bf16[256,1024]{1,0:T(8,128)(2,1)S(1)} collective-permute-done((bf16[256,1024]{1,0:T(8,128)(2,1)S(1)}, bf16[256,1024]{1,0:T(8,128)(2,1)S(1)}, u32[]{:S(2)}, u32[]{:S(2)}) %collective-permute-start.6) | collective-permute-done | bytes 524320 | tf_op jit(solution)/shard_map/ppermute | solution.py:67
  150.0 8.7 %collective-permute-done.18.refs_2_ = bf16[2048,256]{1,0:T(8,128)(2,1)} collective-permute-done((bf16[2048,256]{1,0:T(8,128)(2,1)S(1)}, bf16[2048,256]{1,0:T(8,128)(2,1)}, u32[]{:S(2)}, u32[]{:S(2)}) %collective-permute-start.18) | collective-permute-done | bytes 1048608 | tf_op jit(solution)/shard_map/ppermute | solution.py:21
  162.2 4.5 collective-permute-done.10
  172.6 8.4 %collective-permute-done.13 = bf16[256,1024]{1,0:T(8,128)(2,1)S(1)} collective-permute-done((bf16[256,1024]{1,0:T(8,128)(2,1)S(1)}, bf16[256,1024]{1,0:T(8,128)(2,1)S(1)}, u32[]{:S(2)}, u32[]{:S(2)}) %collective-permute-start.13) | collective-permute-done | bytes 524320 | tf_op jit(solution)/shard_map/ppermute | solution.py:67
  190.8 57.8 %collective-permute-done.55.refs_4_ = bf16[2048,1024]{1,0:T(8,128)(2,1)} collective-permute-done((bf16[2048,1024]{1,0:T(8,128)(2,1)}, bf16[2048,1024]{1,0:T(8,128)(2,1)}, u32[]{:S(2)}, u32[]{:S(2)}) %collective-permute-start.55) | collective-permute-done | bytes 4194336 | tf_op jit(solution)/shard_map/ppermute | solution.py:21
  252.5 9.4 %shard_map.65.refs_0_ = bf16[512,256]{1,0:T(8,128)(2,1)S(1)} custom-call(bf16[512,8192]{1,0:T(8,128)(2,1)} %fusion.32.a_ref, bf16[2048,256]{1,0:T(8,128)(2,1)S(1)} %copy_bitcast_fusion.refs_0_, bf16[2048,256]{1,0:T(8,128)(2,1)} %collective-permute-done.17.refs_1_, bf16[2048,256]{1,0:T(8,128)(2,1)} %collective-permute-done.18.refs_2_, ...), custom_call_target="tpu_custom_call" | custom-call | flops 2147483648 | bytes 12845056 | tf_op jit(solution)/shard_map/pallas_call | solution.py:106
  262.4 7.4 %collective-permute-done.21.refs_2_ = bf16[512,256]{1,0:T(8,128)(2,1)S(1)} collective-permute-done((bf16[512,256]{1,0:T(8,128)(2,1)S(1)}, bf16[512,256]{1,0:T(8,128)(2,1)S(1)}, u32[]{:S(2)}, u32[]{:S(2)}) %collective-permute-start.21) | collective-permute-done | bytes 262176 | tf_op jit(solution)/shard_map/ppermute | solution.py:21
  272.2 9.5 %shard_map.64.q_ref = bf16[512,512]{1,0:T(8,128)(2,1)S(1)} custom-call(bf16[512,8192]{1,0:T(8,128)(2,1)} %fusion.32.a_ref, bf16[2048,512]{1,0:T(8,128)(2,1)S(1)} %copy-done.1, bf16[2048,512]{1,0:T(8,128)(2,1)S(1)} %copy-done.8, bf16[2048,512]{1,0:T(8,128)(2,1)S(1)} %copy-done.6, bf16[2048,512]{1,0:T(8,128)(2,1)S(1)} %copy-done.10, ...), custom_call_target="tpu_custom_call" | custom-call | flops 4294967296 | bytes 17301504 | tf_op jit(solution)/shard_map/pallas_call | solution.py:106
  281.7 19.0 %shard_map.66 = bf16[512,512]{1,0:T(8,128)(2,1)S(1)} custom-call(s32[1]{0:T(128)} %bitcast.r_ref, bf16[512,512]{1,0:T(8,128)(2,1)S(1)} %shard_map.64.q_ref, bf16[512,256]{1,0:T(8,128)(2,1)S(1)} %shard_map.65.refs_0_, bf16[512,256]{1,0:T(8,128)(2,1)S(1)} %collective-permute-done.20.refs_1_, bf16[512,256]{1,0:T(8,128)(2,1)S(1)} %collective-permute-done.21.refs_2_, ...), custom_call_target="tpu_custom_call" | custom-call | flops 2147483648 | bytes 2097152 | tf_op jit(solution)/shard_map/pallas_call | solution.py:164
  327.2 11.4 %shard_map.67.q_ref = bf16[512,512]{1,0:T(8,128)(2,1)S(1)} custom-call(bf16[512,8192]{1,0:T(8,128)(2,1)} %fusion.32.a_ref, bf16[2048,512]{1,0:T(8,128)(2,1)S(1)} %get-tuple-element.7.refs_0_, bf16[2048,512]{1,0:T(8,128)(2,1)} %collective-permute-done.37.refs_1_, bf16[2048,512]{1,0:T(8,128)(2,1)} %collective-permute-done.38.refs_2_, ...), custom_call_target="tpu_custom_call" | custom-call | flops 4294967296 | bytes 17301504 | tf_op jit(solution)/shard_map/pallas_call | solution.py:106
  341.4 19.0 %shard_map.68 = bf16[512,512]{1,0:T(8,128)(2,1)S(1)} custom-call(s32[1]{0:T(128)} %bitcast.r_ref, bf16[512,512]{1,0:T(8,128)(2,1)S(1)} %shard_map.67.q_ref, bf16[512,256]{1,0:T(8,128)(2,1)S(1)} %shard_map.65.refs_0_, bf16[512,256]{1,0:T(8,128)(2,1)S(1)} %collective-permute-done.20.refs_1_, bf16[512,256]{1,0:T(8,128)(2,1)S(1)} %collective-permute-done.21.refs_2_, ...), custom_call_target="tpu_custom_call" | custom-call | flops 2147483648 | bytes 2097152 | tf_op jit(solution)/shard_map/pallas_call | solution.py:164
  362.1 6.2 %collective-permute-done.36 = bf16[256,512]{1,0:T(8,128)(2,1)S(1)} collective-permute-done((bf16[256,512]{1,0:T(8,128)(2,1)S(1)}, bf16[256,512]{1,0:T(8,128)(2,1)S(1)}, u32[]{:S(2)}, u32[]{:S(2)}) %collective-permute-start.36) | collective-permute-done | bytes 262176 | tf_op jit(solution)/shard_map/ppermute | solution.py:67
  385.8 4.5 collective-permute-done.47
  401.1 4.7 dynamic_update_slice.160
  413.3 4.6 dynamic_update_slice.163
  424.7 4.5 dynamic_update_slice.166
  429.2 4.5 dynamic_update_slice.167
  440.9 4.6 dynamic_update_slice.170
  445.5 4.5 dynamic_update_slice.171
  457.3 4.5 dynamic_update_slice.174
  468.0 4.5 dynamic_update_slice.176
  479.9 4.5 dynamic_update_slice.179
  491.1 4.5 dynamic_update_slice.182
  495.6 4.5 dynamic_update_slice.183
  507.5 4.7 dynamic_update_slice.186
  512.2 4.5 dynamic_update_slice.187
  524.6 4.7 dynamic_update_slice.190
  537.5 20.3 %shard_map.69 = bf16[512,1024]{1,0:T(8,128)(2,1)} custom-call(bf16[512,4096]{1,0:T(8,128)(2,1)S(1)} %copy-done.3, bf16[512,4096]{1,0:T(8,128)(2,1)S(1)} %copy-done.2, bf16[2048,1024]{1,0:T(8,128)(2,1)} %refs_2_, bf16[2048,1024]{1,0:T(8,128)(2,1)} %collective-permute-done.54.refs_3_, bf16[2048,1024]{1,0:T(8,128)(2,1)} %collective-permute-done.55.refs_4_, ...), custom_call_target="tpu_custom_call" | custom-call | flops 8589934592 | bytes 26214400 | tf_op jit(solution)/shard_map/pallas_call | solution.py:233
  (282 shorter events, 210.4 us)
Async XLA Ops:
  2.5 46.6 %collective-permute-start.15 = (bf16[2048,512]{1,0:T(8,128)(2,1)S(1)}, bf16[2048,512]{1,0:T(8,128)(2,1)S(1)}, u32[]{:S(2)}, u32[]{:S(2)}) collective-permute-start(bf16[2048,512]{1,0:T(8,128)(2,1)S(1)} %get-tuple-element.14.refs_0_), channel_id=1, source_target_pairs={{0,16},{8,24},{16,0},{24,8},{1,17},{9,25},{17,1},{25,9},{2,18},{10... | collective-permute-start | bytes 6291464 | tf_op jit(solution)/shard_map/ppermute | solution.py:21
  2.6 49.3 %collective-permute-start.14 = (bf16[2048,512]{1,0:T(8,128)(2,1)S(1)}, bf16[2048,512]{1,0:T(8,128)(2,1)S(1)}, u32[]{:S(2)}, u32[]{:S(2)}) collective-permute-start(bf16[2048,512]{1,0:T(8,128)(2,1)S(1)} %get-tuple-element.14.refs_0_), channel_id=1, source_target_pairs={{0,8},{8,0},{16,24},{24,16},{1,9},{9,1},{17,25},{25,17},{2,10},{10... | collective-permute-start | bytes 6291464 | tf_op jit(solution)/shard_map/ppermute | solution.py:21
  55.8 46.9 %collective-permute-start.38 = (bf16[2048,512]{1,0:T(8,128)(2,1)S(1)}, bf16[2048,512]{1,0:T(8,128)(2,1)}, u32[]{:S(2)}, u32[]{:S(2)}) collective-permute-start(bf16[2048,512]{1,0:T(8,128)(2,1)S(1)} %get-tuple-element.7.refs_0_), channel_id=1, source_target_pairs={{0,16},{8,24},{16,0},{24,8},{1,17},{9,25},{17,1},{25,9},{2,18},{10... | collective-permute-start | bytes 6291464 | tf_op jit(solution)/shard_map/ppermute | solution.py:21
  62.5 43.9 %collective-permute-start = (bf16[256,1024]{1,0:T(8,128)(2,1)}, bf16[256,1024]{1,0:T(8,128)(2,1)}, u32[]{:S(2)}, u32[]{:S(2)}) collective-permute-start(bf16[256,1024]{1,0:T(8,128)(2,1)} %get-tuple-element.17), channel_id=1, source_target_pairs={{0,2},{2,4},{4,6},{6,7},{7,5},{5,3},{3,1},{1,0},{8,10},{10,12},{12... | collective-permute-start | bytes 1572872 | tf_op jit(solution)/shard_map/ppermute | solution.py:67
  64.0 43.8 %collective-permute-start.1 = (bf16[256,1024]{1,0:T(8,128)(2,1)}, bf16[256,1024]{1,0:T(8,128)(2,1)}, u32[]{:S(2)}, u32[]{:S(2)}) collective-permute-start(bf16[256,1024]{1,0:T(8,128)(2,1)} %get-tuple-element.17), channel_id=1, source_target_pairs={{2,0},{4,2},{6,4},{7,6},{5,7},{3,5},{1,3},{0,1},{10,8},{12,10},{14... | collective-permute-start | bytes 1572872 | tf_op jit(solution)/shard_map/ppermute | solution.py:67
  64.0 45.1 %collective-permute-start.3 = (bf16[256,1024]{1,0:T(8,128)(2,1)}, bf16[256,1024]{1,0:T(8,128)(2,1)}, u32[]{:S(2)}, u32[]{:S(2)}) collective-permute-start(bf16[256,1024]{1,0:T(8,128)(2,1)} %get-tuple-element.15), channel_id=1, source_target_pairs={{2,0},{4,2},{6,4},{7,6},{5,7},{3,5},{1,3},{0,1},{10,8},{12,10},{14... | collective-permute-start | bytes 1572872 | tf_op jit(solution)/shard_map/ppermute | solution.py:67
  66.7 68.3 %collective-permute-start.37 = (bf16[2048,512]{1,0:T(8,128)(2,1)S(1)}, bf16[2048,512]{1,0:T(8,128)(2,1)}, u32[]{:S(2)}, u32[]{:S(2)}) collective-permute-start(bf16[2048,512]{1,0:T(8,128)(2,1)S(1)} %get-tuple-element.7.refs_0_), channel_id=1, source_target_pairs={{0,8},{8,0},{16,24},{24,16},{1,9},{9,1},{17,25},{25,17},{2,10},{10... | collective-permute-start | bytes 6291464 | tf_op jit(solution)/shard_map/ppermute | solution.py:21
  102.8 32.4 %collective-permute-start.39 = (bf16[2048,512]{1,0:T(8,128)(2,1)}, bf16[2048,512]{1,0:T(8,128)(2,1)}, u32[]{:S(2)}, u32[]{:S(2)}) collective-permute-start(bf16[2048,512]{1,0:T(8,128)(2,1)} %collective-permute-done.38.refs_2_), channel_id=1, source_target_pairs={{0,8},{8,0},{16,24},{24,16},{1,9},{9,1},{17,25},{25,17},{2,10},{10... | collective-permute-start | bytes 6291464 | tf_op jit(solution)/shard_map/ppermute | solution.py:21
  106.4 13.8 %collective-permute-start.2 = (bf16[256,1024]{1,0:T(8,128)(2,1)}, bf16[256,1024]{1,0:T(8,128)(2,1)S(1)}, u32[]{:S(2)}, u32[]{:S(2)}) collective-permute-start(bf16[256,1024]{1,0:T(8,128)(2,1)} %get-tuple-element.15), channel_id=1, source_target_pairs={{0,2},{2,4},{4,6},{6,7},{7,5},{5,3},{3,1},{1,0},{8,10},{10,12},{12... | collective-permute-start | bytes 1572872 | tf_op jit(solution)/shard_map/ppermute | solution.py:67
  107.8 23.7 %collective-permute-start.4 = (bf16[256,1024]{1,0:T(8,128)(2,1)}, bf16[256,1024]{1,0:T(8,128)(2,1)S(1)}, u32[]{:S(2)}, u32[]{:S(2)}) collective-permute-start(bf16[256,1024]{1,0:T(8,128)(2,1)} %collective-permute-done), channel_id=1, source_target_pairs={{0,2},{2,4},{4,6},{6,7},{7,5},{5,3},{3,1},{1,0},{8,10},{10,12},{12... | collective-permute-start | bytes 1572872 | tf_op jit(solution)/shard_map/ppermute | solution.py:67
  109.1 28.8 %collective-permute-start.5 = (bf16[256,1024]{1,0:T(8,128)(2,1)}, bf16[256,1024]{1,0:T(8,128)(2,1)S(1)}, u32[]{:S(2)}, u32[]{:S(2)}) collective-permute-start(bf16[256,1024]{1,0:T(8,128)(2,1)} %collective-permute-done.1), channel_id=1, source_target_pairs={{2,0},{4,2},{6,4},{7,6},{5,7},{3,5},{1,3},{0,1},{10,8},{12,10},{14... | collective-permute-start | bytes 1572872 | tf_op jit(solution)/shard_map/ppermute | solution.py:67
  120.3 16.3 %collective-permute-start.7 = (bf16[256,1024]{1,0:T(8,128)(2,1)}, bf16[256,1024]{1,0:T(8,128)(2,1)S(1)}, u32[]{:S(2)}, u32[]{:S(2)}) collective-permute-start(bf16[256,1024]{1,0:T(8,128)(2,1)} %collective-permute-done.3), channel_id=1, source_target_pairs={{2,0},{4,2},{6,4},{7,6},{5,7},{3,5},{1,3},{0,1},{10,8},{12,10},{14... | collective-permute-start | bytes 1572872 | tf_op jit(solution)/shard_map/ppermute | solution.py:67
  131.5 12.8 %collective-permute-start.6 = (bf16[256,1024]{1,0:T(8,128)(2,1)S(1)}, bf16[256,1024]{1,0:T(8,128)(2,1)S(1)}, u32[]{:S(2)}, u32[]{:S(2)}) collective-permute-start(bf16[256,1024]{1,0:T(8,128)(2,1)S(1)} %collective-permute-done.2), channel_id=1, source_target_pairs={{0,2},{2,4},{4,6},{6,7},{7,5},{5,3},{3,1},{1,0},{8,10},{10,12},{12... | collective-permute-start | bytes 1572872 | tf_op jit(solution)/shard_map/ppermute | solution.py:67
  135.0 23.7 %collective-permute-start.18 = (bf16[2048,256]{1,0:T(8,128)(2,1)S(1)}, bf16[2048,256]{1,0:T(8,128)(2,1)}, u32[]{:S(2)}, u32[]{:S(2)}) collective-permute-start(bf16[2048,256]{1,0:T(8,128)(2,1)S(1)} %copy_bitcast_fusion.refs_0_), channel_id=1, source_target_pairs={{0,16},{8,24},{16,0},{24,8},{1,17},{9,25},{17,1},{25,9},{2,18},{10... | collective-permute-start | bytes 3145736 | tf_op jit(solution)/shard_map/ppermute | solution.py:21
  135.2 27.0 %collective-permute-start.8 = (bf16[256,1024]{1,0:T(8,128)(2,1)S(1)}, bf16[256,1024]{1,0:T(8,128)(2,1)S(1)}, u32[]{:S(2)}, u32[]{:S(2)}) collective-permute-start(bf16[256,1024]{1,0:T(8,128)(2,1)S(1)} %collective-permute-done.4), channel_id=1, source_target_pairs={{0,2},{2,4},{4,6},{6,7},{7,5},{5,3},{3,1},{1,0},{8,10},{10,12},{12... | collective-permute-start | bytes 1572872 | tf_op jit(solution)/shard_map/ppermute | solution.py:67
  136.5 112.0 %collective-permute-start.55 = (bf16[2048,1024]{1,0:T(8,128)(2,1)}, bf16[2048,1024]{1,0:T(8,128)(2,1)}, u32[]{:S(2)}, u32[]{:S(2)}) collective-permute-start(bf16[2048,1024]{1,0:T(8,128)(2,1)} %refs_2_), channel_id=1, source_target_pairs={{0,16},{8,24},{16,0},{24,8},{1,17},{9,25},{17,1},{25,9},{2,18},{10... | collective-permute-start | bytes 12582920 | tf_op jit(solution)/shard_map/ppermute | solution.py:21
  144.3 22.5 %collective-permute-start.10 = (bf16[256,1024]{1,0:T(8,128)(2,1)S(1)}, bf16[256,1024]{1,0:T(8,128)(2,1)S(1)}, u32[]{:S(2)}, u32[]{:S(2)}) collective-permute-start(bf16[256,1024]{1,0:T(8,128)(2,1)S(1)} %collective-permute-done.6), channel_id=1, source_target_pairs={{0,2},{2,4},{4,6},{6,7},{7,5},{5,3},{3,1},{1,0},{8,10},{10,12},{12... | collective-permute-start | bytes 1572872 | tf_op jit(solution)/shard_map/ppermute | solution.py:67
  149.6 19.6 %collective-permute-start.9 = (bf16[256,1024]{1,0:T(8,128)(2,1)S(1)}, bf16[256,1024]{1,0:T(8,128)(2,1)S(1)}, u32[]{:S(2)}, u32[]{:S(2)}) collective-permute-start(bf16[256,1024]{1,0:T(8,128)(2,1)S(1)} %collective-permute-done.5), channel_id=1, source_target_pairs={{2,0},{4,2},{6,4},{7,6},{5,7},{3,5},{1,3},{0,1},{10,8},{12,10},{14... | collective-permute-start | bytes 1572872 | tf_op jit(solution)/shard_map/ppermute | solution.py:67
  158.7 91.8 %collective-permute-start.17 = (bf16[2048,256]{1,0:T(8,128)(2,1)S(1)}, bf16[2048,256]{1,0:T(8,128)(2,1)}, u32[]{:S(2)}, u32[]{:S(2)}) collective-permute-start(bf16[2048,256]{1,0:T(8,128)(2,1)S(1)} %copy_bitcast_fusion.refs_0_), channel_id=1, source_target_pairs={{0,8},{8,0},{16,24},{24,16},{1,9},{9,1},{17,25},{25,17},{2,10},{10... | collective-permute-start | bytes 3145736 | tf_op jit(solution)/shard_map/ppermute | solution.py:21
  162.2 88.3 %collective-permute-start.19 = (bf16[2048,256]{1,0:T(8,128)(2,1)}, bf16[2048,256]{1,0:T(8,128)(2,1)}, u32[]{:S(2)}, u32[]{:S(2)}) collective-permute-start(bf16[2048,256]{1,0:T(8,128)(2,1)} %collective-permute-done.18.refs_2_), channel_id=1, source_target_pairs={{0,8},{8,0},{16,24},{24,16},{1,9},{9,1},{17,25},{25,17},{2,10},{10... | collective-permute-start | bytes 3145736 | tf_op jit(solution)/shard_map/ppermute | solution.py:21
  166.7 14.5 %collective-permute-start.12 = (bf16[256,1024]{1,0:T(8,128)(2,1)S(1)}, bf16[256,1024]{1,0:T(8,128)(2,1)S(1)}, u32[]{:S(2)}, u32[]{:S(2)}) collective-permute-start(bf16[256,1024]{1,0:T(8,128)(2,1)S(1)} %collective-permute-done.8), channel_id=1, source_target_pairs={{0,2},{2,4},{4,6},{6,7},{7,5},{5,3},{3,1},{1,0},{8,10},{10,12},{12... | collective-permute-start | bytes 1572872 | tf_op jit(solution)/shard_map/ppermute | solution.py:67
  188.1 345.0 %collective-permute-start.54 = (bf16[2048,1024]{1,0:T(8,128)(2,1)}, bf16[2048,1024]{1,0:T(8,128)(2,1)}, u32[]{:S(2)}, u32[]{:S(2)}) collective-permute-start(bf16[2048,1024]{1,0:T(8,128)(2,1)} %refs_2_), channel_id=1, source_target_pairs={{0,8},{8,0},{16,24},{24,16},{1,9},{9,1},{17,25},{25,17},{2,10},{10... | collective-permute-start | bytes 12582920 | tf_op jit(solution)/shard_map/ppermute | solution.py:21
  248.6 284.5 %collective-permute-start.56 = (bf16[2048,1024]{1,0:T(8,128)(2,1)}, bf16[2048,1024]{1,0:T(8,128)(2,1)}, u32[]{:S(2)}, u32[]{:S(2)}) collective-permute-start(bf16[2048,1024]{1,0:T(8,128)(2,1)} %collective-permute-done.55.refs_4_), channel_id=1, source_target_pairs={{0,8},{8,0},{16,24},{24,16},{1,9},{9,1},{17,25},{25,17},{2,10},{10... | collective-permute-start | bytes 12582920 | tf_op jit(solution)/shard_map/ppermute | solution.py:21
  262.1 19.6 %collective-permute-start.20 = (bf16[512,256]{1,0:T(8,128)(2,1)S(1)}, bf16[512,256]{1,0:T(8,128)(2,1)S(1)}, u32[]{:S(2)}, u32[]{:S(2)}) collective-permute-start(bf16[512,256]{1,0:T(8,128)(2,1)S(1)} %shard_map.65.refs_0_), channel_id=1, source_target_pairs={{0,8},{8,0},{16,24},{24,16},{1,9},{9,1},{17,25},{25,17},{2,10},{10... | collective-permute-start | bytes 786440 | tf_op jit(solution)/shard_map/ppermute | solution.py:21
  321.5 17.1 %collective-permute-start.31 = (bf16[256,512]{1,0:T(8,128)(2,1)S(1)}, bf16[256,512]{1,0:T(8,128)(2,1)S(1)}, u32[]{:S(2)}, u32[]{:S(2)}) collective-permute-start(bf16[256,512]{1,0:T(8,128)(2,1)S(1)} %collective-permute-done.27), channel_id=1, source_target_pairs={{0,2},{2,4},{4,6},{6,7},{7,5},{5,3},{3,1},{1,0},{8,10},{10,12},{12... | collective-permute-start | bytes 786440 | tf_op jit(solution)/shard_map/ppermute | solution.py:67
  323.8 16.2 %collective-permute-start.32 = (bf16[256,512]{1,0:T(8,128)(2,1)S(1)}, bf16[256,512]{1,0:T(8,128)(2,1)S(1)}, u32[]{:S(2)}, u32[]{:S(2)}) collective-permute-start(bf16[256,512]{1,0:T(8,128)(2,1)S(1)} %collective-permute-done.28), channel_id=1, source_target_pairs={{2,0},{4,2},{6,4},{7,6},{5,7},{3,5},{1,3},{0,1},{10,8},{12,10},{14... | collective-permute-start | bytes 786440 | tf_op jit(solution)/shard_map/ppermute | solution.py:67
  326.7 33.7 %collective-permute-start.34 = (bf16[256,512]{1,0:T(8,128)(2,1)S(1)}, bf16[256,512]{1,0:T(8,128)(2,1)S(1)}, u32[]{:S(2)}, u32[]{:S(2)}) collective-permute-start(bf16[256,512]{1,0:T(8,128)(2,1)S(1)} %collective-permute-done.30), channel_id=1, source_target_pairs={{2,0},{4,2},{6,4},{7,6},{5,7},{3,5},{1,3},{0,1},{10,8},{12,10},{14... | collective-permute-start | bytes 786440 | tf_op jit(solution)/shard_map/ppermute | solution.py:67
  338.6 22.0 %collective-permute-start.33 = (bf16[256,512]{1,0:T(8,128)(2,1)S(1)}, bf16[256,512]{1,0:T(8,128)(2,1)S(1)}, u32[]{:S(2)}, u32[]{:S(2)}) collective-permute-start(bf16[256,512]{1,0:T(8,128)(2,1)S(1)} %collective-permute-done.29), channel_id=1, source_target_pairs={{0,2},{2,4},{4,6},{6,7},{7,5},{5,3},{3,1},{1,0},{8,10},{10,12},{12... | collective-permute-start | bytes 786440 | tf_op jit(solution)/shard_map/ppermute | solution.py:67
  340.0 22.1 %collective-permute-start.35 = (bf16[256,512]{1,0:T(8,128)(2,1)S(1)}, bf16[256,512]{1,0:T(8,128)(2,1)S(1)}, u32[]{:S(2)}, u32[]{:S(2)}) collective-permute-start(bf16[256,512]{1,0:T(8,128)(2,1)S(1)} %collective-permute-done.31), channel_id=1, source_target_pairs={{0,2},{2,4},{4,6},{6,7},{7,5},{5,3},{3,1},{1,0},{8,10},{10,12},{12... | collective-permute-start | bytes 786440 | tf_op jit(solution)/shard_map/ppermute | solution.py:67
  392.7 123.9 %collective-permute-start.50 = (bf16[256,512]{1,0:T(8,128)(2,1)}, bf16[256,512]{1,0:T(8,128)(2,1)}, u32[]{:S(2)}, u32[]{:S(2)}) collective-permute-start(bf16[256,512]{1,0:T(8,128)(2,1)} %collective-permute-done.46), channel_id=1, source_target_pairs={{0,2},{2,4},{4,6},{6,7},{7,5},{5,3},{3,1},{1,0},{8,10},{10,12},{12... | collective-permute-start | bytes 786440 | tf_op jit(solution)/shard_map/ppermute | solution.py:67
  393.8 130.8 %collective-permute-start.52 = (bf16[256,512]{1,0:T(8,128)(2,1)}, bf16[256,512]{1,0:T(8,128)(2,1)}, u32[]{:S(2)}, u32[]{:S(2)}) collective-permute-start(bf16[256,512]{1,0:T(8,128)(2,1)} %collective-permute-done.48), channel_id=1, source_target_pairs={{0,2},{2,4},{4,6},{6,7},{7,5},{5,3},{3,1},{1,0},{8,10},{10,12},{12... | collective-permute-start | bytes 786440 | tf_op jit(solution)/shard_map/ppermute | solution.py:67
  397.6 131.6 %collective-permute-start.53 = (bf16[256,512]{1,0:T(8,128)(2,1)}, bf16[256,512]{1,0:T(8,128)(2,1)}, u32[]{:S(2)}, u32[]{:S(2)}) collective-permute-start(bf16[256,512]{1,0:T(8,128)(2,1)} %collective-permute-done.51), channel_id=1, source_target_pairs={{2,0},{4,2},{6,4},{7,6},{5,7},{3,5},{1,3},{0,1},{10,8},{12,10},{14... | collective-permute-start | bytes 786440 | tf_op jit(solution)/shard_map/ppermute | solution.py:67
  (82 other events, 1538.0 us)

commit v2 on v0

v2 whole, which is shorter than its diff:
```python
import functools
import math

import jax
import jax.numpy as jnp
from jax import lax
from jax.experimental import pallas as pl
from jax.experimental.pallas import tpu as pltpu
from jax.sharding import PartitionSpec as P

HD = 128
CHUNKS = 2
MIB = 1 << 20


def after(array, *earlier):
    if not earlier:
        return array
    return lax.optimization_barrier((array, *earlier))[0]


def swap(array, axis, mask):
    return lax.ppermute(array, axis, [(i, i ^ mask) for i in range(lax.axis_size(axis))])


def row_bits():
    return [1 << b for b in reversed(range((lax.axis_size("row")).bit_length() - 1))]


def exchange_row(array, *earlier):
    bit = row_bits()[0]
    return {0: array, bit: swap(after(array, *earlier), "row", bit)}


def gather_row(pieces, *earlier):
    pieces = dict(pieces)
    for bit in row_bits()[1:]:
        sent = {j: after(p, *earlier) if j > 0 else p for j, p in pieces.items()}
        pieces.update({j ^ bit: swap(p, "row", bit) for j, p in sent.items()})
    return [pieces[j] for j in range(len(pieces))]


def far(pieces):
    return pieces[row_bits()[0]]


def order_pair(mine, other, col_index, bit, axis_dim):
    upper = col_index // 2**bit % 2 == 1
    lower_part = jnp.where(upper, other, mine)
    upper_part = jnp.where(upper, mine, other)
    return jnp.concatenate([lower_part, upper_part], axis=axis_dim)


def ring_order(n):
    return list(range(0, n, 2)) + list(range(1, n, 2))[::-1]


def ring_source(c, hops, n):
    at = jnp.where(c % 2 == 0, c // 2, n - 1 - c // 2)
    at = (at - hops) % n
    return jnp.where(at < n // 2, 2 * at, 2 * (n - 1 - at) + 1)


def ring_gather(block, place, into, starts):
    n = lax.axis_size("col")
    c = lax.axis_index("col")
    order = ring_order(n)
    up = [(order[i], order[(i + 1) % n]) for i in range(n)]
    down = [(b, a) for a, b in up]
    rows = block.shape[0] // 2
    below = above = block
    into = place(into, c, 0, block)
    for hop in range(1, n // 2 + 1):
        if hop in starts:
            below, above = lax.optimization_barrier((below, above, *starts[hop]))[:2]
        if hop == n // 2:
            below, above = below[:rows], above[rows:]
        below = lax.ppermute(below, "col", up)
        above = lax.ppermute(above, "col", down)
        below, above = lax.optimization_barrier((below, above))
        into = place(into, ring_source(c, hop, n), 0, below)
        into = place(into, ring_source(c, -hop, n), rows if hop == n // 2 else 0, above)
    return into


def project_kernel(parts, heads, panel_ref, *refs):
    weights = refs[:parts]
    scale_ref, cos_ref, sin_ref, o_ref, a_buf, w_buf, acc, a_sem, w_sem = refs[parts:]
    slots, _, depth = panel_ref.shape
    per = slots // parts

    def a_copy(k):
        return pltpu.make_async_copy(panel_ref.at[k], a_buf.at[k], a_sem.at[k])

    def w_copy(k, p, s):
        return pltpu.make_async_copy(
            weights[p].at[pl.ds(s * depth, depth), :], w_buf.at[k], w_sem.at[k]
        )

    for p in range(parts):
        for s in range(per):
            a_copy(p * per + s).start()
            w_copy(p * per + s, p, s).start()
    acc[...] = jnp.zeros_like(acc)

    def body(k, carry):
        a_copy(k).wait()
        w_copy(k, 0, 0).wait()
        acc[...] += jnp.dot(a_buf[k], w_buf[k], preferred_element_type=jnp.float32)
        return carry

    lax.fori_loop(0, slots, body, 0)
    for h in range(acc.shape[1] // HD):
        at = pl.ds(h * HD, HD)
        x = acc[:, at] * scale_ref[...]
        if h < heads:
            x = x * cos_ref[...] + pltpu.roll(x, HD // 2, 1) * sin_ref[...]
        o_ref[:, at] = x.astype(o_ref.dtype)


def project(panel, weights, scale, cos, sin, heads):
    slots, tok, depth = panel.shape
    parts = len(weights)
    cols = weights[0].shape[1]
    hbm = pl.BlockSpec(memory_space=pl.ANY)
    vmem = pl.BlockSpec(memory_space=pltpu.VMEM)
    return pl.pallas_call(
        functools.partial(project_kernel, parts, heads),
        in_specs=[hbm] * (1 + parts) + [vmem] * 3,
        out_specs=vmem,
        out_shape=jax.ShapeDtypeStruct((tok, cols), jnp.bfloat16),
        scratch_shapes=[
            pltpu.VMEM((slots, tok, depth), jnp.bfloat16),
            pltpu.VMEM((slots, depth, cols), jnp.bfloat16),
            pltpu.VMEM((tok, cols), jnp.float32),
            pltpu.SemaphoreType.DMA((slots,)),
            pltpu.SemaphoreType.DMA((slots,)),
        ],
        compiler_params=pltpu.CompilerParams(vmem_limit_bytes=60 * MIB),
        cost_estimate=pl.CostEstimate(
            flops=2 * slots * tok * depth * cols,
            bytes_accessed=2 * (slots * depth * (tok + cols) + tok * cols),
            transcendentals=0,
        ),
    )(panel, *weights, scale, cos, sin)


def attend_kernel(parts, chunks, pair, r_ref, *refs):
    chunk_refs, pieces = refs[:chunks], refs[chunks : chunks + parts]
    o_ref, q_ref, turned, top, total, acc = refs[chunks + parts :]
    r = r_ref[0]
    tok = q_ref.shape[0]
    step = pl.program_id(0)
    per = pl.num_programs(0) // chunks
    for i in range(chunks):

        @pl.when(step // per == i)
        def _():
            q_ref[...] = chunk_refs[i][...]

    dims = (((1,), (1,)), ((), ()))

    @pl.when(step == 0)
    def _():
        for j in range(parts):
            turned[j] = pieces[j][:, HD:].T

    def scores(j, g):
        return lax.dot_general(
            pieces[j][:, :HD],
            q_ref[:, g * HD : (g + 1) * HD],
            dims,
            preferred_element_type=jnp.float32,
        )

    key = lax.broadcasted_iota(jnp.int32, (tok, tok), 0)
    query = lax.broadcasted_iota(jnp.int32, (tok, tok), 1)
    for g in range(pair):
        s = jnp.where(key <= query, scores(0, g), -jnp.inf)
        m = jnp.max(s, axis=0, keepdims=True)
        p = jnp.exp2(s - m)
        top[g] = m
        total[g] = jnp.sum(p, axis=0, keepdims=True)
        acc[g] = jnp.dot(turned[0], p.astype(jnp.bfloat16), preferred_element_type=jnp.float32)
    for j in range(1, parts):

        @pl.when(jnp.bitwise_xor(r, j) < r)
        def _():
            for g in range(pair):
                s = scores(j, g)
                m = jnp.maximum(top[g], jnp.max(s, axis=0, keepdims=True))
                keep = jnp.exp2(top[g] - m)
                p = jnp.exp2(s - m)
                top[g] = m
                total[g] = total[g] * keep + jnp.sum(p, axis=0, keepdims=True)
                acc[g] = acc[g] * keep + jnp.dot(
                    turned[j], p.astype(jnp.bfloat16), preferred_element_type=jnp.float32
                )

    for g in range(pair):
        o_ref[:, g * HD : (g + 1) * HD] = (acc[g] / total[g]).T.astype(o_ref.dtype)


def attend(r, queries, pieces):
    tok, cols = queries[0].shape
    chunks, parts = len(queries), len(pieces)
    pair = 2 if cols // HD % 2 == 0 else 1
    per = cols // (HD * pair)
    heads = chunks * cols // HD

    def query_spec(i):
        return pl.BlockSpec((tok, pair * HD), lambda h, r: (0, jnp.clip(h - i * per, 0, per - 1)))

    return pl.pallas_call(
        functools.partial(attend_kernel, parts, chunks, pair),
        grid_spec=pltpu.PrefetchScalarGridSpec(
            num_scalar_prefetch=1,
            grid=(chunks * per,),
            in_specs=[query_spec(i) for i in range(chunks)]
            + [pl.BlockSpec((tok, 2 * HD), lambda h, r: (0, 0)) for _ in pieces],
            out_specs=pl.BlockSpec((tok, pair * HD), lambda h, r: (0, h)),
            scratch_shapes=[
                pltpu.VMEM((tok, pair * HD), jnp.bfloat16),
                pltpu.VMEM((parts, HD, tok), jnp.bfloat16),
                pltpu.VMEM((pair, 1, tok), jnp.float32),
                pltpu.VMEM((pair, 1, tok), jnp.float32),
                pltpu.VMEM((pair, HD, tok), jnp.float32),
            ],
        ),
        out_shape=jax.ShapeDtypeStruct((tok, chunks * cols), jnp.bfloat16),
        compiler_params=pltpu.CompilerParams(
            dimension_semantics=("arbitrary",), vmem_limit_bytes=32 * MIB
        ),
        cost_estimate=pl.CostEstimate(
            flops=4 * heads * tok * tok * parts * HD,
            bytes_accessed=4 * tok * heads * HD + parts * 4 * tok * HD,
            transcendentals=heads * tok * tok * parts,
        ),
    )(r.reshape(1), *queries, *pieces)


def finish_kernel(parts, panel_ref, *refs):
    weights = refs[:parts]
    o_ref, a_buf, w_buf, acc, a_sem, w_sem = refs[-6:]
    slots, _, depth = panel_ref.shape
    per = slots // parts

    def a_copy(k):
        return pltpu.make_async_copy(panel_ref.at[k], a_buf.at[k], a_sem.at[k])

    def w_copy(k, p, s):
        return pltpu.make_async_copy(
            weights[p].at[pl.ds(s * depth, depth), :], w_buf.at[k], w_sem.at[k]
        )

    for p in range(parts):
        for s in range(per):
            a_copy(p * per + s).start()
            w_copy(p * per + s, p, s).start()
    acc[...] = jnp.zeros_like(acc)

    def body(k, carry):
        a_copy(k).wait()
        w_copy(k, 0, 0).wait()
        acc[...] += jnp.dot(a_buf[k], w_buf[k], preferred_element_type=jnp.float32)
        return carry

    lax.fori_loop(0, slots, body, 0)
    o_ref[...] = acc[...].astype(o_ref.dtype)


def finish(panel, weights, chunk, result=None):
    slots, tok, depth = panel.shape
    parts = len(weights)
    cols = weights[0].shape[1]
    hbm = pl.BlockSpec(memory_space=pl.ANY)
    old = [] if result is None else [result]
    return pl.pallas_call(
        functools.partial(finish_kernel, parts),
        grid=(1,),
        in_specs=[hbm] * (1 + parts + len(old)),
        out_specs=pl.BlockSpec((tok, cols), lambda i: (0, chunk)),
        out_shape=jax.ShapeDtypeStruct((tok, CHUNKS * cols), jnp.bfloat16),
        input_output_aliases={1 + parts: 0} if old else {},
        scratch_shapes=[
            pltpu.VMEM((slots, tok, depth), jnp.bfloat16),
            pltpu.VMEM((slots, depth, cols), jnp.bfloat16),
            pltpu.VMEM((tok, cols), jnp.float32),
            pltpu.SemaphoreType.DMA((slots,)),
            pltpu.SemaphoreType.DMA((slots,)),
        ],
        compiler_params=pltpu.CompilerParams(vmem_limit_bytes=60 * MIB),
        cost_estimate=pl.CostEstimate(
            flops=2 * slots * tok * depth * cols,
            bytes_accessed=2 * (slots * depth * (tok + cols) + tok * cols),
            transcendentals=0,
        ),
    )(panel, *weights, *old)


def per_device(hidden, norm_gain, wq, wk, wv, wo):
    tok, feat = hidden.shape
    n_row, n_col = lax.axis_size("row"), lax.axis_size("col")
    r, c = lax.axis_index("row"), lax.axis_index("col")
    depth = feat * n_col
    rows = wq.shape[0]
    cols = wq.shape[1]

    kv_cols = wk.shape[1]
    group = max(1, HD // kv_cols)
    stacked = jnp.stack((wk, wv), axis=1)
    for bit in range(group.bit_length() - 1):
        other = swap(stacked, "col", 1 << bit)
        stacked = order_pair(stacked, other, c, bit, 2)
    stacked = stacked.reshape(rows, 2 * HD)

    wide = cols // CHUNKS
    kv_parts = exchange_row(stacked)
    q_parts = []
    earlier = far(kv_parts)
    for j in range(CHUNKS):
        q_parts.append(exchange_row(wq[:, j * wide : (j + 1) * wide], earlier))
        earlier = far(q_parts[-1])

    per = rows // feat

    def slot_of(source):
        return (source // per ^ r) * per + source % per

    def put(into, source, first, piece):
        return lax.dynamic_update_slice(into, piece[None], (slot_of(source), first, 0))

    wider = hidden.astype(jnp.float32)
    squares = lax.psum(jnp.sum(wider * wider, axis=1, keepdims=True), "col")
    scale = lax.rsqrt(squares / depth + 1e-05)
    gain = lax.dynamic_slice(norm_gain, (c * feat,), (feat,))
    scaled = (wider * gain).astype(jnp.bfloat16)
    panel = jnp.zeros((n_col, tok, feat), jnp.bfloat16)
    panel = ring_gather(scaled, put, panel, {2: [far(kv_parts)]})

    half = HD // 2
    positions = r * tok + jnp.arange(tok)
    freqs = 10000.0 ** (-jnp.arange(half).astype(jnp.float32) / half)
    angles = positions.astype(jnp.float32)[:, None] * freqs[None, :]
    cosine, sine = jnp.cos(angles), jnp.sin(angles)
    cosine = jnp.concatenate([cosine, cosine], axis=1)
    sine = jnp.concatenate([-sine, sine], axis=1)
    factor = HD ** (-0.5) * math.log2(math.e)

    kv = project(panel, gather_row(kv_parts), scale, cosine, sine, 1)
    kv_own = exchange_row(kv)
    kv_pieces = gather_row(kv_own)
    scale = after(scale, kv)
    queries = []
    for j in range(CHUNKS):
        weights = gather_row(q_parts[j], *queries)
        queries.append(
            project(panel, weights, scale, cosine * factor, sine * factor, wide // HD)
        )
    heads = attend(r, queries, kv_pieces)

    o_parts = []
    earlier = far(kv_own)
    for j in range(CHUNKS):
        o_parts.append(exchange_row(wo[:, j * wide : (j + 1) * wide], earlier))
        earlier = far(o_parts[-1])
    gathered = jnp.zeros((n_col, tok, cols), jnp.bfloat16)
    gathered = ring_gather(heads, put, gathered, {})
    result = None
    for j in range(CHUNKS):
        weights = gather_row(o_parts[j], *([gathered] if j > 0 else []))
        result = finish(gathered, weights, j, result)
    return result


def solution(mesh):
    in_specs = (
        P("row", "col"),
        P(),
        P("row", "col"),
        P("row", "col"),
        P("row", "col"),
        P("row", "col"),
    )
    out_specs = P("row", "col")
    return jax.shard_map(
        per_device, mesh=mesh, in_specs=in_specs, out_specs=out_specs, check_vma=False
    )
```

time: 539 us -> 318 us (0.59)
  waiting for transfers between devices: 410 us -> 127 us
  matrix products: 68.2 us -> 0 us
  Pallas kernels: 0 us -> 57.5 us
  local copies, waits for them, and re-layouts: 3.65 us -> 43.4 us
  blocking collectives: 18 us -> 52.9 us
  starting transfers between devices: 0.16 us -> 26.4 us
  other arithmetic: 23.8 us -> 8.76 us
  between operations: 13.3 us -> 0.44 us
    all_gather x5 -> x0, waiting for transfers between devices: 408 us -> none  [the longest x1 128 us: per_device(): head_panel = lax.all_gather(heads, 'col', axis=1, tiled=True)]
    ppermute x0 -> x34, waiting for transfers between devices: none -> 127 us  [the longest x8 88.4 us: ring_gather(): below = lax.ppermute(below, 'col', up)]
    dot_general x4 -> x0, matrix products: 61.2 us -> none  [the longest x1 16.6 us: per_device(): jnp.einsum('agtn,nad->agtd', probs.astype(jnp.bfloat16), value_piece, pre...]
    pallas_call x0 -> x6, Pallas kernels: none -> 57.5 us  [the longest x3 27.1 us: project(): pl.pallas_call(functools.partial(project_kernel, parts, heads), in_specs=...]
    psum x0 -> x1, blocking collectives: none -> 52.9 us  [per_device(): squares = lax.psum(jnp.sum(wider * wider, axis=1, keepdims=True), 'col')]
    ppermute x0 -> x34, starting transfers between devices: none -> 26.4 us  [the longest x18 9.69 us: swap(): lax.ppermute(array, axis, [(i, i ^ mask) for i in range(lax.axis_size(axi...]
    dynamic_update_slice x0 -> x17, local copies, waits for them, and re-layouts: none -> 24.6 us  [put(): lax.dynamic_update_slice(into, piece[None], (slot_of(source), first, 0))]
    reduce_sum x2 -> x1, other arithmetic: 19.6 us -> 0.28 us  [per_device(): squares = lax.psum(jnp.sum(wider * wider, axis=1, keepdims=True), 'col')]
  transfers between devices with their start and end apart: 5 -> 34, of which waited for: 5 -> 17; matrix products, arithmetic and copies ran while one was open for 15% -> 15% of each run, Pallas kernels for 0% -> 16%
where the time goes in v2:
time: 318 us; the launch traced here: 317 us
  waiting for transfers between devices  127 us (40%)
  Pallas kernels  57.5 us (18%)
  blocking collectives  52.9 us (17%)
  local copies, waits for them, and re-layouts  43.4 us (14%)
  starting transfers between devices  26.4 us (8%)
  other arithmetic  8.76 us (3%)
    ppermute x8, waiting for transfers between devices, ring_gather(): below = lax.ppermute(below, 'col', up)  88.4 us
    psum x1, blocking collectives, per_device(): squares = lax.psum(jnp.sum(wider * wider, axis=1, keepdims=True), 'col')  52.9 us
    ppermute x18, waiting for transfers between devices, swap(): lax.ppermute(array, axis, [(i, i ^ mask) for i in range(lax.axis_size(axi...  31.7 us
    pallas_call x3, Pallas kernels, project(): pl.pallas_call(functools.partial(project_kernel, parts, heads), in_specs=...  27.1 us
    dynamic_update_slice x17, local copies, waits for them, and re-layouts, put(): lax.dynamic_update_slice(into, piece[None], (slot_of(source), first, 0))  24.6 us
    pallas_call x2, Pallas kernels, finish(): pl.pallas_call(functools.partial(finish_kernel, parts), grid=(1,), in_spe...  16.4 us
    pallas_call x1, Pallas kernels, attend(): pl.pallas_call(functools.partial(attend_kernel, parts, chunks, pair), gri...  14 us
    ppermute x18, starting transfers between devices, swap(): lax.ppermute(array, axis, [(i, i ^ mask) for i in range(lax.axis_size(axi...  9.69 us
  transfers between devices with their start and end apart: 34, of which 17 were waited for; matrix products, arithmetic and copies ran while one was open for 15% of the time, Pallas kernels for 16%

profile of v2, /device:TPU:2, one launch (start us, length us, event | category | flops | bytes accessed | tf_op | source)
XLA Modules:
  0.0 316.7 jit_solution(5204848158356737190)
XLA Ops:
  0.0 2.4 copy_bitcast_fusion.refs_0_
  2.4 4.4 %broadcast.47.clone = bf16[8,512,1024]{2,1,0:T(8,128)(2,1)} broadcast(bf16[]{:T(256)} %constant.328.clone.1), dimensions={} | broadcast | bytes 8388610 | tf_op jit(solution)/shard_map/broadcast.3
  8.0 2.1 collective-permute-start
  11.7 15.9 %collective-permute-done.2.refs_2_ = bf16[2048,256]{1,0:T(8,128)(2,1)} collective-permute-done((bf16[2048,256]{1,0:T(8,128)(2,1)}, bf16[2048,256]{1,0:T(8,128)(2,1)}, u32[]{:S(2)}, u32[]{:S(2)}) %collective-permute-start.2) | collective-permute-done | bytes 1048608 | tf_op jit(solution)/shard_map/ppermute | solution.py:23
  27.9 5.2 %collective-permute-done = bf16[512,1024]{1,0:T(8,128)(2,1)} collective-permute-done((bf16[512,1024]{1,0:T(8,128)(2,1)S(1)}, bf16[512,1024]{1,0:T(8,128)(2,1)}, u32[]{:S(2)}, u32[]{:S(2)}) %collective-permute-start) | collective-permute-done | bytes 1048608 | tf_op jit(solution)/shard_map/ppermute | solution.py:78
  38.4 19.9 %collective-permute-done.3 = bf16[512,1024]{1,0:T(8,128)(2,1)} collective-permute-done((bf16[512,1024]{1,0:T(8,128)(2,1)}, bf16[512,1024]{1,0:T(8,128)(2,1)}, u32[]{:S(2)}, u32[]{:S(2)}) %collective-permute-start.3) | collective-permute-done | bytes 1048608 | tf_op jit(solution)/shard_map/ppermute | solution.py:78
  62.1 52.9 %psum.7 = f32[512,1]{1,0:T(8,128)S(1)} all-reduce(f32[512,1]{1,0:T(8,128)S(1)} %copy.10), channel_id=1, replica_groups=mesh['row'=4,'col'=8] {'col'}, use_global_device_ids=true, to_apply=%region_1.0 | all-reduce | flops 512 | bytes 4096 | tf_op jit(solution)/shard_map/psum | solution.py:334
  115.0 2.3 broadcast_multiply_fusion
  118.1 2.3 bitcast_dynamic-update-slice_fusion.12
  120.4 2.3 bitcast_dynamic-update-slice_fusion.11
  124.9 2.2 collective-permute-start.8
  128.4 2.4 bitcast_dynamic-update-slice_fusion.10
  130.8 2.3 bitcast_dynamic-update-slice_fusion.9
  133.1 5.1 %collective-permute-done.7 = bf16[256,1024]{1,0:T(8,128)(2,1)S(1)} collective-permute-done((bf16[256,1024]{1,0:T(8,128)(2,1)S(1)}, bf16[256,1024]{1,0:T(8,128)(2,1)S(1)}, u32[]{:S(2)}, u32[]{:S(2)}) %collective-permute-start.7) | collective-permute-done | bytes 524320 | tf_op jit(solution)/shard_map/ppermute | solution.py:78
  139.5 2.3 bitcast_dynamic-update-slice_fusion.8
  141.8 2.3 bitcast_dynamic-update-slice_fusion.7
  146.8 7.2 %shard_map.64.refs_2_ = bf16[512,256]{1,0:T(8,128)(2,1)} custom-call(bf16[8,512,1024]{2,1,0:T(8,128)(2,1)} %bitcast_dynamic-update-slice_fusion.16.panel_ref, bf16[2048,256]{1,0:T(8,128)(2,1)} %copy_bitcast_fusion.refs_0_, bf16[2048,256]{1,0:T(8,128)(2,1)} %copy-done.7, bf16[2048,256]{1,0:T(8,128)(2,1)} %collective-permute-done.2.refs_2_, ...), custom_call_target="tpu_custom_call" | custom-call | flops 2147483648 | bytes 12845056 | tf_op jit(solution)/shard_map/pallas_call | solution.py:127
  154.1 9.9 %shard_map.65.refs_0_ = bf16[512,512]{1,0:T(8,128)(2,1)} custom-call(bf16[8,512,1024]{2,1,0:T(8,128)(2,1)} %bitcast_dynamic-update-slice_fusion.16.panel_ref, bf16[2048,512]{1,0:T(8,128)(2,1)} %get-tuple-element.40.refs_0_, bf16[2048,512]{1,0:T(8,128)(2,1)} %collective-permute-done.9.refs_1_, bf16[2048,512]{1,0:T(8,128)(2,1)} %collective-permute-done.10.refs_2_, ...), custom_call_target="tpu_custom_call" | custom-call | flops 4294967296 | bytes 17301504 | tf_op jit(solution)/shard_map/pallas_call | solution.py:127
  164.0 10.8 %collective-permute-done.15.refs_2_ = bf16[2048,512]{1,0:T(8,128)(2,1)} collective-permute-done((bf16[2048,512]{1,0:T(8,128)(2,1)S(1)}, bf16[2048,512]{1,0:T(8,128)(2,1)}, u32[]{:S(2)}, u32[]{:S(2)}) %collective-permute-start.15) | collective-permute-done | bytes 2097184 | tf_op jit(solution)/shard_map/ppermute | solution.py:23
  176.0 4.5 %fusion.4 = (bf16[2048,512]{1,0:T(8,128)(2,1)}, bf16[2048,512]{1,0:T(8,128)(2,1)}) fusion(bf16[2048,1024]{1,0:T(8,128)(2,1)} %param.11), kind=kLoop, calls=%fused_computation.34 | loop fusion | bytes 8388608 | tf_op jit(solution)/shard_map/slice | solution.py:365
  180.8 2.7 collective-permute-done.18.refs_4_
  184.8 10.0 %shard_map.66.refs_1_ = bf16[512,512]{1,0:T(8,128)(2,1)} custom-call(bf16[8,512,1024]{2,1,0:T(8,128)(2,1)} %bitcast_dynamic-update-slice_fusion.16.panel_ref, bf16[2048,512]{1,0:T(8,128)(2,1)} %copy-done.3, bf16[2048,512]{1,0:T(8,128)(2,1)} %collective-permute-done.14.refs_1_, bf16[2048,512]{1,0:T(8,128)(2,1)} %collective-permute-done.15.refs_2_, ...), custom_call_target="tpu_custom_call" | custom-call | flops 4294967296 | bytes 17301504 | tf_op jit(solution)/shard_map/pallas_call | solution.py:127
  195.9 14.0 %shard_map.67 = bf16[512,1024]{1,0:T(8,128)(2,1)S(1)} custom-call(s32[1]{0:T(128)} %bitcast.r_ref, bf16[512,512]{1,0:T(8,128)(2,1)S(1)} %copy-done, bf16[512,512]{1,0:T(8,128)(2,1)S(1)} %copy-done.1, bf16[512,256]{1,0:T(8,128)(2,1)S(1)} %copy-done.2, bf16[512,256]{1,0:T(8,128)(2,1)S(1)} %collective-permute-done.17.refs_3_, ...), custom_call_target="tpu_custom_call" | custom-call | flops 4294967296 | bytes 3145728 | tf_op jit(solution)/shard_map/pallas_call | solution.py:214
  211.9 19.9 %collective-permute-done.20 = bf16[512,1024]{1,0:T(8,128)(2,1)S(1)} collective-permute-done((bf16[512,1024]{1,0:T(8,128)(2,1)S(1)}, bf16[512,1024]{1,0:T(8,128)(2,1)S(1)}, u32[]{:S(2)}, u32[]{:S(2)}) %collective-permute-start.20) | collective-permute-done | bytes 1048608 | tf_op jit(solution)/shard_map/ppermute | solution.py:78
  234.4 3.7 %collective-permute-start.32 = (bf16[2048,512]{1,0:T(8,128)(2,1)}, bf16[2048,512]{1,0:T(8,128)(2,1)}, u32[]{:S(2)}, u32[]{:S(2)}) collective-permute-start(bf16[2048,512]{1,0:T(8,128)(2,1)} %get-tuple-element.52.refs_0_), channel_id=1, source_target_pairs={{0,8},{8,0},{16,24},{24,16},{1,9},{9,1},{17,25},{25,17},{2,10},{10... | collective-permute-start | bytes 6291464 | tf_op jit(solution)/shard_map/ppermute | solution.py:23
  238.2 4.4 %broadcast.47 = bf16[8,512,1024]{2,1,0:T(8,128)(2,1)} broadcast(bf16[]{:T(256)} %constant.328.clone.1), dimensions={} | broadcast | bytes 8388610 | tf_op jit(solution)/shard_map/broadcast.3
  243.6 11.5 %collective-permute-done.22 = bf16[512,1024]{1,0:T(8,128)(2,1)S(1)} collective-permute-done((bf16[512,1024]{1,0:T(8,128)(2,1)S(1)}, bf16[512,1024]{1,0:T(8,128)(2,1)S(1)}, u32[]{:S(2)}, u32[]{:S(2)}) %collective-permute-start.22) | collective-permute-done | bytes 1048608 | tf_op jit(solution)/shard_map/ppermute | solution.py:78
  262.0 17.3 %collective-permute-done.24 = bf16[512,1024]{1,0:T(8,128)(2,1)S(1)} collective-permute-done((bf16[512,1024]{1,0:T(8,128)(2,1)S(1)}, bf16[512,1024]{1,0:T(8,128)(2,1)S(1)}, u32[]{:S(2)}, u32[]{:S(2)}) %collective-permute-start.24) | collective-permute-done | bytes 1048608 | tf_op jit(solution)/shard_map/ppermute | solution.py:78
  285.5 9.5 %collective-permute-done.26 = bf16[256,1024]{1,0:T(8,128)(2,1)S(1)} collective-permute-done((bf16[256,1024]{1,0:T(8,128)(2,1)S(1)}, bf16[256,1024]{1,0:T(8,128)(2,1)S(1)}, u32[]{:S(2)}, u32[]{:S(2)}) %collective-permute-start.26) | collective-permute-done | bytes 524320 | tf_op jit(solution)/shard_map/ppermute | solution.py:78
  297.8 2.3 collective-permute-done.33.refs_3_
  300.1 8.2 %shard_map.68.refs_4_ = bf16[512,1024]{1,0:T(8,128)(2,1)} custom-call(bf16[8,512,1024]{2,1,0:T(8,128)(2,1)} %bitcast_dynamic-update-slice_fusion.14.panel_ref, bf16[2048,512]{1,0:T(8,128)(2,1)} %get-tuple-element.52.refs_0_, bf16[2048,512]{1,0:T(8,128)(2,1)} %collective-permute-done.32.refs_1_, bf16[2048,512]{1,0:T(8,128)(2,1)} %collective-permute-done.29.refs_2_, ...), custom_call_target="tpu_custom_call" | custom-call | flops 4294967296 | bytes 17301504 | tf_op jit(solution)/shard_map/pallas_call | solution.py:278
  308.3 8.2 %shard_map.69 = bf16[512,1024]{1,0:T(8,128)(2,1)} custom-call(bf16[8,512,1024]{2,1,0:T(8,128)(2,1)} %bitcast_dynamic-update-slice_fusion.14.panel_ref, bf16[2048,512]{1,0:T(8,128)(2,1)} %get-tuple-element.53.refs_0_, bf16[2048,512]{1,0:T(8,128)(2,1)} %collective-permute-done.28.refs_1_, ...), custom_call_target="tpu_custom_call", output_to_operand_aliasing={{}: (5, {})} | custom-call | flops 4294967296 | bytes 17301504 | tf_op jit(solution)/shard_map/pallas_call | solution.py:278
  (95 shorter events, 46.0 us)
Async XLA Ops:
  2.4 25.2 %collective-permute-start.2 = (bf16[2048,256]{1,0:T(8,128)(2,1)}, bf16[2048,256]{1,0:T(8,128)(2,1)}, u32[]{:S(2)}, u32[]{:S(2)}) collective-permute-start(bf16[2048,256]{1,0:T(8,128)(2,1)} %copy_bitcast_fusion.refs_0_), channel_id=1, source_target_pairs={{0,16},{8,24},{16,0},{24,8},{1,17},{9,25},{17,1},{25,9},{2,18},{10... | collective-permute-start | bytes 3145736 | tf_op jit(solution)/shard_map/ppermute | solution.py:23
  8.0 25.1 %collective-permute-start = (bf16[512,1024]{1,0:T(8,128)(2,1)S(1)}, bf16[512,1024]{1,0:T(8,128)(2,1)}, u32[]{:S(2)}, u32[]{:S(2)}) collective-permute-start(bf16[512,1024]{1,0:T(8,128)(2,1)S(1)} %get-tuple-element.58), channel_id=1, source_target_pairs={{0,2},{2,4},{4,6},{6,7},{7,5},{5,3},{3,1},{1,0},{8,10},{10,12},{12... | collective-permute-start | bytes 3145736 | tf_op jit(solution)/shard_map/ppermute | solution.py:78
  10.1 24.5 %collective-permute-start.1 = (bf16[512,1024]{1,0:T(8,128)(2,1)S(1)}, bf16[512,1024]{1,0:T(8,128)(2,1)}, u32[]{:S(2)}, u32[]{:S(2)}) collective-permute-start(bf16[512,1024]{1,0:T(8,128)(2,1)S(1)} %get-tuple-element.58), channel_id=1, source_target_pairs={{2,0},{4,2},{6,4},{7,6},{5,7},{3,5},{1,3},{0,1},{10,8},{12,10},{14... | collective-permute-start | bytes 3145736 | tf_op jit(solution)/shard_map/ppermute | solution.py:79
  27.6 90.5 %collective-permute-start.10 = (bf16[2048,512]{1,0:T(8,128)(2,1)}, bf16[2048,512]{1,0:T(8,128)(2,1)}, u32[]{:S(2)}, u32[]{:S(2)}) collective-permute-start(bf16[2048,512]{1,0:T(8,128)(2,1)} %get-tuple-element.40.refs_0_), channel_id=1, source_target_pairs={{0,16},{8,24},{16,0},{24,8},{1,17},{9,25},{17,1},{25,9},{2,18},{10... | collective-permute-start | bytes 6291464 | tf_op jit(solution)/shard_map/ppermute | solution.py:23
  34.5 23.7 %collective-permute-start.3 = (bf16[512,1024]{1,0:T(8,128)(2,1)}, bf16[512,1024]{1,0:T(8,128)(2,1)}, u32[]{:S(2)}, u32[]{:S(2)}) collective-permute-start(bf16[512,1024]{1,0:T(8,128)(2,1)} %collective-permute-done), channel_id=1, source_target_pairs={{0,2},{2,4},{4,6},{6,7},{7,5},{5,3},{3,1},{1,0},{8,10},{10,12},{12... | collective-permute-start | bytes 3145736 | tf_op jit(solution)/shard_map/ppermute | solution.py:78
  36.1 23.5 %collective-permute-start.4 = (bf16[512,1024]{1,0:T(8,128)(2,1)}, bf16[512,1024]{1,0:T(8,128)(2,1)}, u32[]{:S(2)}, u32[]{:S(2)}) collective-permute-start(bf16[512,1024]{1,0:T(8,128)(2,1)} %collective-permute-done.1), channel_id=1, source_target_pairs={{2,0},{4,2},{6,4},{7,6},{5,7},{3,5},{1,3},{0,1},{10,8},{12,10},{14... | collective-permute-start | bytes 3145736 | tf_op jit(solution)/shard_map/ppermute | solution.py:79
  36.6 117.5 %collective-permute-start.9 = (bf16[2048,512]{1,0:T(8,128)(2,1)}, bf16[2048,512]{1,0:T(8,128)(2,1)}, u32[]{:S(2)}, u32[]{:S(2)}) collective-permute-start(bf16[2048,512]{1,0:T(8,128)(2,1)} %get-tuple-element.40.refs_0_), channel_id=1, source_target_pairs={{0,8},{8,0},{16,24},{24,16},{1,9},{9,1},{17,25},{25,17},{2,10},{10... | collective-permute-start | bytes 6291464 | tf_op jit(solution)/shard_map/ppermute | solution.py:23
  59.6 63.1 %collective-permute-start.5 = (bf16[512,1024]{1,0:T(8,128)(2,1)}, bf16[512,1024]{1,0:T(8,128)(2,1)}, u32[]{:S(2)}, u32[]{:S(2)}) collective-permute-start(bf16[512,1024]{1,0:T(8,128)(2,1)} %collective-permute-done.3), channel_id=1, source_target_pairs={{0,2},{2,4},{4,6},{6,7},{7,5},{5,3},{3,1},{1,0},{8,10},{10,12},{12... | collective-permute-start | bytes 3145736 | tf_op jit(solution)/shard_map/ppermute | solution.py:78
  61.1 61.5 %collective-permute-start.6 = (bf16[512,1024]{1,0:T(8,128)(2,1)}, bf16[512,1024]{1,0:T(8,128)(2,1)}, u32[]{:S(2)}, u32[]{:S(2)}) collective-permute-start(bf16[512,1024]{1,0:T(8,128)(2,1)} %collective-permute-done.4), channel_id=1, source_target_pairs={{2,0},{4,2},{6,4},{7,6},{5,7},{3,5},{1,3},{0,1},{10,8},{12,10},{14... | collective-permute-start | bytes 3145736 | tf_op jit(solution)/shard_map/ppermute | solution.py:79
  118.1 36.0 %collective-permute-start.11 = (bf16[2048,512]{1,0:T(8,128)(2,1)}, bf16[2048,512]{1,0:T(8,128)(2,1)}, u32[]{:S(2)}, u32[]{:S(2)}) collective-permute-start(bf16[2048,512]{1,0:T(8,128)(2,1)} %collective-permute-done.10.refs_2_), channel_id=1, source_target_pairs={{0,8},{8,0},{16,24},{24,16},{1,9},{9,1},{17,25},{25,17},{2,10},{10... | collective-permute-start | bytes 6291464 | tf_op jit(solution)/shard_map/ppermute | solution.py:23
  123.7 14.5 %collective-permute-start.7 = (bf16[256,1024]{1,0:T(8,128)(2,1)S(1)}, bf16[256,1024]{1,0:T(8,128)(2,1)S(1)}, u32[]{:S(2)}, u32[]{:S(2)}) collective-permute-start(bf16[256,1024]{1,0:T(8,128)(2,1)S(1)} %slice.24), channel_id=1, source_target_pairs={{0,2},{2,4},{4,6},{6,7},{7,5},{5,3},{3,1},{1,0},{8,10},{10,12},{12... | collective-permute-start | bytes 1572872 | tf_op jit(solution)/shard_map/ppermute | solution.py:78
  124.9 14.7 %collective-permute-start.8 = (bf16[256,1024]{1,0:T(8,128)(2,1)S(1)}, bf16[256,1024]{1,0:T(8,128)(2,1)S(1)}, u32[]{:S(2)}, u32[]{:S(2)}) collective-permute-start(bf16[256,1024]{1,0:T(8,128)(2,1)S(1)} %slice.25), channel_id=1, source_target_pairs={{2,0},{4,2},{6,4},{7,6},{5,7},{3,5},{1,3},{0,1},{10,8},{12,10},{14... | collective-permute-start | bytes 1572872 | tf_op jit(solution)/shard_map/ppermute | solution.py:79
  127.1 47.7 %collective-permute-start.15 = (bf16[2048,512]{1,0:T(8,128)(2,1)S(1)}, bf16[2048,512]{1,0:T(8,128)(2,1)}, u32[]{:S(2)}, u32[]{:S(2)}) collective-permute-start(bf16[2048,512]{1,0:T(8,128)(2,1)S(1)} %get-tuple-element.42.refs_0_), channel_id=1, source_target_pairs={{0,16},{8,24},{16,0},{24,8},{1,17},{9,25},{17,1},{25,9},{2,18},{10... | collective-permute-start | bytes 6291464 | tf_op jit(solution)/shard_map/ppermute | solution.py:23
  138.2 7.6 %collective-permute-start.12 = (bf16[2048,256]{1,0:T(8,128)(2,1)}, bf16[2048,256]{1,0:T(8,128)(2,1)S(1)}, u32[]{:S(2)}, u32[]{:S(2)}) collective-permute-start(bf16[2048,256]{1,0:T(8,128)(2,1)} %copy_bitcast_fusion.refs_0_), channel_id=1, source_target_pairs={{0,8},{8,0},{16,24},{24,16},{1,9},{9,1},{17,25},{25,17},{2,10},{10... | collective-permute-start | bytes 3145736 | tf_op jit(solution)/shard_map/ppermute | solution.py:23
  145.8 39.0 %collective-permute-start.14 = (bf16[2048,512]{1,0:T(8,128)(2,1)S(1)}, bf16[2048,512]{1,0:T(8,128)(2,1)}, u32[]{:S(2)}, u32[]{:S(2)}) collective-permute-start(bf16[2048,512]{1,0:T(8,128)(2,1)S(1)} %get-tuple-element.42.refs_0_), channel_id=1, source_target_pairs={{0,8},{8,0},{16,24},{24,16},{1,9},{9,1},{17,25},{25,17},{2,10},{10... | collective-permute-start | bytes 6291464 | tf_op jit(solution)/shard_map/ppermute | solution.py:23
  174.8 10.0 %collective-permute-start.16 = (bf16[2048,512]{1,0:T(8,128)(2,1)}, bf16[2048,512]{1,0:T(8,128)(2,1)}, u32[]{:S(2)}, u32[]{:S(2)}) collective-permute-start(bf16[2048,512]{1,0:T(8,128)(2,1)} %collective-permute-done.15.refs_2_), channel_id=1, source_target_pairs={{0,8},{8,0},{16,24},{24,16},{1,9},{9,1},{17,25},{25,17},{2,10},{10... | collective-permute-start | bytes 6291464 | tf_op jit(solution)/shard_map/ppermute | solution.py:23
  174.8 8.7 %collective-permute-start.18 = (bf16[512,256]{1,0:T(8,128)(2,1)S(1)}, bf16[512,256]{1,0:T(8,128)(2,1)S(1)}, u32[]{:S(2)}, u32[]{:S(2)}) collective-permute-start(bf16[512,256]{1,0:T(8,128)(2,1)S(1)} %copy-done.2), channel_id=1, source_target_pairs={{0,16},{8,24},{16,0},{24,8},{1,17},{9,25},{17,1},{25,9},{2,18},{10... | collective-permute-start | bytes 786440 | tf_op jit(solution)/shard_map/ppermute | solution.py:23
  180.5 14.3 %collective-permute-start.17 = (bf16[512,256]{1,0:T(8,128)(2,1)S(1)}, bf16[512,256]{1,0:T(8,128)(2,1)S(1)}, u32[]{:S(2)}, u32[]{:S(2)}) collective-permute-start(bf16[512,256]{1,0:T(8,128)(2,1)S(1)} %copy-done.2), channel_id=1, source_target_pairs={{0,8},{8,0},{16,24},{24,16},{1,9},{9,1},{17,25},{25,17},{2,10},{10... | collective-permute-start | bytes 786440 | tf_op jit(solution)/shard_map/ppermute | solution.py:23
  183.5 54.6 %collective-permute-start.29 = (bf16[2048,512]{1,0:T(8,128)(2,1)}, bf16[2048,512]{1,0:T(8,128)(2,1)}, u32[]{:S(2)}, u32[]{:S(2)}) collective-permute-start(bf16[2048,512]{1,0:T(8,128)(2,1)} %get-tuple-element.52.refs_0_), channel_id=1, source_target_pairs={{0,16},{8,24},{16,0},{24,8},{1,17},{9,25},{17,1},{25,9},{2,18},{10... | collective-permute-start | bytes 6291464 | tf_op jit(solution)/shard_map/ppermute | solution.py:23
  184.7 10.1 %collective-permute-start.19 = (bf16[512,256]{1,0:T(8,128)(2,1)S(1)}, bf16[512,256]{1,0:T(8,128)(2,1)S(1)}, u32[]{:S(2)}, u32[]{:S(2)}) collective-permute-start(bf16[512,256]{1,0:T(8,128)(2,1)S(1)} %collective-permute-done.18.refs_4_), channel_id=1, source_target_pairs={{0,8},{8,0},{16,24},{24,16},{1,9},{9,1},{17,25},{25,17},{2,10},{10... | collective-permute-start | bytes 786440 | tf_op jit(solution)/shard_map/ppermute | solution.py:23
  209.9 22.0 %collective-permute-start.20 = (bf16[512,1024]{1,0:T(8,128)(2,1)S(1)}, bf16[512,1024]{1,0:T(8,128)(2,1)S(1)}, u32[]{:S(2)}, u32[]{:S(2)}) collective-permute-start(bf16[512,1024]{1,0:T(8,128)(2,1)S(1)} %shard_map.67), channel_id=1, source_target_pairs={{0,2},{2,4},{4,6},{6,7},{7,5},{5,3},{3,1},{1,0},{8,10},{10,12},{12... | collective-permute-start | bytes 3145736 | tf_op jit(solution)/shard_map/ppermute | solution.py:78
  210.2 22.1 %collective-permute-start.21 = (bf16[512,1024]{1,0:T(8,128)(2,1)S(1)}, bf16[512,1024]{1,0:T(8,128)(2,1)S(1)}, u32[]{:S(2)}, u32[]{:S(2)}) collective-permute-start(bf16[512,1024]{1,0:T(8,128)(2,1)S(1)} %shard_map.67), channel_id=1, source_target_pairs={{2,0},{4,2},{6,4},{7,6},{5,7},{3,5},{1,3},{0,1},{10,8},{12,10},{14... | collective-permute-start | bytes 3145736 | tf_op jit(solution)/shard_map/ppermute | solution.py:79
  232.3 22.7 %collective-permute-start.22 = (bf16[512,1024]{1,0:T(8,128)(2,1)S(1)}, bf16[512,1024]{1,0:T(8,128)(2,1)S(1)}, u32[]{:S(2)}, u32[]{:S(2)}) collective-permute-start(bf16[512,1024]{1,0:T(8,128)(2,1)S(1)} %collective-permute-done.20), channel_id=1, source_target_pairs={{0,2},{2,4},{4,6},{6,7},{7,5},{5,3},{3,1},{1,0},{8,10},{10,12},{12... | collective-permute-start | bytes 3145736 | tf_op jit(solution)/shard_map/ppermute | solution.py:78
  232.3 23.3 %collective-permute-start.23 = (bf16[512,1024]{1,0:T(8,128)(2,1)S(1)}, bf16[512,1024]{1,0:T(8,128)(2,1)S(1)}, u32[]{:S(2)}, u32[]{:S(2)}) collective-permute-start(bf16[512,1024]{1,0:T(8,128)(2,1)S(1)} %collective-permute-done.21), channel_id=1, source_target_pairs={{2,0},{4,2},{6,4},{7,6},{5,7},{3,5},{1,3},{0,1},{10,8},{12,10},{14... | collective-permute-start | bytes 3145736 | tf_op jit(solution)/shard_map/ppermute | solution.py:79
  234.4 63.4 %collective-permute-start.32 = (bf16[2048,512]{1,0:T(8,128)(2,1)}, bf16[2048,512]{1,0:T(8,128)(2,1)}, u32[]{:S(2)}, u32[]{:S(2)}) collective-permute-start(bf16[2048,512]{1,0:T(8,128)(2,1)} %get-tuple-element.52.refs_0_), channel_id=1, source_target_pairs={{0,8},{8,0},{16,24},{24,16},{1,9},{9,1},{17,25},{25,17},{2,10},{10... | collective-permute-start | bytes 6291464 | tf_op jit(solution)/shard_map/ppermute | solution.py:23
  238.1 70.2 %collective-permute-start.28 = (bf16[2048,512]{1,0:T(8,128)(2,1)S(1)}, bf16[2048,512]{1,0:T(8,128)(2,1)}, u32[]{:S(2)}, u32[]{:S(2)}) collective-permute-start(bf16[2048,512]{1,0:T(8,128)(2,1)S(1)} %copy-done.4), channel_id=1, source_target_pairs={{0,8},{8,0},{16,24},{24,16},{1,9},{9,1},{17,25},{25,17},{2,10},{10... | collective-permute-start | bytes 6291464 | tf_op jit(solution)/shard_map/ppermute | solution.py:23
  238.1 59.5 %collective-permute-start.30 = (bf16[2048,512]{1,0:T(8,128)(2,1)S(1)}, bf16[2048,512]{1,0:T(8,128)(2,1)}, u32[]{:S(2)}, u32[]{:S(2)}) collective-permute-start(bf16[2048,512]{1,0:T(8,128)(2,1)S(1)} %copy-done.4), channel_id=1, source_target_pairs={{0,16},{8,24},{16,0},{24,8},{1,17},{9,25},{17,1},{25,9},{2,18},{10... | collective-permute-start | bytes 6291464 | tf_op jit(solution)/shard_map/ppermute | solution.py:23
  255.7 23.7 %collective-permute-start.24 = (bf16[512,1024]{1,0:T(8,128)(2,1)S(1)}, bf16[512,1024]{1,0:T(8,128)(2,1)S(1)}, u32[]{:S(2)}, u32[]{:S(2)}) collective-permute-start(bf16[512,1024]{1,0:T(8,128)(2,1)S(1)} %collective-permute-done.22), channel_id=1, source_target_pairs={{0,2},{2,4},{4,6},{6,7},{7,5},{5,3},{3,1},{1,0},{8,10},{10,12},{12... | collective-permute-start | bytes 3145736 | tf_op jit(solution)/shard_map/ppermute | solution.py:78
  257.0 24.2 %collective-permute-start.25 = (bf16[512,1024]{1,0:T(8,128)(2,1)S(1)}, bf16[512,1024]{1,0:T(8,128)(2,1)S(1)}, u32[]{:S(2)}, u32[]{:S(2)}) collective-permute-start(bf16[512,1024]{1,0:T(8,128)(2,1)S(1)} %collective-permute-done.23), channel_id=1, source_target_pairs={{2,0},{4,2},{6,4},{7,6},{5,7},{3,5},{1,3},{0,1},{10,8},{12,10},{14... | collective-permute-start | bytes 3145736 | tf_op jit(solution)/shard_map/ppermute | solution.py:79
  281.3 13.8 %collective-permute-start.26 = (bf16[256,1024]{1,0:T(8,128)(2,1)S(1)}, bf16[256,1024]{1,0:T(8,128)(2,1)S(1)}, u32[]{:S(2)}, u32[]{:S(2)}) collective-permute-start(bf16[256,1024]{1,0:T(8,128)(2,1)S(1)} %slice.28), channel_id=1, source_target_pairs={{0,2},{2,4},{4,6},{6,7},{7,5},{5,3},{3,1},{1,0},{8,10},{10,12},{12... | collective-permute-start | bytes 1572872 | tf_op jit(solution)/shard_map/ppermute | solution.py:78
  281.5 14.5 %collective-permute-start.27 = (bf16[256,1024]{1,0:T(8,128)(2,1)S(1)}, bf16[256,1024]{1,0:T(8,128)(2,1)S(1)}, u32[]{:S(2)}, u32[]{:S(2)}) collective-permute-start(bf16[256,1024]{1,0:T(8,128)(2,1)S(1)} %slice.29), channel_id=1, source_target_pairs={{2,0},{4,2},{6,4},{7,6},{5,7},{3,5},{1,3},{0,1},{10,8},{12,10},{14... | collective-permute-start | bytes 1572872 | tf_op jit(solution)/shard_map/ppermute | solution.py:79
  297.6 10.7 %collective-permute-start.31 = (bf16[2048,512]{1,0:T(8,128)(2,1)}, bf16[2048,512]{1,0:T(8,128)(2,1)}, u32[]{:S(2)}, u32[]{:S(2)}) collective-permute-start(bf16[2048,512]{1,0:T(8,128)(2,1)} %collective-permute-done.30.refs_2_), channel_id=1, source_target_pairs={{0,8},{8,0},{16,24},{24,16},{1,9},{9,1},{17,25},{25,17},{2,10},{10... | collective-permute-start | bytes 6291464 | tf_op jit(solution)/shard_map/ppermute | solution.py:23
  (11 other events, 252.2 us)

commit v3 on v2

v3 whole, which is shorter than its diff:
```python
import functools
import math

import jax
import jax.numpy as jnp
from jax import lax
from jax.experimental import pallas as pl
from jax.experimental.pallas import tpu as pltpu
from jax.sharding import PartitionSpec as P

HD = 128
MIB = 1 << 20


def after(array, *earlier):
    if not earlier:
        return array
    return lax.optimization_barrier((array, *earlier))[0]


def swap(array, axis, mask):
    return lax.ppermute(array, axis, [(i, i ^ mask) for i in range(lax.axis_size(axis))])


def row_bits():
    return [1 << b for b in reversed(range((lax.axis_size("row")).bit_length() - 1))]


def exchange(array, *earlier):
    return swap(after(array, *earlier), "row", row_bits()[0])


def gather_near(array, *earlier):
    pieces = {0: after(array, *earlier)}
    for bit in row_bits()[1:]:
        pieces.update({j ^ bit: swap(p, "row", bit) for j, p in pieces.items()})
    return [pieces[j] for j in range(len(pieces))]


def order_pair(mine, other, col_index, bit, axis_dim):
    upper = col_index // 2**bit % 2 == 1
    lower_part = jnp.where(upper, other, mine)
    upper_part = jnp.where(upper, mine, other)
    return jnp.concatenate([lower_part, upper_part], axis=axis_dim)


def ring_order(n):
    return list(range(0, n, 2)) + list(range(1, n, 2))[::-1]


def ring_source(c, hops, n):
    at = jnp.where(c % 2 == 0, c // 2, n - 1 - c // 2)
    at = (at - hops) % n
    return jnp.where(at < n // 2, 2 * at, 2 * (n - 1 - at) + 1)


class Ring:
    def __init__(self, block):
        n = lax.axis_size("col")
        order = ring_order(n)
        self.n, self.hops = n, 0
        self.up = [(order[i], order[(i + 1) % n]) for i in range(n)]
        self.down = [(b, a) for a, b in self.up]
        self.found = [(lax.axis_index("col"), 0, block)]
        self.last = [block, block]

    def hop(self, *earlier, beside=()):
        if self.hops == self.n // 2:
            return beside
        c, own = self.found[0][0], self.found[0][2]
        rows = own.shape[0] // 2
        self.hops += 1
        end = self.hops == self.n // 2
        below, above = self.last
        if end:
            below, above = below[:rows], above[rows:]
        if earlier:
            below, above = lax.optimization_barrier((below, above, *earlier))[:2]
        below = lax.ppermute(below, "col", self.up)
        above = lax.ppermute(above, "col", self.down)
        below, above, *beside = lax.optimization_barrier((below, above, *beside))
        self.last = [below, above]
        self.found.append((ring_source(c, self.hops, self.n), 0, self.last[0]))
        self.found.append((ring_source(c, -self.hops, self.n), rows if end else 0, self.last[1]))
        return beside


class Panel:
    def __init__(self, slots_ref, rings, buffer, sems):
        self.slots_ref, self.rings, self.buffer, self.sems = slots_ref, rings, buffer, sems
        widths = [blocks[0].shape[1] for blocks in rings]
        self.firsts = [sum(widths[:i]) for i in range(len(rings))]

    def copy(self, ring, i):
        ref = self.rings[ring][i]
        rows, cols = ref.shape
        n = len(self.rings[ring])
        slot = self.slots_ref[i]
        first = rows if i == n - 1 else 0
        sem = n - 1 if i == n - 1 else slot
        into = self.buffer.at[slot, pl.ds(first, rows), pl.ds(self.firsts[ring], cols)]
        return pltpu.make_async_copy(ref, into, self.sems.at[ring, sem])

    def start(self):
        for ring, blocks in enumerate(self.rings):
            for i in reversed(range(len(blocks))):
                self.copy(ring, i).start()

    def wait_far(self):
        for ring, blocks in enumerate(self.rings):
            for i in (len(blocks) - 2, len(blocks) - 1):
                self.copy(ring, i).wait()

    def wait(self, k):
        for ring, blocks in enumerate(self.rings):
            rows, cols = blocks[0].shape
            into = self.buffer.at[k, :, pl.ds(self.firsts[ring], cols)]

            @pl.when(k != self.slots_ref[len(blocks) - 1])
            def _():
                pltpu.make_async_copy(blocks[0], into, self.sems.at[ring, k]).wait()


class Weights:
    def __init__(self, near, far, first, buffer, sems):
        self.near, self.far, self.first = near, far, first
        self.buffer, self.sems = buffer, sems

    def start(self, k):
        slots, depth, cols = self.buffer.shape
        per = slots // (len(self.near) + len(self.far))
        p, rows = k // per, pl.ds(k % per * depth, depth)
        if p < len(self.near):
            sources = [self.near[p].at[rows, pl.ds(self.first, cols)]]
        else:
            sources = [ref.at[rows, :] for ref in self.far[p - len(self.near)]]
        at = 0
        for source in sources:
            wide = source.shape[1]
            into = self.buffer.at[k, :, pl.ds(at, wide)]
            pltpu.make_async_copy(source, into, self.sems.at[k]).start()
            at += wide

    def wait(self, k):
        into = self.buffer.at[k]
        pltpu.make_async_copy(into, into, self.sems.at[k]).wait()


def multiply(panel, weights, acc):
    slots = weights.buffer.shape[0]
    panel.start()
    for k in range(slots):
        weights.start(k)
    acc[...] = jnp.zeros_like(acc)
    panel.wait_far()

    def body(k, carry):
        panel.wait(k)
        weights.wait(k)
        acc[...] += jnp.dot(
            panel.buffer[k], weights.buffer[k], preferred_element_type=jnp.float32
        )
        return carry

    lax.fori_loop(0, slots, body, 0)


def take(refs, *counts):
    out, at = [], 0
    for n in counts:
        out.append(refs[at : at + n])
        at += n
    return *out, refs[at:]


def stacked_weights(refs, near, far, first, buffer, sems):
    chunks = (len(refs) - near) // far
    return Weights(
        refs[:near],
        [refs[near + i * chunks : near + (i + 1) * chunks] for i in range(far)],
        first,
        buffer,
        sems,
    )


def project_kernel(n_blocks, near, far, count, first, heads, factor, slots_ref, *refs):
    blocks, weights, (scale_ref, cos_ref, sin_ref), rest = take(refs, n_blocks, count, 3)
    o_ref, w_buf, acc, panel_buf, panel_sem, sems = rest
    panel = Panel(slots_ref, [blocks], panel_buf, panel_sem)
    multiply(panel, stacked_weights(weights, near, far, first, w_buf, sems), acc)
    scale = scale_ref[...] * factor
    for h in range(acc.shape[1] // HD):
        at = pl.ds(h * HD, HD)
        x = acc[:, at] * scale
        if h < heads:
            x = x * cos_ref[...] + pltpu.roll(x, HD // 2, 1) * sin_ref[...]
        o_ref[:, at] = x.astype(o_ref.dtype)


def project(found, slots, near, far, first, heads, factor, scale, cos, sin):
    blocks = [piece for _, _, piece in found]
    tok, depth = blocks[0].shape
    count = len(blocks) - 1
    weights = [*near, *[w for chunks in far for w in chunks]]
    cols = sum(w.shape[1] for w in far[0])
    hbm = pl.BlockSpec(memory_space=pl.ANY)
    vmem = pl.BlockSpec(memory_space=pltpu.VMEM)
    return pl.pallas_call(
        functools.partial(
            project_kernel, len(blocks), len(near), len(far), len(weights), first, heads, factor
        ),
        in_specs=[pl.BlockSpec(memory_space=pltpu.SMEM)]
        + [hbm] * (len(blocks) + len(weights))
        + [vmem] * 3,
        out_specs=vmem,
        out_shape=jax.ShapeDtypeStruct((tok, cols), jnp.bfloat16),
        scratch_shapes=[
            pltpu.VMEM((count, depth, cols), jnp.bfloat16),
            pltpu.VMEM((tok, cols), jnp.float32),
            pltpu.VMEM((count, tok, depth), jnp.bfloat16),
            pltpu.SemaphoreType.DMA((1, count + 1)),
            pltpu.SemaphoreType.DMA((count,)),
        ],
        compiler_params=pltpu.CompilerParams(vmem_limit_bytes=60 * MIB),
        cost_estimate=pl.CostEstimate(
            flops=2 * count * tok * depth * cols,
            bytes_accessed=2 * (count * depth * (tok + cols) + tok * cols),
            transcendentals=0,
        ),
    )(slots, *blocks, *weights, scale, cos, sin)


def attend_kernel(parts, chunks, pair, r_ref, *refs):
    chunk_refs, pieces = refs[:chunks], refs[chunks : chunks + parts]
    o_ref, q_ref, turned, top, total, acc = refs[chunks + parts :]
    r = r_ref[0]
    tok = q_ref.shape[0]
    step = pl.program_id(0)
    per = pl.num_programs(0) // chunks
    for i in range(chunks):

        @pl.when(step // per == i)
        def _():
            q_ref[...] = chunk_refs[i][...]

    dims = (((1,), (1,)), ((), ()))

    @pl.when(step == 0)
    def _():
        for j in range(parts):
            turned[j] = pieces[j][:, HD:].T

    def scores(j, g):
        return lax.dot_general(
            pieces[j][:, :HD],
            q_ref[:, g * HD : (g + 1) * HD],
            dims,
            preferred_element_type=jnp.float32,
        )

    key = lax.broadcasted_iota(jnp.int32, (tok, tok), 0)
    query = lax.broadcasted_iota(jnp.int32, (tok, tok), 1)
    for g in range(pair):
        s = jnp.where(key <= query, scores(0, g), -jnp.inf)
        m = jnp.max(s, axis=0, keepdims=True)
        p = jnp.exp2(s - m)
        top[g] = m
        total[g] = jnp.sum(p, axis=0, keepdims=True)
        acc[g] = jnp.dot(turned[0], p.astype(jnp.bfloat16), preferred_element_type=jnp.float32)
    for j in range(1, parts):

        @pl.when(jnp.bitwise_xor(r, j) < r)
        def _():
            for g in range(pair):
                s = scores(j, g)
                m = jnp.maximum(top[g], jnp.max(s, axis=0, keepdims=True))
                keep = jnp.exp2(top[g] - m)
                p = jnp.exp2(s - m)
                top[g] = m
                total[g] = total[g] * keep + jnp.sum(p, axis=0, keepdims=True)
                acc[g] = acc[g] * keep + jnp.dot(
                    turned[j], p.astype(jnp.bfloat16), preferred_element_type=jnp.float32
                )

    for g in range(pair):
        o_ref[:, g * HD : (g + 1) * HD] = (acc[g] / total[g]).T.astype(o_ref.dtype)


def attend(r, queries, pieces):
    tok, cols = queries[0].shape
    chunks, parts = len(queries), len(pieces)
    pair = 2 if cols // HD % 2 == 0 else 1
    per = cols // (HD * pair)
    heads = chunks * cols // HD

    def query_spec(i):
        return pl.BlockSpec((tok, pair * HD), lambda h, r: (0, jnp.clip(h - i * per, 0, per - 1)))

    return pl.pallas_call(
        functools.partial(attend_kernel, parts, chunks, pair),
        grid_spec=pltpu.PrefetchScalarGridSpec(
            num_scalar_prefetch=1,
            grid=(chunks * per,),
            in_specs=[query_spec(i) for i in range(chunks)]
            + [pl.BlockSpec((tok, 2 * HD), lambda h, r: (0, 0)) for _ in pieces],
            out_specs=pl.BlockSpec((tok, pair * HD), lambda h, r: (0, h)),
            scratch_shapes=[
                pltpu.VMEM((tok, pair * HD), jnp.bfloat16),
                pltpu.VMEM((parts, HD, tok), jnp.bfloat16),
                pltpu.VMEM((pair, 1, tok), jnp.float32),
                pltpu.VMEM((pair, 1, tok), jnp.float32),
                pltpu.VMEM((pair, HD, tok), jnp.float32),
            ],
        ),
        out_shape=jax.ShapeDtypeStruct((tok, chunks * cols), jnp.bfloat16),
        compiler_params=pltpu.CompilerParams(
            dimension_semantics=("arbitrary",), vmem_limit_bytes=32 * MIB
        ),
        cost_estimate=pl.CostEstimate(
            flops=4 * heads * tok * tok * parts * HD,
            bytes_accessed=4 * tok * heads * HD + parts * 4 * tok * HD,
            transcendentals=heads * tok * tok * parts,
        ),
    )(r.reshape(1), *queries, *pieces)


def finish_kernel(n_blocks, rings, near, far, count, first, slots_ref, *refs):
    blocks, weights, rest = take(refs, n_blocks * rings, count)
    o_ref, w_buf, acc, panel_buf, panel_sem, sems = rest[-6:]
    by_ring = [blocks[i * n_blocks : (i + 1) * n_blocks] for i in range(rings)]
    panel = Panel(slots_ref, by_ring, panel_buf, panel_sem)
    multiply(panel, stacked_weights(weights, near, far, first, w_buf, sems), acc)
    o_ref[...] = acc[...].astype(o_ref.dtype)


def finish(rings, slots, near, far, first, total, result=None):
    blocks = [piece for found in rings for _, _, piece in found]
    n_blocks = len(rings[0])
    tok = blocks[0].shape[0]
    depth = sum(found[0][2].shape[1] for found in rings)
    count = n_blocks - 1
    weights = [*near, *[w for chunks in far for w in chunks]]
    cols = sum(w.shape[1] for w in far[0])
    hbm = pl.BlockSpec(memory_space=pl.ANY)
    old = [] if result is None else [result]
    return pl.pallas_call(
        functools.partial(
            finish_kernel, n_blocks, len(rings), len(near), len(far), len(weights), first
        ),
        grid=(1,),
        in_specs=[pl.BlockSpec(memory_space=pltpu.SMEM)]
        + [hbm] * (len(blocks) + len(weights) + len(old)),
        out_specs=pl.BlockSpec((tok, cols), lambda i: (0, first // cols)),
        out_shape=jax.ShapeDtypeStruct((tok, total), jnp.bfloat16),
        input_output_aliases={1 + len(blocks) + len(weights): 0} if old else {},
        scratch_shapes=[
            pltpu.VMEM((count, depth, cols), jnp.bfloat16),
            pltpu.VMEM((tok, cols), jnp.float32),
            pltpu.VMEM((count, tok, depth), jnp.bfloat16),
            pltpu.SemaphoreType.DMA((len(rings), count + 1)),
            pltpu.SemaphoreType.DMA((count,)),
        ],
        compiler_params=pltpu.CompilerParams(vmem_limit_bytes=60 * MIB),
        cost_estimate=pl.CostEstimate(
            flops=2 * count * tok * depth * cols,
            bytes_accessed=2 * (count * depth * (tok + cols) + tok * cols),
            transcendentals=0,
        ),
    )(slots, *blocks, *weights, *old)


def per_device(hidden, norm_gain, wq, wk, wv, wo):
    tok, feat = hidden.shape
    n_row, n_col = lax.axis_size("row"), lax.axis_size("col")
    r, c = lax.axis_index("row"), lax.axis_index("col")
    depth = feat * n_col
    rows = wq.shape[0]
    cols = wq.shape[1]

    kv_cols = wk.shape[1]
    group = max(1, HD // kv_cols)
    stacked = jnp.stack((wk, wv), axis=1)
    for bit in range(group.bit_length() - 1):
        other = swap(stacked, "col", 1 << bit)
        stacked = order_pair(stacked, other, c, bit, 2)
    stacked = stacked.reshape(rows, 2 * HD)

    unit = cols // HD // 4
    late = max(1, unit) * HD
    early = cols - late
    sizes = [n * HD for n in (unit, unit, unit // 2, unit - unit // 2) if n > 0] or [early]

    def early_chunk(i):
        return wq[:, sum(sizes[:i]) : sum(sizes[: i + 1])]

    per = rows // feat
    wider = hidden.astype(jnp.float32)
    gain = lax.dynamic_slice(norm_gain, (c * feat,), (feat,))
    squares = jnp.sum(wider * wider, axis=1)
    for bit in range(n_col.bit_length() - 1):
        squares += swap(squares, "col", 1 << bit)
    kv_near, q_near = gather_near(stacked), gather_near(wq)
    ring = Ring((wider * gain).astype(jnp.bfloat16))
    kv_other, squares = ring.hop(beside=[exchange(stacked), squares])
    q_other = []
    last = kv_other
    ties = [[*kv_near, *q_near], gather_near(kv_other)]
    for i in range(n_col // 2 - 1):
        beside = [exchange(early_chunk(i), last)] if i < len(sizes) else []
        beside = ring.hop(*(ties[i] if i < len(ties) else []), beside=beside)
        q_other += beside
        last = q_other[-1]
        if i == 0:
            o_near = gather_near(wo, *ring.last)
            ties.append(o_near)
    for i in range(len(q_other), len(sizes)):
        q_other.append(exchange(early_chunk(i), q_other[-1]))
    kv_far = ties[1]
    found = ring.found
    slots = jnp.stack([(source // per ^ r) * per + source % per for source, _, _ in found])
    scale = lax.rsqrt(squares / depth + 1e-05)[:, None]

    half = HD // 2
    positions = r * tok + jnp.arange(tok)
    freqs = 10000.0 ** (-jnp.arange(half).astype(jnp.float32) / half)
    angles = positions.astype(jnp.float32)[:, None] * freqs[None, :]
    cosine, sine = jnp.cos(angles), jnp.sin(angles)
    cosine = jnp.concatenate([cosine, cosine], axis=1)
    sine = jnp.concatenate([-sine, sine], axis=1)
    factor = HD ** (-0.5) * math.log2(math.e)

    kv_far = [[w] for w in kv_far]
    kv = project(found, slots, kv_near, kv_far, 0, 1, 1.0, scale, cosine, sine)
    kv_other = exchange(kv)
    last_other = exchange(wq[:, early:], kv_other)
    kv_pieces = [*gather_near(kv), *gather_near(kv_other)]
    scale = after(scale, kv)
    ended = len(q_other) - 1
    q_far = [gather_near(w, *([kv] if i == ended else [])) for i, w in enumerate(q_other)]
    q_far = list(zip(*q_far))
    queries = project(
        found, slots, q_near, q_far, 0, early // HD, factor, scale, cosine, sine
    )
    heads = attend(r, [queries], kv_pieces)

    o_other = exchange(wo[:, :early], last_other, heads)
    o_last_other = exchange(wo[:, early:], o_other)
    ring = Ring(heads)
    ring.hop()
    q_far = [[w] for w in gather_near(last_other, heads)]
    scale = after(scale, *ring.last)
    ring.hop()
    queries = project(
        found, slots, q_near, q_far, early, late // HD, factor, scale, cosine, sine
    )
    last_ring = Ring(attend(r, [queries], kv_pieces))
    for _ in range(n_col // 2):
        arrived = ring.last
        ring.hop(*last_ring.last)
        last_ring.hop(*arrived)

    rings = [ring.found, last_ring.found]
    o_far = [[w] for w in gather_near(o_other, ring.last[1])]
    result = finish(rings, slots, o_near, o_far, 0, cols)
    o_far = [[w] for w in gather_near(o_last_other, result)]
    return finish(rings, slots, o_near, o_far, early, cols, result)


def solution(mesh):
    in_specs = (
        P("row", "col"),
        P(),
        P("row", "col"),
        P("row", "col"),
        P("row", "col"),
        P("row", "col"),
    )
    out_specs = P("row", "col")
    return jax.shard_map(
        per_device, mesh=mesh, in_specs=in_specs, out_specs=out_specs, check_vma=False
    )
```

time: 318 us -> 309 us (0.972); the launches traced: 317 us -> 303 us
  blocking collectives: 52.9 us -> 0 us
  waiting for transfers between devices: 127 us -> 161 us
  local copies, waits for them, and re-layouts: 43.4 us -> 20.4 us
  starting transfers between devices: 26.4 us -> 45.5 us
  Pallas kernels: 57.5 us -> 70.3 us
  other arithmetic: 8.76 us -> 5.16 us
    psum x1 -> x0, blocking collectives: 52.9 us -> none  [per_device(): squares = lax.psum(jnp.sum(wider * wider, axis=1, keepdims=True), 'col')]
    ppermute x18 -> x25, waiting for transfers between devices: 31.7 us -> 70.2 us  [swap(): lax.ppermute(array, axis, [(i, i ^ mask) for i in range(lax.axis_size(axi...]
    dynamic_update_slice x17 -> x0, local copies, waits for them, and re-layouts: 24.6 us -> none  [put(): lax.dynamic_update_slice(into, piece[None], (slot_of(source), first, 0))]
    pallas_call x5, Pallas kernels: 43.6 us -> 56.4 us  [the longest x3 33.4 us: project(): pl.pallas_call(functools.partial(project_kernel, len(blocks), len(near),...]
    ppermute x18 -> x25, starting transfers between devices: 9.69 us -> 20.6 us  [swap(): lax.ppermute(array, axis, [(i, i ^ mask) for i in range(lax.axis_size(axi...]
    ppermute x16 -> x24, starting transfers between devices: 16.7 us -> 24.9 us  [the longest x12 15.4 us: hop(): above = lax.ppermute(above, 'col', self.down)]
    another operation x2 -> x1, local copies, waits for them, and re-layouts: 8.71 us -> 0.63 us  [per_device(): jnp.stack([(source // per ^ r) * per + source % per for source, _, _ in f...]
    unnamed x16 -> x74, local copies, waits for them, and re-layouts: 1.55 us -> 6.04 us
  transfers between devices with their start and end apart: 34 -> 49, of which waited for: 17 -> 28; matrix products, arithmetic and copies ran while one was open for 15% -> 6% of each run, Pallas kernels for 16% -> 20%
where the time goes in v3:
time: 309 us; the launch traced here: 303 us
  waiting for transfers between devices  161 us (52%)
  Pallas kernels  70.3 us (23%)
  starting transfers between devices  45.5 us (15%)
  local copies, waits for them, and re-layouts  20.4 us (7%)
  other arithmetic  5.16 us (2%)
    ppermute x12, waiting for transfers between devices, hop(): below = lax.ppermute(below, 'col', self.up)  84.3 us
    ppermute x25, waiting for transfers between devices, swap(): lax.ppermute(array, axis, [(i, i ^ mask) for i in range(lax.axis_size(axi...  70.2 us
    pallas_call x3, Pallas kernels, project(): pl.pallas_call(functools.partial(project_kernel, len(blocks), len(near),...  33.4 us
    pallas_call x2, Pallas kernels, finish(): pl.pallas_call(functools.partial(finish_kernel, n_blocks, len(rings), len...  23 us
    ppermute x25, starting transfers between devices, swap(): lax.ppermute(array, axis, [(i, i ^ mask) for i in range(lax.axis_size(axi...  20.6 us
    ppermute x12, starting transfers between devices, hop(): above = lax.ppermute(above, 'col', self.down)  15.4 us
    pallas_call x2, Pallas kernels, attend(): pl.pallas_call(functools.partial(attend_kernel, parts, chunks, pair), gri...  13.9 us
    ppermute x12, starting transfers between devices, hop(): below = lax.ppermute(below, 'col', self.up)  9.52 us
  transfers between devices with their start and end apart: 49, of which 28 were waited for; matrix products, arithmetic and copies ran while one was open for 6% of the time, Pallas kernels for 20%

profile of v3, /device:TPU:2, one launch (start us, length us, event | category | flops | bytes accessed | tf_op | source)
XLA Modules:
  0.0 303.3 jit_solution(3577988273129075494)
XLA Ops:
  4.2 2.1 collective-permute-done.3
  9.9 2.6 collective-permute-start.5
  14.5 20.0 %collective-permute-done.5 = f32[512]{0:T(512)S(1)} collective-permute-done((f32[512]{0:T(512)S(1)}, f32[512]{0:T(512)S(1)}, u32[]{:S(2)}, u32[]{:S(2)}) %collective-permute-start.5) | collective-permute-done | bytes 2080 | tf_op jit(solution)/shard_map/ppermute | solution.py:22
  39.9 21.6 %collective-permute-done.10.refs_11_ = bf16[2048,256]{1,0:T(8,128)(2,1)} collective-permute-done((bf16[2048,256]{1,0:T(8,128)(2,1)S(1)}, bf16[2048,256]{1,0:T(8,128)(2,1)}, u32[]{:S(2)}, u32[]{:S(2)}) %collective-permute-start.10) | collective-permute-done | bytes 1048608 | tf_op jit(solution)/shard_map/ppermute | solution.py:22
  63.0 8.1 %collective-permute-done.11.refs_12_ = bf16[2048,256]{1,0:T(8,128)(2,1)S(1)} collective-permute-done((bf16[2048,256]{1,0:T(8,128)(2,1)S(1)}, bf16[2048,256]{1,0:T(8,128)(2,1)S(1)}, u32[]{:S(2)}, u32[]{:S(2)}) %collective-permute-start.11) | collective-permute-done | bytes 1048608 | tf_op jit(solution)/shard_map/ppermute | solution.py:22
  75.2 21.2 %collective-permute-done.12.refs_5_ = bf16[512,1024]{1,0:T(8,128)(2,1)S(1)} collective-permute-done((bf16[512,1024]{1,0:T(8,128)(2,1)S(1)}, bf16[512,1024]{1,0:T(8,128)(2,1)S(1)}, u32[]{:S(2)}, u32[]{:S(2)}) %collective-permute-start.12) | collective-permute-done | bytes 1048608 | tf_op jit(solution)/shard_map/ppermute | solution.py:79
  106.9 5.5 %collective-permute-done.18.refs_13_ = bf16[2048,128]{1,0:T(8,128)(2,1)} collective-permute-done((bf16[2048,128]{1,0:T(8,128)(2,1)}, bf16[2048,128]{1,0:T(8,128)(2,1)}, u32[]{:S(2)}, u32[]{:S(2)}) %collective-permute-start.18) | collective-permute-done | bytes 524320 | tf_op jit(solution)/shard_map/ppermute | solution.py:22
  112.4 2.6 collective-permute-done.16.refs_7_
  118.3 8.7 %shard_map.64.refs_1_ = bf16[512,256]{1,0:T(8,128)(2,1)} custom-call(s32[9]{0:T(128)} %stack.48.slots_ref, bf16[512,1024]{1,0:T(8,128)(2,1)} %copy-done.8, bf16[512,1024]{1,0:T(8,128)(2,1)} %copy-done.11, bf16[512,1024]{1,0:T(8,128)(2,1)} %copy-done.12, bf16[512,1024]{1,0:T(8,128)(2,1)} %copy-done.13, bf16[512,1024]{1,0:T(8,128)(2,1)} %copy-done.14, ...), custom_call_target="tpu_custom_call" | custom-call | flops 2147483648 | bytes 12845056 | tf_op jit(solution)/shard_map/pallas_call | solution.py:209
  127.0 2.6 collective-permute-start.25
  129.7 7.1 %collective-permute-done.25.refs_3_ = bf16[512,256]{1,0:T(8,128)(2,1)S(1)} collective-permute-done((bf16[512,256]{1,0:T(8,128)(2,1)}, bf16[512,256]{1,0:T(8,128)(2,1)S(1)}, u32[]{:S(2)}, u32[]{:S(2)}) %collective-permute-start.25) | collective-permute-done | bytes 262176 | tf_op jit(solution)/shard_map/ppermute | solution.py:22
  138.5 3.8 %slice.51 = bf16[2048,768]{1,0:T(8,128)(2,1)} slice(bf16[2048,1024]{1,0:T(8,128)(2,1)} %refs_18_.1), slice={[0:2048], [0:768]} | slice | bytes 6291456 | tf_op jit(solution)/shard_map/slice | solution.py:447
  144.5 16.2 %shard_map.65.refs_0_ = bf16[512,768]{1,0:T(8,128)(2,1)} custom-call(s32[9]{0:T(128)} %stack.48.slots_ref, bf16[512,1024]{1,0:T(8,128)(2,1)} %copy-done.8, bf16[512,1024]{1,0:T(8,128)(2,1)} %copy-done.11, bf16[512,1024]{1,0:T(8,128)(2,1)} %copy-done.12, bf16[512,1024]{1,0:T(8,128)(2,1)} %copy-done.13, bf16[512,1024]{1,0:T(8,128)(2,1)} %copy-done.14, ...), custom_call_target="tpu_custom_call" | custom-call | flops 6442450944 | bytes 21757952 | tf_op jit(solution)/shard_map/pallas_call | solution.py:209
  161.9 10.5 %shard_map.66.refs_0_ = bf16[512,768]{1,0:T(8,128)(2,1)S(1)} custom-call(s32[1]{0:T(128)} %bitcast.9.r_ref, bf16[512,768]{1,0:T(8,128)(2,1)S(1)} %copy-done.2, bf16[512,256]{1,0:T(8,128)(2,1)S(1)} %copy-done.4, bf16[512,256]{1,0:T(8,128)(2,1)S(1)} %collective-permute-done.24.refs_2_, bf16[512,256]{1,0:T(8,128)(2,1)S(1)} %collective-permute-done.25.refs_3_, ...), custom_call_target="tpu_custom_call" | custom-call | flops 3221225472 | bytes 2621440 | tf_op jit(solution)/shard_map/pallas_call | solution.py:300
  172.5 2.3 collective-permute-start.27
  174.9 2.5 collective-permute-start.32
  177.4 14.2 %collective-permute-done.27.refs_1_ = bf16[512,768]{1,0:T(8,128)(2,1)S(1)} collective-permute-done((bf16[512,768]{1,0:T(8,128)(2,1)S(1)}, bf16[512,768]{1,0:T(8,128)(2,1)S(1)}, u32[]{:S(2)}, u32[]{:S(2)}) %collective-permute-start.27) | collective-permute-done | bytes 786464 | tf_op jit(solution)/shard_map/ppermute | solution.py:79
  191.5 2.1 collective-permute-done.28.refs_2_
  196.6 8.5 %shard_map.67.refs_0_ = bf16[512,256]{1,0:T(8,128)(2,1)} custom-call(s32[9]{0:T(128)} %stack.48.slots_ref, bf16[512,1024]{1,0:T(8,128)(2,1)} %copy-done.8, bf16[512,1024]{1,0:T(8,128)(2,1)} %copy-done.11, bf16[512,1024]{1,0:T(8,128)(2,1)} %copy-done.12, bf16[512,1024]{1,0:T(8,128)(2,1)} %copy-done.13, bf16[512,1024]{1,0:T(8,128)(2,1)} %copy-done.14, ...), custom_call_target="tpu_custom_call" | custom-call | flops 2147483648 | bytes 12845056 | tf_op jit(solution)/shard_map/pallas_call | solution.py:209
  206.1 3.4 %shard_map.68.refs_9_ = bf16[512,256]{1,0:T(8,128)(2,1)S(1)} custom-call(s32[1]{0:T(128)} %bitcast.9.r_ref, bf16[512,256]{1,0:T(8,128)(2,1)S(1)} %copy-done.3, bf16[512,256]{1,0:T(8,128)(2,1)S(1)} %copy-done.4, bf16[512,256]{1,0:T(8,128)(2,1)S(1)} %collective-permute-done.24.refs_2_, bf16[512,256]{1,0:T(8,128)(2,1)S(1)} %collective-permute-done.25.refs_3_, ...), custom_call_target="tpu_custom_call" | custom-call | flops 1073741824 | bytes 1572864 | tf_op jit(solution)/shard_map/pallas_call | solution.py:300
  209.4 3.9 %collective-permute-done.29.refs_3_ = bf16[512,768]{1,0:T(8,128)(2,1)} collective-permute-done((bf16[512,768]{1,0:T(8,128)(2,1)S(1)}, bf16[512,768]{1,0:T(8,128)(2,1)}, u32[]{:S(2)}, u32[]{:S(2)}) %collective-permute-start.29) | collective-permute-done | bytes 786464 | tf_op jit(solution)/shard_map/ppermute | solution.py:79
  213.3 2.2 collective-permute-done.30.refs_4_
  219.6 21.8 %collective-permute-done.35.refs_10_ = bf16[512,256]{1,0:T(8,128)(2,1)S(1)} collective-permute-done((bf16[512,256]{1,0:T(8,128)(2,1)S(1)}, bf16[512,256]{1,0:T(8,128)(2,1)S(1)}, u32[]{:S(2)}, u32[]{:S(2)}) %collective-permute-start.35) | collective-permute-done | bytes 262176 | tf_op jit(solution)/shard_map/ppermute | solution.py:79
  243.6 8.9 %collective-permute-done.37.refs_7_ = bf16[256,768]{1,0:T(8,128)(2,1)S(1)} collective-permute-done((bf16[256,768]{1,0:T(8,128)(2,1)S(1)}, bf16[256,768]{1,0:T(8,128)(2,1)S(1)}, u32[]{:S(2)}, u32[]{:S(2)}) %collective-permute-start.37) | collective-permute-done | bytes 393248 | tf_op jit(solution)/shard_map/ppermute | solution.py:79
  254.7 2.3 slice.50
  257.0 2.1 collective-permute-start.46
  259.1 2.2 collective-permute-done.39.refs_12_
  263.5 5.9 %collective-permute-done.41.refs_14_ = bf16[512,256]{1,0:T(8,128)(2,1)S(1)} collective-permute-done((bf16[512,256]{1,0:T(8,128)(2,1)S(1)}, bf16[512,256]{1,0:T(8,128)(2,1)S(1)}, u32[]{:S(2)}, u32[]{:S(2)}) %collective-permute-start.41) | collective-permute-done | bytes 262176 | tf_op jit(solution)/shard_map/ppermute | solution.py:79
  272.4 2.9 collective-permute-done.43.refs_16_
  276.2 14.1 %shard_map.69.refs_22_ = bf16[512,1024]{1,0:T(8,128)(2,1)} custom-call(s32[9]{0:T(128)} %stack.48.slots_ref, bf16[512,768]{1,0:T(8,128)(2,1)} %copy-done, bf16[512,768]{1,0:T(8,128)(2,1)} %copy-done.20, bf16[512,768]{1,0:T(8,128)(2,1)} %copy-done.21, bf16[512,768]{1,0:T(8,128)(2,1)} %collective-permute-done.29.refs_3_, ...), custom_call_target="tpu_custom_call" | custom-call | flops 6442450944 | bytes 21757952 | tf_op jit(solution)/shard_map/pallas_call | solution.py:347
  290.4 2.9 collective-permute-done.48.refs_21_
  294.3 8.9 %shard_map.70 = bf16[512,1024]{1,0:T(8,128)(2,1)} custom-call(s32[9]{0:T(128)} %stack.48.slots_ref, bf16[512,768]{1,0:T(8,128)(2,1)} %copy-done, bf16[512,768]{1,0:T(8,128)(2,1)} %copy-done.20, bf16[512,768]{1,0:T(8,128)(2,1)} %copy-done.21, bf16[512,768]{1,0:T(8,128)(2,1)} %collective-permute-done.29.refs_3_, ...), custom_call_target="tpu_custom_call", output_to_operand_aliasing={{}: (23, {})} | custom-call | flops 2147483648 | bytes 12845056 | tf_op jit(solution)/shard_map/pallas_call | solution.py:347
  (172 shorter events, 59.0 us)
Async XLA Ops:
  0.0 37.8 %collective-permute-start.7 = (bf16[2048,1024]{1,0:T(8,128)(2,1)}, bf16[2048,1024]{1,0:T(8,128)(2,1)}, u32[]{:S(2)}, u32[]{:S(2)}) collective-permute-start(bf16[2048,1024]{1,0:T(8,128)(2,1)} %refs_9_.3), channel_id=1, source_target_pairs={{0,8},{8,0},{16,24},{24,16},{1,9},{9,1},{17,25},{25,17},{2,10},{10... | collective-permute-start | bytes 12582920 | tf_op jit(solution)/shard_map/ppermute | solution.py:22
  7.9 27.8 %collective-permute-start = (bf16[512,1024]{1,0:T(8,128)(2,1)S(1)}, bf16[512,1024]{1,0:T(8,128)(2,1)S(1)}, u32[]{:S(2)}, u32[]{:S(2)}) collective-permute-start(bf16[512,1024]{1,0:T(8,128)(2,1)S(1)} %get-tuple-element.133.refs_0_), channel_id=1, source_target_pairs={{0,2},{2,4},{4,6},{6,7},{7,5},{5,3},{3,1},{1,0},{8,10},{10,12},{12... | collective-permute-start | bytes 3145736 | tf_op jit(solution)/shard_map/ppermute | solution.py:79
  8.3 27.4 %collective-permute-start.1 = (bf16[512,1024]{1,0:T(8,128)(2,1)S(1)}, bf16[512,1024]{1,0:T(8,128)(2,1)S(1)}, u32[]{:S(2)}, u32[]{:S(2)}) collective-permute-start(bf16[512,1024]{1,0:T(8,128)(2,1)S(1)} %get-tuple-element.133.refs_0_), channel_id=1, source_target_pairs={{2,0},{4,2},{6,4},{7,6},{5,7},{3,5},{1,3},{0,1},{10,8},{12,10},{14... | collective-permute-start | bytes 3145736 | tf_op jit(solution)/shard_map/ppermute | solution.py:80
  9.9 24.5 %collective-permute-start.5 = (f32[512]{0:T(512)S(1)}, f32[512]{0:T(512)S(1)}, u32[]{:S(2)}, u32[]{:S(2)}) collective-permute-start(f32[512]{0:T(512)S(1)} %add.192), channel_id=1, source_target_pairs={{0,4},{1,5},{2,6},{3,7},{4,0},{5,1},{6,2},{7,3},{8,12},{9,13},{10,... | collective-permute-start | bytes 6152 | tf_op jit(solution)/shard_map/ppermute | solution.py:22
  13.9 23.4 %collective-permute-start.2 = (bf16[2048,256]{1,0:T(8,128)(2,1)S(1)}, bf16[2048,256]{1,0:T(8,128)(2,1)S(1)}, u32[]{:S(2)}, u32[]{:S(2)}) collective-permute-start(bf16[2048,256]{1,0:T(8,128)(2,1)S(1)} %copy_bitcast_fusion.refs_9_), channel_id=1, source_target_pairs={{0,16},{8,24},{16,0},{24,8},{1,17},{9,25},{17,1},{25,9},{2,18},{10... | collective-permute-start | bytes 3145736 | tf_op jit(solution)/shard_map/ppermute | solution.py:22
  37.2 24.3 %collective-permute-start.10 = (bf16[2048,256]{1,0:T(8,128)(2,1)S(1)}, bf16[2048,256]{1,0:T(8,128)(2,1)}, u32[]{:S(2)}, u32[]{:S(2)}) collective-permute-start(bf16[2048,256]{1,0:T(8,128)(2,1)S(1)} %get-tuple-element.71), channel_id=1, source_target_pairs={{0,16},{8,24},{16,0},{24,8},{1,17},{9,25},{17,1},{25,9},{2,18},{10... | collective-permute-start | bytes 3145736 | tf_op jit(solution)/shard_map/ppermute | solution.py:22
  37.8 24.5 %collective-permute-start.8 = (bf16[512,1024]{1,0:T(8,128)(2,1)S(1)}, bf16[512,1024]{1,0:T(8,128)(2,1)S(1)}, u32[]{:S(2)}, u32[]{:S(2)}) collective-permute-start(bf16[512,1024]{1,0:T(8,128)(2,1)S(1)} %collective-permute-done.refs_1_), channel_id=1, source_target_pairs={{0,2},{2,4},{4,6},{6,7},{7,5},{5,3},{3,1},{1,0},{8,10},{10,12},{12... | collective-permute-start | bytes 3145736 | tf_op jit(solution)/shard_map/ppermute | solution.py:79
  39.1 23.5 %collective-permute-start.9 = (bf16[512,1024]{1,0:T(8,128)(2,1)S(1)}, bf16[512,1024]{1,0:T(8,128)(2,1)S(1)}, u32[]{:S(2)}, u32[]{:S(2)}) collective-permute-start(bf16[512,1024]{1,0:T(8,128)(2,1)S(1)} %collective-permute-done.1.refs_2_), channel_id=1, source_target_pairs={{2,0},{4,2},{6,4},{7,6},{5,7},{3,5},{1,3},{0,1},{10,8},{12,10},{14... | collective-permute-start | bytes 3145736 | tf_op jit(solution)/shard_map/ppermute | solution.py:80
  62.5 38.0 %collective-permute-start.15 = (bf16[2048,1024]{1,0:T(8,128)(2,1)S(1)}, bf16[2048,1024]{1,0:T(8,128)(2,1)S(1)}, u32[]{:S(2)}, u32[]{:S(2)}) collective-permute-start(bf16[2048,1024]{1,0:T(8,128)(2,1)S(1)} %copy-done.6), channel_id=1, source_target_pairs={{0,8},{8,0},{16,24},{24,16},{1,9},{9,1},{17,25},{25,17},{2,10},{10... | collective-permute-start | bytes 12582920 | tf_op jit(solution)/shard_map/ppermute | solution.py:22
  71.2 25.2 %collective-permute-start.12 = (bf16[512,1024]{1,0:T(8,128)(2,1)S(1)}, bf16[512,1024]{1,0:T(8,128)(2,1)S(1)}, u32[]{:S(2)}, u32[]{:S(2)}) collective-permute-start(bf16[512,1024]{1,0:T(8,128)(2,1)S(1)} %collective-permute-done.8.refs_3_), channel_id=1, source_target_pairs={{0,2},{2,4},{4,6},{6,7},{7,5},{5,3},{3,1},{1,0},{8,10},{10,12},{12... | collective-permute-start | bytes 3145736 | tf_op jit(solution)/shard_map/ppermute | solution.py:79
  71.6 24.9 %collective-permute-start.13 = (bf16[512,1024]{1,0:T(8,128)(2,1)S(1)}, bf16[512,1024]{1,0:T(8,128)(2,1)S(1)}, u32[]{:S(2)}, u32[]{:S(2)}) collective-permute-start(bf16[512,1024]{1,0:T(8,128)(2,1)S(1)} %collective-permute-done.9.refs_4_), channel_id=1, source_target_pairs={{2,0},{4,2},{6,4},{7,6},{5,7},{3,5},{1,3},{0,1},{10,8},{12,10},{14... | collective-permute-start | bytes 3145736 | tf_op jit(solution)/shard_map/ppermute | solution.py:80
  73.2 24.6 %collective-permute-start.14 = (bf16[2048,256]{1,0:T(8,128)(2,1)S(1)}, bf16[2048,256]{1,0:T(8,128)(2,1)S(1)}, u32[]{:S(2)}, u32[]{:S(2)}) collective-permute-start(bf16[2048,256]{1,0:T(8,128)(2,1)S(1)} %get-tuple-element.77), channel_id=1, source_target_pairs={{0,16},{8,24},{16,0},{24,8},{1,17},{9,25},{17,1},{25,9},{2,18},{10... | collective-permute-start | bytes 3145736 | tf_op jit(solution)/shard_map/ppermute | solution.py:22
  99.6 12.8 %collective-permute-start.18 = (bf16[2048,128]{1,0:T(8,128)(2,1)}, bf16[2048,128]{1,0:T(8,128)(2,1)}, u32[]{:S(2)}, u32[]{:S(2)}) collective-permute-start(bf16[2048,128]{1,0:T(8,128)(2,1)} %get-tuple-element.84), channel_id=1, source_target_pairs={{0,16},{8,24},{16,0},{24,8},{1,17},{9,25},{17,1},{25,9},{2,18},{10... | collective-permute-start | bytes 1572872 | tf_op jit(solution)/shard_map/ppermute | solution.py:22
  106.4 36.8 %collective-permute-start.20 = (bf16[2048,256]{1,0:T(8,128)(2,1)}, bf16[2048,256]{1,0:T(8,128)(2,1)}, u32[]{:S(2)}, u32[]{:S(2)}) collective-permute-start(bf16[2048,256]{1,0:T(8,128)(2,1)} %collective-permute-done.10.refs_11_), channel_id=1, source_target_pairs={{0,8},{8,0},{16,24},{24,16},{1,9},{9,1},{17,25},{25,17},{2,10},{10... | collective-permute-start | bytes 3145736 | tf_op jit(solution)/shard_map/ppermute | solution.py:22
  106.4 36.7 %collective-permute-start.21 = (bf16[2048,256]{1,0:T(8,128)(2,1)}, bf16[2048,256]{1,0:T(8,128)(2,1)}, u32[]{:S(2)}, u32[]{:S(2)}) collective-permute-start(bf16[2048,256]{1,0:T(8,128)(2,1)} %copy-done.34), channel_id=1, source_target_pairs={{0,8},{8,0},{16,24},{24,16},{1,9},{9,1},{17,25},{25,17},{2,10},{10... | collective-permute-start | bytes 3145736 | tf_op jit(solution)/shard_map/ppermute | solution.py:22
  118.2 25.4 %collective-permute-start.22 = (bf16[2048,128]{1,0:T(8,128)(2,1)}, bf16[2048,128]{1,0:T(8,128)(2,1)}, u32[]{:S(2)}, u32[]{:S(2)}) collective-permute-start(bf16[2048,128]{1,0:T(8,128)(2,1)} %collective-permute-done.18.refs_13_), channel_id=1, source_target_pairs={{0,8},{8,0},{16,24},{24,16},{1,9},{9,1},{17,25},{25,17},{2,10},{10... | collective-permute-start | bytes 1572872 | tf_op jit(solution)/shard_map/ppermute | solution.py:22
  127.0 16.7 %collective-permute-start.23 = (bf16[2048,128]{1,0:T(8,128)(2,1)}, bf16[2048,128]{1,0:T(8,128)(2,1)S(1)}, u32[]{:S(2)}, u32[]{:S(2)}) collective-permute-start(bf16[2048,128]{1,0:T(8,128)(2,1)} %collective-permute-done.19.refs_14_), channel_id=1, source_target_pairs={{0,8},{8,0},{16,24},{24,16},{1,9},{9,1},{17,25},{25,17},{2,10},{10... | collective-permute-start | bytes 1572872 | tf_op jit(solution)/shard_map/ppermute | solution.py:22
  136.8 35.7 %collective-permute-start.31 = (bf16[2048,256]{1,0:T(8,128)(2,1)}, bf16[2048,256]{1,0:T(8,128)(2,1)}, u32[]{:S(2)}, u32[]{:S(2)}) collective-permute-start(bf16[2048,256]{1,0:T(8,128)(2,1)} %get-tuple-element.96), channel_id=1, source_target_pairs={{0,16},{8,24},{16,0},{24,8},{1,17},{9,25},{17,1},{25,9},{2,18},{10... | collective-permute-start | bytes 3145736 | tf_op jit(solution)/shard_map/ppermute | solution.py:22
  143.2 17.6 %collective-permute-start.24 = (bf16[512,256]{1,0:T(8,128)(2,1)S(1)}, bf16[512,256]{1,0:T(8,128)(2,1)S(1)}, u32[]{:S(2)}, u32[]{:S(2)}) collective-permute-start(bf16[512,256]{1,0:T(8,128)(2,1)S(1)} %copy-done.4), channel_id=1, source_target_pairs={{0,8},{8,0},{16,24},{24,16},{1,9},{9,1},{17,25},{25,17},{2,10},{10... | collective-permute-start | bytes 786440 | tf_op jit(solution)/shard_map/ppermute | solution.py:22
  143.2 17.6 %collective-permute-start.26 = (bf16[512,256]{1,0:T(8,128)(2,1)S(1)}, bf16[512,256]{1,0:T(8,128)(2,1)S(1)}, u32[]{:S(2)}, u32[]{:S(2)}) collective-permute-start(bf16[512,256]{1,0:T(8,128)(2,1)S(1)} %collective-permute-done.25.refs_3_), channel_id=1, source_target_pairs={{0,8},{8,0},{16,24},{24,16},{1,9},{9,1},{17,25},{25,17},{2,10},{10... | collective-permute-start | bytes 786440 | tf_op jit(solution)/shard_map/ppermute | solution.py:22
  172.4 80.2 %collective-permute-start.45 = (bf16[2048,768]{1,0:T(8,128)(2,1)}, bf16[2048,768]{1,0:T(8,128)(2,1)}, u32[]{:S(2)}, u32[]{:S(2)}) collective-permute-start(bf16[2048,768]{1,0:T(8,128)(2,1)} %slice.51), channel_id=1, source_target_pairs={{0,16},{8,24},{16,0},{24,8},{1,17},{9,25},{17,1},{25,9},{2,18},{10... | collective-permute-start | bytes 9437192 | tf_op jit(solution)/shard_map/ppermute | solution.py:22
  172.5 19.0 %collective-permute-start.27 = (bf16[512,768]{1,0:T(8,128)(2,1)S(1)}, bf16[512,768]{1,0:T(8,128)(2,1)S(1)}, u32[]{:S(2)}, u32[]{:S(2)}) collective-permute-start(bf16[512,768]{1,0:T(8,128)(2,1)S(1)} %shard_map.66.refs_0_), channel_id=1, source_target_pairs={{0,2},{2,4},{4,6},{6,7},{7,5},{5,3},{3,1},{1,0},{8,10},{10,12},{12... | collective-permute-start | bytes 2359304 | tf_op jit(solution)/shard_map/ppermute | solution.py:79
  174.9 18.8 %collective-permute-start.28 = (bf16[512,768]{1,0:T(8,128)(2,1)S(1)}, bf16[512,768]{1,0:T(8,128)(2,1)S(1)}, u32[]{:S(2)}, u32[]{:S(2)}) collective-permute-start(bf16[512,768]{1,0:T(8,128)(2,1)S(1)} %shard_map.66.refs_0_), channel_id=1, source_target_pairs={{2,0},{4,2},{6,4},{7,6},{5,7},{3,5},{1,3},{0,1},{10,8},{12,10},{14... | collective-permute-start | bytes 2359304 | tf_op jit(solution)/shard_map/ppermute | solution.py:80
  174.9 21.7 %collective-permute-start.32 = (bf16[2048,256]{1,0:T(8,128)(2,1)}, bf16[2048,256]{1,0:T(8,128)(2,1)}, u32[]{:S(2)}, u32[]{:S(2)}) collective-permute-start(bf16[2048,256]{1,0:T(8,128)(2,1)} %collective-permute-done.31.refs_11_), channel_id=1, source_target_pairs={{0,8},{8,0},{16,24},{24,16},{1,9},{9,1},{17,25},{25,17},{2,10},{10... | collective-permute-start | bytes 3145736 | tf_op jit(solution)/shard_map/ppermute | solution.py:22
  193.7 19.7 %collective-permute-start.29 = (bf16[512,768]{1,0:T(8,128)(2,1)S(1)}, bf16[512,768]{1,0:T(8,128)(2,1)}, u32[]{:S(2)}, u32[]{:S(2)}) collective-permute-start(bf16[512,768]{1,0:T(8,128)(2,1)S(1)} %collective-permute-done.27.refs_1_), channel_id=1, source_target_pairs={{0,2},{2,4},{4,6},{6,7},{7,5},{5,3},{3,1},{1,0},{8,10},{10,12},{12... | collective-permute-start | bytes 2359304 | tf_op jit(solution)/shard_map/ppermute | solution.py:79
  195.5 20.1 %collective-permute-start.30 = (bf16[512,768]{1,0:T(8,128)(2,1)S(1)}, bf16[512,768]{1,0:T(8,128)(2,1)}, u32[]{:S(2)}, u32[]{:S(2)}) collective-permute-start(bf16[512,768]{1,0:T(8,128)(2,1)S(1)} %collective-permute-done.28.refs_2_), channel_id=1, source_target_pairs={{2,0},{4,2},{6,4},{7,6},{5,7},{3,5},{1,3},{0,1},{10,8},{12,10},{14... | collective-permute-start | bytes 2359304 | tf_op jit(solution)/shard_map/ppermute | solution.py:80
  215.6 25.8 %collective-permute-start.33 = (bf16[512,768]{1,0:T(8,128)(2,1)}, bf16[512,768]{1,0:T(8,128)(2,1)S(1)}, u32[]{:S(2)}, u32[]{:S(2)}) collective-permute-start(bf16[512,768]{1,0:T(8,128)(2,1)} %collective-permute-done.29.refs_3_), channel_id=1, source_target_pairs={{0,2},{2,4},{4,6},{6,7},{7,5},{5,3},{3,1},{1,0},{8,10},{10,12},{12... | collective-permute-start | bytes 2359304 | tf_op jit(solution)/shard_map/ppermute | solution.py:79
  215.6 25.8 %collective-permute-start.34 = (bf16[512,768]{1,0:T(8,128)(2,1)}, bf16[512,768]{1,0:T(8,128)(2,1)S(1)}, u32[]{:S(2)}, u32[]{:S(2)}) collective-permute-start(bf16[512,768]{1,0:T(8,128)(2,1)} %collective-permute-done.30.refs_4_), channel_id=1, source_target_pairs={{2,0},{4,2},{6,4},{7,6},{5,7},{3,5},{1,3},{0,1},{10,8},{12,10},{14... | collective-permute-start | bytes 2359304 | tf_op jit(solution)/shard_map/ppermute | solution.py:80
  217.6 23.8 %collective-permute-start.35 = (bf16[512,256]{1,0:T(8,128)(2,1)S(1)}, bf16[512,256]{1,0:T(8,128)(2,1)S(1)}, u32[]{:S(2)}, u32[]{:S(2)}) collective-permute-start(bf16[512,256]{1,0:T(8,128)(2,1)S(1)} %shard_map.68.refs_9_), channel_id=1, source_target_pairs={{0,2},{2,4},{4,6},{6,7},{7,5},{5,3},{3,1},{1,0},{8,10},{10,12},{12... | collective-permute-start | bytes 786440 | tf_op jit(solution)/shard_map/ppermute | solution.py:79
  217.6 23.8 %collective-permute-start.36 = (bf16[512,256]{1,0:T(8,128)(2,1)S(1)}, bf16[512,256]{1,0:T(8,128)(2,1)S(1)}, u32[]{:S(2)}, u32[]{:S(2)}) collective-permute-start(bf16[512,256]{1,0:T(8,128)(2,1)S(1)} %shard_map.68.refs_9_), channel_id=1, source_target_pairs={{2,0},{4,2},{6,4},{7,6},{5,7},{3,5},{1,3},{0,1},{10,8},{12,10},{14... | collective-permute-start | bytes 786440 | tf_op jit(solution)/shard_map/ppermute | solution.py:80
  252.6 23.5 %collective-permute-start.47 = (bf16[2048,768]{1,0:T(8,128)(2,1)}, bf16[2048,768]{1,0:T(8,128)(2,1)}, u32[]{:S(2)}, u32[]{:S(2)}) collective-permute-start(bf16[2048,768]{1,0:T(8,128)(2,1)} %collective-permute-done.45.refs_20_), channel_id=1, source_target_pairs={{0,8},{8,0},{16,24},{24,16},{1,9},{9,1},{17,25},{25,17},{2,10},{10... | collective-permute-start | bytes 9437192 | tf_op jit(solution)/shard_map/ppermute | solution.py:22
  257.0 33.3 %collective-permute-start.46 = (bf16[2048,256]{1,0:T(8,128)(2,1)}, bf16[2048,256]{1,0:T(8,128)(2,1)}, u32[]{:S(2)}, u32[]{:S(2)}) collective-permute-start(bf16[2048,256]{1,0:T(8,128)(2,1)} %slice.50), channel_id=1, source_target_pairs={{0,16},{8,24},{16,0},{24,8},{1,17},{9,25},{17,1},{25,9},{2,18},{10... | collective-permute-start | bytes 3145736 | tf_op jit(solution)/shard_map/ppermute | solution.py:22
  (54 other events, 1063.8 us)

commit v4 on v3

v4 whole, which is shorter than its diff:
```python
import functools
import math

import jax
import jax.numpy as jnp
from jax import lax
from jax.experimental import pallas as pl
from jax.experimental.pallas import tpu as pltpu
from jax.sharding import PartitionSpec as P

HD = 128
MIB = 1 << 20


def after(array, *earlier):
    if not earlier:
        return array
    return lax.optimization_barrier((array, *earlier))[0]


def swap(array, axis, mask):
    return lax.ppermute(array, axis, [(i, i ^ mask) for i in range(lax.axis_size(axis))])


def row_bits():
    return [1 << b for b in reversed(range((lax.axis_size("row")).bit_length() - 1))]


def exchange(array, *earlier):
    return swap(after(array, *earlier), "row", row_bits()[0])


def gather_near(array, *earlier):
    pieces = {0: after(array, *earlier)}
    for bit in row_bits()[1:]:
        pieces.update({j ^ bit: swap(p, "row", bit) for j, p in pieces.items()})
    return [pieces[j] for j in range(len(pieces))]


def order_pair(mine, other, col_index, bit, axis_dim):
    upper = col_index // 2**bit % 2 == 1
    lower_part = jnp.where(upper, other, mine)
    upper_part = jnp.where(upper, mine, other)
    return jnp.concatenate([lower_part, upper_part], axis=axis_dim)


def ring_order(n):
    return list(range(0, n, 2)) + list(range(1, n, 2))[::-1]


def ring_source(c, hops, n):
    at = jnp.where(c % 2 == 0, c // 2, n - 1 - c // 2)
    at = (at - hops) % n
    return jnp.where(at < n // 2, 2 * at, 2 * (n - 1 - at) + 1)


class Ring:
    def __init__(self, block):
        n = lax.axis_size("col")
        order = ring_order(n)
        self.n, self.hops = n, 0
        self.up = [(order[i], order[(i + 1) % n]) for i in range(n)]
        self.down = [(b, a) for a, b in self.up]
        self.found = [(lax.axis_index("col"), 0, block)]
        self.last = [block, block]

    def hop(self, *earlier, beside=()):
        if self.hops == self.n // 2:
            return beside
        c, own = self.found[0][0], self.found[0][2]
        rows = own.shape[0] // 2
        self.hops += 1
        end = self.hops == self.n // 2
        below, above = self.last
        if end:
            below, above = below[:rows], above[rows:]
        if earlier:
            below, above = lax.optimization_barrier((below, above, *earlier))[:2]
        below = lax.ppermute(below, "col", self.up)
        above = lax.ppermute(above, "col", self.down)
        below, above, *beside = lax.optimization_barrier((below, above, *beside))
        self.last = [below, above]
        self.found.append((ring_source(c, self.hops, self.n), 0, self.last[0]))
        self.found.append((ring_source(c, -self.hops, self.n), rows if end else 0, self.last[1]))
        return beside


class Panel:
    def __init__(self, blocks, first, buffer, sems):
        self.blocks, self.first, self.buffer, self.sems = blocks, first, buffer, sems

    def start(self, i):
        n, tok, cols = self.buffer.shape
        sources = [(0, self.blocks[i])] if i < n - 1 else [(0, self.blocks[i]), (tok // 2, self.blocks[n])]
        for at, ref in sources:
            rows = ref.shape[0]
            into = self.buffer.at[i, pl.ds(at, rows), :]
            pltpu.make_async_copy(ref.at[:, pl.ds(self.first, cols)], into, self.sems.at[i]).start()

    def wait(self, i):
        into = self.buffer.at[i]
        pltpu.make_async_copy(into, into, self.sems.at[i]).wait()


class Weights:
    def __init__(self, refs, near, far, stride, first_row, first, buffer, sems):
        chunks = (len(refs) - near) // far
        self.near = refs[:near]
        self.far = [refs[near + i * chunks : near + (i + 1) * chunks] for i in range(far)]
        self.stride, self.first_row, self.first = stride, first_row, first
        self.buffer, self.sems = buffer, sems

    def start(self, i, slot):
        blocks, depth, cols = self.buffer.shape
        parts = len(self.near) + len(self.far)
        per = blocks // parts
        s = slot % per
        for p in range(parts):

            @pl.when(slot // per == p)
            def _():
                if p < len(self.near):
                    row = pl.multiple_of(s * self.stride + self.first_row, HD)
                    sources = [self.near[p].at[pl.ds(row, depth), pl.ds(self.first, cols)]]
                else:
                    row = pl.multiple_of(s * depth, HD)
                    sources = [ref.at[pl.ds(row, depth), :] for ref in self.far[p - len(self.near)]]
                at = 0
                for source in sources:
                    wide = source.shape[1]
                    into = self.buffer.at[i, :, pl.ds(at, wide)]
                    pltpu.make_async_copy(source, into, self.sems.at[i]).start()
                    at += wide

    def wait(self, i):
        into = self.buffer.at[i]
        pltpu.make_async_copy(into, into, self.sems.at[i]).wait()


def multiply(slots_ref, panel, groups):
    blocks = panel.buffer.shape[0]
    for i in range(blocks):
        panel.start(i)
        for weights, _ in groups:
            weights.start(i, slots_ref[i])

    def body(i, carry):
        panel.wait(i)
        for weights, acc in groups:
            weights.wait(i)
            acc[...] += jnp.dot(
                panel.buffer[i], weights.buffer[i], preferred_element_type=jnp.float32
            )
        return carry

    lax.fori_loop(0, blocks, body, 0)


def take(refs, *counts):
    out, at = [], 0
    for n in counts:
        out.append(refs[at : at + n])
        at += n
    return *out, refs[at:]


def project_kernel(n_blocks, plan, slots_ref, *refs):
    n = len(plan)
    blocks, weights, (scale_ref, cos_ref, sin_ref), outs, w_bufs, accs, rest = take(
        refs, n_blocks, sum(p[0] for p in plan), 3, n, n, n
    )
    panel_buf, panel_sem, sems = rest
    depth = panel_buf.shape[2]
    groups, at = [], 0
    for g, (count, near, far, first, _, _) in enumerate(plan):
        stack = Weights(
            weights[at : at + count], near, far, depth, 0, first, w_bufs[g], sems.at[g]
        )
        accs[g][...] = jnp.zeros_like(accs[g])
        groups.append((stack, accs[g]))
        at += count
    multiply(slots_ref, Panel(blocks, 0, panel_buf, panel_sem), groups)
    for acc, o_ref, (*_, heads, factor) in zip(accs, outs, plan):
        scale = scale_ref[...] * factor
        for h in range(acc.shape[1] // HD):
            at = pl.ds(h * HD, HD)
            x = acc[:, at] * scale
            if h < heads:
                x = x * cos_ref[...] + pltpu.roll(x, HD // 2, 1) * sin_ref[...]
            o_ref[:, at] = x.astype(o_ref.dtype)


def project(blocks, slots, groups, scale, cos, sin):
    tok, depth = blocks[0].shape
    count = len(blocks) - 1
    stacks = [[*near, *[w for chunks in far for w in chunks]] for near, far, *_ in groups]
    widths = [sum(w.shape[1] for w in far[0]) for _, far, *_ in groups]
    plan = [
        (len(stack), len(near), len(far), *rest)
        for stack, (near, far, *rest) in zip(stacks, groups)
    ]
    weights = [w for stack in stacks for w in stack]
    hbm = pl.BlockSpec(memory_space=pl.ANY)
    vmem = pl.BlockSpec(memory_space=pltpu.VMEM)
    return pl.pallas_call(
        functools.partial(project_kernel, len(blocks), plan),
        in_specs=[pl.BlockSpec(memory_space=pltpu.SMEM)]
        + [hbm] * (len(blocks) + len(weights))
        + [vmem] * 3,
        out_specs=[vmem] * len(groups),
        out_shape=[jax.ShapeDtypeStruct((tok, w), jnp.bfloat16) for w in widths],
        scratch_shapes=[pltpu.VMEM((count, depth, w), jnp.bfloat16) for w in widths]
        + [pltpu.VMEM((tok, w), jnp.float32) for w in widths]
        + [
            pltpu.VMEM((count, tok, depth), jnp.bfloat16),
            pltpu.SemaphoreType.DMA((count,)),
            pltpu.SemaphoreType.DMA((len(groups), count)),
        ],
        compiler_params=pltpu.CompilerParams(vmem_limit_bytes=60 * MIB),
        cost_estimate=pl.CostEstimate(
            flops=2 * count * tok * depth * sum(widths),
            bytes_accessed=2 * (count * depth * (tok + sum(widths)) + tok * sum(widths)),
            transcendentals=0,
        ),
    )(slots, *blocks, *weights, scale, cos, sin)


def attend_kernel(parts, chunks, pair, r_ref, *refs):
    chunk_refs, pieces = refs[:chunks], refs[chunks : chunks + parts]
    o_ref, q_ref, turned, top, total, acc = refs[chunks + parts :]
    r = r_ref[0]
    tok = q_ref.shape[0]
    step = pl.program_id(0)
    per = pl.num_programs(0) // chunks
    for i in range(chunks):

        @pl.when(step // per == i)
        def _():
            q_ref[...] = chunk_refs[i][...]

    dims = (((1,), (1,)), ((), ()))

    @pl.when(step == 0)
    def _():
        for j in range(parts):
            turned[j] = pieces[j][:, HD:].T

    def scores(j, g):
        return lax.dot_general(
            pieces[j][:, :HD],
            q_ref[:, g * HD : (g + 1) * HD],
            dims,
            preferred_element_type=jnp.float32,
        )

    key = lax.broadcasted_iota(jnp.int32, (tok, tok), 0)
    query = lax.broadcasted_iota(jnp.int32, (tok, tok), 1)
    for g in range(pair):
        s = jnp.where(key <= query, scores(0, g), -jnp.inf)
        m = jnp.max(s, axis=0, keepdims=True)
        p = jnp.exp2(s - m)
        top[g] = m
        total[g] = jnp.sum(p, axis=0, keepdims=True)
        acc[g] = jnp.dot(turned[0], p.astype(jnp.bfloat16), preferred_element_type=jnp.float32)
    for j in range(1, parts):

        @pl.when(jnp.bitwise_xor(r, j) < r)
        def _():
            for g in range(pair):
                s = scores(j, g)
                m = jnp.maximum(top[g], jnp.max(s, axis=0, keepdims=True))
                keep = jnp.exp2(top[g] - m)
                p = jnp.exp2(s - m)
                top[g] = m
                total[g] = total[g] * keep + jnp.sum(p, axis=0, keepdims=True)
                acc[g] = acc[g] * keep + jnp.dot(
                    turned[j], p.astype(jnp.bfloat16), preferred_element_type=jnp.float32
                )

    for g in range(pair):
        o_ref[:, g * HD : (g + 1) * HD] = (acc[g] / total[g]).T.astype(o_ref.dtype)


def attend(r, queries, pieces):
    tok, cols = queries[0].shape
    chunks, parts = len(queries), len(pieces)
    pair = 2 if cols // HD % 2 == 0 else 1
    per = cols // (HD * pair)
    heads = chunks * cols // HD

    def query_spec(i):
        return pl.BlockSpec((tok, pair * HD), lambda h, r: (0, jnp.clip(h - i * per, 0, per - 1)))

    return pl.pallas_call(
        functools.partial(attend_kernel, parts, chunks, pair),
        grid_spec=pltpu.PrefetchScalarGridSpec(
            num_scalar_prefetch=1,
            grid=(chunks * per,),
            in_specs=[query_spec(i) for i in range(chunks)]
            + [pl.BlockSpec((tok, 2 * HD), lambda h, r: (0, 0)) for _ in pieces],
            out_specs=pl.BlockSpec((tok, pair * HD), lambda h, r: (0, h)),
            scratch_shapes=[
                pltpu.VMEM((tok, pair * HD), jnp.bfloat16),
                pltpu.VMEM((parts, HD, tok), jnp.bfloat16),
                pltpu.VMEM((pair, 1, tok), jnp.float32),
                pltpu.VMEM((pair, 1, tok), jnp.float32),
                pltpu.VMEM((pair, HD, tok), jnp.float32),
            ],
        ),
        out_shape=jax.ShapeDtypeStruct((tok, chunks * cols), jnp.bfloat16),
        compiler_params=pltpu.CompilerParams(
            dimension_semantics=("arbitrary",), vmem_limit_bytes=32 * MIB
        ),
        cost_estimate=pl.CostEstimate(
            flops=4 * heads * tok * tok * parts * HD,
            bytes_accessed=4 * tok * heads * HD + parts * 4 * tok * HD,
            transcendentals=heads * tok * tok * parts,
        ),
    )(r.reshape(1), *queries, *pieces)


def finish_kernel(n_blocks, near, far, count, stride, first, column, slots_ref, *refs):
    blocks, weights, rest = take(refs, n_blocks, count)
    *old, o_ref, w_buf, panel_buf, acc, panel_sem, sems = rest
    acc[...] = old[0][...] if old else jnp.zeros_like(acc)
    stack = Weights(weights, near, far, stride, first, 0, w_buf, sems)
    multiply(slots_ref, Panel(blocks, column, panel_buf, panel_sem), [(stack, acc)])
    o_ref[...] = acc[...].astype(o_ref.dtype)


def finish(blocks, slots, column, near, far, stride, first, wide, dtype, total=None):
    tok = blocks[0].shape[0]
    count = len(blocks) - 1
    weights = [*near, *far]
    cols = near[0].shape[1]
    hbm = pl.BlockSpec(memory_space=pl.ANY)
    vmem = pl.BlockSpec(memory_space=pltpu.VMEM)
    old = [] if total is None else [total]
    return pl.pallas_call(
        functools.partial(
            finish_kernel, len(blocks), len(near), len(far), len(weights), stride, first, column
        ),
        in_specs=[pl.BlockSpec(memory_space=pltpu.SMEM)]
        + [hbm] * (len(blocks) + len(weights))
        + [vmem] * len(old),
        out_specs=vmem,
        out_shape=jax.ShapeDtypeStruct((tok, cols), dtype),
        scratch_shapes=[
            pltpu.VMEM((count, wide, cols), jnp.bfloat16),
            pltpu.VMEM((count, tok, wide), jnp.bfloat16),
            pltpu.VMEM((tok, cols), jnp.float32),
            pltpu.SemaphoreType.DMA((count,)),
            pltpu.SemaphoreType.DMA((count,)),
        ],
        compiler_params=pltpu.CompilerParams(vmem_limit_bytes=60 * MIB),
        cost_estimate=pl.CostEstimate(
            flops=2 * count * tok * wide * cols,
            bytes_accessed=2 * count * wide * (tok + cols) + 8 * tok * cols,
            transcendentals=0,
        ),
    )(slots, *blocks, *weights, *old)


def per_device(hidden, norm_gain, wq, wk, wv, wo):
    tok, feat = hidden.shape
    n_row, n_col = lax.axis_size("row"), lax.axis_size("col")
    r, c = lax.axis_index("row"), lax.axis_index("col")
    depth = feat * n_col
    rows = wq.shape[0]
    cols = wq.shape[1]

    kv_cols = wk.shape[1]
    group = max(1, HD // kv_cols)
    stacked = jnp.stack((wk, wv), axis=1)
    for bit in range(group.bit_length() - 1):
        other = swap(stacked, "col", 1 << bit)
        stacked = order_pair(stacked, other, c, bit, 2)
    stacked = stacked.reshape(rows, 2 * HD)

    n_heads = cols // HD
    first_heads = n_heads // 2
    quarter, eighth = n_heads // 4, n_heads // 8
    if eighth > 0:
        sizes = [quarter, first_heads - quarter, eighth, eighth, n_heads - first_heads - 2 * eighth]
    else:
        sizes = [first_heads, n_heads - first_heads]
    early = 2 if eighth > 0 else 1
    wide = first_heads * HD

    def chunk(i):
        return wq[:, sum(sizes[:i]) * HD : sum(sizes[: i + 1]) * HD]

    def columns(far):
        return [list(chunks) for chunks in zip(*far)]

    per = rows // feat
    wider = hidden.astype(jnp.float32)
    gain = lax.dynamic_slice(norm_gain, (c * feat,), (feat,))
    squares = jnp.sum(wider * wider, axis=1)
    for bit in range(n_col.bit_length() - 1):
        squares += swap(squares, "col", 1 << bit)
    ring = Ring((wider * gain).astype(jnp.bfloat16))
    kv_other, squares, *kv_near = ring.hop(
        beside=[exchange(stacked), squares, *gather_near(stacked)]
    )
    near = len(kv_near)
    at, q_far, pending = 0, [], None
    for i in range(n_col // 2 - 1):
        beside = []
        if i == 0:
            beside += gather_near(kv_other) + gather_near(wq)
        if i == 1:
            beside += gather_near(wo)
        if pending is not None:
            beside += gather_near(pending)
        sent = at < len(sizes) - 1
        if sent:
            beside.append(exchange(chunk(at), ring.last[0]))
        beside = ring.hop(beside=beside)
        if i == 0:
            kv_far, q_near, beside = take(beside, near, near)
        if i == 1:
            o_near, beside = take(beside, near)
        if pending is not None:
            far, beside = take(beside, near)
            q_far.append(far)
        pending = beside[0] if sent else None
        at += sent
    blocks = [piece for _, _, piece in ring.found]
    slots = jnp.stack([(source // per ^ r) * per + source % per for source, _, _ in ring.found])
    scale = lax.rsqrt(squares / depth + 1e-05)[:, None]

    half = HD // 2
    positions = r * tok + jnp.arange(tok)
    freqs = 10000.0 ** (-jnp.arange(half).astype(jnp.float32) / half)
    angles = positions.astype(jnp.float32)[:, None] * freqs[None, :]
    cosine, sine = jnp.cos(angles), jnp.sin(angles)
    cosine = jnp.concatenate([cosine, cosine], axis=1)
    sine = jnp.concatenate([-sine, sine], axis=1)
    factor = HD ** (-0.5) * math.log2(math.e)

    beside = gather_near(pending) if pending is not None else []
    sent = at < len(sizes) - 1
    if sent:
        beside.append(exchange(chunk(at), blocks[-1]))
    kv_group = kv_near, columns([kv_far]), 0, 1, 1.0
    q_group = q_near, columns(q_far[:early]), 0, first_heads, factor
    out = project(blocks, slots, [kv_group, q_group], scale, cosine, sine)
    kv, queries, *beside = lax.optimization_barrier((*out, *beside))
    if pending is not None:
        far, beside = take(beside, near)
        q_far.append(far)
    kv_other = exchange(kv)
    beside = gather_near(kv) + (gather_near(beside[0]) if sent else [])
    kv_other, *beside = lax.optimization_barrier((kv_other, *beside))
    kv_pieces, far = take(beside, near)
    if sent:
        q_far.append(far)
    kv_pieces = [*kv_pieces, *gather_near(kv_other)]
    last_other = exchange(chunk(len(sizes) - 1), kv_other)
    heads = attend(r, [queries], kv_pieces)

    ring = Ring(heads)
    (last_other,) = ring.hop(beside=[last_other])

    def o_rows(first, wide):
        return wo.reshape(-1, cols, wo.shape[1])[:, first : first + wide].reshape(-1, wo.shape[1])

    o_first = exchange(o_rows(0, wide), last_other)
    q_far.append(gather_near(last_other))
    q_group = q_near, columns(q_far[early:]), wide, n_heads - first_heads, factor
    (queries,) = ring.hop(
        beside=project(blocks, slots, [q_group], scale, cosine, sine)
    )
    (heads,) = ring.hop(beside=[attend(r, [queries], kv_pieces)])
    second = Ring(heads)
    for _ in range(n_col // 2):
        arrived = ring.last
        ring.hop(*second.last)
        second.hop(*arrived)

    blocks = [piece for _, _, piece in ring.found]
    o_far = gather_near(o_first, *second.last)
    total = finish(blocks, slots, 0, o_near, o_far, cols, 0, wide, jnp.float32)
    blocks = [piece for _, _, piece in second.found]
    rest = cols - wide
    parts = [(0, rest // 2), (rest // 2, rest - rest // 2)] if rest >= 2 * HD else [(0, rest)]
    earlier = o_first
    others = []
    for first, part in parts:
        others.append(exchange(o_rows(wide + first, part), earlier))
        earlier = others[-1]
    for j, (first, part) in enumerate(parts):
        dtype = jnp.bfloat16 if j == len(parts) - 1 else jnp.float32
        o_far = gather_near(others[j], total)
        total = finish(
            blocks, slots, first, o_near, o_far, cols, wide + first, part, dtype, total
        )
    return total


def solution(mesh):
    in_specs = (
        P("row", "col"),
        P(),
        P("row", "col"),
        P("row", "col"),
        P("row", "col"),
        P("row", "col"),
    )
    out_specs = P("row", "col")
    return jax.shard_map(
        per_device, mesh=mesh, in_specs=in_specs, out_specs=out_specs, check_vma=False
    )
```

time: 309 us -> 340 us (1.10); the launches traced: 303 us -> 339 us
  waiting for transfers between devices: 161 us -> 207 us
  starting transfers between devices: 45.5 us -> 35 us
    ppermute x25 -> x27, waiting for transfers between devices: 70.2 us -> 143 us  [swap(): lax.ppermute(array, axis, [(i, i ^ mask) for i in range(lax.axis_size(axi...]
    ppermute x12, waiting for transfers between devices: 84.3 us -> 53.5 us  [hop(): below = lax.ppermute(below, 'col', self.up)]
    ppermute x25 -> x27, starting transfers between devices: 20.6 us -> 10.4 us  [swap(): lax.ppermute(array, axis, [(i, i ^ mask) for i in range(lax.axis_size(axi...]
    ppermute x12, starting transfers between devices: 15.4 us -> 11.4 us  [hop(): above = lax.ppermute(above, 'col', self.down)]
    ppermute x12, starting transfers between devices: 9.52 us -> 13.2 us  [hop(): below = lax.ppermute(below, 'col', self.up)]
  transfers between devices with their start and end apart: 49 -> 51, of which waited for: 28 -> 34; matrix products, arithmetic and copies ran while one was open for 6% -> 6% of each run, Pallas kernels for 20% -> 18%
where the time goes in v4:
time: 340 us; the launch traced here: 339 us
  waiting for transfers between devices  207 us (61%)
  Pallas kernels  70.2 us (21%)
  starting transfers between devices  35 us (10%)
  local copies, waits for them, and re-layouts  20.7 us (6%)
  other arithmetic  5.11 us (2%)
    ppermute x27, waiting for transfers between devices, swap(): lax.ppermute(array, axis, [(i, i ^ mask) for i in range(lax.axis_size(axi...  143 us
    ppermute x12, waiting for transfers between devices, hop(): below = lax.ppermute(below, 'col', self.up)  53.5 us
    pallas_call x2, Pallas kernels, project(): pl.pallas_call(functools.partial(project_kernel, len(blocks), plan), in_s...  28.1 us
    pallas_call x3, Pallas kernels, finish(): pl.pallas_call(functools.partial(finish_kernel, len(blocks), len(near), l...  27.9 us
    pallas_call x2, Pallas kernels, attend(): pl.pallas_call(functools.partial(attend_kernel, parts, chunks, pair), gri...  14.2 us
    ppermute x12, starting transfers between devices, hop(): below = lax.ppermute(below, 'col', self.up)  13.2 us
    ppermute x12, starting transfers between devices, hop(): above = lax.ppermute(above, 'col', self.down)  11.4 us
    ppermute x27, starting transfers between devices, swap(): lax.ppermute(array, axis, [(i, i ^ mask) for i in range(lax.axis_size(axi...  10.4 us
  transfers between devices with their start and end apart: 51, of which 34 were waited for; matrix products, arithmetic and copies ran while one was open for 6% of the time, Pallas kernels for 18%

profile of v4, /device:TPU:2, one launch (start us, length us, event | category | flops | bytes accessed | tf_op | source)
XLA Modules:
  0.0 338.8 jit_solution(12255075275915722790)
XLA Ops:
  0.7 1.8 fusion.1
  4.5 23.6 %collective-permute-done.3 = f32[512]{0:T(512)S(1)} collective-permute-done((f32[512]{0:T(512)S(1)}, f32[512]{0:T(512)S(1)}, u32[]{:S(2)}, u32[]{:S(2)}) %collective-permute-start.3) | collective-permute-done | bytes 2080 | tf_op jit(solution)/shard_map/ppermute | solution.py:22
  28.1 3.6 %collective-permute-done.4 = f32[512]{0:T(512)S(1)} collective-permute-done((f32[512]{0:T(512)S(1)}, f32[512]{0:T(512)S(1)}, u32[]{:S(2)}, u32[]{:S(2)}) %collective-permute-start.4) | collective-permute-done | bytes 2080 | tf_op jit(solution)/shard_map/ppermute | solution.py:22
  34.8 19.3 %collective-permute-done.5 = f32[512]{0:T(512)S(1)} collective-permute-done((f32[512]{0:T(512)S(1)}, f32[512]{0:T(512)S(1)}, u32[]{:S(2)}, u32[]{:S(2)}) %collective-permute-start.5) | collective-permute-done | bytes 2080 | tf_op jit(solution)/shard_map/ppermute | solution.py:22
  58.6 1.7 collective-permute-start.7
  61.0 21.8 %collective-permute-done.11.refs_15_ = bf16[2048,256]{1,0:T(8,128)(2,1)} collective-permute-done((bf16[2048,256]{1,0:T(8,128)(2,1)S(1)}, bf16[2048,256]{1,0:T(8,128)(2,1)}, u32[]{:S(2)}, u32[]{:S(2)}) %collective-permute-start.11) | collective-permute-done | bytes 1048608 | tf_op jit(solution)/shard_map/ppermute | solution.py:22
  85.5 1.7 collective-permute-start.12
  89.4 23.1 %collective-permute-done.16.refs_16_ = bf16[2048,256]{1,0:T(8,128)(2,1)} collective-permute-done((bf16[2048,256]{1,0:T(8,128)(2,1)}, bf16[2048,256]{1,0:T(8,128)(2,1)}, u32[]{:S(2)}, u32[]{:S(2)}) %collective-permute-start.16) | collective-permute-done | bytes 1048608 | tf_op jit(solution)/shard_map/ppermute | solution.py:22
  112.7 2.9 fusion.5
  123.4 7.0 %collective-permute-done.20.refs_11_ = bf16[2048,128]{1,0:T(8,128)(2,1)} collective-permute-done((bf16[2048,128]{1,0:T(8,128)(2,1)}, bf16[2048,128]{1,0:T(8,128)(2,1)}, u32[]{:S(2)}, u32[]{:S(2)}) %collective-permute-start.20) | collective-permute-done | bytes 524320 | tf_op jit(solution)/shard_map/ppermute | solution.py:22
  133.9 16.5 %shard_map.64 = (bf16[512,256]{1,0:T(8,128)(2,1)}, bf16[512,512]{1,0:T(8,128)(2,1)}) custom-call(s32[9]{0:T(128)} %stack.48.slots_ref, bf16[512,1024]{1,0:T(8,128)(2,1)} %copy-done.7, bf16[512,1024]{1,0:T(8,128)(2,1)} %copy-done.10, bf16[512,1024]{1,0:T(8,128)(2,1)} %copy-done.11, bf16[512,1024]{1,0:T(8,128)(2,1)} %collective-permute-done.7.refs_3_, ...), custom_call_target="tpu_custom_call" | custom-call | flops 6442450944 | bytes 21757952 | tf_op jit(solution)/shard_map/pallas_call | solution.py:205
  153.2 7.1 %collective-permute-done.23.refs_3_ = bf16[512,256]{1,0:T(8,128)(2,1)S(1)} collective-permute-done((bf16[512,256]{1,0:T(8,128)(2,1)}, bf16[512,256]{1,0:T(8,128)(2,1)S(1)}, u32[]{:S(2)}, u32[]{:S(2)}) %collective-permute-start.23) | collective-permute-done | bytes 262176 | tf_op jit(solution)/shard_map/ppermute | solution.py:22
  166.0 7.1 %shard_map.65.refs_0_ = bf16[512,512]{1,0:T(8,128)(2,1)S(1)} custom-call(s32[1]{0:T(128)} %bitcast.9.r_ref, bf16[512,512]{1,0:T(8,128)(2,1)S(1)} %copy-done.3, bf16[512,256]{1,0:T(8,128)(2,1)S(1)} %copy-done.4, bf16[512,256]{1,0:T(8,128)(2,1)S(1)} %collective-permute-done.24.refs_2_, bf16[512,256]{1,0:T(8,128)(2,1)S(1)} %collective-permute-done.23.refs_3_, ...), custom_call_target="tpu_custom_call" | custom-call | flops 2147483648 | bytes 2097152 | tf_op jit(solution)/shard_map/pallas_call | solution.py:294
  173.1 1.8 collective-permute-start.27
  175.2 11.3 %collective-permute-done.27.refs_1_ = bf16[512,512]{1,0:T(8,128)(2,1)S(1)} collective-permute-done((bf16[512,512]{1,0:T(8,128)(2,1)S(1)}, bf16[512,512]{1,0:T(8,128)(2,1)S(1)}, u32[]{:S(2)}, u32[]{:S(2)}) %collective-permute-start.27) | collective-permute-done | bytes 524320 | tf_op jit(solution)/shard_map/ppermute | solution.py:79
  186.5 2.1 collective-permute-done.28.refs_2_
  192.9 11.6 %shard_map.66.refs_0_ = bf16[512,512]{1,0:T(8,128)(2,1)} custom-call(s32[9]{0:T(128)} %stack.48.slots_ref, bf16[512,1024]{1,0:T(8,128)(2,1)} %copy-done.7, bf16[512,1024]{1,0:T(8,128)(2,1)} %copy-done.10, bf16[512,1024]{1,0:T(8,128)(2,1)} %copy-done.11, bf16[512,1024]{1,0:T(8,128)(2,1)} %collective-permute-done.7.refs_3_, ...), custom_call_target="tpu_custom_call" | custom-call | flops 4294967296 | bytes 17301504 | tf_op jit(solution)/shard_map/pallas_call | solution.py:205
  207.2 1.8 slice.58
  209.2 7.1 %shard_map.67.refs_0_ = bf16[512,512]{1,0:T(8,128)(2,1)S(1)} custom-call(s32[1]{0:T(128)} %bitcast.9.r_ref, bf16[512,512]{1,0:T(8,128)(2,1)S(1)} %copy-done.2, bf16[512,256]{1,0:T(8,128)(2,1)S(1)} %copy-done.5, bf16[512,256]{1,0:T(8,128)(2,1)S(1)} %collective-permute-done.24.refs_2_, bf16[512,256]{1,0:T(8,128)(2,1)S(1)} %collective-permute-done.23.refs_3_, ...), custom_call_target="tpu_custom_call" | custom-call | flops 2147483648 | bytes 2097152 | tf_op jit(solution)/shard_map/pallas_call | solution.py:294
  216.3 2.8 collective-permute-done.33.refs_5_
  224.6 14.5 %collective-permute-done.37.refs_7_ = bf16[256,512]{1,0:T(8,128)(2,1)S(1)} collective-permute-done((bf16[256,512]{1,0:T(8,128)(2,1)S(1)}, bf16[256,512]{1,0:T(8,128)(2,1)S(1)}, u32[]{:S(2)}, u32[]{:S(2)}) %collective-permute-start.37) | collective-permute-done | bytes 262176 | tf_op jit(solution)/shard_map/ppermute | solution.py:79
  242.2 10.0 %collective-permute-done.39.refs_3_ = bf16[512,512]{1,0:T(8,128)(2,1)S(1)} collective-permute-done((bf16[512,512]{1,0:T(8,128)(2,1)S(1)}, bf16[512,512]{1,0:T(8,128)(2,1)S(1)}, u32[]{:S(2)}, u32[]{:S(2)}) %collective-permute-start.39) | collective-permute-done | bytes 524320 | tf_op jit(solution)/shard_map/ppermute | solution.py:79
  254.8 9.2 %collective-permute-done.41.refs_5_ = bf16[512,512]{1,0:T(8,128)(2,1)S(1)} collective-permute-done((bf16[512,512]{1,0:T(8,128)(2,1)S(1)}, bf16[512,512]{1,0:T(8,128)(2,1)S(1)}, u32[]{:S(2)}, u32[]{:S(2)}) %collective-permute-start.41) | collective-permute-done | bytes 524320 | tf_op jit(solution)/shard_map/ppermute | solution.py:79
  267.0 4.3 %collective-permute-done.43.refs_7_ = bf16[256,512]{1,0:T(8,128)(2,1)S(1)} collective-permute-done((bf16[256,512]{1,0:T(8,128)(2,1)S(1)}, bf16[256,512]{1,0:T(8,128)(2,1)S(1)}, u32[]{:S(2)}, u32[]{:S(2)}) %collective-permute-start.43) | collective-permute-done | bytes 262176 | tf_op jit(solution)/shard_map/ppermute | solution.py:79
  272.1 3.8 %fusion.3 = (bf16[2,256,1024]{2,1,0:T(8,128)(2,1)}, bf16[2,256,1024]{2,1,0:T(8,128)(2,1)}) fusion(bf16[2,1024,1024]{2,1,0:T(8,128)(2,1)} %bitcast.13), kind=kLoop, calls=%fused_computation.14 | loop fusion | bytes 4194304 | tf_op jit(solution)/shard_map/slice | solution.py:467
  276.3 11.0 %shard_map.68.refs_13_ = f32[512,1024]{1,0:T(8,128)} custom-call(s32[9]{0:T(128)} %stack.48.slots_ref, bf16[512,512]{1,0:T(8,128)(2,1)} %copy-done.1, bf16[512,512]{1,0:T(8,128)(2,1)} %copy-done.36, bf16[512,512]{1,0:T(8,128)(2,1)} %collective-permute-done.28.refs_2_, bf16[512,512]{1,0:T(8,128)(2,1)} %collective-permute-done.30.refs_3_, ...), custom_call_target="tpu_custom_call" | custom-call | flops 4294967296 | bytes 16777216 | tf_op jit(solution)/shard_map/pallas_call | solution.py:339
  287.4 13.7 %collective-permute-done.46.refs_11_ = bf16[512,1024]{1,0:T(8,128)(2,1)S(1)} collective-permute-done((bf16[512,1024]{1,0:T(8,128)(2,1)}, bf16[512,1024]{1,0:T(8,128)(2,1)S(1)}, u32[]{:S(2)}, u32[]{:S(2)}) %collective-permute-start.46) | collective-permute-done | bytes 1048608 | tf_op jit(solution)/shard_map/ppermute | solution.py:22
  301.4 2.4 collective-permute-done.49.refs_12_
  303.8 8.7 %shard_map.69.refs_13_ = f32[512,1024]{1,0:T(8,128)} custom-call(s32[9]{0:T(128)} %stack.48.slots_ref, bf16[512,512]{1,0:T(8,128)(2,1)} %copy-done, bf16[512,512]{1,0:T(8,128)(2,1)} %copy-done.17, bf16[512,512]{1,0:T(8,128)(2,1)} %copy-done.18, bf16[512,512]{1,0:T(8,128)(2,1)} %copy-done.19, bf16[512,512]{1,0:T(8,128)(2,1)} %copy-done.20, ...), custom_call_target="tpu_custom_call" | custom-call | flops 2147483648 | bytes 10485760 | tf_op jit(solution)/shard_map/pallas_call | solution.py:339
  312.5 14.1 %collective-permute-done.47.refs_11_ = bf16[512,1024]{1,0:T(8,128)(2,1)S(1)} collective-permute-done((bf16[512,1024]{1,0:T(8,128)(2,1)S(1)}, bf16[512,1024]{1,0:T(8,128)(2,1)S(1)}, u32[]{:S(2)}, u32[]{:S(2)}) %collective-permute-start.47) | collective-permute-done | bytes 1048608 | tf_op jit(solution)/shard_map/ppermute | solution.py:22
  326.6 2.7 collective-permute-done.50.refs_12_
  330.3 8.3 %shard_map.70 = bf16[512,1024]{1,0:T(8,128)(2,1)} custom-call(s32[9]{0:T(128)} %stack.48.slots_ref, bf16[512,512]{1,0:T(8,128)(2,1)} %copy-done, bf16[512,512]{1,0:T(8,128)(2,1)} %copy-done.17, bf16[512,512]{1,0:T(8,128)(2,1)} %copy-done.18, bf16[512,512]{1,0:T(8,128)(2,1)} %copy-done.19, bf16[512,512]{1,0:T(8,128)(2,1)} %copy-done.20, ...), custom_call_target="tpu_custom_call" | custom-call | flops 2147483648 | bytes 10485760 | tf_op jit(solution)/shard_map/pallas_call | solution.py:339
  (184 shorter events, 59.1 us)
Async XLA Ops:
  0.0 85.5 %collective-permute-start.10 = (bf16[2048,1024]{1,0:T(8,128)(2,1)}, bf16[2048,1024]{1,0:T(8,128)(2,1)}, u32[]{:S(2)}, u32[]{:S(2)}) collective-permute-start(bf16[2048,1024]{1,0:T(8,128)(2,1)} %refs_9_), channel_id=1, source_target_pairs={{0,8},{8,0},{16,24},{24,16},{1,9},{9,1},{17,25},{25,17},{2,10},{10... | collective-permute-start | bytes 12582920 | tf_op jit(solution)/shard_map/ppermute | solution.py:22
  2.5 51.7 %collective-permute-start = (bf16[512,1024]{1,0:T(8,128)(2,1)S(1)}, bf16[512,1024]{1,0:T(8,128)(2,1)S(1)}, u32[]{:S(2)}, u32[]{:S(2)}) collective-permute-start(bf16[512,1024]{1,0:T(8,128)(2,1)S(1)} %get-tuple-element.167.refs_0_), channel_id=1, source_target_pairs={{0,2},{2,4},{4,6},{6,7},{7,5},{5,3},{3,1},{1,0},{8,10},{10,12},{12... | collective-permute-start | bytes 3145736 | tf_op jit(solution)/shard_map/ppermute | solution.py:79
  4.1 24.0 %collective-permute-start.3 = (f32[512]{0:T(512)S(1)}, f32[512]{0:T(512)S(1)}, u32[]{:S(2)}, u32[]{:S(2)}) collective-permute-start(f32[512]{0:T(512)S(1)} %get-tuple-element.166), channel_id=1, source_target_pairs={{0,1},{1,0},{2,3},{3,2},{4,5},{5,4},{6,7},{7,6},{8,9},{9,8},{10,11... | collective-permute-start | bytes 6152 | tf_op jit(solution)/shard_map/ppermute | solution.py:22
  28.1 28.1 %collective-permute-start.1 = (bf16[512,1024]{1,0:T(8,128)(2,1)S(1)}, bf16[512,1024]{1,0:T(8,128)(2,1)S(1)}, u32[]{:S(2)}, u32[]{:S(2)}) collective-permute-start(bf16[512,1024]{1,0:T(8,128)(2,1)S(1)} %get-tuple-element.167.refs_0_), channel_id=1, source_target_pairs={{2,0},{4,2},{6,4},{7,6},{5,7},{3,5},{1,3},{0,1},{10,8},{12,10},{14... | collective-permute-start | bytes 3145736 | tf_op jit(solution)/shard_map/ppermute | solution.py:80
  31.8 22.4 %collective-permute-start.5 = (f32[512]{0:T(512)S(1)}, f32[512]{0:T(512)S(1)}, u32[]{:S(2)}, u32[]{:S(2)}) collective-permute-start(f32[512]{0:T(512)S(1)} %add.192), channel_id=1, source_target_pairs={{0,4},{1,5},{2,6},{3,7},{4,0},{5,1},{6,2},{7,3},{8,12},{9,13},{10,... | collective-permute-start | bytes 6152 | tf_op jit(solution)/shard_map/ppermute | solution.py:22
  34.2 23.7 %collective-permute-start.2 = (bf16[2048,256]{1,0:T(8,128)(2,1)S(1)}, bf16[2048,256]{1,0:T(8,128)(2,1)S(1)}, u32[]{:S(2)}, u32[]{:S(2)}) collective-permute-start(bf16[2048,256]{1,0:T(8,128)(2,1)S(1)} %copy_bitcast_fusion.refs_9_), channel_id=1, source_target_pairs={{0,16},{8,24},{16,0},{24,8},{1,17},{9,25},{17,1},{25,9},{2,18},{10... | collective-permute-start | bytes 3145736 | tf_op jit(solution)/shard_map/ppermute | solution.py:22
  54.2 35.2 %collective-permute-start.14 = (bf16[2048,1024]{1,0:T(8,128)(2,1)}, bf16[2048,1024]{1,0:T(8,128)(2,1)}, u32[]{:S(2)}, u32[]{:S(2)}) collective-permute-start(bf16[2048,1024]{1,0:T(8,128)(2,1)} %refs_9_.3), channel_id=1, source_target_pairs={{0,8},{8,0},{16,24},{24,16},{1,9},{9,1},{17,25},{25,17},{2,10},{10... | collective-permute-start | bytes 12582920 | tf_op jit(solution)/shard_map/ppermute | solution.py:22
  58.0 24.9 %collective-permute-start.11 = (bf16[2048,256]{1,0:T(8,128)(2,1)S(1)}, bf16[2048,256]{1,0:T(8,128)(2,1)}, u32[]{:S(2)}, u32[]{:S(2)}) collective-permute-start(bf16[2048,256]{1,0:T(8,128)(2,1)S(1)} %get-tuple-element.85), channel_id=1, source_target_pairs={{0,16},{8,24},{16,0},{24,8},{1,17},{9,25},{17,1},{25,9},{2,18},{10... | collective-permute-start | bytes 3145736 | tf_op jit(solution)/shard_map/ppermute | solution.py:22
  58.6 24.6 %collective-permute-start.7 = (bf16[512,1024]{1,0:T(8,128)(2,1)S(1)}, bf16[512,1024]{1,0:T(8,128)(2,1)}, u32[]{:S(2)}, u32[]{:S(2)}) collective-permute-start(bf16[512,1024]{1,0:T(8,128)(2,1)S(1)} %collective-permute-done.refs_1_), channel_id=1, source_target_pairs={{0,2},{2,4},{4,6},{6,7},{7,5},{5,3},{3,1},{1,0},{8,10},{10,12},{12... | collective-permute-start | bytes 3145736 | tf_op jit(solution)/shard_map/ppermute | solution.py:79
  60.3 24.3 %collective-permute-start.8 = (bf16[512,1024]{1,0:T(8,128)(2,1)S(1)}, bf16[512,1024]{1,0:T(8,128)(2,1)}, u32[]{:S(2)}, u32[]{:S(2)}) collective-permute-start(bf16[512,1024]{1,0:T(8,128)(2,1)S(1)} %collective-permute-done.1.refs_2_), channel_id=1, source_target_pairs={{2,0},{4,2},{6,4},{7,6},{5,7},{3,5},{1,3},{0,1},{10,8},{12,10},{14... | collective-permute-start | bytes 3145736 | tf_op jit(solution)/shard_map/ppermute | solution.py:80
  85.5 27.0 %collective-permute-start.12 = (bf16[512,1024]{1,0:T(8,128)(2,1)}, bf16[512,1024]{1,0:T(8,128)(2,1)S(1)}, u32[]{:S(2)}, u32[]{:S(2)}) collective-permute-start(bf16[512,1024]{1,0:T(8,128)(2,1)} %collective-permute-done.7.refs_3_), channel_id=1, source_target_pairs={{0,2},{2,4},{4,6},{6,7},{7,5},{5,3},{3,1},{1,0},{8,10},{10,12},{12... | collective-permute-start | bytes 3145736 | tf_op jit(solution)/shard_map/ppermute | solution.py:79
  87.3 25.2 %collective-permute-start.16 = (bf16[2048,256]{1,0:T(8,128)(2,1)}, bf16[2048,256]{1,0:T(8,128)(2,1)}, u32[]{:S(2)}, u32[]{:S(2)}) collective-permute-start(bf16[2048,256]{1,0:T(8,128)(2,1)} %get-tuple-element.89), channel_id=1, source_target_pairs={{0,16},{8,24},{16,0},{24,8},{1,17},{9,25},{17,1},{25,9},{2,18},{10... | collective-permute-start | bytes 3145736 | tf_op jit(solution)/shard_map/ppermute | solution.py:22
  87.8 24.9 %collective-permute-start.13 = (bf16[512,1024]{1,0:T(8,128)(2,1)}, bf16[512,1024]{1,0:T(8,128)(2,1)S(1)}, u32[]{:S(2)}, u32[]{:S(2)}) collective-permute-start(bf16[512,1024]{1,0:T(8,128)(2,1)} %collective-permute-done.8.refs_4_), channel_id=1, source_target_pairs={{2,0},{4,2},{6,4},{7,6},{5,7},{3,5},{1,3},{0,1},{10,8},{12,10},{14... | collective-permute-start | bytes 3145736 | tf_op jit(solution)/shard_map/ppermute | solution.py:80
  88.2 24.5 %collective-permute-start.15 = (bf16[2048,256]{1,0:T(8,128)(2,1)}, bf16[2048,256]{1,0:T(8,128)(2,1)}, u32[]{:S(2)}, u32[]{:S(2)}) collective-permute-start(bf16[2048,256]{1,0:T(8,128)(2,1)} %collective-permute-done.11.refs_15_), channel_id=1, source_target_pairs={{0,8},{8,0},{16,24},{24,16},{1,9},{9,1},{17,25},{25,17},{2,10},{10... | collective-permute-start | bytes 3145736 | tf_op jit(solution)/shard_map/ppermute | solution.py:22
  112.7 20.5 %collective-permute-start.19 = (bf16[2048,256]{1,0:T(8,128)(2,1)}, bf16[2048,256]{1,0:T(8,128)(2,1)}, u32[]{:S(2)}, u32[]{:S(2)}) collective-permute-start(bf16[2048,256]{1,0:T(8,128)(2,1)} %collective-permute-done.16.refs_16_), channel_id=1, source_target_pairs={{0,8},{8,0},{16,24},{24,16},{1,9},{9,1},{17,25},{25,17},{2,10},{10... | collective-permute-start | bytes 3145736 | tf_op jit(solution)/shard_map/ppermute | solution.py:22
  116.3 14.0 %collective-permute-start.20 = (bf16[2048,128]{1,0:T(8,128)(2,1)}, bf16[2048,128]{1,0:T(8,128)(2,1)}, u32[]{:S(2)}, u32[]{:S(2)}) collective-permute-start(bf16[2048,128]{1,0:T(8,128)(2,1)} %get-tuple-element.93), channel_id=1, source_target_pairs={{0,16},{8,24},{16,0},{24,8},{1,17},{9,25},{17,1},{25,9},{2,18},{10... | collective-permute-start | bytes 1572872 | tf_op jit(solution)/shard_map/ppermute | solution.py:22
  117.6 13.9 %collective-permute-start.17 = (bf16[256,1024]{1,0:T(8,128)(2,1)}, bf16[256,1024]{1,0:T(8,128)(2,1)S(1)}, u32[]{:S(2)}, u32[]{:S(2)}) collective-permute-start(bf16[256,1024]{1,0:T(8,128)(2,1)} %slice.44), channel_id=1, source_target_pairs={{0,2},{2,4},{4,6},{6,7},{7,5},{5,3},{3,1},{1,0},{8,10},{10,12},{12... | collective-permute-start | bytes 1572872 | tf_op jit(solution)/shard_map/ppermute | solution.py:79
  118.8 14.3 %collective-permute-start.18 = (bf16[256,1024]{1,0:T(8,128)(2,1)}, bf16[256,1024]{1,0:T(8,128)(2,1)S(1)}, u32[]{:S(2)}, u32[]{:S(2)}) collective-permute-start(bf16[256,1024]{1,0:T(8,128)(2,1)} %slice.45), channel_id=1, source_target_pairs={{2,0},{4,2},{6,4},{7,6},{5,7},{3,5},{1,3},{0,1},{10,8},{12,10},{14... | collective-permute-start | bytes 1572872 | tf_op jit(solution)/shard_map/ppermute | solution.py:80
  133.1 17.3 %collective-permute-start.22 = (bf16[2048,128]{1,0:T(8,128)(2,1)}, bf16[2048,128]{1,0:T(8,128)(2,1)S(1)}, u32[]{:S(2)}, u32[]{:S(2)}) collective-permute-start(bf16[2048,128]{1,0:T(8,128)(2,1)} %get-tuple-element.110), channel_id=1, source_target_pairs={{0,16},{8,24},{16,0},{24,8},{1,17},{9,25},{17,1},{25,9},{2,18},{10... | collective-permute-start | bytes 1572872 | tf_op jit(solution)/shard_map/ppermute | solution.py:22
  133.7 16.8 %collective-permute-start.21 = (bf16[2048,128]{1,0:T(8,128)(2,1)}, bf16[2048,128]{1,0:T(8,128)(2,1)S(1)}, u32[]{:S(2)}, u32[]{:S(2)}) collective-permute-start(bf16[2048,128]{1,0:T(8,128)(2,1)} %collective-permute-done.20.refs_11_), channel_id=1, source_target_pairs={{0,8},{8,0},{16,24},{24,16},{1,9},{9,1},{17,25},{25,17},{2,10},{10... | collective-permute-start | bytes 1572872 | tf_op jit(solution)/shard_map/ppermute | solution.py:22
  161.1 27.5 %collective-permute-start.29 = (bf16[2048,256]{1,0:T(8,128)(2,1)S(1)}, bf16[2048,256]{1,0:T(8,128)(2,1)S(1)}, u32[]{:S(2)}, u32[]{:S(2)}) collective-permute-start(bf16[2048,256]{1,0:T(8,128)(2,1)S(1)} %copy-done.33), channel_id=1, source_target_pairs={{0,16},{8,24},{16,0},{24,8},{1,17},{9,25},{17,1},{25,9},{2,18},{10... | collective-permute-start | bytes 3145736 | tf_op jit(solution)/shard_map/ppermute | solution.py:22
  189.6 14.9 %collective-permute-start.30 = (bf16[512,512]{1,0:T(8,128)(2,1)S(1)}, bf16[512,512]{1,0:T(8,128)(2,1)}, u32[]{:S(2)}, u32[]{:S(2)}) collective-permute-start(bf16[512,512]{1,0:T(8,128)(2,1)S(1)} %collective-permute-done.27.refs_1_), channel_id=1, source_target_pairs={{0,2},{2,4},{4,6},{6,7},{7,5},{5,3},{3,1},{1,0},{8,10},{10,12},{12... | collective-permute-start | bytes 1572872 | tf_op jit(solution)/shard_map/ppermute | solution.py:79
  191.3 13.9 %collective-permute-start.31 = (bf16[512,512]{1,0:T(8,128)(2,1)}, bf16[512,512]{1,0:T(8,128)(2,1)}, u32[]{:S(2)}, u32[]{:S(2)}) collective-permute-start(bf16[512,512]{1,0:T(8,128)(2,1)} %collective-permute-done.28.refs_2_), channel_id=1, source_target_pairs={{2,0},{4,2},{6,4},{7,6},{5,7},{3,5},{1,3},{0,1},{10,8},{12,10},{14... | collective-permute-start | bytes 1572872 | tf_op jit(solution)/shard_map/ppermute | solution.py:80
  205.2 13.8 %collective-permute-start.33 = (bf16[512,512]{1,0:T(8,128)(2,1)}, bf16[512,512]{1,0:T(8,128)(2,1)S(1)}, u32[]{:S(2)}, u32[]{:S(2)}) collective-permute-start(bf16[512,512]{1,0:T(8,128)(2,1)} %collective-permute-done.30.refs_3_), channel_id=1, source_target_pairs={{0,2},{2,4},{4,6},{6,7},{7,5},{5,3},{3,1},{1,0},{8,10},{10,12},{12... | collective-permute-start | bytes 1572872 | tf_op jit(solution)/shard_map/ppermute | solution.py:79
  206.3 14.1 %collective-permute-start.34 = (bf16[512,512]{1,0:T(8,128)(2,1)}, bf16[512,512]{1,0:T(8,128)(2,1)S(1)}, u32[]{:S(2)}, u32[]{:S(2)}) collective-permute-start(bf16[512,512]{1,0:T(8,128)(2,1)} %collective-permute-done.31.refs_4_), channel_id=1, source_target_pairs={{2,0},{4,2},{6,4},{7,6},{5,7},{3,5},{1,3},{0,1},{10,8},{12,10},{14... | collective-permute-start | bytes 1572872 | tf_op jit(solution)/shard_map/ppermute | solution.py:80
  209.1 62.9 %collective-permute-start.45 = (bf16[1024,1024]{1,0:T(8,128)(2,1)S(1)}, bf16[1024,1024]{1,0:T(8,128)(2,1)S(1)}, u32[]{:S(2)}, u32[]{:S(2)}) collective-permute-start(bf16[1024,1024]{1,0:T(8,128)(2,1)S(1)} %bitcast.22), channel_id=1, source_target_pairs={{0,16},{8,24},{16,0},{24,8},{1,17},{9,25},{17,1},{25,9},{2,18},{10... | collective-permute-start | bytes 6291464 | tf_op jit(solution)/shard_map/ppermute | solution.py:22
  220.4 19.1 %collective-permute-start.35 = (bf16[512,512]{1,0:T(8,128)(2,1)S(1)}, bf16[512,512]{1,0:T(8,128)(2,1)S(1)}, u32[]{:S(2)}, u32[]{:S(2)}) collective-permute-start(bf16[512,512]{1,0:T(8,128)(2,1)S(1)} %shard_map.67.refs_0_), channel_id=1, source_target_pairs={{0,2},{2,4},{4,6},{6,7},{7,5},{5,3},{3,1},{1,0},{8,10},{10,12},{12... | collective-permute-start | bytes 1572872 | tf_op jit(solution)/shard_map/ppermute | solution.py:79
  220.9 18.5 %collective-permute-start.36 = (bf16[512,512]{1,0:T(8,128)(2,1)S(1)}, bf16[512,512]{1,0:T(8,128)(2,1)S(1)}, u32[]{:S(2)}, u32[]{:S(2)}) collective-permute-start(bf16[512,512]{1,0:T(8,128)(2,1)S(1)} %shard_map.67.refs_0_), channel_id=1, source_target_pairs={{2,0},{4,2},{6,4},{7,6},{5,7},{3,5},{1,3},{0,1},{10,8},{12,10},{14... | collective-permute-start | bytes 1572872 | tf_op jit(solution)/shard_map/ppermute | solution.py:80
  222.5 16.6 %collective-permute-start.37 = (bf16[256,512]{1,0:T(8,128)(2,1)S(1)}, bf16[256,512]{1,0:T(8,128)(2,1)S(1)}, u32[]{:S(2)}, u32[]{:S(2)}) collective-permute-start(bf16[256,512]{1,0:T(8,128)(2,1)S(1)} %slice.49), channel_id=1, source_target_pairs={{0,2},{2,4},{4,6},{6,7},{7,5},{5,3},{3,1},{1,0},{8,10},{10,12},{12... | collective-permute-start | bytes 786440 | tf_op jit(solution)/shard_map/ppermute | solution.py:79
  223.1 16.4 %collective-permute-start.38 = (bf16[256,512]{1,0:T(8,128)(2,1)S(1)}, bf16[256,512]{1,0:T(8,128)(2,1)S(1)}, u32[]{:S(2)}, u32[]{:S(2)}) collective-permute-start(bf16[256,512]{1,0:T(8,128)(2,1)S(1)} %slice.50), channel_id=1, source_target_pairs={{2,0},{4,2},{6,4},{7,6},{5,7},{3,5},{1,3},{0,1},{10,8},{12,10},{14... | collective-permute-start | bytes 786440 | tf_op jit(solution)/shard_map/ppermute | solution.py:80
  276.0 25.1 %collective-permute-start.46 = (bf16[512,1024]{1,0:T(8,128)(2,1)}, bf16[512,1024]{1,0:T(8,128)(2,1)S(1)}, u32[]{:S(2)}, u32[]{:S(2)}) collective-permute-start(bf16[512,1024]{1,0:T(8,128)(2,1)} %bitcast.15), channel_id=1, source_target_pairs={{0,16},{8,24},{16,0},{24,8},{1,17},{9,25},{17,1},{25,9},{2,18},{10... | collective-permute-start | bytes 3145736 | tf_op jit(solution)/shard_map/ppermute | solution.py:22
  301.1 25.6 %collective-permute-start.47 = (bf16[512,1024]{1,0:T(8,128)(2,1)S(1)}, bf16[512,1024]{1,0:T(8,128)(2,1)S(1)}, u32[]{:S(2)}, u32[]{:S(2)}) collective-permute-start(bf16[512,1024]{1,0:T(8,128)(2,1)S(1)} %bitcast.23), channel_id=1, source_target_pairs={{0,16},{8,24},{16,0},{24,8},{1,17},{9,25},{17,1},{25,9},{2,18},{10... | collective-permute-start | bytes 3145736 | tf_op jit(solution)/shard_map/ppermute | solution.py:22
  (61 other events, 812.3 us)

commit v5 on v2

v5 whole, which is shorter than its diff:
```python
import functools
import math

import jax
import jax.numpy as jnp
from jax import lax
from jax.experimental import pallas as pl
from jax.experimental.pallas import tpu as pltpu
from jax.sharding import PartitionSpec as P

HD = 128
MIB = 1 << 20
SHORT = pl.CostEstimate(flops=1, bytes_accessed=1, transcendentals=0)


def after(array, *earlier):
    if not earlier:
        return array
    return lax.optimization_barrier((array, *earlier))[0]


def swap(array, axis, mask):
    return lax.ppermute(array, axis, [(i, i ^ mask) for i in range(lax.axis_size(axis))])


def row_bits():
    return [1 << b for b in reversed(range((lax.axis_size("row")).bit_length() - 1))]


def exchange(array, *earlier):
    return swap(after(array, *earlier), "row", row_bits()[0])


def gather_near(array, *earlier):
    pieces = {0: after(array, *earlier)}
    for bit in row_bits()[1:]:
        pieces.update({j ^ bit: swap(p, "row", bit) for j, p in pieces.items()})
    return [pieces[j] for j in range(len(pieces))]


def order_pair(mine, other, col_index, bit, axis_dim):
    upper = col_index // 2**bit % 2 == 1
    lower_part = jnp.where(upper, other, mine)
    upper_part = jnp.where(upper, mine, other)
    return jnp.concatenate([lower_part, upper_part], axis=axis_dim)


def ring_order(n):
    return list(range(0, n, 2)) + list(range(1, n, 2))[::-1]


def ring_source(c, hops, n):
    at = jnp.where(c % 2 == 0, c // 2, n - 1 - c // 2)
    at = (at - hops) % n
    return jnp.where(at < n // 2, 2 * at, 2 * (n - 1 - at) + 1)


class Ring:
    def __init__(self, block):
        n = lax.axis_size("col")
        order = ring_order(n)
        self.n, self.hops = n, 0
        self.up = [(order[i], order[(i + 1) % n]) for i in range(n)]
        self.down = [(b, a) for a, b in self.up]
        self.found = [(lax.axis_index("col"), 0, block)]
        self.last = [block, block]

    def hop(self, *earlier, beside=()):
        if self.hops == self.n // 2:
            return beside
        c, own = self.found[0][0], self.found[0][2]
        rows = own.shape[0] // 2
        self.hops += 1
        end = self.hops == self.n // 2
        below, above = self.last
        if end:
            below, above = below[:rows], above[rows:]
        if earlier:
            below, above = lax.optimization_barrier((below, above, *earlier))[:2]
        below = lax.ppermute(below, "col", self.up)
        above = lax.ppermute(above, "col", self.down)
        below, above, *beside = lax.optimization_barrier((below, above, *beside))
        self.last = [below, above]
        self.found.append((ring_source(c, self.hops, self.n), 0, self.last[0]))
        self.found.append((ring_source(c, -self.hops, self.n), rows if end else 0, self.last[1]))
        return beside


def blank(shape):
    return pl.pallas_call(
        lambda o_ref: None,
        out_specs=pl.BlockSpec(memory_space=pl.ANY),
        out_shape=jax.ShapeDtypeStruct(shape, jnp.bfloat16),
    )()


def take(refs, *counts):
    out, at = [], 0
    for n in counts:
        out.append(refs[at : at + n])
        at += n
    return *out, refs[at:]


def multiply(steps, a_buf, w_bufs, accs, a_sem, w_sem):
    for i, (left, rights) in enumerate(steps):
        pltpu.make_async_copy(left, a_buf.at[i], a_sem.at[i]).start()
        for g, chunks in enumerate(rights):
            at = 0
            for chunk in chunks:
                wide = chunk.shape[1]
                into = w_bufs[g].at[i, :, pl.ds(at, wide)]
                pltpu.make_async_copy(chunk, into, w_sem.at[g, i]).start()
                at += wide

    def body(i, carry):
        pltpu.make_async_copy(a_buf.at[i], a_buf.at[i], a_sem.at[i]).wait()
        for g, acc in enumerate(accs):
            pltpu.make_async_copy(w_bufs[g].at[i], w_bufs[g].at[i], w_sem.at[g, i]).wait()
            acc[...] += jnp.dot(a_buf[i], w_bufs[g][i], preferred_element_type=jnp.float32)
        return carry

    lax.fori_loop(0, len(steps), body, 0)


def project_kernel(near, far, chunks, first, heads, factor, panel_ref, *refs):
    near_refs, far_refs, (scale_ref, cos_ref, sin_ref), rest = take(refs, near, far * chunks, 3)
    o_ref, a_buf, w_buf, acc, a_sem, w_sem = rest
    slots, _, depth = panel_ref.shape
    per = slots // (near + far)
    cols = acc.shape[1]
    steps = []
    for k in range(slots):
        p, rows = k // per, pl.ds(k % per * depth, depth)
        if p < near:
            right = [near_refs[p].at[rows, pl.ds(first, cols)]]
        else:
            at = (p - near) * chunks
            right = [ref.at[rows, :] for ref in far_refs[at : at + chunks]]
        steps.append((panel_ref.at[k], [right]))
    acc[...] = jnp.zeros_like(acc)
    multiply(steps, a_buf, [w_buf], [acc], a_sem, w_sem)
    scale = scale_ref[...] * factor
    for h in range(cols // HD):
        at = pl.ds(h * HD, HD)
        x = acc[:, at] * scale
        if h < heads:
            x = x * cos_ref[...] + pltpu.roll(x, HD // 2, 1) * sin_ref[...]
        o_ref[:, at] = x.astype(o_ref.dtype)


def project(panel, near, far, first, heads, factor, scale, cos, sin):
    slots, tok, depth = panel.shape
    chunks = len(far[0])
    cols = sum(w.shape[1] for w in far[0])
    hbm = pl.BlockSpec(memory_space=pl.ANY)
    vmem = pl.BlockSpec(memory_space=pltpu.VMEM)
    return pl.pallas_call(
        functools.partial(project_kernel, len(near), len(far), chunks, first, heads, factor),
        in_specs=[hbm] * (1 + len(near) + len(far) * chunks) + [vmem] * 3,
        out_specs=vmem,
        out_shape=jax.ShapeDtypeStruct((tok, cols), jnp.bfloat16),
        scratch_shapes=[
            pltpu.VMEM((slots, tok, depth), jnp.bfloat16),
            pltpu.VMEM((slots, depth, cols), jnp.bfloat16),
            pltpu.VMEM((tok, cols), jnp.float32),
            pltpu.SemaphoreType.DMA((slots,)),
            pltpu.SemaphoreType.DMA((1, slots)),
        ],
        compiler_params=pltpu.CompilerParams(vmem_limit_bytes=60 * MIB),
        cost_estimate=SHORT,
    )(panel, *near, *[w for pieces in far for w in pieces], scale, cos, sin)


def attend_kernel(parts, chunks, pair, r_ref, *refs):
    chunk_refs, pieces = refs[:chunks], refs[chunks : chunks + parts]
    o_ref, q_ref, turned, top, total, acc = refs[chunks + parts :]
    r = r_ref[0]
    tok = q_ref.shape[0]
    step = pl.program_id(0)
    per = pl.num_programs(0) // chunks
    for i in range(chunks):

        @pl.when(step // per == i)
        def _():
            q_ref[...] = chunk_refs[i][...]

    dims = (((1,), (1,)), ((), ()))

    @pl.when(step == 0)
    def _():
        for j in range(parts):
            turned[j] = pieces[j][:, HD:].T

    def scores(j, g):
        return lax.dot_general(
            pieces[j][:, :HD],
            q_ref[:, g * HD : (g + 1) * HD],
            dims,
            preferred_element_type=jnp.float32,
        )

    key = lax.broadcasted_iota(jnp.int32, (tok, tok), 0)
    query = lax.broadcasted_iota(jnp.int32, (tok, tok), 1)
    for g in range(pair):
        s = jnp.where(key <= query, scores(0, g), -jnp.inf)
        m = jnp.max(s, axis=0, keepdims=True)
        p = jnp.exp2(s - m)
        top[g] = m
        total[g] = jnp.sum(p, axis=0, keepdims=True)
        acc[g] = jnp.dot(turned[0], p.astype(jnp.bfloat16), preferred_element_type=jnp.float32)
    for j in range(1, parts):

        @pl.when(jnp.bitwise_xor(r, j) < r)
        def _():
            for g in range(pair):
                s = scores(j, g)
                m = jnp.maximum(top[g], jnp.max(s, axis=0, keepdims=True))
                keep = jnp.exp2(top[g] - m)
                p = jnp.exp2(s - m)
                top[g] = m
                total[g] = total[g] * keep + jnp.sum(p, axis=0, keepdims=True)
                acc[g] = acc[g] * keep + jnp.dot(
                    turned[j], p.astype(jnp.bfloat16), preferred_element_type=jnp.float32
                )

    for g in range(pair):
        o_ref[:, g * HD : (g + 1) * HD] = (acc[g] / total[g]).T.astype(o_ref.dtype)


def attend(r, queries, pieces):
    tok, cols = queries[0].shape
    chunks, parts = len(queries), len(pieces)
    pair = 2 if cols // HD % 2 == 0 else 1
    per = cols // (HD * pair)
    heads = chunks * cols // HD

    def query_spec(i):
        return pl.BlockSpec((tok, pair * HD), lambda h, r: (0, jnp.clip(h - i * per, 0, per - 1)))

    return pl.pallas_call(
        functools.partial(attend_kernel, parts, chunks, pair),
        grid_spec=pltpu.PrefetchScalarGridSpec(
            num_scalar_prefetch=1,
            grid=(chunks * per,),
            in_specs=[query_spec(i) for i in range(chunks)]
            + [pl.BlockSpec((tok, 2 * HD), lambda h, r: (0, 0)) for _ in pieces],
            out_specs=pl.BlockSpec((tok, pair * HD), lambda h, r: (0, h)),
            scratch_shapes=[
                pltpu.VMEM((tok, pair * HD), jnp.bfloat16),
                pltpu.VMEM((parts, HD, tok), jnp.bfloat16),
                pltpu.VMEM((pair, 1, tok), jnp.float32),
                pltpu.VMEM((pair, 1, tok), jnp.float32),
                pltpu.VMEM((pair, HD, tok), jnp.float32),
            ],
        ),
        out_shape=jax.ShapeDtypeStruct((tok, chunks * cols), jnp.bfloat16),
        compiler_params=pltpu.CompilerParams(
            dimension_semantics=("arbitrary",), vmem_limit_bytes=32 * MIB
        ),
        cost_estimate=SHORT,
    )(r.reshape(1), *queries, *pieces)


def finish_kernel(plan, n_refs, *refs):
    arrays, (*old, o_ref, a_buf, w_buf, acc, a_sem, w_sem) = take(refs, n_refs)
    depth = a_buf.shape[2]
    steps = []
    for panel, slot, column, weights, row in plan:
        left = arrays[panel].at[slot, :, pl.ds(column, depth)]
        steps.append((left, [[arrays[weights].at[pl.ds(row, depth), :]]]))
    acc[...] = old[0][...] if old else jnp.zeros_like(acc)
    multiply(steps, a_buf, [w_buf], [acc], a_sem, w_sem)
    o_ref[...] = acc[...].astype(o_ref.dtype)


def finish(arrays, plan, depth, dtype, total=None):
    tok = arrays[plan[0][0]].shape[1]
    cols = arrays[plan[0][3]].shape[1]
    n = len(plan)
    hbm = pl.BlockSpec(memory_space=pl.ANY)
    vmem = pl.BlockSpec(memory_space=pltpu.VMEM)
    old = [] if total is None else [total]
    return pl.pallas_call(
        functools.partial(finish_kernel, plan, len(arrays)),
        in_specs=[hbm] * len(arrays) + [vmem] * len(old),
        out_specs=vmem,
        out_shape=jax.ShapeDtypeStruct((tok, cols), dtype),
        scratch_shapes=[
            pltpu.VMEM((n, tok, depth), jnp.bfloat16),
            pltpu.VMEM((n, depth, cols), jnp.bfloat16),
            pltpu.VMEM((tok, cols), jnp.float32),
            pltpu.SemaphoreType.DMA((n,)),
            pltpu.SemaphoreType.DMA((1, n)),
        ],
        compiler_params=pltpu.CompilerParams(vmem_limit_bytes=60 * MIB),
        cost_estimate=SHORT,
    )(*arrays, *old)


def per_device(hidden, norm_gain, wq, wk, wv, wo):
    tok, feat = hidden.shape
    n_row, n_col = lax.axis_size("row"), lax.axis_size("col")
    r, c = lax.axis_index("row"), lax.axis_index("col")
    depth = feat * n_col
    rows = wq.shape[0]
    cols = wq.shape[1]

    kv_cols = wk.shape[1]
    group = max(1, HD // kv_cols)
    stacked = jnp.stack((wk, wv), axis=1)
    for bit in range(group.bit_length() - 1):
        other = swap(stacked, "col", 1 << bit)
        stacked = order_pair(stacked, other, c, bit, 2)
    stacked = stacked.reshape(rows, 2 * HD)

    n_heads = cols // HD
    first_heads = n_heads // 2
    late_heads = n_heads - first_heads
    if n_heads >= 4:
        sizes = [first_heads // 2, first_heads - first_heads // 2, late_heads // 2]
        sizes.append(late_heads - late_heads // 2)
    else:
        sizes = [first_heads, late_heads]
    early = 2 if n_heads >= 4 else 1
    wide, rest = first_heads * HD, late_heads * HD
    chunks = [
        wq[:, sum(sizes[:i]) * HD : sum(sizes[: i + 1]) * HD] for i in range(len(sizes))
    ]

    def by_block(far):
        return [list(pieces) for pieces in zip(*far)]

    half = HD // 2
    positions = r * tok + jnp.arange(tok)
    freqs = 10000.0 ** (-jnp.arange(half).astype(jnp.float32) / half)
    angles = positions.astype(jnp.float32)[:, None] * freqs[None, :]
    cosine, sine = jnp.cos(angles), jnp.sin(angles)
    cosine = jnp.concatenate([cosine, cosine], axis=1)
    sine = jnp.concatenate([-sine, sine], axis=1)
    factor = HD ** (-0.5) * math.log2(math.e)

    per = rows // feat

    def put(panel, found):
        for source, first, piece in found:
            slot = (source // per ^ r) * per + source % per
            panel = lax.dynamic_update_slice(panel, piece[None], (slot, first, 0))
        return panel

    wider = hidden.astype(jnp.float32)
    gain = lax.dynamic_slice(norm_gain, (c * feat,), (feat,))
    squares = jnp.sum(wider * wider, axis=1)
    ring = Ring((wider * gain).astype(jnp.bfloat16))
    hops = n_col // 2
    sq_bits = n_col.bit_length() - 1
    x_sent = exchange(stacked)
    gathering = gather_near(stacked)
    got_near = []
    panel = put(blank((n_col, tok, feat)), ring.found)
    for i in range(hops):
        last_hop = i == hops - 1
        beside = [panel, cosine, sine, *gathering]
        if i < sq_bits:
            beside.append(swap(squares, "col", 1 << i))
        ahead = chunks[i : i + 1] if i < len(sizes) - 1 else []
        if not last_hop and x_sent is not None:
            beside.append(x_sent)
        beside = ring.hop(beside=[*beside, *ahead])
        (panel, cosine, sine), near, beside = take(beside, 3, len(gathering))
        panel = put(panel, ring.found[-2:])
        got_near.append(near)
        if i < sq_bits:
            squares, beside = squares + beside[0], beside[1:]
        if last_hop:
            break
        gathering = []
        if x_sent is not None:
            gathering = gather_near(beside[0])
            beside = beside[1:]
        x_sent = exchange(beside[0]) if ahead else None
        if i == hops - 2:
            gathering = [*gathering, *gather_near(after(wq, ring.last[0]))]
    blocks_near = len(got_near[0])
    kv_near, kv_far = got_near[0], got_near[1]
    q_near = got_near[-1][-blocks_near:]
    q_far = [near[:blocks_near] for near in got_near[2:] if len(near) > 0]
    scale = lax.rsqrt(squares / depth + 1e-05)[:, None]

    kv = project(panel, kv_near, by_block([kv_far]), 0, 1, 1.0, scale, cosine, sine)
    kv, *arrived = lax.optimization_barrier((kv, *([x_sent] if x_sent is not None else [])))
    scale = after(scale, kv)
    queries = project(
        panel, q_near, by_block(q_far[:early]), 0, first_heads, factor, scale, cosine, sine
    )
    beside = [exchange(kv), queries, *gather_near(kv)]
    for piece in arrived:
        beside += gather_near(piece)
    kv_other, queries, *beside = lax.optimization_barrier(tuple(beside))
    kv_pieces, far = take(beside, blocks_near)
    late_far = [far] if arrived else []
    kv_pieces = [*kv_pieces, *gather_near(kv_other)]
    last_other = exchange(after(chunks[-1], kv_other))
    heads = attend(r, [queries], kv_pieces)

    def o_rows(first, wide):
        return wo.reshape(-1, cols, wo.shape[1])[:, first : first + wide].reshape(-1, wo.shape[1])

    o_first = o_rows(0, wide)
    ring = Ring(heads)
    first_panel = put(blank((n_col, tok, wide)), ring.found)
    second_panel = blank((n_col, tok, rest))
    last_other, o_first, first_panel, second_panel = ring.hop(
        beside=[last_other, o_first, first_panel, second_panel]
    )
    first_panel = put(first_panel, ring.found[-2:])
    o_first = exchange(o_first)
    far = gather_near(last_other)
    late_far = by_block([*late_far, far])
    parts = [(0, rest // 2), (rest // 2, rest - rest // 2)] if rest >= 2 * HD else [(0, rest)]
    o_parts = [o_rows(wide + first, part) for first, part in parts]
    queries = project(
        panel, q_near, late_far, wide, late_heads, factor, scale, cosine, sine
    )
    queries, first_panel, *o_parts = ring.hop(beside=[queries, first_panel, *o_parts])
    first_panel = put(first_panel, ring.found[-2:])
    o_near = gather_near(after(wo, queries))
    beside = ring.hop(beside=[attend(r, [queries], kv_pieces), first_panel, *o_near])
    (heads, first_panel), o_near = take(beside, 2)
    first_panel = put(first_panel, ring.found[-2:])
    second = Ring(heads)
    second_panel = put(second_panel, second.found)
    others, gathered, sent = [], [], o_first
    for i in range(hops):
        arrived, hop = ring.last, ring.hops
        ring.hop(*second.last)
        beside = [first_panel, second_panel]
        if gathered and i in (1, 3):
            beside += gathered[-1]
        if i in (0, 2) and len(others) < len(parts):
            beside.append(sent)
        (first_panel, second_panel), beside = take(second.hop(*arrived, beside=beside), 2)
        if ring.hops > hop:
            first_panel = put(first_panel, ring.found[-2:])
        second_panel = put(second_panel, second.found[-2:])
        if gathered and i in (1, 3):
            gathered[-1], beside = take(beside, blocks_near)
        if i in (0, 2) and len(others) < len(parts):
            gathered.append(gather_near(beside[0]))
            sent = exchange(after(o_parts[len(others)], beside[0]))
            others.append(sent)

    while len(gathered) < len(parts):
        gathered.append(gather_near(others[len(gathered) - 1]))
    half = n_col // 2
    unit = math.gcd(wide, rest)
    arrays = [first_panel, second_panel, *o_near, *gathered[0]]
    plan = []
    for k in range(n_col):
        p, s = k // per, k % per
        for at in range(0, wide, unit):
            row = s * cols + at if p < blocks_near else s * wide + at
            plan.append((0, k, at, 2 + p, row))
        for at in range(0, rest, unit):
            if p < blocks_near:
                plan.append((1, k, at, 2 + p, s * cols + wide + at))
    total = finish(arrays, plan, unit, jnp.float32)
    for j, (first, part) in enumerate(parts):
        if j + 1 < len(gathered):
            far = gathered[j + 1]
        else:
            far = gather_near(after(others[j], total))
        plan = [
            (0, k, first, 1 + k // per - blocks_near, k % per * part) for k in range(half, n_col)
        ]
        dtype = jnp.bfloat16 if j == len(parts) - 1 else jnp.float32
        total = finish([second_panel, *far], plan, part, dtype, total)
    return total


def solution(mesh):
    in_specs = (
        P("row", "col"),
        P(),
        P("row", "col"),
        P("row", "col"),
        P("row", "col"),
        P("row", "col"),
    )
    out_specs = P("row", "col")
    return jax.shard_map(
        per_device, mesh=mesh, in_specs=in_specs, out_specs=out_specs, check_vma=False
    )
```

time: 318 us -> 304 us (0.956)
  blocking collectives: 52.9 us -> 0 us
  waiting for transfers between devices: 127 us -> 143 us
  starting transfers between devices: 26.4 us -> 36.8 us
  Pallas kernels: 57.5 us -> 66.1 us
  local copies, waits for them, and re-layouts: 43.4 us -> 49.3 us
  other arithmetic: 8.76 us -> 5.36 us
    ppermute x18 -> x25, waiting for transfers between devices: 31.7 us -> 95.2 us  [swap(): lax.ppermute(array, axis, [(i, i ^ mask) for i in range(lax.axis_size(axi...]
    psum x1 -> x0, blocking collectives: 52.9 us -> none  [per_device(): squares = lax.psum(jnp.sum(wider * wider, axis=1, keepdims=True), 'col')]
    ppermute x16 -> x24, waiting for transfers between devices: 95.5 us -> 47.7 us  [the longest x12 36.4 us: hop(): below = lax.ppermute(below, 'col', self.up)]
    another operation x2 -> x0, local copies, waits for them, and re-layouts: 8.71 us -> none
    pallas_call x5 -> x9, Pallas kernels: 43.6 us -> 52 us  [the longest x3 28.6 us: project(): pl.pallas_call(functools.partial(project_kernel, len(near), len(far), chu...]
    ppermute x16 -> x24, starting transfers between devices: 16.7 us -> 24.5 us  [the longest x12 18.3 us: hop(): below = lax.ppermute(below, 'col', self.up)]
    dynamic_update_slice x17 -> x26, local copies, waits for them, and re-layouts: 24.6 us -> 30.4 us  [put(): panel = lax.dynamic_update_slice(panel, piece[None], (slot, first, 0))]
    unnamed x16 -> x40, local copies, waits for them, and re-layouts: 1.55 us -> 5.59 us
  transfers between devices with their start and end apart: 34 -> 49, of which waited for: 17 -> 26; matrix products, arithmetic and copies ran while one was open for 15% -> 15% of each run, Pallas kernels for 16% -> 20%
where the time goes in v5:
time: 304 us; the launch traced here: 301 us
  waiting for transfers between devices  143 us (47%)
  Pallas kernels  66.1 us (22%)
  local copies, waits for them, and re-layouts  49.3 us (16%)
  starting transfers between devices  36.8 us (12%)
  other arithmetic  5.36 us (2%)
    ppermute x25, waiting for transfers between devices, swap(): lax.ppermute(array, axis, [(i, i ^ mask) for i in range(lax.axis_size(axi...  95.2 us
    ppermute x12, waiting for transfers between devices, hop(): below = lax.ppermute(below, 'col', self.up)  36.4 us
    dynamic_update_slice x26, local copies, waits for them, and re-layouts, put(): panel = lax.dynamic_update_slice(panel, piece[None], (slot, first, 0))  30.4 us
    pallas_call x3, Pallas kernels, project(): pl.pallas_call(functools.partial(project_kernel, len(near), len(far), chu...  28.6 us
    pallas_call x3, Pallas kernels, finish(): pl.pallas_call(functools.partial(finish_kernel, plan, len(arrays)), in_sp...  23.4 us
    ppermute x12, starting transfers between devices, hop(): below = lax.ppermute(below, 'col', self.up)  18.3 us
    pallas_call x2, Pallas kernels, attend(): pl.pallas_call(functools.partial(attend_kernel, parts, chunks, pair), gri...  14.1 us
    ppermute x25, starting transfers between devices, swap(): lax.ppermute(array, axis, [(i, i ^ mask) for i in range(lax.axis_size(axi...  12.3 us
  transfers between devices with their start and end apart: 49, of which 26 were waited for; matrix products, arithmetic and copies ran while one was open for 15% of the time, Pallas kernels for 20%

profile of v5, /device:TPU:2, one launch (start us, length us, event | category | flops | bytes accessed | tf_op | source)
XLA Modules:
  0.0 301.0 jit_solution(15799111083505232942)
XLA Ops:
  6.8 2.0 collective-permute-start.3
  9.9 4.3 %fusion.5 = (bf16[2048,256]{1,0:T(8,128)(2,1)}, bf16[2048,256]{1,0:T(8,128)(2,1)}, bf16[2048,256]{1,0:T(8,128)(2,1)}, bf16[2048,256]{1,0:T(8,128)(2,1)}) fusion(bf16[2048,1024]{1,0:T(8,128)(2,1)} %refs_0_.1), kind=kLoop, calls=%fused_computation.42 | loop fusion | bytes 8388608 | tf_op jit(solution)/shard_map/slice | solution.py:328
  15.1 13.0 %collective-permute-done.3 = f32[512]{0:T(512)S(1)} collective-permute-done((f32[512]{0:T(512)S(1)}, f32[512]{0:T(512)S(1)}, u32[]{:S(2)}, u32[]{:S(2)}) %collective-permute-start.3) | collective-permute-done | bytes 2080 | tf_op jit(solution)/shard_map/ppermute | solution.py:23
  29.5 2.6 collective-permute-done.4.refs_2_
  37.3 2.3 bitcast_dynamic-update-slice_fusion.4
  39.6 18.8 %collective-permute-done.8 = f32[512]{0:T(512)S(1)} collective-permute-done((f32[512]{0:T(512)S(1)}, f32[512]{0:T(512)S(1)}, u32[]{:S(2)}, u32[]{:S(2)}) %collective-permute-start.8) | collective-permute-done | bytes 2080 | tf_op jit(solution)/shard_map/ppermute | solution.py:23
  62.2 2.8 collective-permute-start.13
  65.1 2.3 bitcast_dynamic-update-slice_fusion.3
  67.4 2.3 bitcast_dynamic-update-slice_fusion.2
  69.7 17.6 %collective-permute-done.13 = f32[512]{0:T(512)S(1)} collective-permute-done((f32[512]{0:T(512)S(1)}, f32[512]{0:T(512)S(1)}, u32[]{:S(2)}, u32[]{:S(2)}) %collective-permute-start.13) | collective-permute-done | bytes 2080 | tf_op jit(solution)/shard_map/ppermute | solution.py:23
  95.3 8.0 %collective-permute-done.15 = bf16[256,1024]{1,0:T(8,128)(2,1)} collective-permute-done((bf16[256,1024]{1,0:T(8,128)(2,1)}, bf16[256,1024]{1,0:T(8,128)(2,1)}, u32[]{:S(2)}, u32[]{:S(2)}) %collective-permute-start.15) | collective-permute-done | bytes 524320 | tf_op jit(solution)/shard_map/ppermute | solution.py:80
  103.3 2.1 collective-permute-done.16
  105.4 1.9 bitcast_dynamic-update-slice_fusion.22
  109.2 7.1 %shard_map.65.refs_1_ = bf16[512,256]{1,0:T(8,128)(2,1)} custom-call(bf16[8,512,1024]{2,1,0:T(8,128)(2,1)} %bitcast_dynamic-update-slice_fusion.21.panel_ref, bf16[2048,256]{1,0:T(8,128)(2,1)} %copy-done.6, bf16[2048,256]{1,0:T(8,128)(2,1)} %collective-permute-done.2.refs_1_, bf16[2048,256]{1,0:T(8,128)(2,1)} %collective-permute-done.4.refs_2_, ...), custom_call_target="tpu_custom_call" | custom-call | flops 1 | bytes 1 | tf_op jit(solution)/shard_map/pallas_call | solution.py:158
  119.1 10.7 %shard_map.66.refs_0_ = bf16[512,512]{1,0:T(8,128)(2,1)} custom-call(bf16[8,512,1024]{2,1,0:T(8,128)(2,1)} %bitcast_dynamic-update-slice_fusion.21.panel_ref, bf16[2048,1024]{1,0:T(8,128)(2,1)} %refs_0_.1, bf16[2048,1024]{1,0:T(8,128)(2,1)} %collective-permute-done.18.refs_1_, bf16[2048,256]{1,0:T(8,128)(2,1)} %copy-done.10, ...), custom_call_target="tpu_custom_call" | custom-call | flops 1 | bytes 1 | tf_op jit(solution)/shard_map/pallas_call | solution.py:158
  135.1 7.1 %shard_map.67 = bf16[512,512]{1,0:T(8,128)(2,1)S(1)} custom-call(s32[1]{0:T(128)} %bitcast.r_ref, bf16[512,512]{1,0:T(8,128)(2,1)S(1)} %copy-done.2, bf16[512,256]{1,0:T(8,128)(2,1)S(1)} %copy-done, bf16[512,256]{1,0:T(8,128)(2,1)S(1)} %collective-permute-done.21.refs_2_, bf16[512,256]{1,0:T(8,128)(2,1)S(1)} %collective-permute-done.20.refs_3_, ...), custom_call_target="tpu_custom_call" | custom-call | flops 1 | bytes 1 | tf_op jit(solution)/shard_map/pallas_call | solution.py:241
  144.3 3.3 %slice.52 = bf16[2,512,1024]{2,1,0:T(8,128)(2,1)} slice(bf16[2,1024,1024]{2,1,0:T(8,128)(2,1)} %bitcast.67), slice={[0:2], [0:512], [0:1024]} | slice | bytes 4194304 | tf_op jit(solution)/shard_map/slice | solution.py:407
  148.4 7.2 %collective-permute-done.24 = bf16[512,512]{1,0:T(8,128)(2,1)S(1)} collective-permute-done((bf16[512,512]{1,0:T(8,128)(2,1)S(1)}, bf16[512,512]{1,0:T(8,128)(2,1)S(1)}, u32[]{:S(2)}, u32[]{:S(2)}) %collective-permute-start.24) | collective-permute-done | bytes 524320 | tf_op jit(solution)/shard_map/ppermute | solution.py:80
  155.6 2.0 collective-permute-done.25
  162.9 1.9 bitcast_dynamic-update-slice_fusion.18
  164.8 10.8 %shard_map.70.refs_0_ = bf16[512,512]{1,0:T(8,128)(2,1)} custom-call(bf16[8,512,1024]{2,1,0:T(8,128)(2,1)} %bitcast_dynamic-update-slice_fusion.21.panel_ref, bf16[2048,1024]{1,0:T(8,128)(2,1)} %refs_0_.1, bf16[2048,1024]{1,0:T(8,128)(2,1)} %collective-permute-done.18.refs_1_, bf16[2048,256]{1,0:T(8,128)(2,1)} %collective-permute-done.19.refs_2_, ...), custom_call_target="tpu_custom_call" | custom-call | flops 1 | bytes 1 | tf_op jit(solution)/shard_map/pallas_call | solution.py:158
  178.9 7.1 %shard_map.71 = bf16[512,512]{1,0:T(8,128)(2,1)S(1)} custom-call(s32[1]{0:T(128)} %bitcast.r_ref, bf16[512,512]{1,0:T(8,128)(2,1)S(1)} %copy-done.1, bf16[512,256]{1,0:T(8,128)(2,1)S(1)} %copy-done, bf16[512,256]{1,0:T(8,128)(2,1)S(1)} %collective-permute-done.21.refs_2_, bf16[512,256]{1,0:T(8,128)(2,1)S(1)} %collective-permute-done.20.refs_3_, ...), custom_call_target="tpu_custom_call" | custom-call | flops 1 | bytes 1 | tf_op jit(solution)/shard_map/pallas_call | solution.py:241
  186.8 1.9 bitcast_dynamic-update-slice_fusion.16
  196.1 27.6 %collective-permute-done.35.refs_4_ = bf16[1024,1024]{1,0:T(8,128)(2,1)S(1)} collective-permute-done((bf16[1024,1024]{1,0:T(8,128)(2,1)S(1)}, bf16[1024,1024]{1,0:T(8,128)(2,1)S(1)}, u32[]{:S(2)}, u32[]{:S(2)}) %collective-permute-start.35) | collective-permute-done | bytes 2097184 | tf_op jit(solution)/shard_map/ppermute | solution.py:23
  225.9 6.7 %collective-permute-done.36 = bf16[256,512]{1,0:T(8,128)(2,1)S(1)} collective-permute-done((bf16[256,512]{1,0:T(8,128)(2,1)S(1)}, bf16[256,512]{1,0:T(8,128)(2,1)S(1)}, u32[]{:S(2)}, u32[]{:S(2)}) %collective-permute-start.36) | collective-permute-done | bytes 262176 | tf_op jit(solution)/shard_map/ppermute | solution.py:80
  239.4 7.8 %collective-permute-done.38 = bf16[512,512]{1,0:T(8,128)(2,1)S(1)} collective-permute-done((bf16[512,512]{1,0:T(8,128)(2,1)S(1)}, bf16[512,512]{1,0:T(8,128)(2,1)S(1)}, u32[]{:S(2)}, u32[]{:S(2)}) %collective-permute-start.38) | collective-permute-done | bytes 524320 | tf_op jit(solution)/shard_map/ppermute | solution.py:80
  252.1 7.8 %collective-permute-done.43.refs_1_ = bf16[512,1024]{1,0:T(8,128)(2,1)S(1)} collective-permute-done((bf16[512,1024]{1,0:T(8,128)(2,1)S(1)}, bf16[512,1024]{1,0:T(8,128)(2,1)S(1)}, u32[]{:S(2)}, u32[]{:S(2)}) %collective-permute-start.43) | collective-permute-done | bytes 1048608 | tf_op jit(solution)/shard_map/ppermute | solution.py:23
  265.7 4.8 %collective-permute-done.44 = bf16[256,512]{1,0:T(8,128)(2,1)S(1)} collective-permute-done((bf16[256,512]{1,0:T(8,128)(2,1)S(1)}, bf16[256,512]{1,0:T(8,128)(2,1)S(1)}, u32[]{:S(2)}, u32[]{:S(2)}) %collective-permute-start.44) | collective-permute-done | bytes 262176 | tf_op jit(solution)/shard_map/ppermute | solution.py:80
  273.4 11.6 %shard_map.72.refs_3_ = f32[512,1024]{1,0:T(8,128)} custom-call(bf16[8,512,512]{2,1,0:T(8,128)(2,1)} %bitcast_dynamic-update-slice_fusion.25.refs_0_, bf16[8,512,512]{2,1,0:T(8,128)(2,1)} %bitcast_dynamic-update-slice_fusion.23.refs_1_.refs_0_, bf16[2048,1024]{1,0:T(8,128)(2,1)} %refs_2_, bf16[2048,1024]{1,0:T(8,128)(2,1)} %copy-done.5, ...), custom_call_target="tpu_custom_call" | custom-call | flops 1 | bytes 1 | tf_op jit(solution)/shard_map/pallas_call | solution.py:284
  285.1 6.1 %shard_map.73.refs_3_ = f32[512,1024]{1,0:T(8,128)} custom-call(bf16[8,512,512]{2,1,0:T(8,128)(2,1)} %bitcast_dynamic-update-slice_fusion.23.refs_1_.refs_0_, bf16[512,1024]{1,0:T(8,128)(2,1)} %copy-done.11, bf16[512,1024]{1,0:T(8,128)(2,1)} %copy-done.13, f32[512,1024]{1,0:T(8,128)} %shard_map.72.refs_3_), custom_call_target="tpu_custom_call" | custom-call | flops 1 | bytes 1 | tf_op jit(solution)/shard_map/pallas_call | solution.py:284
  291.3 2.9 collective-permute-done.48.refs_2_
  295.2 5.6 %shard_map.74 = bf16[512,1024]{1,0:T(8,128)(2,1)} custom-call(bf16[8,512,512]{2,1,0:T(8,128)(2,1)} %bitcast_dynamic-update-slice_fusion.23.refs_1_.refs_0_, bf16[512,1024]{1,0:T(8,128)(2,1)} %collective-permute-done.47.refs_1_, bf16[512,1024]{1,0:T(8,128)(2,1)} %copy-done.14, f32[512,1024]{1,0:T(8,128)} %shard_map.73.refs_3_), custom_call_target="tpu_custom_call" | custom-call | flops 1 | bytes 1 | tf_op jit(solution)/shard_map/pallas_call | solution.py:284
  (165 shorter events, 80.6 us)
Async XLA Ops:
  3.0 25.1 %collective-permute-start = (bf16[512,1024]{1,0:T(8,128)(2,1)}, bf16[512,1024]{1,0:T(8,128)(2,1)S(1)}, u32[]{:S(2)}, u32[]{:S(2)}) collective-permute-start(bf16[512,1024]{1,0:T(8,128)(2,1)} %get-tuple-element.218), channel_id=1, source_target_pairs={{0,2},{2,4},{4,6},{6,7},{7,5},{5,3},{3,1},{1,0},{8,10},{10,12},{12... | collective-permute-start | bytes 3145736 | tf_op jit(solution)/shard_map/ppermute | solution.py:80
  4.6 24.9 %collective-permute-start.1 = (bf16[512,1024]{1,0:T(8,128)(2,1)}, bf16[512,1024]{1,0:T(8,128)(2,1)}, u32[]{:S(2)}, u32[]{:S(2)}) collective-permute-start(bf16[512,1024]{1,0:T(8,128)(2,1)} %get-tuple-element.218), channel_id=1, source_target_pairs={{2,0},{4,2},{6,4},{7,6},{5,7},{3,5},{1,3},{0,1},{10,8},{12,10},{14... | collective-permute-start | bytes 3145736 | tf_op jit(solution)/shard_map/ppermute | solution.py:81
  6.3 23.2 %collective-permute-start.2 = (bf16[2048,256]{1,0:T(8,128)(2,1)S(1)}, bf16[2048,256]{1,0:T(8,128)(2,1)}, u32[]{:S(2)}, u32[]{:S(2)}) collective-permute-start(bf16[2048,256]{1,0:T(8,128)(2,1)S(1)} %copy_bitcast_fusion.refs_0_), channel_id=1, source_target_pairs={{0,8},{8,0},{16,24},{24,16},{1,9},{9,1},{17,25},{25,17},{2,10},{10... | collective-permute-start | bytes 3145736 | tf_op jit(solution)/shard_map/ppermute | solution.py:23
  6.4 25.7 %collective-permute-start.4 = (bf16[2048,256]{1,0:T(8,128)(2,1)S(1)}, bf16[2048,256]{1,0:T(8,128)(2,1)}, u32[]{:S(2)}, u32[]{:S(2)}) collective-permute-start(bf16[2048,256]{1,0:T(8,128)(2,1)S(1)} %copy_bitcast_fusion.refs_0_), channel_id=1, source_target_pairs={{0,16},{8,24},{16,0},{24,8},{1,17},{9,25},{17,1},{25,9},{2,18},{10... | collective-permute-start | bytes 3145736 | tf_op jit(solution)/shard_map/ppermute | solution.py:23
  6.8 21.3 %collective-permute-start.3 = (f32[512]{0:T(512)S(1)}, f32[512]{0:T(512)S(1)}, u32[]{:S(2)}, u32[]{:S(2)}) collective-permute-start(f32[512]{0:T(512)S(1)} %fusion.1), channel_id=1, source_target_pairs={{0,1},{1,0},{2,3},{3,2},{4,5},{5,4},{6,7},{7,6},{8,9},{9,8},{10,11... | collective-permute-start | bytes 6152 | tf_op jit(solution)/shard_map/ppermute | solution.py:23
  32.1 26.3 %collective-permute-start.5 = (bf16[512,1024]{1,0:T(8,128)(2,1)S(1)}, bf16[512,1024]{1,0:T(8,128)(2,1)}, u32[]{:S(2)}, u32[]{:S(2)}) collective-permute-start(bf16[512,1024]{1,0:T(8,128)(2,1)S(1)} %collective-permute-done), channel_id=1, source_target_pairs={{0,2},{2,4},{4,6},{6,7},{7,5},{5,3},{3,1},{1,0},{8,10},{10,12},{12... | collective-permute-start | bytes 3145736 | tf_op jit(solution)/shard_map/ppermute | solution.py:80
  33.7 24.7 %collective-permute-start.6 = (bf16[512,1024]{1,0:T(8,128)(2,1)}, bf16[512,1024]{1,0:T(8,128)(2,1)S(1)}, u32[]{:S(2)}, u32[]{:S(2)}) collective-permute-start(bf16[512,1024]{1,0:T(8,128)(2,1)} %collective-permute-done.1), channel_id=1, source_target_pairs={{2,0},{4,2},{6,4},{7,6},{5,7},{3,5},{1,3},{0,1},{10,8},{12,10},{14... | collective-permute-start | bytes 3145736 | tf_op jit(solution)/shard_map/ppermute | solution.py:81
  34.1 24.3 %collective-permute-start.7 = (bf16[2048,256]{1,0:T(8,128)(2,1)}, bf16[2048,256]{1,0:T(8,128)(2,1)}, u32[]{:S(2)}, u32[]{:S(2)}) collective-permute-start(bf16[2048,256]{1,0:T(8,128)(2,1)} %collective-permute-done.4.refs_2_), channel_id=1, source_target_pairs={{0,8},{8,0},{16,24},{24,16},{1,9},{9,1},{17,25},{25,17},{2,10},{10... | collective-permute-start | bytes 3145736 | tf_op jit(solution)/shard_map/ppermute | solution.py:23
  34.1 25.8 %collective-permute-start.9 = (bf16[2048,256]{1,0:T(8,128)(2,1)}, bf16[2048,256]{1,0:T(8,128)(2,1)S(1)}, u32[]{:S(2)}, u32[]{:S(2)}) collective-permute-start(bf16[2048,256]{1,0:T(8,128)(2,1)} %get-tuple-element.118), channel_id=1, source_target_pairs={{0,16},{8,24},{16,0},{24,8},{1,17},{9,25},{17,1},{25,9},{2,18},{10... | collective-permute-start | bytes 3145736 | tf_op jit(solution)/shard_map/ppermute | solution.py:23
  34.4 24.0 %collective-permute-start.8 = (f32[512]{0:T(512)S(1)}, f32[512]{0:T(512)S(1)}, u32[]{:S(2)}, u32[]{:S(2)}) collective-permute-start(f32[512]{0:T(512)S(1)} %add.301), channel_id=1, source_target_pairs={{0,2},{1,3},{2,0},{3,1},{4,6},{5,7},{6,4},{7,5},{8,10},{9,11},{10,... | collective-permute-start | bytes 6152 | tf_op jit(solution)/shard_map/ppermute | solution.py:23
  59.9 27.4 %collective-permute-start.10 = (bf16[512,1024]{1,0:T(8,128)(2,1)}, bf16[512,1024]{1,0:T(8,128)(2,1)S(1)}, u32[]{:S(2)}, u32[]{:S(2)}) collective-permute-start(bf16[512,1024]{1,0:T(8,128)(2,1)} %collective-permute-done.5), channel_id=1, source_target_pairs={{0,2},{2,4},{4,6},{6,7},{7,5},{5,3},{3,1},{1,0},{8,10},{10,12},{12... | collective-permute-start | bytes 3145736 | tf_op jit(solution)/shard_map/ppermute | solution.py:80
  61.5 25.8 %collective-permute-start.11 = (bf16[512,1024]{1,0:T(8,128)(2,1)}, bf16[512,1024]{1,0:T(8,128)(2,1)S(1)}, u32[]{:S(2)}, u32[]{:S(2)}) collective-permute-start(bf16[512,1024]{1,0:T(8,128)(2,1)} %copy-done.15), channel_id=1, source_target_pairs={{2,0},{4,2},{6,4},{7,6},{5,7},{3,5},{1,3},{0,1},{10,8},{12,10},{14... | collective-permute-start | bytes 3145736 | tf_op jit(solution)/shard_map/ppermute | solution.py:81
  61.9 25.4 %collective-permute-start.12 = (bf16[2048,256]{1,0:T(8,128)(2,1)S(1)}, bf16[2048,256]{1,0:T(8,128)(2,1)}, u32[]{:S(2)}, u32[]{:S(2)}) collective-permute-start(bf16[2048,256]{1,0:T(8,128)(2,1)S(1)} %collective-permute-done.9.refs_2_), channel_id=1, source_target_pairs={{0,8},{8,0},{16,24},{24,16},{1,9},{9,1},{17,25},{25,17},{2,10},{10... | collective-permute-start | bytes 3145736 | tf_op jit(solution)/shard_map/ppermute | solution.py:23
  61.9 25.9 %collective-permute-start.14 = (bf16[2048,256]{1,0:T(8,128)(2,1)}, bf16[2048,256]{1,0:T(8,128)(2,1)}, u32[]{:S(2)}, u32[]{:S(2)}) collective-permute-start(bf16[2048,256]{1,0:T(8,128)(2,1)} %get-tuple-element.126), channel_id=1, source_target_pairs={{0,16},{8,24},{16,0},{24,8},{1,17},{9,25},{17,1},{25,9},{2,18},{10... | collective-permute-start | bytes 3145736 | tf_op jit(solution)/shard_map/ppermute | solution.py:23
  62.2 25.1 %collective-permute-start.13 = (f32[512]{0:T(512)S(1)}, f32[512]{0:T(512)S(1)}, u32[]{:S(2)}, u32[]{:S(2)}) collective-permute-start(f32[512]{0:T(512)S(1)} %add.312), channel_id=1, source_target_pairs={{0,4},{1,5},{2,6},{3,7},{4,0},{5,1},{6,2},{7,3},{8,12},{9,13},{10,... | collective-permute-start | bytes 6152 | tf_op jit(solution)/shard_map/ppermute | solution.py:23
  87.8 17.6 %collective-permute-start.18 = (bf16[2048,1024]{1,0:T(8,128)(2,1)}, bf16[2048,1024]{1,0:T(8,128)(2,1)}, u32[]{:S(2)}, u32[]{:S(2)}) collective-permute-start(bf16[2048,1024]{1,0:T(8,128)(2,1)} %refs_0_.1), channel_id=1, source_target_pairs={{0,8},{8,0},{16,24},{24,16},{1,9},{9,1},{17,25},{25,17},{2,10},{10... | collective-permute-start | bytes 12582920 | tf_op jit(solution)/shard_map/ppermute | solution.py:23
  87.8 17.6 %collective-permute-start.17 = (bf16[2048,256]{1,0:T(8,128)(2,1)}, bf16[2048,256]{1,0:T(8,128)(2,1)}, u32[]{:S(2)}, u32[]{:S(2)}) collective-permute-start(bf16[2048,256]{1,0:T(8,128)(2,1)} %collective-permute-done.14.refs_3_), channel_id=1, source_target_pairs={{0,8},{8,0},{16,24},{24,16},{1,9},{9,1},{17,25},{25,17},{2,10},{10... | collective-permute-start | bytes 3145736 | tf_op jit(solution)/shard_map/ppermute | solution.py:23
  89.2 14.1 %collective-permute-start.15 = (bf16[256,1024]{1,0:T(8,128)(2,1)}, bf16[256,1024]{1,0:T(8,128)(2,1)}, u32[]{:S(2)}, u32[]{:S(2)}) collective-permute-start(bf16[256,1024]{1,0:T(8,128)(2,1)} %slice.42), channel_id=1, source_target_pairs={{0,2},{2,4},{4,6},{6,7},{7,5},{5,3},{3,1},{1,0},{8,10},{10,12},{12... | collective-permute-start | bytes 1572872 | tf_op jit(solution)/shard_map/ppermute | solution.py:80
  91.6 13.9 %collective-permute-start.16 = (bf16[256,1024]{1,0:T(8,128)(2,1)}, bf16[256,1024]{1,0:T(8,128)(2,1)}, u32[]{:S(2)}, u32[]{:S(2)}) collective-permute-start(bf16[256,1024]{1,0:T(8,128)(2,1)} %slice.43), channel_id=1, source_target_pairs={{2,0},{4,2},{6,4},{7,6},{5,7},{3,5},{1,3},{0,1},{10,8},{12,10},{14... | collective-permute-start | bytes 1572872 | tf_op jit(solution)/shard_map/ppermute | solution.py:81
  92.9 24.8 %collective-permute-start.19 = (bf16[2048,256]{1,0:T(8,128)(2,1)}, bf16[2048,256]{1,0:T(8,128)(2,1)}, u32[]{:S(2)}, u32[]{:S(2)}) collective-permute-start(bf16[2048,256]{1,0:T(8,128)(2,1)} %get-tuple-element.144), channel_id=1, source_target_pairs={{0,16},{8,24},{16,0},{24,8},{1,17},{9,25},{17,1},{25,9},{2,18},{10... | collective-permute-start | bytes 3145736 | tf_op jit(solution)/shard_map/ppermute | solution.py:23
  130.9 26.7 %collective-permute-start.26 = (bf16[2048,256]{1,0:T(8,128)(2,1)S(1)}, bf16[2048,256]{1,0:T(8,128)(2,1)}, u32[]{:S(2)}, u32[]{:S(2)}) collective-permute-start(bf16[2048,256]{1,0:T(8,128)(2,1)S(1)} %copy-done.17), channel_id=1, source_target_pairs={{0,16},{8,24},{16,0},{24,8},{1,17},{9,25},{17,1},{25,9},{2,18},{10... | collective-permute-start | bytes 3145736 | tf_op jit(solution)/shard_map/ppermute | solution.py:23
  158.6 17.0 %collective-permute-start.27 = (bf16[512,512]{1,0:T(8,128)(2,1)}, bf16[512,512]{1,0:T(8,128)(2,1)S(1)}, u32[]{:S(2)}, u32[]{:S(2)}) collective-permute-start(bf16[512,512]{1,0:T(8,128)(2,1)} %copy-done.18), channel_id=1, source_target_pairs={{0,2},{2,4},{4,6},{6,7},{7,5},{5,3},{3,1},{1,0},{8,10},{10,12},{12... | collective-permute-start | bytes 1572872 | tf_op jit(solution)/shard_map/ppermute | solution.py:80
  160.2 15.4 %collective-permute-start.28 = (bf16[512,512]{1,0:T(8,128)(2,1)}, bf16[512,512]{1,0:T(8,128)(2,1)}, u32[]{:S(2)}, u32[]{:S(2)}) collective-permute-start(bf16[512,512]{1,0:T(8,128)(2,1)} %collective-permute-done.25), channel_id=1, source_target_pairs={{2,0},{4,2},{6,4},{7,6},{5,7},{3,5},{1,3},{0,1},{10,8},{12,10},{14... | collective-permute-start | bytes 1572872 | tf_op jit(solution)/shard_map/ppermute | solution.py:81
  175.6 16.0 %collective-permute-start.32 = (bf16[2048,1024]{1,0:T(8,128)(2,1)}, bf16[2048,1024]{1,0:T(8,128)(2,1)S(1)}, u32[]{:S(2)}, u32[]{:S(2)}) collective-permute-start(bf16[2048,1024]{1,0:T(8,128)(2,1)} %refs_2_), channel_id=1, source_target_pairs={{0,8},{8,0},{16,24},{24,16},{1,9},{9,1},{17,25},{25,17},{2,10},{10... | collective-permute-start | bytes 12582920 | tf_op jit(solution)/shard_map/ppermute | solution.py:23
  175.7 48.0 %collective-permute-start.35 = (bf16[1024,1024]{1,0:T(8,128)(2,1)S(1)}, bf16[1024,1024]{1,0:T(8,128)(2,1)S(1)}, u32[]{:S(2)}, u32[]{:S(2)}) collective-permute-start(bf16[1024,1024]{1,0:T(8,128)(2,1)S(1)} %bitcast.69), channel_id=1, source_target_pairs={{0,16},{8,24},{16,0},{24,8},{1,17},{9,25},{17,1},{25,9},{2,18},{10... | collective-permute-start | bytes 6291464 | tf_op jit(solution)/shard_map/ppermute | solution.py:23
  175.7 14.2 %collective-permute-start.30 = (bf16[512,512]{1,0:T(8,128)(2,1)S(1)}, bf16[512,512]{1,0:T(8,128)(2,1)S(1)}, u32[]{:S(2)}, u32[]{:S(2)}) collective-permute-start(bf16[512,512]{1,0:T(8,128)(2,1)S(1)} %collective-permute-done.27), channel_id=1, source_target_pairs={{0,2},{2,4},{4,6},{6,7},{7,5},{5,3},{3,1},{1,0},{8,10},{10,12},{12... | collective-permute-start | bytes 1572872 | tf_op jit(solution)/shard_map/ppermute | solution.py:80
  177.4 14.1 %collective-permute-start.31 = (bf16[512,512]{1,0:T(8,128)(2,1)}, bf16[512,512]{1,0:T(8,128)(2,1)S(1)}, u32[]{:S(2)}, u32[]{:S(2)}) collective-permute-start(bf16[512,512]{1,0:T(8,128)(2,1)} %collective-permute-done.28), channel_id=1, source_target_pairs={{2,0},{4,2},{6,4},{7,6},{5,7},{3,5},{1,3},{0,1},{10,8},{12,10},{14... | collective-permute-start | bytes 1572872 | tf_op jit(solution)/shard_map/ppermute | solution.py:81
  191.5 32.2 %collective-permute-start.33 = (bf16[512,512]{1,0:T(8,128)(2,1)S(1)}, bf16[512,512]{1,0:T(8,128)(2,1)S(1)}, u32[]{:S(2)}, u32[]{:S(2)}) collective-permute-start(bf16[512,512]{1,0:T(8,128)(2,1)S(1)} %shard_map.71), channel_id=1, source_target_pairs={{0,2},{2,4},{4,6},{6,7},{7,5},{5,3},{3,1},{1,0},{8,10},{10,12},{12... | collective-permute-start | bytes 1572872 | tf_op jit(solution)/shard_map/ppermute | solution.py:80
  193.1 30.6 %collective-permute-start.34 = (bf16[512,512]{1,0:T(8,128)(2,1)S(1)}, bf16[512,512]{1,0:T(8,128)(2,1)S(1)}, u32[]{:S(2)}, u32[]{:S(2)}) collective-permute-start(bf16[512,512]{1,0:T(8,128)(2,1)S(1)} %shard_map.71), channel_id=1, source_target_pairs={{2,0},{4,2},{6,4},{7,6},{5,7},{3,5},{1,3},{0,1},{10,8},{12,10},{14... | collective-permute-start | bytes 1572872 | tf_op jit(solution)/shard_map/ppermute | solution.py:81
  223.7 24.7 %collective-permute-start.40 = (bf16[1024,1024]{1,0:T(8,128)(2,1)S(1)}, bf16[1024,1024]{1,0:T(8,128)(2,1)S(1)}, u32[]{:S(2)}, u32[]{:S(2)}) collective-permute-start(bf16[1024,1024]{1,0:T(8,128)(2,1)S(1)} %collective-permute-done.35.refs_4_), channel_id=1, source_target_pairs={{0,8},{8,0},{16,24},{24,16},{1,9},{9,1},{17,25},{25,17},{2,10},{10... | collective-permute-start | bytes 6291464 | tf_op jit(solution)/shard_map/ppermute | solution.py:23
  236.0 23.9 %collective-permute-start.43 = (bf16[512,1024]{1,0:T(8,128)(2,1)S(1)}, bf16[512,1024]{1,0:T(8,128)(2,1)S(1)}, u32[]{:S(2)}, u32[]{:S(2)}) collective-permute-start(bf16[512,1024]{1,0:T(8,128)(2,1)S(1)} %bitcast.70), channel_id=1, source_target_pairs={{0,16},{8,24},{16,0},{24,8},{1,17},{9,25},{17,1},{25,9},{2,18},{10... | collective-permute-start | bytes 3145736 | tf_op jit(solution)/shard_map/ppermute | solution.py:23
  261.7 29.5 %collective-permute-start.47 = (bf16[512,1024]{1,0:T(8,128)(2,1)}, bf16[512,1024]{1,0:T(8,128)(2,1)}, u32[]{:S(2)}, u32[]{:S(2)}) collective-permute-start(bf16[512,1024]{1,0:T(8,128)(2,1)} %bitcast.19), channel_id=1, source_target_pairs={{0,16},{8,24},{16,0},{24,8},{1,17},{9,25},{17,1},{25,9},{2,18},{10... | collective-permute-start | bytes 3145736 | tf_op jit(solution)/shard_map/ppermute | solution.py:23
  (37 other events, 485.6 us)

commit v6 on v5

--- a/solution.py
+++ b/solution.py
@@ -318,8 +318,9 @@
     first_heads = n_heads // 2
     late_heads = n_heads - first_heads
     if n_heads >= 4:
-        sizes = [first_heads // 2, first_heads - first_heads // 2, late_heads // 2]
-        sizes.append(late_heads - late_heads // 2)
+        last_heads = max(1, late_heads // 4)
+        sizes = [first_heads // 2, first_heads - first_heads // 2, late_heads - last_heads]
+        sizes.append(last_heads)
     else:
         sizes = [first_heads, late_heads]
     early = 2 if n_heads >= 4 else 1
@@ -348,30 +349,32 @@
             panel = lax.dynamic_update_slice(panel, piece[None], (slot, first, 0))
         return panel
 
-    wider = hidden.astype(jnp.float32)
-    gain = lax.dynamic_slice(norm_gain, (c * feat,), (feat,))
-    squares = jnp.sum(wider * wider, axis=1)
-    ring = Ring((wider * gain).astype(jnp.bfloat16))
+    def put_hidden(panel, found):
+        sums = []
+        for source, first, piece in found:
+            wider = piece.astype(jnp.float32)
+            sums.append(jnp.sum(wider * wider, axis=1))
+            gain = lax.dynamic_slice(norm_gain, (source * feat,), (feat,))
+            panel = put(panel, [(source, first, (wider * gain).astype(jnp.bfloat16))])
+        return panel, sums
+
+    ring = Ring(hidden)
     hops = n_col // 2
-    sq_bits = n_col.bit_length() - 1
     x_sent = exchange(stacked)
     gathering = gather_near(stacked)
     got_near = []
-    panel = put(blank((n_col, tok, feat)), ring.found)
+    panel, (squares,) = put_hidden(blank((n_col, tok, feat)), ring.found)
     for i in range(hops):
         last_hop = i == hops - 1
-        beside = [panel, cosine, sine, *gathering]
-        if i < sq_bits:
-            beside.append(swap(squares, "col", 1 << i))
+        beside = [panel, squares, cosine, sine, *gathering]
         ahead = chunks[i : i + 1] if i < len(sizes) - 1 else []
         if not last_hop and x_sent is not None:
             beside.append(x_sent)
         beside = ring.hop(beside=[*beside, *ahead])
-        (panel, cosine, sine), near, beside = take(beside, 3, len(gathering))
-        panel = put(panel, ring.found[-2:])
+        (panel, squares, cosine, sine), near, beside = take(beside, 4, len(gathering))
+        panel, sums = put_hidden(panel, ring.found[-2:])
+        squares += jnp.concatenate(sums) if last_hop else sums[0] + sums[1]
         got_near.append(near)
-        if i < sq_bits:
-            squares, beside = squares + beside[0], beside[1:]
         if last_hop:
             break
         gathering = []
@@ -388,25 +391,25 @@
     scale = lax.rsqrt(squares / depth + 1e-05)[:, None]
 
     kv = project(panel, kv_near, by_block([kv_far]), 0, 1, 1.0, scale, cosine, sine)
-    kv, *arrived = lax.optimization_barrier((kv, *([x_sent] if x_sent is not None else [])))
     scale = after(scale, kv)
     queries = project(
         panel, q_near, by_block(q_far[:early]), 0, first_heads, factor, scale, cosine, sine
     )
     beside = [exchange(kv), queries, *gather_near(kv)]
-    for piece in arrived:
-        beside += gather_near(piece)
+    if x_sent is not None:
+        beside.append(x_sent)
     kv_other, queries, *beside = lax.optimization_barrier(tuple(beside))
-    kv_pieces, far = take(beside, blocks_near)
-    late_far = [far] if arrived else []
+    kv_pieces, arrived = take(beside, blocks_near)
     kv_pieces = [*kv_pieces, *gather_near(kv_other)]
+    late_far = [gather_near(piece) for piece in arrived]
     last_other = exchange(after(chunks[-1], kv_other))
     heads = attend(r, [queries], kv_pieces)
 
     def o_rows(first, wide):
         return wo.reshape(-1, cols, wo.shape[1])[:, first : first + wide].reshape(-1, wo.shape[1])
 
-    o_first = o_rows(0, wide)
+    split = cols - rest // 2 if rest >= 2 * HD else cols
+    o_first = o_rows(0, split)
     ring = Ring(heads)
     first_panel = put(blank((n_col, tok, wide)), ring.found)
     second_panel = blank((n_col, tok, rest))
@@ -417,12 +420,10 @@
     o_first = exchange(o_first)
     far = gather_near(last_other)
     late_far = by_block([*late_far, far])
-    parts = [(0, rest // 2), (rest // 2, rest - rest // 2)] if rest >= 2 * HD else [(0, rest)]
-    o_parts = [o_rows(wide + first, part) for first, part in parts]
     queries = project(
         panel, q_near, late_far, wide, late_heads, factor, scale, cosine, sine
     )
-    queries, first_panel, *o_parts = ring.hop(beside=[queries, first_panel, *o_parts])
+    queries, first_panel = ring.hop(beside=[queries, first_panel])
     first_panel = put(first_panel, ring.found[-2:])
     o_near = gather_near(after(wo, queries))
     beside = ring.hop(beside=[attend(r, [queries], kv_pieces), first_panel, *o_near])
@@ -430,51 +431,49 @@
     first_panel = put(first_panel, ring.found[-2:])
     second = Ring(heads)
     second_panel = put(second_panel, second.found)
-    others, gathered, sent = [], [], o_first
+    o_last = [o_rows(split, cols - split)] if split < cols else []
+    plan = []
+    for k in range(n_col):
+        p, s = k // per, k % per
+        plan.append((0, k, 0, 1 + p, s * (cols if p < blocks_near else split)))
     for i in range(hops):
         arrived, hop = ring.last, ring.hops
         ring.hop(*second.last)
-        beside = [first_panel, second_panel]
-        if gathered and i in (1, 3):
-            beside += gathered[-1]
-        if i in (0, 2) and len(others) < len(parts):
-            beside.append(sent)
-        (first_panel, second_panel), beside = take(second.hop(*arrived, beside=beside), 2)
+        beside = [first_panel, second_panel, *o_last]
+        if i == hops - 3:
+            beside.append(o_first)
+        if i == hops - 2:
+            beside += gather_near(o_first)
+        if i == hops - 1:
+            beside.append(finish([first_panel, *o_near, *o_far], plan, wide, jnp.float32))
+        beside = second.hop(*arrived, beside=beside)
+        (first_panel, second_panel), o_last, beside = take(beside, 2, len(o_last))
         if ring.hops > hop:
             first_panel = put(first_panel, ring.found[-2:])
         second_panel = put(second_panel, second.found[-2:])
-        if gathered and i in (1, 3):
-            gathered[-1], beside = take(beside, blocks_near)
-        if i in (0, 2) and len(others) < len(parts):
-            gathered.append(gather_near(beside[0]))
-            sent = exchange(after(o_parts[len(others)], beside[0]))
-            others.append(sent)
-
-    while len(gathered) < len(parts):
-        gathered.append(gather_near(others[len(gathered) - 1]))
-    half = n_col // 2
-    unit = math.gcd(wide, rest)
-    arrays = [first_panel, second_panel, *o_near, *gathered[0]]
+        if i == hops - 3:
+            (o_first,) = beside
+            o_other, o_last = [exchange(after(w, o_first)) for w in o_last], []
+        if i == hops - 2:
+            o_far = beside
+    (total,) = beside
+
+    part = math.gcd(rest, split - wide)
     plan = []
     for k in range(n_col):
         p, s = k // per, k % per
-        for at in range(0, wide, unit):
-            row = s * cols + at if p < blocks_near else s * wide + at
-            plan.append((0, k, at, 2 + p, row))
-        for at in range(0, rest, unit):
-            if p < blocks_near:
-                plan.append((1, k, at, 2 + p, s * cols + wide + at))
-    total = finish(arrays, plan, unit, jnp.float32)
-    for j, (first, part) in enumerate(parts):
-        if j + 1 < len(gathered):
-            far = gathered[j + 1]
-        else:
-            far = gather_near(after(others[j], total))
+        near = p < blocks_near
+        for at in range(0, rest if near else split - wide, part):
+            plan.append((0, k, at, 1 + p, s * (cols if near else split) + wide + at))
+    dtype = jnp.float32 if o_other else jnp.bfloat16
+    total = finish([second_panel, *o_near, *o_far], plan, part, dtype, total)
+    if o_other:
+        far = gather_near(after(o_other[0], total))
         plan = [
-            (0, k, first, 1 + k // per - blocks_near, k % per * part) for k in range(half, n_col)
+            (0, k, split - wide, 1 + k // per - blocks_near, k % per * (cols - split))
+            for k in range(n_col // 2, n_col)
         ]
-        dtype = jnp.bfloat16 if j == len(parts) - 1 else jnp.float32
-        total = finish([second_panel, *far], plan, part, dtype, total)
+        total = finish([second_panel, *far], plan, cols - split, jnp.bfloat16, total)
     return total
 
 

time: 304 us -> 302 us (level)
  other arithmetic: 5.36 us -> 19.1 us
  starting transfers between devices: 36.8 us -> 29.2 us
  local copies, waits for them, and re-layouts: 49.3 us -> 41.9 us
    ppermute x12, waiting for transfers between devices: 36.4 us -> 88 us  [hop(): below = lax.ppermute(below, 'col', self.up)]
    ppermute x25 -> x20, waiting for transfers between devices: 95.2 us -> 44.1 us  [swap(): lax.ppermute(array, axis, [(i, i ^ mask) for i in range(lax.axis_size(axi...]
    dynamic_update_slice x26 -> x18, local copies, waits for them, and re-layouts: 30.4 us -> 18.7 us  [put(): panel = lax.dynamic_update_slice(panel, piece[None], (slot, first, 0))]
    dynamic_update_slice x1 -> x9, other arithmetic: 1.74 us -> 10.5 us  [put(): panel = lax.dynamic_update_slice(panel, piece[None], (slot, first, 0))]
    ppermute x25 -> x20, starting transfers between devices: 12.3 us -> 4.36 us  [swap(): lax.ppermute(array, axis, [(i, i ^ mask) for i in range(lax.axis_size(axi...]
    slice x1 -> x3, local copies, waits for them, and re-layouts: 4.27 us -> 6.27 us  [per_device(): wq[:, sum(sizes[:i]) * HD:sum(sizes[:i + 1]) * HD]]
    unnamed x40 -> x30, local copies, waits for them, and re-layouts: 5.59 us -> 7.04 us
  transfers between devices with their start and end apart: 49 -> 44, of which waited for: 26 -> 23; matrix products, arithmetic and copies ran while one was open for 15% -> 18% of each run, Pallas kernels for 20% -> 20%
where the time goes in v6:
time: 302 us; the launch traced here: 301 us
  waiting for transfers between devices  143 us (47%)
  Pallas kernels  66.7 us (22%)
  local copies, waits for them, and re-layouts  41.9 us (14%)
  starting transfers between devices  29.2 us (10%)
  other arithmetic  19.1 us (6%)
    ppermute x12, waiting for transfers between devices, hop(): below = lax.ppermute(below, 'col', self.up)  88 us
    ppermute x20, waiting for transfers between devices, swap(): lax.ppermute(array, axis, [(i, i ^ mask) for i in range(lax.axis_size(axi...  44.1 us
    pallas_call x3, Pallas kernels, project(): pl.pallas_call(functools.partial(project_kernel, len(near), len(far), chu...  28.5 us
    pallas_call x3, Pallas kernels, finish(): pl.pallas_call(functools.partial(finish_kernel, plan, len(arrays)), in_sp...  24.1 us
    ppermute x12, starting transfers between devices, hop(): below = lax.ppermute(below, 'col', self.up)  19.1 us
    dynamic_update_slice x18, local copies, waits for them, and re-layouts, put(): panel = lax.dynamic_update_slice(panel, piece[None], (slot, first, 0))  18.7 us
    pallas_call x2, Pallas kernels, attend(): pl.pallas_call(functools.partial(attend_kernel, parts, chunks, pair), gri...  14.1 us
    ppermute x12, waiting for transfers between devices, hop(): above = lax.ppermute(above, 'col', self.down)  10.9 us
  transfers between devices with their start and end apart: 44, of which 23 were waited for; matrix products, arithmetic and copies ran while one was open for 18% of the time, Pallas kernels for 20%

profile of v6, /device:TPU:2, one launch (start us, length us, event | category | flops | bytes accessed | tf_op | source)
XLA Modules:
  0.0 300.6 jit_solution(17306625149180350558)
XLA Ops:
  2.0 2.3 copy_bitcast_fusion.refs_0_
  4.7 2.7 slice.38
  7.5 1.8 fusion.36
  9.3 2.1 pad_maximum_fusion
  12.9 1.7 fusion.40
  14.6 10.5 %collective-permute-done = bf16[512,1024]{1,0:T(8,128)(2,1)S(1)} collective-permute-done((bf16[512,1024]{1,0:T(8,128)(2,1)}, bf16[512,1024]{1,0:T(8,128)(2,1)S(1)}, u32[]{:S(2)}, u32[]{:S(2)}) %collective-permute-start) | collective-permute-done | bytes 1048608 | tf_op jit(solution)/shard_map/ppermute | solution.py:80
  26.4 3.8 %collective-permute-done.3.refs_2_ = bf16[2048,256]{1,0:T(8,128)(2,1)} collective-permute-done((bf16[2048,256]{1,0:T(8,128)(2,1)}, bf16[2048,256]{1,0:T(8,128)(2,1)}, u32[]{:S(2)}, u32[]{:S(2)}) %collective-permute-start.3) | collective-permute-done | bytes 1048608 | tf_op jit(solution)/shard_map/ppermute | solution.py:23
  35.5 19.5 %collective-permute-done.4 = bf16[512,1024]{1,0:T(8,128)(2,1)S(1)} collective-permute-done((bf16[512,1024]{1,0:T(8,128)(2,1)S(1)}, bf16[512,1024]{1,0:T(8,128)(2,1)S(1)}, u32[]{:S(2)}, u32[]{:S(2)}) %collective-permute-start.4) | collective-permute-done | bytes 1048608 | tf_op jit(solution)/shard_map/ppermute | solution.py:80
  63.2 19.4 %collective-permute-done.8 = bf16[512,1024]{1,0:T(8,128)(2,1)S(1)} collective-permute-done((bf16[512,1024]{1,0:T(8,128)(2,1)S(1)}, bf16[512,1024]{1,0:T(8,128)(2,1)S(1)}, u32[]{:S(2)}, u32[]{:S(2)}) %collective-permute-start.8) | collective-permute-done | bytes 1048608 | tf_op jit(solution)/shard_map/ppermute | solution.py:80
  92.2 8.6 %collective-permute-done.12 = bf16[256,1024]{1,0:T(8,128)(2,1)S(1)} collective-permute-done((bf16[256,1024]{1,0:T(8,128)(2,1)S(1)}, bf16[256,1024]{1,0:T(8,128)(2,1)S(1)}, u32[]{:S(2)}, u32[]{:S(2)}) %collective-permute-start.12) | collective-permute-done | bytes 524320 | tf_op jit(solution)/shard_map/ppermute | solution.py:80
  105.5 7.1 %shard_map.65.refs_1_ = bf16[512,256]{1,0:T(8,128)(2,1)} custom-call(bf16[8,512,1024]{2,1,0:T(8,128)(2,1)} %fusion.33.panel_ref, bf16[2048,256]{1,0:T(8,128)(2,1)} %copy_bitcast_fusion.refs_0_, bf16[2048,256]{1,0:T(8,128)(2,1)} %collective-permute-done.2.refs_1_, bf16[2048,256]{1,0:T(8,128)(2,1)} %collective-permute-done.3.refs_2_, ...), custom_call_target="tpu_custom_call" | custom-call | flops 1 | bytes 1 | tf_op jit(solution)/shard_map/pallas_call | solution.py:158
  114.2 10.7 %shard_map.66.refs_0_ = bf16[512,512]{1,0:T(8,128)(2,1)} custom-call(bf16[8,512,1024]{2,1,0:T(8,128)(2,1)} %fusion.33.panel_ref, bf16[2048,1024]{1,0:T(8,128)(2,1)} %refs_0_.1, bf16[2048,1024]{1,0:T(8,128)(2,1)} %collective-permute-done.15.refs_1_, bf16[2048,256]{1,0:T(8,128)(2,1)} %copy-done.8, bf16[2048,256]{1,0:T(8,128)(2,1)} %copy-done.10, ...), custom_call_target="tpu_custom_call" | custom-call | flops 1 | bytes 1 | tf_op jit(solution)/shard_map/pallas_call | solution.py:158
  126.3 5.1 %collective-permute-done.16.refs_3_ = bf16[512,256]{1,0:T(8,128)(2,1)S(1)} collective-permute-done((bf16[512,256]{1,0:T(8,128)(2,1)}, bf16[512,256]{1,0:T(8,128)(2,1)S(1)}, u32[]{:S(2)}, u32[]{:S(2)}) %collective-permute-start.16) | collective-permute-done | bytes 262176 | tf_op jit(solution)/shard_map/ppermute | solution.py:23
  132.0 1.9 slice.41
  135.9 7.1 %shard_map.67 = bf16[512,512]{1,0:T(8,128)(2,1)S(1)} custom-call(s32[1]{0:T(128)} %bitcast.r_ref, bf16[512,512]{1,0:T(8,128)(2,1)S(1)} %copy-done.2, bf16[512,256]{1,0:T(8,128)(2,1)S(1)} %copy-done, bf16[512,256]{1,0:T(8,128)(2,1)S(1)} %collective-permute-done.17.refs_2_, bf16[512,256]{1,0:T(8,128)(2,1)S(1)} %collective-permute-done.16.refs_3_, ...), custom_call_target="tpu_custom_call" | custom-call | flops 1 | bytes 1 | tf_op jit(solution)/shard_map/pallas_call | solution.py:241
  145.1 3.9 %slice.48 = bf16[2,768,1024]{2,1,0:T(8,128)(2,1)} slice(bf16[2,1024,1024]{2,1,0:T(8,128)(2,1)} %bitcast.84), slice={[0:2], [0:768], [0:1024]} | slice | bytes 6291456 | tf_op jit(solution)/shard_map/slice | solution.py:409
  149.8 6.4 %collective-permute-done.20 = bf16[512,512]{1,0:T(8,128)(2,1)} collective-permute-done((bf16[512,512]{1,0:T(8,128)(2,1)S(1)}, bf16[512,512]{1,0:T(8,128)(2,1)}, u32[]{:S(2)}, u32[]{:S(2)}) %collective-permute-start.20) | collective-permute-done | bytes 524320 | tf_op jit(solution)/shard_map/ppermute | solution.py:80
  156.2 1.8 collective-permute-done.21
  161.3 1.9 bitcast_dynamic-update-slice_fusion.12
  163.2 1.9 bitcast_dynamic-update-slice_fusion.11
  167.0 10.7 %shard_map.70.refs_0_ = bf16[512,512]{1,0:T(8,128)(2,1)} custom-call(bf16[8,512,1024]{2,1,0:T(8,128)(2,1)} %fusion.33.panel_ref, bf16[2048,1024]{1,0:T(8,128)(2,1)} %refs_0_.1, bf16[2048,1024]{1,0:T(8,128)(2,1)} %collective-permute-done.15.refs_1_, bf16[2048,384]{1,0:T(8,128)(2,1)} %collective-permute-done.18.refs_2_, ...), custom_call_target="tpu_custom_call" | custom-call | flops 1 | bytes 1 | tf_op jit(solution)/shard_map/pallas_call | solution.py:158
  177.9 1.7 collective-permute-start.27
  180.0 2.3 slice.49
  183.3 7.1 %shard_map.71 = bf16[512,512]{1,0:T(8,128)(2,1)S(1)} custom-call(s32[1]{0:T(128)} %bitcast.r_ref, bf16[512,512]{1,0:T(8,128)(2,1)S(1)} %copy-done.1, bf16[512,256]{1,0:T(8,128)(2,1)S(1)} %copy-done, bf16[512,256]{1,0:T(8,128)(2,1)S(1)} %collective-permute-done.17.refs_2_, bf16[512,256]{1,0:T(8,128)(2,1)S(1)} %collective-permute-done.16.refs_3_, ...), custom_call_target="tpu_custom_call" | custom-call | flops 1 | bytes 1 | tf_op jit(solution)/shard_map/pallas_call | solution.py:241
  191.2 1.9 bitcast_dynamic-update-slice_fusion.9
  200.4 13.3 %collective-permute-done.32 = bf16[256,512]{1,0:T(8,128)(2,1)S(1)} collective-permute-done((bf16[256,512]{1,0:T(8,128)(2,1)S(1)}, bf16[256,512]{1,0:T(8,128)(2,1)S(1)}, u32[]{:S(2)}, u32[]{:S(2)}) %collective-permute-start.32) | collective-permute-done | bytes 262176 | tf_op jit(solution)/shard_map/ppermute | solution.py:80
  220.4 28.1 %collective-permute-done.36.refs_3_ = bf16[1536,1024]{1,0:T(8,128)(2,1)S(1)} collective-permute-done((bf16[1536,1024]{1,0:T(8,128)(2,1)}, bf16[1536,1024]{1,0:T(8,128)(2,1)S(1)}, u32[]{:S(2)}, u32[]{:S(2)}) %collective-permute-start.36) | collective-permute-done | bytes 3145760 | tf_op jit(solution)/shard_map/ppermute | solution.py:23
  252.7 10.3 %collective-permute-done.37 = bf16[512,512]{1,0:T(8,128)(2,1)S(1)} collective-permute-done((bf16[512,512]{1,0:T(8,128)(2,1)S(1)}, bf16[512,512]{1,0:T(8,128)(2,1)S(1)}, u32[]{:S(2)}, u32[]{:S(2)}) %collective-permute-start.37) | collective-permute-done | bytes 524320 | tf_op jit(solution)/shard_map/ppermute | solution.py:80
  269.1 8.8 %shard_map.72.refs_5_ = f32[512,1024]{1,0:T(8,128)} custom-call(bf16[8,512,512]{2,1,0:T(8,128)(2,1)} %bitcast_dynamic-update-slice_fusion.16.refs_0_, bf16[2048,1024]{1,0:T(8,128)(2,1)} %refs_1_.1, bf16[2048,1024]{1,0:T(8,128)(2,1)} %copy-done.3, bf16[1536,1024]{1,0:T(8,128)(2,1)} %copy-done.4, bf16[1536,1024]{1,0:T(8,128)(2,1)} %copy-done.5), custom_call_target="tpu_custom_call" | custom-call | flops 1 | bytes 1 | tf_op jit(solution)/shard_map/pallas_call | solution.py:284
  281.1 9.7 %shard_map.73.refs_3_ = f32[512,1024]{1,0:T(8,128)} custom-call(bf16[8,512,512]{2,1,0:T(8,128)(2,1)} %bitcast_dynamic-update-slice_fusion.14.refs_0_, bf16[2048,1024]{1,0:T(8,128)(2,1)} %refs_1_.1, bf16[2048,1024]{1,0:T(8,128)(2,1)} %copy-done.3, bf16[1536,1024]{1,0:T(8,128)(2,1)} %copy-done.4, bf16[1536,1024]{1,0:T(8,128)(2,1)} %copy-done.5, ...), custom_call_target="tpu_custom_call" | custom-call | flops 1 | bytes 1 | tf_op jit(solution)/shard_map/pallas_call | solution.py:284
  290.9 2.9 collective-permute-done.43.refs_2_
  294.8 5.6 %shard_map.74 = bf16[512,1024]{1,0:T(8,128)(2,1)} custom-call(bf16[8,512,512]{2,1,0:T(8,128)(2,1)} %bitcast_dynamic-update-slice_fusion.14.refs_0_, bf16[512,1024]{1,0:T(8,128)(2,1)} %collective-permute-done.42.refs_1_, bf16[512,1024]{1,0:T(8,128)(2,1)} %copy-done.11, f32[512,1024]{1,0:T(8,128)} %shard_map.73.refs_3_), custom_call_target="tpu_custom_call" | custom-call | flops 1 | bytes 1 | tf_op jit(solution)/shard_map/pallas_call | solution.py:284
  (156 shorter events, 77.6 us)
Async XLA Ops:
  0.0 25.1 %collective-permute-start = (bf16[512,1024]{1,0:T(8,128)(2,1)}, bf16[512,1024]{1,0:T(8,128)(2,1)S(1)}, u32[]{:S(2)}, u32[]{:S(2)}) collective-permute-start(bf16[512,1024]{1,0:T(8,128)(2,1)} %param.6), channel_id=1, source_target_pairs={{0,2},{2,4},{4,6},{6,7},{7,5},{5,3},{3,1},{1,0},{8,10},{10,12},{12... | collective-permute-start | bytes 3145736 | tf_op jit(solution)/shard_map/ppermute | solution.py:80
  1.6 24.8 %collective-permute-start.1 = (bf16[512,1024]{1,0:T(8,128)(2,1)}, bf16[512,1024]{1,0:T(8,128)(2,1)S(1)}, u32[]{:S(2)}, u32[]{:S(2)}) collective-permute-start(bf16[512,1024]{1,0:T(8,128)(2,1)} %param.6), channel_id=1, source_target_pairs={{2,0},{4,2},{6,4},{7,6},{5,7},{3,5},{1,3},{0,1},{10,8},{12,10},{14... | collective-permute-start | bytes 3145736 | tf_op jit(solution)/shard_map/ppermute | solution.py:81
  4.3 22.1 %collective-permute-start.2 = (bf16[2048,256]{1,0:T(8,128)(2,1)}, bf16[2048,256]{1,0:T(8,128)(2,1)}, u32[]{:S(2)}, u32[]{:S(2)}) collective-permute-start(bf16[2048,256]{1,0:T(8,128)(2,1)} %copy_bitcast_fusion.refs_0_), channel_id=1, source_target_pairs={{0,8},{8,0},{16,24},{24,16},{1,9},{9,1},{17,25},{25,17},{2,10},{10... | collective-permute-start | bytes 3145736 | tf_op jit(solution)/shard_map/ppermute | solution.py:23
  4.3 25.9 %collective-permute-start.3 = (bf16[2048,256]{1,0:T(8,128)(2,1)}, bf16[2048,256]{1,0:T(8,128)(2,1)}, u32[]{:S(2)}, u32[]{:S(2)}) collective-permute-start(bf16[2048,256]{1,0:T(8,128)(2,1)} %copy_bitcast_fusion.refs_0_), channel_id=1, source_target_pairs={{0,16},{8,24},{16,0},{24,8},{1,17},{9,25},{17,1},{25,9},{2,18},{10... | collective-permute-start | bytes 3145736 | tf_op jit(solution)/shard_map/ppermute | solution.py:23
  30.2 24.8 %collective-permute-start.4 = (bf16[512,1024]{1,0:T(8,128)(2,1)S(1)}, bf16[512,1024]{1,0:T(8,128)(2,1)S(1)}, u32[]{:S(2)}, u32[]{:S(2)}) collective-permute-start(bf16[512,1024]{1,0:T(8,128)(2,1)S(1)} %collective-permute-done), channel_id=1, source_target_pairs={{0,2},{2,4},{4,6},{6,7},{7,5},{5,3},{3,1},{1,0},{8,10},{10,12},{12... | collective-permute-start | bytes 3145736 | tf_op jit(solution)/shard_map/ppermute | solution.py:80
  31.8 24.5 %collective-permute-start.5 = (bf16[512,1024]{1,0:T(8,128)(2,1)S(1)}, bf16[512,1024]{1,0:T(8,128)(2,1)S(1)}, u32[]{:S(2)}, u32[]{:S(2)}) collective-permute-start(bf16[512,1024]{1,0:T(8,128)(2,1)S(1)} %collective-permute-done.1), channel_id=1, source_target_pairs={{2,0},{4,2},{6,4},{7,6},{5,7},{3,5},{1,3},{0,1},{10,8},{12,10},{14... | collective-permute-start | bytes 3145736 | tf_op jit(solution)/shard_map/ppermute | solution.py:81
  32.2 24.1 %collective-permute-start.6 = (bf16[2048,256]{1,0:T(8,128)(2,1)}, bf16[2048,256]{1,0:T(8,128)(2,1)S(1)}, u32[]{:S(2)}, u32[]{:S(2)}) collective-permute-start(bf16[2048,256]{1,0:T(8,128)(2,1)} %collective-permute-done.3.refs_2_), channel_id=1, source_target_pairs={{0,8},{8,0},{16,24},{24,16},{1,9},{9,1},{17,25},{25,17},{2,10},{10... | collective-permute-start | bytes 3145736 | tf_op jit(solution)/shard_map/ppermute | solution.py:23
  32.2 25.6 %collective-permute-start.7 = (bf16[2048,256]{1,0:T(8,128)(2,1)S(1)}, bf16[2048,256]{1,0:T(8,128)(2,1)S(1)}, u32[]{:S(2)}, u32[]{:S(2)}) collective-permute-start(bf16[2048,256]{1,0:T(8,128)(2,1)S(1)} %get-tuple-element.112), channel_id=1, source_target_pairs={{0,16},{8,24},{16,0},{24,8},{1,17},{9,25},{17,1},{25,9},{2,18},{10... | collective-permute-start | bytes 3145736 | tf_op jit(solution)/shard_map/ppermute | solution.py:23
  57.8 24.8 %collective-permute-start.8 = (bf16[512,1024]{1,0:T(8,128)(2,1)S(1)}, bf16[512,1024]{1,0:T(8,128)(2,1)S(1)}, u32[]{:S(2)}, u32[]{:S(2)}) collective-permute-start(bf16[512,1024]{1,0:T(8,128)(2,1)S(1)} %collective-permute-done.4), channel_id=1, source_target_pairs={{0,2},{2,4},{4,6},{6,7},{7,5},{5,3},{3,1},{1,0},{8,10},{10,12},{12... | collective-permute-start | bytes 3145736 | tf_op jit(solution)/shard_map/ppermute | solution.py:80
  59.4 24.5 %collective-permute-start.9 = (bf16[512,1024]{1,0:T(8,128)(2,1)S(1)}, bf16[512,1024]{1,0:T(8,128)(2,1)S(1)}, u32[]{:S(2)}, u32[]{:S(2)}) collective-permute-start(bf16[512,1024]{1,0:T(8,128)(2,1)S(1)} %collective-permute-done.5), channel_id=1, source_target_pairs={{2,0},{4,2},{6,4},{7,6},{5,7},{3,5},{1,3},{0,1},{10,8},{12,10},{14... | collective-permute-start | bytes 3145736 | tf_op jit(solution)/shard_map/ppermute | solution.py:81
  59.8 24.1 %collective-permute-start.10 = (bf16[2048,256]{1,0:T(8,128)(2,1)S(1)}, bf16[2048,256]{1,0:T(8,128)(2,1)S(1)}, u32[]{:S(2)}, u32[]{:S(2)}) collective-permute-start(bf16[2048,256]{1,0:T(8,128)(2,1)S(1)} %collective-permute-done.7.refs_2_), channel_id=1, source_target_pairs={{0,8},{8,0},{16,24},{24,16},{1,9},{9,1},{17,25},{25,17},{2,10},{10... | collective-permute-start | bytes 3145736 | tf_op jit(solution)/shard_map/ppermute | solution.py:23
  59.8 25.6 %collective-permute-start.11 = (bf16[2048,256]{1,0:T(8,128)(2,1)S(1)}, bf16[2048,256]{1,0:T(8,128)(2,1)S(1)}, u32[]{:S(2)}, u32[]{:S(2)}) collective-permute-start(bf16[2048,256]{1,0:T(8,128)(2,1)S(1)} %get-tuple-element.120), channel_id=1, source_target_pairs={{0,16},{8,24},{16,0},{24,8},{1,17},{9,25},{17,1},{25,9},{2,18},{10... | collective-permute-start | bytes 3145736 | tf_op jit(solution)/shard_map/ppermute | solution.py:23
  86.4 16.0 %collective-permute-start.15 = (bf16[2048,1024]{1,0:T(8,128)(2,1)}, bf16[2048,1024]{1,0:T(8,128)(2,1)}, u32[]{:S(2)}, u32[]{:S(2)}) collective-permute-start(bf16[2048,1024]{1,0:T(8,128)(2,1)} %refs_0_.1), channel_id=1, source_target_pairs={{0,8},{8,0},{16,24},{24,16},{1,9},{9,1},{17,25},{25,17},{2,10},{10... | collective-permute-start | bytes 12582920 | tf_op jit(solution)/shard_map/ppermute | solution.py:23
  86.4 14.4 %collective-permute-start.12 = (bf16[256,1024]{1,0:T(8,128)(2,1)S(1)}, bf16[256,1024]{1,0:T(8,128)(2,1)S(1)}, u32[]{:S(2)}, u32[]{:S(2)}) collective-permute-start(bf16[256,1024]{1,0:T(8,128)(2,1)S(1)} %slice.39), channel_id=1, source_target_pairs={{0,2},{2,4},{4,6},{6,7},{7,5},{5,3},{3,1},{1,0},{8,10},{10,12},{12... | collective-permute-start | bytes 1572872 | tf_op jit(solution)/shard_map/ppermute | solution.py:80
  88.8 37.5 %collective-permute-start.18 = (bf16[2048,384]{1,0:T(8,128)(2,1)}, bf16[2048,384]{1,0:T(8,128)(2,1)}, u32[]{:S(2)}, u32[]{:S(2)}) collective-permute-start(bf16[2048,384]{1,0:T(8,128)(2,1)} %slice.38), channel_id=1, source_target_pairs={{0,16},{8,24},{16,0},{24,8},{1,17},{9,25},{17,1},{25,9},{2,18},{10... | collective-permute-start | bytes 4718600 | tf_op jit(solution)/shard_map/ppermute | solution.py:23
  112.6 18.8 %collective-permute-start.16 = (bf16[512,256]{1,0:T(8,128)(2,1)}, bf16[512,256]{1,0:T(8,128)(2,1)S(1)}, u32[]{:S(2)}, u32[]{:S(2)}) collective-permute-start(bf16[512,256]{1,0:T(8,128)(2,1)} %shard_map.65.refs_1_), channel_id=1, source_target_pairs={{0,16},{8,24},{16,0},{24,8},{1,17},{9,25},{17,1},{25,9},{2,18},{10... | collective-permute-start | bytes 786440 | tf_op jit(solution)/shard_map/ppermute | solution.py:23
  113.3 18.1 %collective-permute-start.17 = (bf16[512,256]{1,0:T(8,128)(2,1)}, bf16[512,256]{1,0:T(8,128)(2,1)S(1)}, u32[]{:S(2)}, u32[]{:S(2)}) collective-permute-start(bf16[512,256]{1,0:T(8,128)(2,1)} %shard_map.65.refs_1_), channel_id=1, source_target_pairs={{0,8},{8,0},{16,24},{24,16},{1,9},{9,1},{17,25},{25,17},{2,10},{10... | collective-permute-start | bytes 786440 | tf_op jit(solution)/shard_map/ppermute | solution.py:23
  131.4 33.6 %collective-permute-start.25 = (bf16[2048,384]{1,0:T(8,128)(2,1)}, bf16[2048,384]{1,0:T(8,128)(2,1)S(1)}, u32[]{:S(2)}, u32[]{:S(2)}) collective-permute-start(bf16[2048,384]{1,0:T(8,128)(2,1)} %collective-permute-done.18.refs_2_), channel_id=1, source_target_pairs={{0,8},{8,0},{16,24},{24,16},{1,9},{9,1},{17,25},{25,17},{2,10},{10... | collective-permute-start | bytes 4718600 | tf_op jit(solution)/shard_map/ppermute | solution.py:23
  133.8 16.0 %collective-permute-start.22 = (bf16[2048,128]{1,0:T(8,128)(2,1)}, bf16[2048,128]{1,0:T(8,128)(2,1)}, u32[]{:S(2)}, u32[]{:S(2)}) collective-permute-start(bf16[2048,128]{1,0:T(8,128)(2,1)} %slice.41), channel_id=1, source_target_pairs={{0,16},{8,24},{16,0},{24,8},{1,17},{9,25},{17,1},{25,9},{2,18},{10... | collective-permute-start | bytes 1572872 | tf_op jit(solution)/shard_map/ppermute | solution.py:23
  159.3 18.4 %collective-permute-start.23 = (bf16[512,512]{1,0:T(8,128)(2,1)}, bf16[512,512]{1,0:T(8,128)(2,1)S(1)}, u32[]{:S(2)}, u32[]{:S(2)}) collective-permute-start(bf16[512,512]{1,0:T(8,128)(2,1)} %collective-permute-done.20), channel_id=1, source_target_pairs={{0,2},{2,4},{4,6},{6,7},{7,5},{5,3},{3,1},{1,0},{8,10},{10,12},{12... | collective-permute-start | bytes 1572872 | tf_op jit(solution)/shard_map/ppermute | solution.py:80
  160.9 16.8 %collective-permute-start.24 = (bf16[512,512]{1,0:T(8,128)(2,1)}, bf16[512,512]{1,0:T(8,128)(2,1)}, u32[]{:S(2)}, u32[]{:S(2)}) collective-permute-start(bf16[512,512]{1,0:T(8,128)(2,1)} %collective-permute-done.21), channel_id=1, source_target_pairs={{2,0},{4,2},{6,4},{7,6},{5,7},{3,5},{1,3},{0,1},{10,8},{12,10},{14... | collective-permute-start | bytes 1572872 | tf_op jit(solution)/shard_map/ppermute | solution.py:81
  177.7 16.0 %collective-permute-start.29 = (bf16[2048,1024]{1,0:T(8,128)(2,1)}, bf16[2048,1024]{1,0:T(8,128)(2,1)S(1)}, u32[]{:S(2)}, u32[]{:S(2)}) collective-permute-start(bf16[2048,1024]{1,0:T(8,128)(2,1)} %refs_1_.1), channel_id=1, source_target_pairs={{0,8},{8,0},{16,24},{24,16},{1,9},{9,1},{17,25},{25,17},{2,10},{10... | collective-permute-start | bytes 12582920 | tf_op jit(solution)/shard_map/ppermute | solution.py:23
  177.8 70.7 %collective-permute-start.36 = (bf16[1536,1024]{1,0:T(8,128)(2,1)}, bf16[1536,1024]{1,0:T(8,128)(2,1)S(1)}, u32[]{:S(2)}, u32[]{:S(2)}) collective-permute-start(bf16[1536,1024]{1,0:T(8,128)(2,1)} %bitcast.86), channel_id=1, source_target_pairs={{0,16},{8,24},{16,0},{24,8},{1,17},{9,25},{17,1},{25,9},{2,18},{10... | collective-permute-start | bytes 9437192 | tf_op jit(solution)/shard_map/ppermute | solution.py:23
  177.9 15.2 %collective-permute-start.27 = (bf16[512,512]{1,0:T(8,128)(2,1)S(1)}, bf16[512,512]{1,0:T(8,128)(2,1)S(1)}, u32[]{:S(2)}, u32[]{:S(2)}) collective-permute-start(bf16[512,512]{1,0:T(8,128)(2,1)S(1)} %collective-permute-done.23), channel_id=1, source_target_pairs={{0,2},{2,4},{4,6},{6,7},{7,5},{5,3},{3,1},{1,0},{8,10},{10,12},{12... | collective-permute-start | bytes 1572872 | tf_op jit(solution)/shard_map/ppermute | solution.py:80
  193.7 21.6 %collective-permute-start.30 = (bf16[512,512]{1,0:T(8,128)(2,1)S(1)}, bf16[512,512]{1,0:T(8,128)(2,1)S(1)}, u32[]{:S(2)}, u32[]{:S(2)}) collective-permute-start(bf16[512,512]{1,0:T(8,128)(2,1)S(1)} %shard_map.71), channel_id=1, source_target_pairs={{0,2},{2,4},{4,6},{6,7},{7,5},{5,3},{3,1},{1,0},{8,10},{10,12},{12... | collective-permute-start | bytes 1572872 | tf_op jit(solution)/shard_map/ppermute | solution.py:80
  195.2 20.1 %collective-permute-start.31 = (bf16[512,512]{1,0:T(8,128)(2,1)S(1)}, bf16[512,512]{1,0:T(8,128)(2,1)S(1)}, u32[]{:S(2)}, u32[]{:S(2)}) collective-permute-start(bf16[512,512]{1,0:T(8,128)(2,1)S(1)} %shard_map.71), channel_id=1, source_target_pairs={{2,0},{4,2},{6,4},{7,6},{5,7},{3,5},{1,3},{0,1},{10,8},{12,10},{14... | collective-permute-start | bytes 1572872 | tf_op jit(solution)/shard_map/ppermute | solution.py:81
  196.6 17.1 %collective-permute-start.32 = (bf16[256,512]{1,0:T(8,128)(2,1)S(1)}, bf16[256,512]{1,0:T(8,128)(2,1)S(1)}, u32[]{:S(2)}, u32[]{:S(2)}) collective-permute-start(bf16[256,512]{1,0:T(8,128)(2,1)S(1)} %slice.44), channel_id=1, source_target_pairs={{0,2},{2,4},{4,6},{6,7},{7,5},{5,3},{3,1},{1,0},{8,10},{10,12},{12... | collective-permute-start | bytes 786440 | tf_op jit(solution)/shard_map/ppermute | solution.py:80
  198.2 17.1 %collective-permute-start.33 = (bf16[256,512]{1,0:T(8,128)(2,1)S(1)}, bf16[256,512]{1,0:T(8,128)(2,1)S(1)}, u32[]{:S(2)}, u32[]{:S(2)}) collective-permute-start(bf16[256,512]{1,0:T(8,128)(2,1)S(1)} %slice.45), channel_id=1, source_target_pairs={{2,0},{4,2},{6,4},{7,6},{5,7},{3,5},{1,3},{0,1},{10,8},{12,10},{14... | collective-permute-start | bytes 786440 | tf_op jit(solution)/shard_map/ppermute | solution.py:81
  215.3 33.2 %collective-permute-start.34 = (bf16[512,512]{1,0:T(8,128)(2,1)S(1)}, bf16[512,512]{1,0:T(8,128)(2,1)S(1)}, u32[]{:S(2)}, u32[]{:S(2)}) collective-permute-start(bf16[512,512]{1,0:T(8,128)(2,1)S(1)} %collective-permute-done.30), channel_id=1, source_target_pairs={{0,2},{2,4},{4,6},{6,7},{7,5},{5,3},{3,1},{1,0},{8,10},{10,12},{12... | collective-permute-start | bytes 1572872 | tf_op jit(solution)/shard_map/ppermute | solution.py:80
  216.8 31.7 %collective-permute-start.35 = (bf16[512,512]{1,0:T(8,128)(2,1)S(1)}, bf16[512,512]{1,0:T(8,128)(2,1)S(1)}, u32[]{:S(2)}, u32[]{:S(2)}) collective-permute-start(bf16[512,512]{1,0:T(8,128)(2,1)S(1)} %collective-permute-done.31), channel_id=1, source_target_pairs={{2,0},{4,2},{6,4},{7,6},{5,7},{3,5},{1,3},{0,1},{10,8},{12,10},{14... | collective-permute-start | bytes 1572872 | tf_op jit(solution)/shard_map/ppermute | solution.py:81
  248.5 15.8 %collective-permute-start.39 = (bf16[1536,1024]{1,0:T(8,128)(2,1)S(1)}, bf16[1536,1024]{1,0:T(8,128)(2,1)S(1)}, u32[]{:S(2)}, u32[]{:S(2)}) collective-permute-start(bf16[1536,1024]{1,0:T(8,128)(2,1)S(1)} %collective-permute-done.36.refs_3_), channel_id=1, source_target_pairs={{0,8},{8,0},{16,24},{24,16},{1,9},{9,1},{17,25},{25,17},{2,10},{10... | collective-permute-start | bytes 9437192 | tf_op jit(solution)/shard_map/ppermute | solution.py:23
  250.7 40.1 %collective-permute-start.42 = (bf16[512,1024]{1,0:T(8,128)(2,1)}, bf16[512,1024]{1,0:T(8,128)(2,1)}, u32[]{:S(2)}, u32[]{:S(2)}) collective-permute-start(bf16[512,1024]{1,0:T(8,128)(2,1)} %bitcast.23), channel_id=1, source_target_pairs={{0,16},{8,24},{16,0},{24,8},{1,17},{9,25},{17,1},{25,9},{2,18},{10... | collective-permute-start | bytes 3145736 | tf_op jit(solution)/shard_map/ppermute | solution.py:23
  (27 other events, 271.6 us)

commit v7 on v6

--- a/solution.py
+++ b/solution.py
@@ -262,28 +262,29 @@
     )(r.reshape(1), *queries, *pieces)
 
 
-def finish_kernel(plan, n_refs, *refs):
-    arrays, (*old, o_ref, a_buf, w_buf, acc, a_sem, w_sem) = take(refs, n_refs)
-    depth = a_buf.shape[2]
+def finish_kernel(column, depth, per, first, r_ref, panel_ref, gathered_ref, *refs):
+    *old, o_ref, a_buf, w_buf, acc, a_sem, w_sem = refs
     steps = []
-    for panel, slot, column, weights, row in plan:
-        left = arrays[panel].at[slot, :, pl.ds(column, depth)]
-        steps.append((left, [[arrays[weights].at[pl.ds(row, depth), :]]]))
+    stride = gathered_ref.shape[1] // per
+    for k in range(panel_ref.shape[0]):
+        block = jnp.bitwise_xor(r_ref[0], k // per)
+        left = panel_ref.at[k, :, pl.ds(column, depth)]
+        right = gathered_ref.at[block, pl.ds(k % per * stride + first, depth), :]
+        steps.append((left, [[right]]))
     acc[...] = old[0][...] if old else jnp.zeros_like(acc)
     multiply(steps, a_buf, [w_buf], [acc], a_sem, w_sem)
     o_ref[...] = acc[...].astype(o_ref.dtype)
 
 
-def finish(arrays, plan, depth, dtype, total=None):
-    tok = arrays[plan[0][0]].shape[1]
-    cols = arrays[plan[0][3]].shape[1]
-    n = len(plan)
+def finish(r, panel, column, gathered, per, first, depth, dtype, total=None):
+    n, tok, _ = panel.shape
+    cols = gathered.shape[2]
     hbm = pl.BlockSpec(memory_space=pl.ANY)
     vmem = pl.BlockSpec(memory_space=pltpu.VMEM)
     old = [] if total is None else [total]
     return pl.pallas_call(
-        functools.partial(finish_kernel, plan, len(arrays)),
-        in_specs=[hbm] * len(arrays) + [vmem] * len(old),
+        functools.partial(finish_kernel, column, depth, per, first),
+        in_specs=[pl.BlockSpec(memory_space=pltpu.SMEM)] + [hbm] * 2 + [vmem] * len(old),
         out_specs=vmem,
         out_shape=jax.ShapeDtypeStruct((tok, cols), dtype),
         scratch_shapes=[
@@ -295,7 +296,7 @@
         ],
         compiler_params=pltpu.CompilerParams(vmem_limit_bytes=60 * MIB),
         cost_estimate=SHORT,
-    )(*arrays, *old)
+    )(r.reshape(1), panel, gathered, *old)
 
 
 def per_device(hidden, norm_gain, wq, wk, wv, wo):
@@ -395,85 +396,60 @@
     queries = project(
         panel, q_near, by_block(q_far[:early]), 0, first_heads, factor, scale, cosine, sine
     )
-    beside = [exchange(kv), queries, *gather_near(kv)]
+    beside = [exchange(kv), queries, chunks[-1], *gather_near(kv)]
     if x_sent is not None:
         beside.append(x_sent)
-    kv_other, queries, *beside = lax.optimization_barrier(tuple(beside))
+    kv_other, queries, last_chunk, *beside = lax.optimization_barrier(tuple(beside))
     kv_pieces, arrived = take(beside, blocks_near)
     kv_pieces = [*kv_pieces, *gather_near(kv_other)]
     late_far = [gather_near(piece) for piece in arrived]
-    last_other = exchange(after(chunks[-1], kv_other))
+    last_other = exchange(last_chunk)
+    split = cols - rest // 2 if rest >= 2 * HD else cols
+
+    def o_rows(first, last, *earlier):
+        piece = wo.reshape(-1, cols, wo.shape[1])[:, first:last].reshape(-1, wo.shape[1])
+        return lax.all_gather(after(piece, *earlier), "row")
+
+    o_first = o_rows(0, split, kv_other)
     heads = attend(r, [queries], kv_pieces)
 
-    def o_rows(first, wide):
-        return wo.reshape(-1, cols, wo.shape[1])[:, first : first + wide].reshape(-1, wo.shape[1])
-
-    split = cols - rest // 2 if rest >= 2 * HD else cols
-    o_first = o_rows(0, split)
     ring = Ring(heads)
     first_panel = put(blank((n_col, tok, wide)), ring.found)
     second_panel = blank((n_col, tok, rest))
-    last_other, o_first, first_panel, second_panel = ring.hop(
-        beside=[last_other, o_first, first_panel, second_panel]
+    last_other, first_panel, second_panel = ring.hop(
+        beside=[last_other, first_panel, second_panel]
     )
     first_panel = put(first_panel, ring.found[-2:])
-    o_first = exchange(o_first)
     far = gather_near(last_other)
+    first_panel, *far = ring.hop(beside=[first_panel, *far])
+    first_panel = put(first_panel, ring.found[-2:])
     late_far = by_block([*late_far, far])
     queries = project(
         panel, q_near, late_far, wide, late_heads, factor, scale, cosine, sine
     )
     queries, first_panel = ring.hop(beside=[queries, first_panel])
     first_panel = put(first_panel, ring.found[-2:])
-    o_near = gather_near(after(wo, queries))
-    beside = ring.hop(beside=[attend(r, [queries], kv_pieces), first_panel, *o_near])
-    (heads, first_panel), o_near = take(beside, 2)
-    first_panel = put(first_panel, ring.found[-2:])
+    heads = attend(r, [queries], kv_pieces)
+    for i in range(3, hops):
+        heads, first_panel = ring.hop(beside=[heads, first_panel])
+        first_panel = put(first_panel, ring.found[-2:])
     second = Ring(heads)
     second_panel = put(second_panel, second.found)
-    o_last = [o_rows(split, cols - split)] if split < cols else []
-    plan = []
-    for k in range(n_col):
-        p, s = k // per, k % per
-        plan.append((0, k, 0, 1 + p, s * (cols if p < blocks_near else split)))
+    o_last = None
     for i in range(hops):
-        arrived, hop = ring.last, ring.hops
-        ring.hop(*second.last)
-        beside = [first_panel, second_panel, *o_last]
-        if i == hops - 3:
-            beside.append(o_first)
-        if i == hops - 2:
-            beside += gather_near(o_first)
-        if i == hops - 1:
-            beside.append(finish([first_panel, *o_near, *o_far], plan, wide, jnp.float32))
-        beside = second.hop(*arrived, beside=beside)
-        (first_panel, second_panel), o_last, beside = take(beside, 2, len(o_last))
-        if ring.hops > hop:
-            first_panel = put(first_panel, ring.found[-2:])
+        (second_panel,) = second.hop(beside=[second_panel])
         second_panel = put(second_panel, second.found[-2:])
-        if i == hops - 3:
-            (o_first,) = beside
-            o_other, o_last = [exchange(after(w, o_first)) for w in o_last], []
-        if i == hops - 2:
-            o_far = beside
-    (total,) = beside
-
-    part = math.gcd(rest, split - wide)
-    plan = []
-    for k in range(n_col):
-        p, s = k // per, k % per
-        near = p < blocks_near
-        for at in range(0, rest if near else split - wide, part):
-            plan.append((0, k, at, 1 + p, s * (cols if near else split) + wide + at))
-    dtype = jnp.float32 if o_other else jnp.bfloat16
-    total = finish([second_panel, *o_near, *o_far], plan, part, dtype, total)
-    if o_other:
-        far = gather_near(after(o_other[0], total))
-        plan = [
-            (0, k, split - wide, 1 + k // per - blocks_near, k % per * (cols - split))
-            for k in range(n_col // 2, n_col)
-        ]
-        total = finish([second_panel, *far], plan, cols - split, jnp.bfloat16, total)
+        if i == hops - 3 and split < cols:
+            o_last = o_rows(split, cols, o_first, *second.last)
+
+    total = finish(r, first_panel, 0, o_first, per, 0, wide, jnp.float32)
+    total = after(total, *second.last)
+    dtype = jnp.bfloat16 if o_last is None else jnp.float32
+    total = finish(r, second_panel, 0, o_first, per, wide, split - wide, dtype, total)
+    if o_last is not None:
+        total = finish(
+            r, second_panel, split - wide, o_last, per, 0, cols - split, jnp.bfloat16, total
+        )
     return total
 
 

time: 302 us -> 296 us (0.980)
  waiting for transfers between devices: 143 us -> 126 us
  between operations: 0.75 us -> 14 us
    ppermute x20 -> x15, waiting for transfers between devices: 44.1 us -> 9.65 us  [swap(): lax.ppermute(array, axis, [(i, i ^ mask) for i in range(lax.axis_size(axi...]
    ppermute x12, waiting for transfers between devices: 88 us -> 103 us  [hop(): below = lax.ppermute(below, 'col', self.up)]
    unnamed x30 -> x22, local copies, waits for them, and re-layouts: 7.04 us -> 6.02 us
  transfers between devices with their start and end apart: 44 -> 41, of which waited for: 23 -> 26; matrix products, arithmetic and copies ran while one was open for 18% -> 18% of each run, Pallas kernels for 20% -> 20%
where the time goes in v7:
time: 296 us; the launch traced here: 295 us
  waiting for transfers between devices  126 us (43%)
  Pallas kernels  66.7 us (23%)
  local copies, waits for them, and re-layouts  39.1 us (13%)
  starting transfers between devices  30.2 us (10%)
  other arithmetic  19 us (6%)
  between operations  14 us (5%)
    ppermute x12, waiting for transfers between devices, hop(): below = lax.ppermute(below, 'col', self.up)  103 us
    pallas_call x3, Pallas kernels, project(): pl.pallas_call(functools.partial(project_kernel, len(near), len(far), chu...  28.5 us
    pallas_call x3, Pallas kernels, finish(): pl.pallas_call(functools.partial(finish_kernel, column, depth, per, first...  24.1 us
    dynamic_update_slice x18, local copies, waits for them, and re-layouts, put(): panel = lax.dynamic_update_slice(panel, piece[None], (slot, first, 0))  18.8 us
    ppermute x12, starting transfers between devices, hop(): below = lax.ppermute(below, 'col', self.up)  16.8 us
    pallas_call x2, Pallas kernels, attend(): pl.pallas_call(functools.partial(attend_kernel, parts, chunks, pair), gri...  14.1 us
    ppermute x12, waiting for transfers between devices, hop(): above = lax.ppermute(above, 'col', self.down)  13 us
    dynamic_update_slice x9, other arithmetic, put(): panel = lax.dynamic_update_slice(panel, piece[None], (slot, first, 0))  10.4 us
  transfers between devices with their start and end apart: 41, of which 26 were waited for; matrix products, arithmetic and copies ran while one was open for 18% of the time, Pallas kernels for 20%

profile of v7, /device:TPU:2, one launch (start us, length us, event | category | flops | bytes accessed | tf_op | source)
XLA Modules:
  0.0 295.0 jit_solution(7690806942877598456)
XLA Ops:
  8.6 2.3 copy_bitcast_fusion.refs_0_
  11.3 2.7 slice.38
  15.8 2.1 pad_maximum_fusion
  21.2 10.5 %collective-permute-done = bf16[512,1024]{1,0:T(8,128)(2,1)S(1)} collective-permute-done((bf16[512,1024]{1,0:T(8,128)(2,1)}, bf16[512,1024]{1,0:T(8,128)(2,1)S(1)}, u32[]{:S(2)}, u32[]{:S(2)}) %collective-permute-start) | collective-permute-done | bytes 1048608 | tf_op jit(solution)/shard_map/ppermute | solution.py:80
  32.9 3.8 %collective-permute-done.3.refs_2_ = bf16[2048,256]{1,0:T(8,128)(2,1)} collective-permute-done((bf16[2048,256]{1,0:T(8,128)(2,1)}, bf16[2048,256]{1,0:T(8,128)(2,1)}, u32[]{:S(2)}, u32[]{:S(2)}) %collective-permute-start.3) | collective-permute-done | bytes 1048608 | tf_op jit(solution)/shard_map/ppermute | solution.py:23
  42.1 19.5 %collective-permute-done.4 = bf16[512,1024]{1,0:T(8,128)(2,1)S(1)} collective-permute-done((bf16[512,1024]{1,0:T(8,128)(2,1)S(1)}, bf16[512,1024]{1,0:T(8,128)(2,1)S(1)}, u32[]{:S(2)}, u32[]{:S(2)}) %collective-permute-start.4) | collective-permute-done | bytes 1048608 | tf_op jit(solution)/shard_map/ppermute | solution.py:80
  69.7 19.5 %collective-permute-done.8 = bf16[512,1024]{1,0:T(8,128)(2,1)S(1)} collective-permute-done((bf16[512,1024]{1,0:T(8,128)(2,1)S(1)}, bf16[512,1024]{1,0:T(8,128)(2,1)S(1)}, u32[]{:S(2)}, u32[]{:S(2)}) %collective-permute-start.8) | collective-permute-done | bytes 1048608 | tf_op jit(solution)/shard_map/ppermute | solution.py:80
  98.6 8.8 %collective-permute-done.12 = bf16[256,1024]{1,0:T(8,128)(2,1)S(1)} collective-permute-done((bf16[256,1024]{1,0:T(8,128)(2,1)S(1)}, bf16[256,1024]{1,0:T(8,128)(2,1)S(1)}, u32[]{:S(2)}, u32[]{:S(2)}) %collective-permute-start.12) | collective-permute-done | bytes 524320 | tf_op jit(solution)/shard_map/ppermute | solution.py:80
  111.8 7.1 %shard_map.65.refs_1_ = bf16[512,256]{1,0:T(8,128)(2,1)} custom-call(bf16[8,512,1024]{2,1,0:T(8,128)(2,1)} %fusion.33.panel_ref, bf16[2048,256]{1,0:T(8,128)(2,1)} %copy_bitcast_fusion.refs_0_, bf16[2048,256]{1,0:T(8,128)(2,1)} %collective-permute-done.2.refs_1_, bf16[2048,256]{1,0:T(8,128)(2,1)} %collective-permute-done.3.refs_2_, ...), custom_call_target="tpu_custom_call" | custom-call | flops 1 | bytes 1 | tf_op jit(solution)/shard_map/pallas_call | solution.py:158
  119.6 1.9 slice.41
  121.4 3.9 %slice.49 = bf16[2,768,1024]{2,1,0:T(8,128)(2,1)} slice(bf16[2,1024,1024]{2,1,0:T(8,128)(2,1)} %bitcast.89), slice={[0:2], [0:768], [0:1024]} | slice | bytes 6291456 | tf_op jit(solution)/shard_map/slice | solution.py:410
  126.1 10.7 %shard_map.66.refs_0_ = bf16[512,512]{1,0:T(8,128)(2,1)} custom-call(bf16[8,512,1024]{2,1,0:T(8,128)(2,1)} %fusion.33.panel_ref, bf16[2048,1024]{1,0:T(8,128)(2,1)} %refs_0_.1, bf16[2048,1024]{1,0:T(8,128)(2,1)} %collective-permute-done.15.refs_1_, bf16[2048,256]{1,0:T(8,128)(2,1)} %copy-done.5, bf16[2048,256]{1,0:T(8,128)(2,1)} %copy-done.7, ...), custom_call_target="tpu_custom_call" | custom-call | flops 1 | bytes 1 | tf_op jit(solution)/shard_map/pallas_call | solution.py:158
  140.7 7.1 %shard_map.67 = bf16[512,512]{1,0:T(8,128)(2,1)S(1)} custom-call(s32[1]{0:T(128)} %bitcast.r_ref, bf16[512,512]{1,0:T(8,128)(2,1)S(1)} %copy-done.1, bf16[512,256]{1,0:T(8,128)(2,1)S(1)} %copy-done, bf16[512,256]{1,0:T(8,128)(2,1)S(1)} %collective-permute-done.17.refs_2_, bf16[512,256]{1,0:T(8,128)(2,1)S(1)} %collective-permute-done.16.refs_3_, ...), custom_call_target="tpu_custom_call" | custom-call | flops 1 | bytes 1 | tf_op jit(solution)/shard_map/pallas_call | solution.py:241
  152.5 2.5 collective-permute-done.22.refs_3_
  155.0 6.2 %collective-permute-done.20 = bf16[512,512]{1,0:T(8,128)(2,1)} collective-permute-done((bf16[512,512]{1,0:T(8,128)(2,1)S(1)}, bf16[512,512]{1,0:T(8,128)(2,1)}, u32[]{:S(2)}, u32[]{:S(2)}) %collective-permute-start.20) | collective-permute-done | bytes 524320 | tf_op jit(solution)/shard_map/ppermute | solution.py:80
  161.2 1.9 collective-permute-done.21
  165.9 1.9 bitcast_dynamic-update-slice_fusion.12
  167.7 1.9 bitcast_dynamic-update-slice_fusion.11
  169.6 8.3 %collective-permute-done.23 = bf16[512,512]{1,0:T(8,128)(2,1)} collective-permute-done((bf16[512,512]{1,0:T(8,128)(2,1)}, bf16[512,512]{1,0:T(8,128)(2,1)}, u32[]{:S(2)}, u32[]{:S(2)}) %collective-permute-start.23) | collective-permute-done | bytes 524320 | tf_op jit(solution)/shard_map/ppermute | solution.py:80
  178.0 1.9 collective-permute-done.24
  182.6 1.9 bitcast_dynamic-update-slice_fusion.10
  184.5 1.9 bitcast_dynamic-update-slice_fusion.9
  187.6 10.7 %shard_map.70.refs_0_ = bf16[512,512]{1,0:T(8,128)(2,1)} custom-call(bf16[8,512,1024]{2,1,0:T(8,128)(2,1)} %fusion.33.panel_ref, bf16[2048,1024]{1,0:T(8,128)(2,1)} %refs_0_.1, bf16[2048,1024]{1,0:T(8,128)(2,1)} %collective-permute-done.15.refs_1_, bf16[2048,384]{1,0:T(8,128)(2,1)} %collective-permute-done.18.refs_2_, ...), custom_call_target="tpu_custom_call" | custom-call | flops 1 | bytes 1 | tf_op jit(solution)/shard_map/pallas_call | solution.py:158
  202.3 7.1 %shard_map.71 = bf16[512,512]{1,0:T(8,128)(2,1)S(1)} custom-call(s32[1]{0:T(128)} %bitcast.r_ref, bf16[512,512]{1,0:T(8,128)(2,1)S(1)} %copy-done.2, bf16[512,256]{1,0:T(8,128)(2,1)S(1)} %copy-done, bf16[512,256]{1,0:T(8,128)(2,1)S(1)} %collective-permute-done.17.refs_2_, bf16[512,256]{1,0:T(8,128)(2,1)S(1)} %collective-permute-done.16.refs_3_, ...), custom_call_target="tpu_custom_call" | custom-call | flops 1 | bytes 1 | tf_op jit(solution)/shard_map/pallas_call | solution.py:241
  213.1 11.6 %collective-permute-done.31 = bf16[512,512]{1,0:T(8,128)(2,1)S(1)} collective-permute-done((bf16[512,512]{1,0:T(8,128)(2,1)S(1)}, bf16[512,512]{1,0:T(8,128)(2,1)S(1)}, u32[]{:S(2)}, u32[]{:S(2)}) %collective-permute-start.31) | collective-permute-done | bytes 524320 | tf_op jit(solution)/shard_map/ppermute | solution.py:80
  228.5 2.3 slice.48
  232.5 8.0 %collective-permute-done.33 = bf16[512,512]{1,0:T(8,128)(2,1)S(1)} collective-permute-done((bf16[512,512]{1,0:T(8,128)(2,1)S(1)}, bf16[512,512]{1,0:T(8,128)(2,1)S(1)}, u32[]{:S(2)}, u32[]{:S(2)}) %collective-permute-start.33) | collective-permute-done | bytes 524320 | tf_op jit(solution)/shard_map/ppermute | solution.py:80
  246.9 8.3 %collective-permute-done.35 = bf16[512,512]{1,0:T(8,128)(2,1)S(1)} collective-permute-done((bf16[512,512]{1,0:T(8,128)(2,1)S(1)}, bf16[512,512]{1,0:T(8,128)(2,1)S(1)}, u32[]{:S(2)}, u32[]{:S(2)}) %collective-permute-start.35) | collective-permute-done | bytes 524320 | tf_op jit(solution)/shard_map/ppermute | solution.py:80
  259.3 2.6 collective-permute-done.37
  264.0 8.7 %shard_map.72.refs_0_ = f32[512,1024]{1,0:T(8,128)} custom-call(s32[1]{0:T(128)} %bitcast.r_ref, bf16[8,512,512]{2,1,0:T(8,128)(2,1)} %bitcast_dynamic-update-slice_fusion.14.panel_ref, bf16[4,1536,1024]{2,1,0:T(8,128)(2,1)} %bitcast.86), custom_call_target="tpu_custom_call" | custom-call | flops 1 | bytes 1 | tf_op jit(solution)/shard_map/pallas_call | solution.py:285
  272.8 7.9 %shard_map.73.refs_0_ = f32[512,1024]{1,0:T(8,128)} custom-call(s32[1]{0:T(128)} %bitcast.r_ref, bf16[8,512,512]{2,1,0:T(8,128)(2,1)} %bitcast_dynamic-update-slice_fusion.16.panel_ref, bf16[4,1536,1024]{2,1,0:T(8,128)(2,1)} %bitcast.87, f32[512,1024]{1,0:T(8,128)} %shard_map.72.refs_0_), custom_call_target="tpu_custom_call" | custom-call | flops 1 | bytes 1 | tf_op jit(solution)/shard_map/pallas_call | solution.py:285
  280.7 7.5 %shard_map.74 = bf16[512,1024]{1,0:T(8,128)(2,1)} custom-call(s32[1]{0:T(128)} %bitcast.r_ref, bf16[8,512,512]{2,1,0:T(8,128)(2,1)} %bitcast_dynamic-update-slice_fusion.16.panel_ref, bf16[4,512,1024]{2,1,0:T(8,128)(2,1)} %bitcast.91, f32[512,1024]{1,0:T(8,128)} %shard_map.73.refs_0_), custom_call_target="tpu_custom_call" | custom-call | flops 1 | bytes 1 | tf_op jit(solution)/shard_map/pallas_call | solution.py:285
  (144 shorter events, 78.4 us)
Async XLA Ops:
  6.5 235.1 %all-gather.5.cloned.1.call-start = ((), (), s32[]{:S(2)}) async-start(), calls=%async_computation | async-start | bytes 15728640 | tf_op jit(solution)/shard_map/all_gather | solution.py:411
  6.5 25.1 %collective-permute-start = (bf16[512,1024]{1,0:T(8,128)(2,1)}, bf16[512,1024]{1,0:T(8,128)(2,1)S(1)}, u32[]{:S(2)}, u32[]{:S(2)}) collective-permute-start(bf16[512,1024]{1,0:T(8,128)(2,1)} %param.6), channel_id=1, source_target_pairs={{0,2},{2,4},{4,6},{6,7},{7,5},{5,3},{3,1},{1,0},{8,10},{10,12},{12... | collective-permute-start | bytes 3145736 | tf_op jit(solution)/shard_map/ppermute | solution.py:80
  8.1 24.8 %collective-permute-start.1 = (bf16[512,1024]{1,0:T(8,128)(2,1)}, bf16[512,1024]{1,0:T(8,128)(2,1)S(1)}, u32[]{:S(2)}, u32[]{:S(2)}) collective-permute-start(bf16[512,1024]{1,0:T(8,128)(2,1)} %param.6), channel_id=1, source_target_pairs={{2,0},{4,2},{6,4},{7,6},{5,7},{3,5},{1,3},{0,1},{10,8},{12,10},{14... | collective-permute-start | bytes 3145736 | tf_op jit(solution)/shard_map/ppermute | solution.py:81
  10.8 22.1 %collective-permute-start.2 = (bf16[2048,256]{1,0:T(8,128)(2,1)}, bf16[2048,256]{1,0:T(8,128)(2,1)}, u32[]{:S(2)}, u32[]{:S(2)}) collective-permute-start(bf16[2048,256]{1,0:T(8,128)(2,1)} %copy_bitcast_fusion.refs_0_), channel_id=1, source_target_pairs={{0,8},{8,0},{16,24},{24,16},{1,9},{9,1},{17,25},{25,17},{2,10},{10... | collective-permute-start | bytes 3145736 | tf_op jit(solution)/shard_map/ppermute | solution.py:23
  10.8 25.9 %collective-permute-start.3 = (bf16[2048,256]{1,0:T(8,128)(2,1)}, bf16[2048,256]{1,0:T(8,128)(2,1)}, u32[]{:S(2)}, u32[]{:S(2)}) collective-permute-start(bf16[2048,256]{1,0:T(8,128)(2,1)} %copy_bitcast_fusion.refs_0_), channel_id=1, source_target_pairs={{0,16},{8,24},{16,0},{24,8},{1,17},{9,25},{17,1},{25,9},{2,18},{10... | collective-permute-start | bytes 3145736 | tf_op jit(solution)/shard_map/ppermute | solution.py:23
  36.7 24.8 %collective-permute-start.4 = (bf16[512,1024]{1,0:T(8,128)(2,1)S(1)}, bf16[512,1024]{1,0:T(8,128)(2,1)S(1)}, u32[]{:S(2)}, u32[]{:S(2)}) collective-permute-start(bf16[512,1024]{1,0:T(8,128)(2,1)S(1)} %collective-permute-done), channel_id=1, source_target_pairs={{0,2},{2,4},{4,6},{6,7},{7,5},{5,3},{3,1},{1,0},{8,10},{10,12},{12... | collective-permute-start | bytes 3145736 | tf_op jit(solution)/shard_map/ppermute | solution.py:80
  38.3 24.5 %collective-permute-start.5 = (bf16[512,1024]{1,0:T(8,128)(2,1)S(1)}, bf16[512,1024]{1,0:T(8,128)(2,1)S(1)}, u32[]{:S(2)}, u32[]{:S(2)}) collective-permute-start(bf16[512,1024]{1,0:T(8,128)(2,1)S(1)} %collective-permute-done.1), channel_id=1, source_target_pairs={{2,0},{4,2},{6,4},{7,6},{5,7},{3,5},{1,3},{0,1},{10,8},{12,10},{14... | collective-permute-start | bytes 3145736 | tf_op jit(solution)/shard_map/ppermute | solution.py:81
  38.8 24.1 %collective-permute-start.6 = (bf16[2048,256]{1,0:T(8,128)(2,1)}, bf16[2048,256]{1,0:T(8,128)(2,1)S(1)}, u32[]{:S(2)}, u32[]{:S(2)}) collective-permute-start(bf16[2048,256]{1,0:T(8,128)(2,1)} %collective-permute-done.3.refs_2_), channel_id=1, source_target_pairs={{0,8},{8,0},{16,24},{24,16},{1,9},{9,1},{17,25},{25,17},{2,10},{10... | collective-permute-start | bytes 3145736 | tf_op jit(solution)/shard_map/ppermute | solution.py:23
  38.8 25.6 %collective-permute-start.7 = (bf16[2048,256]{1,0:T(8,128)(2,1)S(1)}, bf16[2048,256]{1,0:T(8,128)(2,1)S(1)}, u32[]{:S(2)}, u32[]{:S(2)}) collective-permute-start(bf16[2048,256]{1,0:T(8,128)(2,1)S(1)} %get-tuple-element.93), channel_id=1, source_target_pairs={{0,16},{8,24},{16,0},{24,8},{1,17},{9,25},{17,1},{25,9},{2,18},{10... | collective-permute-start | bytes 3145736 | tf_op jit(solution)/shard_map/ppermute | solution.py:23
  64.3 24.8 %collective-permute-start.8 = (bf16[512,1024]{1,0:T(8,128)(2,1)S(1)}, bf16[512,1024]{1,0:T(8,128)(2,1)S(1)}, u32[]{:S(2)}, u32[]{:S(2)}) collective-permute-start(bf16[512,1024]{1,0:T(8,128)(2,1)S(1)} %collective-permute-done.4), channel_id=1, source_target_pairs={{0,2},{2,4},{4,6},{6,7},{7,5},{5,3},{3,1},{1,0},{8,10},{10,12},{12... | collective-permute-start | bytes 3145736 | tf_op jit(solution)/shard_map/ppermute | solution.py:80
  65.9 24.5 %collective-permute-start.9 = (bf16[512,1024]{1,0:T(8,128)(2,1)S(1)}, bf16[512,1024]{1,0:T(8,128)(2,1)S(1)}, u32[]{:S(2)}, u32[]{:S(2)}) collective-permute-start(bf16[512,1024]{1,0:T(8,128)(2,1)S(1)} %collective-permute-done.5), channel_id=1, source_target_pairs={{2,0},{4,2},{6,4},{7,6},{5,7},{3,5},{1,3},{0,1},{10,8},{12,10},{14... | collective-permute-start | bytes 3145736 | tf_op jit(solution)/shard_map/ppermute | solution.py:81
  66.4 24.1 %collective-permute-start.10 = (bf16[2048,256]{1,0:T(8,128)(2,1)S(1)}, bf16[2048,256]{1,0:T(8,128)(2,1)S(1)}, u32[]{:S(2)}, u32[]{:S(2)}) collective-permute-start(bf16[2048,256]{1,0:T(8,128)(2,1)S(1)} %collective-permute-done.7.refs_2_), channel_id=1, source_target_pairs={{0,8},{8,0},{16,24},{24,16},{1,9},{9,1},{17,25},{25,17},{2,10},{10... | collective-permute-start | bytes 3145736 | tf_op jit(solution)/shard_map/ppermute | solution.py:23
  66.4 25.6 %collective-permute-start.11 = (bf16[2048,256]{1,0:T(8,128)(2,1)S(1)}, bf16[2048,256]{1,0:T(8,128)(2,1)S(1)}, u32[]{:S(2)}, u32[]{:S(2)}) collective-permute-start(bf16[2048,256]{1,0:T(8,128)(2,1)S(1)} %get-tuple-element.101), channel_id=1, source_target_pairs={{0,16},{8,24},{16,0},{24,8},{1,17},{9,25},{17,1},{25,9},{2,18},{10... | collective-permute-start | bytes 3145736 | tf_op jit(solution)/shard_map/ppermute | solution.py:23
  92.9 15.8 %collective-permute-start.15 = (bf16[2048,1024]{1,0:T(8,128)(2,1)}, bf16[2048,1024]{1,0:T(8,128)(2,1)}, u32[]{:S(2)}, u32[]{:S(2)}) collective-permute-start(bf16[2048,1024]{1,0:T(8,128)(2,1)} %refs_0_.1), channel_id=1, source_target_pairs={{0,8},{8,0},{16,24},{24,16},{1,9},{9,1},{17,25},{25,17},{2,10},{10... | collective-permute-start | bytes 12582920 | tf_op jit(solution)/shard_map/ppermute | solution.py:23
  93.0 14.4 %collective-permute-start.12 = (bf16[256,1024]{1,0:T(8,128)(2,1)S(1)}, bf16[256,1024]{1,0:T(8,128)(2,1)S(1)}, u32[]{:S(2)}, u32[]{:S(2)}) collective-permute-start(bf16[256,1024]{1,0:T(8,128)(2,1)S(1)} %slice.39), channel_id=1, source_target_pairs={{0,2},{2,4},{4,6},{6,7},{7,5},{5,3},{3,1},{1,0},{8,10},{10,12},{12... | collective-permute-start | bytes 1572872 | tf_op jit(solution)/shard_map/ppermute | solution.py:80
  94.6 14.1 %collective-permute-start.13 = (bf16[256,1024]{1,0:T(8,128)(2,1)S(1)}, bf16[256,1024]{1,0:T(8,128)(2,1)S(1)}, u32[]{:S(2)}, u32[]{:S(2)}) collective-permute-start(bf16[256,1024]{1,0:T(8,128)(2,1)S(1)} %slice.40), channel_id=1, source_target_pairs={{2,0},{4,2},{6,4},{7,6},{5,7},{3,5},{1,3},{0,1},{10,8},{12,10},{14... | collective-permute-start | bytes 1572872 | tf_op jit(solution)/shard_map/ppermute | solution.py:81
  95.1 41.7 %collective-permute-start.18 = (bf16[2048,384]{1,0:T(8,128)(2,1)}, bf16[2048,384]{1,0:T(8,128)(2,1)}, u32[]{:S(2)}, u32[]{:S(2)}) collective-permute-start(bf16[2048,384]{1,0:T(8,128)(2,1)} %slice.38), channel_id=1, source_target_pairs={{0,16},{8,24},{16,0},{24,8},{1,17},{9,25},{17,1},{25,9},{2,18},{10... | collective-permute-start | bytes 4718600 | tf_op jit(solution)/shard_map/ppermute | solution.py:23
  118.9 18.8 %collective-permute-start.16 = (bf16[512,256]{1,0:T(8,128)(2,1)}, bf16[512,256]{1,0:T(8,128)(2,1)S(1)}, u32[]{:S(2)}, u32[]{:S(2)}) collective-permute-start(bf16[512,256]{1,0:T(8,128)(2,1)} %shard_map.65.refs_1_), channel_id=1, source_target_pairs={{0,16},{8,24},{16,0},{24,8},{1,17},{9,25},{17,1},{25,9},{2,18},{10... | collective-permute-start | bytes 786440 | tf_op jit(solution)/shard_map/ppermute | solution.py:23
  119.5 18.2 %collective-permute-start.17 = (bf16[512,256]{1,0:T(8,128)(2,1)}, bf16[512,256]{1,0:T(8,128)(2,1)S(1)}, u32[]{:S(2)}, u32[]{:S(2)}) collective-permute-start(bf16[512,256]{1,0:T(8,128)(2,1)} %shard_map.65.refs_1_), channel_id=1, source_target_pairs={{0,8},{8,0},{16,24},{24,16},{1,9},{9,1},{17,25},{25,17},{2,10},{10... | collective-permute-start | bytes 786440 | tf_op jit(solution)/shard_map/ppermute | solution.py:23
  137.8 142.9 %all-gather.7.cloned.1.call-start = ((), (), s32[]{:S(2)}) async-start(), calls=%async_computation.1 | async-start | bytes 5242880 | tf_op jit(solution)/shard_map/all_gather | solution.py:411
  138.1 16.9 %collective-permute-start.22 = (bf16[2048,128]{1,0:T(8,128)(2,1)}, bf16[2048,128]{1,0:T(8,128)(2,1)}, u32[]{:S(2)}, u32[]{:S(2)}) collective-permute-start(bf16[2048,128]{1,0:T(8,128)(2,1)} %slice.41), channel_id=1, source_target_pairs={{0,16},{8,24},{16,0},{24,8},{1,17},{9,25},{17,1},{25,9},{2,18},{10... | collective-permute-start | bytes 1572872 | tf_op jit(solution)/shard_map/ppermute | solution.py:23
  149.4 13.8 %collective-permute-start.21 = (bf16[512,512]{1,0:T(8,128)(2,1)S(1)}, bf16[512,512]{1,0:T(8,128)(2,1)}, u32[]{:S(2)}, u32[]{:S(2)}) collective-permute-start(bf16[512,512]{1,0:T(8,128)(2,1)S(1)} %shard_map.67), channel_id=1, source_target_pairs={{2,0},{4,2},{6,4},{7,6},{5,7},{3,5},{1,3},{0,1},{10,8},{12,10},{14... | collective-permute-start | bytes 1572872 | tf_op jit(solution)/shard_map/ppermute | solution.py:81
  149.8 36.6 %collective-permute-start.28 = (bf16[2048,384]{1,0:T(8,128)(2,1)}, bf16[2048,384]{1,0:T(8,128)(2,1)S(1)}, u32[]{:S(2)}, u32[]{:S(2)}) collective-permute-start(bf16[2048,384]{1,0:T(8,128)(2,1)} %collective-permute-done.18.refs_2_), channel_id=1, source_target_pairs={{0,8},{8,0},{16,24},{24,16},{1,9},{9,1},{17,25},{25,17},{2,10},{10... | collective-permute-start | bytes 4718600 | tf_op jit(solution)/shard_map/ppermute | solution.py:23
  163.1 14.8 %collective-permute-start.23 = (bf16[512,512]{1,0:T(8,128)(2,1)}, bf16[512,512]{1,0:T(8,128)(2,1)}, u32[]{:S(2)}, u32[]{:S(2)}) collective-permute-start(bf16[512,512]{1,0:T(8,128)(2,1)} %collective-permute-done.20), channel_id=1, source_target_pairs={{0,2},{2,4},{4,6},{6,7},{7,5},{5,3},{3,1},{1,0},{8,10},{10,12},{12... | collective-permute-start | bytes 1572872 | tf_op jit(solution)/shard_map/ppermute | solution.py:80
  164.7 15.1 %collective-permute-start.24 = (bf16[512,512]{1,0:T(8,128)(2,1)}, bf16[512,512]{1,0:T(8,128)(2,1)}, u32[]{:S(2)}, u32[]{:S(2)}) collective-permute-start(bf16[512,512]{1,0:T(8,128)(2,1)} %collective-permute-done.21), channel_id=1, source_target_pairs={{2,0},{4,2},{6,4},{7,6},{5,7},{3,5},{1,3},{0,1},{10,8},{12,10},{14... | collective-permute-start | bytes 1572872 | tf_op jit(solution)/shard_map/ppermute | solution.py:81
  165.2 14.6 %collective-permute-start.25 = (bf16[2048,128]{1,0:T(8,128)(2,1)}, bf16[2048,128]{1,0:T(8,128)(2,1)S(1)}, u32[]{:S(2)}, u32[]{:S(2)}) collective-permute-start(bf16[2048,128]{1,0:T(8,128)(2,1)} %collective-permute-done.22.refs_3_), channel_id=1, source_target_pairs={{0,8},{8,0},{16,24},{24,16},{1,9},{9,1},{17,25},{25,17},{2,10},{10... | collective-permute-start | bytes 1572872 | tf_op jit(solution)/shard_map/ppermute | solution.py:23
  180.6 17.6 %collective-permute-start.26 = (bf16[512,512]{1,0:T(8,128)(2,1)}, bf16[512,512]{1,0:T(8,128)(2,1)S(1)}, u32[]{:S(2)}, u32[]{:S(2)}) collective-permute-start(bf16[512,512]{1,0:T(8,128)(2,1)} %collective-permute-done.23), channel_id=1, source_target_pairs={{0,2},{2,4},{4,6},{6,7},{7,5},{5,3},{3,1},{1,0},{8,10},{10,12},{12... | collective-permute-start | bytes 1572872 | tf_op jit(solution)/shard_map/ppermute | solution.py:80
  182.2 16.0 %collective-permute-start.27 = (bf16[512,512]{1,0:T(8,128)(2,1)}, bf16[512,512]{1,0:T(8,128)(2,1)S(1)}, u32[]{:S(2)}, u32[]{:S(2)}) collective-permute-start(bf16[512,512]{1,0:T(8,128)(2,1)} %collective-permute-done.24), channel_id=1, source_target_pairs={{2,0},{4,2},{6,4},{7,6},{5,7},{3,5},{1,3},{0,1},{10,8},{12,10},{14... | collective-permute-start | bytes 1572872 | tf_op jit(solution)/shard_map/ppermute | solution.py:81
  210.2 14.5 %collective-permute-start.31 = (bf16[512,512]{1,0:T(8,128)(2,1)S(1)}, bf16[512,512]{1,0:T(8,128)(2,1)S(1)}, u32[]{:S(2)}, u32[]{:S(2)}) collective-permute-start(bf16[512,512]{1,0:T(8,128)(2,1)S(1)} %shard_map.71), channel_id=1, source_target_pairs={{0,2},{2,4},{4,6},{6,7},{7,5},{5,3},{3,1},{1,0},{8,10},{10,12},{12... | collective-permute-start | bytes 1572872 | tf_op jit(solution)/shard_map/ppermute | solution.py:80
  211.8 14.7 %collective-permute-start.32 = (bf16[512,512]{1,0:T(8,128)(2,1)S(1)}, bf16[512,512]{1,0:T(8,128)(2,1)S(1)}, u32[]{:S(2)}, u32[]{:S(2)}) collective-permute-start(bf16[512,512]{1,0:T(8,128)(2,1)S(1)} %shard_map.71), channel_id=1, source_target_pairs={{2,0},{4,2},{6,4},{7,6},{5,7},{3,5},{1,3},{0,1},{10,8},{12,10},{14... | collective-permute-start | bytes 1572872 | tf_op jit(solution)/shard_map/ppermute | solution.py:81
  226.5 13.9 %collective-permute-start.33 = (bf16[512,512]{1,0:T(8,128)(2,1)S(1)}, bf16[512,512]{1,0:T(8,128)(2,1)S(1)}, u32[]{:S(2)}, u32[]{:S(2)}) collective-permute-start(bf16[512,512]{1,0:T(8,128)(2,1)S(1)} %collective-permute-done.31), channel_id=1, source_target_pairs={{0,2},{2,4},{4,6},{6,7},{7,5},{5,3},{3,1},{1,0},{8,10},{10,12},{12... | collective-permute-start | bytes 1572872 | tf_op jit(solution)/shard_map/ppermute | solution.py:80
  228.0 13.7 %collective-permute-start.34 = (bf16[512,512]{1,0:T(8,128)(2,1)S(1)}, bf16[512,512]{1,0:T(8,128)(2,1)S(1)}, u32[]{:S(2)}, u32[]{:S(2)}) collective-permute-start(bf16[512,512]{1,0:T(8,128)(2,1)S(1)} %collective-permute-done.32), channel_id=1, source_target_pairs={{2,0},{4,2},{6,4},{7,6},{5,7},{3,5},{1,3},{0,1},{10,8},{12,10},{14... | collective-permute-start | bytes 1572872 | tf_op jit(solution)/shard_map/ppermute | solution.py:81
  (20 other events, 152.0 us)
Sparse Core Ops, SparseCore 0:
  137.9 84.0 all-gather.4
  241.8 30.5 all-gather.6

commit v8 on v7

--- a/solution.py
+++ b/solution.py
@@ -55,35 +55,56 @@
     return jnp.where(at < n // 2, 2 * at, 2 * (n - 1 - at) + 1)
 
 
+def take(refs, *counts):
+    out, at = [], 0
+    for n in counts:
+        out.append(refs[at : at + n])
+        at += n
+    return *out, refs[at:]
+
+
 class Ring:
-    def __init__(self, block):
+    def __init__(self, block, pieces):
         n = lax.axis_size("col")
         order = ring_order(n)
         self.n, self.hops = n, 0
         self.up = [(order[i], order[(i + 1) % n]) for i in range(n)]
         self.down = [(b, a) for a, b in self.up]
+        self.rows = block.shape[0]
         self.found = [(lax.axis_index("col"), 0, block)]
-        self.last = [block, block]
-
-    def hop(self, *earlier, beside=()):
+        self.height = self.rows // pieces
+        parts = [block[i * self.height : (i + 1) * self.height] for i in range(pieces)]
+        self.last = [(p, p) for p in parts]
+
+    def hop(self, beside=()):
         if self.hops == self.n // 2:
-            return beside
-        c, own = self.found[0][0], self.found[0][2]
-        rows = own.shape[0] // 2
+            return [], list(beside)
+        c, half = self.found[0][0], self.rows // 2
         self.hops += 1
-        end = self.hops == self.n // 2
-        below, above = self.last
-        if end:
-            below, above = below[:rows], above[rows:]
-        if earlier:
-            below, above = lax.optimization_barrier((below, above, *earlier))[:2]
-        below = lax.ppermute(below, "col", self.up)
-        above = lax.ppermute(above, "col", self.down)
-        below, above, *beside = lax.optimization_barrier((below, above, *beside))
-        self.last = [below, above]
-        self.found.append((ring_source(c, self.hops, self.n), 0, self.last[0]))
-        self.found.append((ring_source(c, -self.hops, self.n), rows if end else 0, self.last[1]))
-        return beside
+        found = []
+        for i, (below, above) in enumerate(self.last):
+            top = i * self.height
+            firsts = [top, top]
+            sends = [(below, self.up), (above, self.down)]
+            if self.hops == self.n // 2:
+                if len(self.last) == 1:
+                    sends = [(below[:half], self.up), (above[half:], self.down)]
+                    firsts = [0, half]
+                else:
+                    sends = [sends[0], None] if top < half else [None, sends[1]]
+            got = [None if s is None else lax.ppermute(s[0], "col", s[1]) for s in sends]
+            more = list(beside) if i == len(self.last) - 1 else []
+            here = [g for g in got if g is not None]
+            here, more = take(lax.optimization_barrier((*here, *more)), len(here))
+            here = list(here)
+            got = [None if g is None else here.pop(0) for g in got]
+            self.last[i] = tuple(got)
+            for way, piece in enumerate(got):
+                if piece is not None:
+                    hops = self.hops if way == 0 else -self.hops
+                    found.append((ring_source(c, hops, self.n), firsts[way], piece))
+        self.found += found
+        return found, list(more)
 
 
 def blank(shape):
@@ -92,14 +113,6 @@
         out_specs=pl.BlockSpec(memory_space=pl.ANY),
         out_shape=jax.ShapeDtypeStruct(shape, jnp.bfloat16),
     )()
-
-
-def take(refs, *counts):
-    out, at = [], 0
-    for n in counts:
-        out.append(refs[at : at + n])
-        at += n
-    return *out, refs[at:]
 
 
 def multiply(steps, a_buf, w_bufs, accs, a_sem, w_sem):
@@ -262,41 +275,52 @@
     )(r.reshape(1), *queries, *pieces)
 
 
-def finish_kernel(column, depth, per, first, r_ref, panel_ref, gathered_ref, *refs):
-    *old, o_ref, a_buf, w_buf, acc, a_sem, w_sem = refs
+def finish_kernel(most, per, first, depth, count, r_ref, panel_ref, gathered_ref, *refs):
+    pieces, (*old, o_ref, a_buf, w_buf, acc, a_sem, w_sem) = take(refs, count)
     steps = []
+    slots, _, wide = panel_ref.shape
     stride = gathered_ref.shape[1] // per
-    for k in range(panel_ref.shape[0]):
+    for k in range(slots):
         block = jnp.bitwise_xor(r_ref[0], k // per)
-        left = panel_ref.at[k, :, pl.ds(column, depth)]
-        right = gathered_ref.at[block, pl.ds(k % per * stride + first, depth), :]
-        steps.append((left, [[right]]))
+        for at in range(0, wide, depth):
+            if at < most:
+                row = k % per * stride + first + at
+                right = gathered_ref.at[block, pl.ds(row, depth), :]
+            else:
+                row = k % per * (wide - most) + at - most
+                right = pieces[k // per].at[pl.ds(row, depth), :]
+            steps.append((panel_ref.at[k, :, pl.ds(at, depth)], [[right]]))
     acc[...] = old[0][...] if old else jnp.zeros_like(acc)
     multiply(steps, a_buf, [w_buf], [acc], a_sem, w_sem)
     o_ref[...] = acc[...].astype(o_ref.dtype)
 
 
-def finish(r, panel, column, gathered, per, first, depth, dtype, total=None):
-    n, tok, _ = panel.shape
+def finish(r, panel, most, gathered, per, first, pieces, dtype, total=None):
+    n, tok, wide = panel.shape
     cols = gathered.shape[2]
+    most = most or wide
+    depth = math.gcd(most, wide)
+    count = n * wide // depth
     hbm = pl.BlockSpec(memory_space=pl.ANY)
     vmem = pl.BlockSpec(memory_space=pltpu.VMEM)
     old = [] if total is None else [total]
     return pl.pallas_call(
-        functools.partial(finish_kernel, column, depth, per, first),
-        in_specs=[pl.BlockSpec(memory_space=pltpu.SMEM)] + [hbm] * 2 + [vmem] * len(old),
+        functools.partial(finish_kernel, most, per, first, depth, len(pieces)),
+        in_specs=[pl.BlockSpec(memory_space=pltpu.SMEM)]
+        + [hbm] * (2 + len(pieces))
+        + [vmem] * len(old),
         out_specs=vmem,
         out_shape=jax.ShapeDtypeStruct((tok, cols), dtype),
         scratch_shapes=[
-            pltpu.VMEM((n, tok, depth), jnp.bfloat16),
-            pltpu.VMEM((n, depth, cols), jnp.bfloat16),
+            pltpu.VMEM((count, tok, depth), jnp.bfloat16),
+            pltpu.VMEM((count, depth, cols), jnp.bfloat16),
             pltpu.VMEM((tok, cols), jnp.float32),
-            pltpu.SemaphoreType.DMA((n,)),
-            pltpu.SemaphoreType.DMA((1, n)),
+            pltpu.SemaphoreType.DMA((count,)),
+            pltpu.SemaphoreType.DMA((1, count)),
         ],
         compiler_params=pltpu.CompilerParams(vmem_limit_bytes=60 * MIB),
         cost_estimate=SHORT,
-    )(r.reshape(1), panel, gathered, *old)
+    )(r.reshape(1), panel, gathered, *pieces, *old)
 
 
 def per_device(hidden, norm_gain, wq, wk, wv, wo):
@@ -319,9 +343,9 @@
     first_heads = n_heads // 2
     late_heads = n_heads - first_heads
     if n_heads >= 4:
-        last_heads = max(1, late_heads // 4)
-        sizes = [first_heads // 2, first_heads - first_heads // 2, late_heads - last_heads]
-        sizes.append(last_heads)
+        eighth = max(1, n_heads // 8)
+        sizes = [first_heads // 2, first_heads - first_heads // 2, eighth]
+        sizes += [n for n in (late_heads - 2 * eighth, eighth) if n > 0]
     else:
         sizes = [first_heads, late_heads]
     early = 2 if n_heads >= 4 else 1
@@ -350,49 +374,48 @@
             panel = lax.dynamic_update_slice(panel, piece[None], (slot, first, 0))
         return panel
 
-    def put_hidden(panel, found):
-        sums = []
+    def put_hidden(panel, squares, found):
         for source, first, piece in found:
             wider = piece.astype(jnp.float32)
-            sums.append(jnp.sum(wider * wider, axis=1))
+            sums = jnp.sum(wider * wider, axis=1)
+            for h in range(2):
+                if first <= h * tok // 2 < first + piece.shape[0]:
+                    at = h * tok // 2 - first
+                    squares[h] += sums[at : at + tok // 2]
             gain = lax.dynamic_slice(norm_gain, (source * feat,), (feat,))
             panel = put(panel, [(source, first, (wider * gain).astype(jnp.bfloat16))])
-        return panel, sums
-
-    ring = Ring(hidden)
+        return panel, squares
+
+    ring = Ring(hidden, 1)
     hops = n_col // 2
     x_sent = exchange(stacked)
-    gathering = gather_near(stacked)
-    got_near = []
-    panel, (squares,) = put_hidden(blank((n_col, tok, feat)), ring.found)
+    got_x = []
+    zeros = [jnp.zeros((tok // 2,), jnp.float32)] * 2
+    panel, squares = put_hidden(blank((n_col, tok, feat)), zeros, ring.found)
     for i in range(hops):
         last_hop = i == hops - 1
-        beside = [panel, squares, cosine, sine, *gathering]
+        tie = ring.last[0][1]
+        sent = [] if x_sent is None else [x_sent]
         ahead = chunks[i : i + 1] if i < len(sizes) - 1 else []
-        if not last_hop and x_sent is not None:
-            beside.append(x_sent)
-        beside = ring.hop(beside=[*beside, *ahead])
-        (panel, squares, cosine, sine), near, beside = take(beside, 4, len(gathering))
-        panel, sums = put_hidden(panel, ring.found[-2:])
-        squares += jnp.concatenate(sums) if last_hop else sums[0] + sums[1]
-        got_near.append(near)
+        beside = [panel, *squares, cosine, sine, *sent, *ahead]
         if last_hop:
-            break
-        gathering = []
-        if x_sent is not None:
-            gathering = gather_near(beside[0])
-            beside = beside[1:]
-        x_sent = exchange(beside[0]) if ahead else None
-        if i == hops - 2:
-            gathering = [*gathering, *gather_near(after(wq, ring.last[0]))]
-    blocks_near = len(got_near[0])
-    kv_near, kv_far = got_near[0], got_near[1]
-    q_near = got_near[-1][-blocks_near:]
-    q_far = [near[:blocks_near] for near in got_near[2:] if len(near) > 0]
-    scale = lax.rsqrt(squares / depth + 1e-05)[:, None]
+            near = gather_near(after(stacked, tie))
+            kv_weights = [*near, *gather_near(after(got_x[0], tie))]
+            beside += kv_weights
+        found, beside = ring.hop(beside)
+        (panel, *squares, cosine, sine), beside = take(beside, 5)
+        panel, squares = put_hidden(panel, squares, found)
+        sent, ahead, kv_weights = take(beside, len(sent), len(ahead))
+        got_x += sent
+        x_sent = exchange(ahead[0]) if ahead else None
+    blocks_near = len(kv_weights) // 2
+    kv_near, kv_far = take(kv_weights, blocks_near)
+    scale = lax.rsqrt(jnp.concatenate(squares) / depth + 1e-05)[:, None]
 
     kv = project(panel, kv_near, by_block([kv_far]), 0, 1, 1.0, scale, cosine, sine)
     scale = after(scale, kv)
+    q_far = [gather_near(after(x, *kv_weights)) for x in got_x[1 : 1 + early]]
+    q_near = gather_near(after(wq, *kv_weights))
     queries = project(
         panel, q_near, by_block(q_far[:early]), 0, first_heads, factor, scale, cosine, sine
     )
@@ -402,55 +425,53 @@
     kv_other, queries, last_chunk, *beside = lax.optimization_barrier(tuple(beside))
     kv_pieces, arrived = take(beside, blocks_near)
     kv_pieces = [*kv_pieces, *gather_near(kv_other)]
-    late_far = [gather_near(piece) for piece in arrived]
+    late_far = [gather_near(piece) for piece in (*got_x[1 + early :], *arrived)]
     last_other = exchange(last_chunk)
     split = cols - rest // 2 if rest >= 2 * HD else cols
 
-    def o_rows(first, last, *earlier):
-        piece = wo.reshape(-1, cols, wo.shape[1])[:, first:last].reshape(-1, wo.shape[1])
-        return lax.all_gather(after(piece, *earlier), "row")
-
-    o_first = o_rows(0, split, kv_other)
+    def o_rows(first, last):
+        return wo.reshape(-1, cols, wo.shape[1])[:, first:last].reshape(-1, wo.shape[1])
+
+    o_most = lax.all_gather(after(o_rows(0, split), kv_other), "row")
+    o_last = [o_rows(split, cols)] if split < cols else []
     heads = attend(r, [queries], kv_pieces)
 
-    ring = Ring(heads)
-    first_panel = put(blank((n_col, tok, wide)), ring.found)
-    second_panel = blank((n_col, tok, rest))
-    last_other, first_panel, second_panel = ring.hop(
-        beside=[last_other, first_panel, second_panel]
-    )
-    first_panel = put(first_panel, ring.found[-2:])
-    far = gather_near(last_other)
-    first_panel, *far = ring.hop(beside=[first_panel, *far])
-    first_panel = put(first_panel, ring.found[-2:])
-    late_far = by_block([*late_far, far])
+    ring = Ring(heads, 1)
+    panels = [put(blank((n_col, tok, wide)), ring.found), blank((n_col, tok, rest))]
+    found, (last_other, *panels) = ring.hop([last_other, *panels])
+    panels[0] = put(panels[0], found)
+    late_far = by_block([*late_far, gather_near(last_other)])
     queries = project(
         panel, q_near, late_far, wide, late_heads, factor, scale, cosine, sine
     )
-    queries, first_panel = ring.hop(beside=[queries, first_panel])
-    first_panel = put(first_panel, ring.found[-2:])
+    found, (queries, panels[0]) = ring.hop([queries, panels[0]])
+    panels[0] = put(panels[0], found)
     heads = attend(r, [queries], kv_pieces)
-    for i in range(3, hops):
-        heads, first_panel = ring.hop(beside=[heads, first_panel])
-        first_panel = put(first_panel, ring.found[-2:])
-    second = Ring(heads)
-    second_panel = put(second_panel, second.found)
-    o_last = None
+    found, (heads, panels[0]) = ring.hop([heads, panels[0]])
+    panels[0] = put(panels[0], found)
+    second = Ring(heads, 1)
+    panels[1] = put(panels[1], second.found)
     for i in range(hops):
-        (second_panel,) = second.hop(beside=[second_panel])
-        second_panel = put(second_panel, second.found[-2:])
-        if i == hops - 3 and split < cols:
-            o_last = o_rows(split, cols, o_first, *second.last)
-
-    total = finish(r, first_panel, 0, o_first, per, 0, wide, jnp.float32)
-    total = after(total, *second.last)
-    dtype = jnp.bfloat16 if o_last is None else jnp.float32
-    total = finish(r, second_panel, 0, o_first, per, wide, split - wide, dtype, total)
-    if o_last is not None:
-        total = finish(
-            r, second_panel, split - wide, o_last, per, 0, cols - split, jnp.bfloat16, total
-        )
-    return total
+        found, (panels[0],) = ring.hop([panels[0]])
+        panels[0] = put(panels[0], found)
+        beside = [panels[1]]
+        if i == hops - 3:
+            beside += o_last
+        if i == hops - 2:
+            beside += [exchange(w) for w in o_last]
+        if i == hops - 1:
+            for w in o_last:
+                beside += [*gather_near(w), *gather_near(o_other)]
+            beside.append(finish(r, panels[0], 0, o_most, per, 0, [], jnp.float32))
+        found, (panels[1], *beside) = second.hop(beside)
+        panels[1] = put(panels[1], found)
+        if i == hops - 3:
+            o_last = beside
+        if i == hops - 2 and o_last:
+            (o_other,) = beside
+    *pieces, total = beside
+
+    return finish(r, panels[1], split - wide, o_most, per, wide, pieces, jnp.bfloat16, total)
 
 
 def solution(mesh):

time: 296 us -> 281 us (0.949)
  waiting for transfers between devices: 126 us -> 110 us
  Pallas kernels: 66.7 us -> 62.9 us
  starting transfers between devices: 30.2 us -> 33.7 us
    ppermute x24, waiting for transfers between devices: 116 us -> 96.4 us  [hop(): lax.ppermute(s[0], 'col', s[1])]
    pallas_call x3 -> x2, Pallas kernels: 24.1 us -> 19.8 us  [finish(): pl.pallas_call(functools.partial(finish_kernel, most, per, first, depth,...]
    ppermute x15 -> x20, starting transfers between devices: 5.35 us -> 9.07 us  [swap(): lax.ppermute(array, axis, [(i, i ^ mask) for i in range(lax.axis_size(axi...]
    ppermute x15 -> x20, waiting for transfers between devices: 9.65 us -> 13.3 us  [swap(): lax.ppermute(array, axis, [(i, i ^ mask) for i in range(lax.axis_size(axi...]
    slice x3 -> x2, local copies, waits for them, and re-layouts: 6.3 us -> 5.17 us  [per_device(): wq[:, sum(sizes[:i]) * HD:sum(sizes[:i + 1]) * HD]]
    unnamed x22 -> x32, local copies, waits for them, and re-layouts: 6.02 us -> 6.56 us
  transfers between devices with their start and end apart: 41 -> 45, of which waited for: 26 -> 25; matrix products, arithmetic and copies ran while one was open for 18% -> 18% of each run, Pallas kernels for 20% -> 19%
where the time goes in v8:
time: 281 us; the launch traced here: 279 us
  waiting for transfers between devices  110 us (39%)
  Pallas kernels  62.9 us (22%)
  local copies, waits for them, and re-layouts  39.8 us (14%)
  starting transfers between devices  33.7 us (12%)
  other arithmetic  19.1 us (7%)
  between operations  14 us (5%)
    ppermute x24, waiting for transfers between devices, hop(): lax.ppermute(s[0], 'col', s[1])  96.4 us
    pallas_call x3, Pallas kernels, project(): pl.pallas_call(functools.partial(project_kernel, len(near), len(far), chu...  28.9 us
    ppermute x24, starting transfers between devices, hop(): lax.ppermute(s[0], 'col', s[1])  24.6 us
    dynamic_update_slice x18, local copies, waits for them, and re-layouts, put(): panel = lax.dynamic_update_slice(panel, piece[None], (slot, first, 0))  20 us
    pallas_call x2, Pallas kernels, finish(): pl.pallas_call(functools.partial(finish_kernel, most, per, first, depth,...  19.8 us
    pallas_call x2, Pallas kernels, attend(): pl.pallas_call(functools.partial(attend_kernel, parts, chunks, pair), gri...  14.1 us
    ppermute x20, waiting for transfers between devices, swap(): lax.ppermute(array, axis, [(i, i ^ mask) for i in range(lax.axis_size(axi...  13.3 us
    dynamic_update_slice x9, other arithmetic, put(): panel = lax.dynamic_update_slice(panel, piece[None], (slot, first, 0))  10.5 us
  transfers between devices with their start and end apart: 45, of which 25 were waited for; matrix products, arithmetic and copies ran while one was open for 18% of the time, Pallas kernels for 19%

profile of v8, /device:TPU:2, one launch (start us, length us, event | category | flops | bytes accessed | tf_op | source)
XLA Modules:
  0.0 279.2 jit_solution(10131278539408127522)
XLA Ops:
  8.6 2.3 copy_bitcast_fusion.refs_0_
  15.7 2.1 pad_maximum_fusion
  17.8 2.1 fusion.38
  19.9 3.1 %fusion.39 = (bf16[2048,256]{1,0:T(8,128)(2,1)}, bf16[2048,256]{1,0:T(8,128)(2,1)S(1)}, bf16[2048,256]{1,0:T(8,128)(2,1)S(1)}) fusion(bf16[2048,1024]{1,0:T(8,128)(2,1)} %refs_0_.1), kind=kLoop, calls=%fused_computation.90 | loop fusion | bytes 6291456 | tf_op jit(solution)/shard_map/slice | solution.py:354
  23.0 8.7 %collective-permute-done = bf16[512,1024]{1,0:T(8,128)(2,1)S(1)} collective-permute-done((bf16[512,1024]{1,0:T(8,128)(2,1)}, bf16[512,1024]{1,0:T(8,128)(2,1)S(1)}, u32[]{:S(2)}, u32[]{:S(2)}) %collective-permute-start) | collective-permute-done | bytes 1048608 | tf_op jit(solution)/shard_map/ppermute | solution.py:95
  32.9 2.6 collective-permute-done.2.refs_2_
  40.9 18.0 %collective-permute-done.3 = bf16[512,1024]{1,0:T(8,128)(2,1)S(1)} collective-permute-done((bf16[512,1024]{1,0:T(8,128)(2,1)S(1)}, bf16[512,1024]{1,0:T(8,128)(2,1)S(1)}, u32[]{:S(2)}, u32[]{:S(2)}) %collective-permute-start.3) | collective-permute-done | bytes 1048608 | tf_op jit(solution)/shard_map/ppermute | solution.py:95
  66.2 16.5 %collective-permute-done.6 = bf16[512,1024]{1,0:T(8,128)(2,1)S(1)} collective-permute-done((bf16[512,1024]{1,0:T(8,128)(2,1)S(1)}, bf16[512,1024]{1,0:T(8,128)(2,1)S(1)}, u32[]{:S(2)}, u32[]{:S(2)}) %collective-permute-start.6) | collective-permute-done | bytes 1048608 | tf_op jit(solution)/shard_map/ppermute | solution.py:95
  90.6 3.2 %collective-permute-done.9 = bf16[256,1024]{1,0:T(8,128)(2,1)S(1)} collective-permute-done((bf16[256,1024]{1,0:T(8,128)(2,1)S(1)}, bf16[256,1024]{1,0:T(8,128)(2,1)S(1)}, u32[]{:S(2)}, u32[]{:S(2)}) %collective-permute-start.9) | collective-permute-done | bytes 524320 | tf_op jit(solution)/shard_map/ppermute | solution.py:95
  101.4 7.1 %shard_map.65.refs_1_ = bf16[512,256]{1,0:T(8,128)(2,1)} custom-call(bf16[8,512,1024]{2,1,0:T(8,128)(2,1)} %fusion.33.panel_ref, bf16[2048,256]{1,0:T(8,128)(2,1)} %copy_bitcast_fusion.refs_0_, bf16[2048,256]{1,0:T(8,128)(2,1)} %copy-done.8, bf16[2048,256]{1,0:T(8,128)(2,1)} %collective-permute-done.2.refs_2_, bf16[2048,256]{1,0:T(8,128)(2,1)} %copy-done.9, ...), custom_call_target="tpu_custom_call" | custom-call | flops 1 | bytes 1 | tf_op jit(solution)/shard_map/pallas_call | solution.py:171
  109.9 4.3 %slice.109 = bf16[2,768,1024]{2,1,0:T(8,128)(2,1)} slice(bf16[2,1024,1024]{2,1,0:T(8,128)(2,1)} %bitcast.89), slice={[0:2], [0:768], [0:1024]} | slice | bytes 6291456 | tf_op jit(solution)/shard_map/slice | solution.py:433
  114.2 10.7 %shard_map.66.refs_0_ = bf16[512,512]{1,0:T(8,128)(2,1)} custom-call(bf16[8,512,1024]{2,1,0:T(8,128)(2,1)} %fusion.33.panel_ref, bf16[2048,1024]{1,0:T(8,128)(2,1)} %refs_0_.1, bf16[2048,1024]{1,0:T(8,128)(2,1)} %collective-permute-done.15.refs_1_, bf16[2048,256]{1,0:T(8,128)(2,1)} %collective-permute-done.5.refs_2_, bf16[2048,256]{1,0:T(8,128)(2,1)} %copy-done.5, ...), custom_call_target="tpu_custom_call" | custom-call | flops 1 | bytes 1 | tf_op jit(solution)/shard_map/pallas_call | solution.py:171
  124.9 3.5 %collective-permute-done.14.refs_3_ = bf16[512,256]{1,0:T(8,128)(2,1)S(1)} collective-permute-done((bf16[512,256]{1,0:T(8,128)(2,1)}, bf16[512,256]{1,0:T(8,128)(2,1)S(1)}, u32[]{:S(2)}, u32[]{:S(2)}) %collective-permute-start.14) | collective-permute-done | bytes 262176 | tf_op jit(solution)/shard_map/ppermute | solution.py:23
  131.1 7.1 %shard_map.67 = bf16[512,512]{1,0:T(8,128)(2,1)S(1)} custom-call(s32[1]{0:T(128)} %bitcast.r_ref, bf16[512,512]{1,0:T(8,128)(2,1)S(1)} %copy-done.1, bf16[512,256]{1,0:T(8,128)(2,1)S(1)} %copy-done, bf16[512,256]{1,0:T(8,128)(2,1)S(1)} %collective-permute-done.18.refs_2_, bf16[512,256]{1,0:T(8,128)(2,1)S(1)} %collective-permute-done.14.refs_3_, ...), custom_call_target="tpu_custom_call" | custom-call | flops 1 | bytes 1 | tf_op jit(solution)/shard_map/pallas_call | solution.py:254
  143.0 2.0 collective-permute-done.23.refs_4_
  145.0 6.7 %collective-permute-done.21 = bf16[512,512]{1,0:T(8,128)(2,1)} collective-permute-done((bf16[512,512]{1,0:T(8,128)(2,1)S(1)}, bf16[512,512]{1,0:T(8,128)(2,1)}, u32[]{:S(2)}, u32[]{:S(2)}) %collective-permute-start.21) | collective-permute-done | bytes 524320 | tf_op jit(solution)/shard_map/ppermute | solution.py:95
  151.6 1.9 collective-permute-done.22
  156.8 1.9 bitcast_dynamic-update-slice_fusion.12
  158.7 1.9 bitcast_dynamic-update-slice_fusion.11
  162.6 11.0 %shard_map.70.refs_0_ = bf16[512,512]{1,0:T(8,128)(2,1)} custom-call(bf16[8,512,1024]{2,1,0:T(8,128)(2,1)} %fusion.33.panel_ref, bf16[2048,1024]{1,0:T(8,128)(2,1)} %refs_0_.1, bf16[2048,1024]{1,0:T(8,128)(2,1)} %collective-permute-done.15.refs_1_, bf16[2048,128]{1,0:T(8,128)(2,1)} %copy-done.11, bf16[2048,256]{1,0:T(8,128)(2,1)} %collective-permute-done.19.refs_3_, ...), custom_call_target="tpu_custom_call" | custom-call | flops 1 | bytes 1 | tf_op jit(solution)/shard_map/pallas_call | solution.py:171
  176.8 7.1 %shard_map.71 = bf16[512,512]{1,0:T(8,128)(2,1)S(1)} custom-call(s32[1]{0:T(128)} %bitcast.r_ref, bf16[512,512]{1,0:T(8,128)(2,1)S(1)} %copy-done.2, bf16[512,256]{1,0:T(8,128)(2,1)S(1)} %copy-done, bf16[512,256]{1,0:T(8,128)(2,1)S(1)} %collective-permute-done.18.refs_2_, bf16[512,256]{1,0:T(8,128)(2,1)S(1)} %collective-permute-done.14.refs_3_, ...), custom_call_target="tpu_custom_call" | custom-call | flops 1 | bytes 1 | tf_op jit(solution)/shard_map/pallas_call | solution.py:254
  183.9 1.9 bitcast_dynamic-update-slice_fusion.10
  185.7 1.9 bitcast_dynamic-update-slice_fusion.9
  191.4 11.2 %collective-permute-done.31 = bf16[512,512]{1,0:T(8,128)(2,1)S(1)} collective-permute-done((bf16[512,512]{1,0:T(8,128)(2,1)S(1)}, bf16[512,512]{1,0:T(8,128)(2,1)S(1)}, u32[]{:S(2)}, u32[]{:S(2)}) %collective-permute-start.31) | collective-permute-done | bytes 524320 | tf_op jit(solution)/shard_map/ppermute | solution.py:95
  209.0 8.0 %collective-permute-done.33 = bf16[512,512]{1,0:T(8,128)(2,1)S(1)} collective-permute-done((bf16[512,512]{1,0:T(8,128)(2,1)S(1)}, bf16[512,512]{1,0:T(8,128)(2,1)S(1)}, u32[]{:S(2)}, u32[]{:S(2)}) %collective-permute-start.33) | collective-permute-done | bytes 524320 | tf_op jit(solution)/shard_map/ppermute | solution.py:95
  217.0 1.9 collective-permute-done.34
  225.6 11.3 %collective-permute-done.35 = bf16[512,512]{1,0:T(8,128)(2,1)S(1)} collective-permute-done((bf16[512,512]{1,0:T(8,128)(2,1)S(1)}, bf16[512,512]{1,0:T(8,128)(2,1)S(1)}, u32[]{:S(2)}, u32[]{:S(2)}) %collective-permute-start.35) | collective-permute-done | bytes 524320 | tf_op jit(solution)/shard_map/ppermute | solution.py:95
  236.9 1.9 collective-permute-done.36
  238.8 3.7 %collective-permute-done.37.refs_2_ = bf16[512,1024]{1,0:T(8,128)(2,1)S(1)} collective-permute-done((bf16[512,1024]{1,0:T(8,128)(2,1)S(1)}, bf16[512,1024]{1,0:T(8,128)(2,1)S(1)}, u32[]{:S(2)}, u32[]{:S(2)}) %collective-permute-start.37) | collective-permute-done | bytes 1048608 | tf_op jit(solution)/shard_map/ppermute | solution.py:23
  245.5 2.0 collective-permute-start.38
  250.0 8.7 %shard_map.72.refs_4_ = f32[512,1024]{1,0:T(8,128)} custom-call(s32[1]{0:T(128)} %bitcast.r_ref, bf16[8,512,512]{2,1,0:T(8,128)(2,1)} %bitcast_dynamic-update-slice_fusion.16.panel_ref, bf16[4,1536,1024]{2,1,0:T(8,128)(2,1)} %bitcast.86), custom_call_target="tpu_custom_call" | custom-call | flops 1 | bytes 1 | tf_op jit(solution)/shard_map/pallas_call | solution.py:307
  261.2 11.1 %shard_map.73 = bf16[512,1024]{1,0:T(8,128)(2,1)} custom-call(s32[1]{0:T(128)} %bitcast.r_ref, bf16[8,512,512]{2,1,0:T(8,128)(2,1)} %bitcast_dynamic-update-slice_fusion.14.panel_ref, bf16[4,1536,1024]{2,1,0:T(8,128)(2,1)} %bitcast.87, bf16[512,1024]{1,0:T(8,128)(2,1)} %bitcast.93, bf16[512,1024]{1,0:T(8,128)(2,1)} %collective-permute-done.40.refs_1_, ...), custom_call_target="tpu_custom_call" | custom-call | flops 1 | bytes 1 | tf_op jit(solution)/shard_map/pallas_call | solution.py:307
  (162 shorter events, 78.0 us)
Async XLA Ops:
  6.5 243.5 %all-gather.3.cloned.1.call-start = ((), (), s32[]{:S(2)}) async-start(), calls=%async_computation | async-start | bytes 15728640 | tf_op jit(solution)/shard_map/all_gather | solution.py:435
  6.5 25.1 %collective-permute-start = (bf16[512,1024]{1,0:T(8,128)(2,1)}, bf16[512,1024]{1,0:T(8,128)(2,1)S(1)}, u32[]{:S(2)}, u32[]{:S(2)}) collective-permute-start(bf16[512,1024]{1,0:T(8,128)(2,1)} %param.6), channel_id=1, source_target_pairs={{0,2},{2,4},{4,6},{6,7},{7,5},{5,3},{3,1},{1,0},{8,10},{10,12},{12... | collective-permute-start | bytes 3145736 | tf_op jit(solution)/shard_map/ppermute | solution.py:95
  8.1 24.8 %collective-permute-start.1 = (bf16[512,1024]{1,0:T(8,128)(2,1)}, bf16[512,1024]{1,0:T(8,128)(2,1)S(1)}, u32[]{:S(2)}, u32[]{:S(2)}) collective-permute-start(bf16[512,1024]{1,0:T(8,128)(2,1)} %param.6), channel_id=1, source_target_pairs={{2,0},{4,2},{6,4},{7,6},{5,7},{3,5},{1,3},{0,1},{10,8},{12,10},{14... | collective-permute-start | bytes 3145736 | tf_op jit(solution)/shard_map/ppermute | solution.py:95
  10.9 24.7 %collective-permute-start.2 = (bf16[2048,256]{1,0:T(8,128)(2,1)}, bf16[2048,256]{1,0:T(8,128)(2,1)}, u32[]{:S(2)}, u32[]{:S(2)}) collective-permute-start(bf16[2048,256]{1,0:T(8,128)(2,1)} %copy_bitcast_fusion.refs_0_), channel_id=1, source_target_pairs={{0,16},{8,24},{16,0},{24,8},{1,17},{9,25},{17,1},{25,9},{2,18},{10... | collective-permute-start | bytes 3145736 | tf_op jit(solution)/shard_map/ppermute | solution.py:23
  35.5 23.4 %collective-permute-start.3 = (bf16[512,1024]{1,0:T(8,128)(2,1)S(1)}, bf16[512,1024]{1,0:T(8,128)(2,1)S(1)}, u32[]{:S(2)}, u32[]{:S(2)}) collective-permute-start(bf16[512,1024]{1,0:T(8,128)(2,1)S(1)} %collective-permute-done), channel_id=1, source_target_pairs={{0,2},{2,4},{4,6},{6,7},{7,5},{5,3},{3,1},{1,0},{8,10},{10,12},{12... | collective-permute-start | bytes 3145736 | tf_op jit(solution)/shard_map/ppermute | solution.py:95
  37.1 23.1 %collective-permute-start.4 = (bf16[512,1024]{1,0:T(8,128)(2,1)S(1)}, bf16[512,1024]{1,0:T(8,128)(2,1)S(1)}, u32[]{:S(2)}, u32[]{:S(2)}) collective-permute-start(bf16[512,1024]{1,0:T(8,128)(2,1)S(1)} %collective-permute-done.1), channel_id=1, source_target_pairs={{2,0},{4,2},{6,4},{7,6},{5,7},{3,5},{1,3},{0,1},{10,8},{12,10},{14... | collective-permute-start | bytes 3145736 | tf_op jit(solution)/shard_map/ppermute | solution.py:95
  37.5 23.0 %collective-permute-start.5 = (bf16[2048,256]{1,0:T(8,128)(2,1)S(1)}, bf16[2048,256]{1,0:T(8,128)(2,1)}, u32[]{:S(2)}, u32[]{:S(2)}) collective-permute-start(bf16[2048,256]{1,0:T(8,128)(2,1)S(1)} %get-tuple-element.100), channel_id=1, source_target_pairs={{0,16},{8,24},{16,0},{24,8},{1,17},{9,25},{17,1},{25,9},{2,18},{10... | collective-permute-start | bytes 3145736 | tf_op jit(solution)/shard_map/ppermute | solution.py:23
  60.5 22.2 %collective-permute-start.6 = (bf16[512,1024]{1,0:T(8,128)(2,1)S(1)}, bf16[512,1024]{1,0:T(8,128)(2,1)S(1)}, u32[]{:S(2)}, u32[]{:S(2)}) collective-permute-start(bf16[512,1024]{1,0:T(8,128)(2,1)S(1)} %collective-permute-done.3), channel_id=1, source_target_pairs={{0,2},{2,4},{4,6},{6,7},{7,5},{5,3},{3,1},{1,0},{8,10},{10,12},{12... | collective-permute-start | bytes 3145736 | tf_op jit(solution)/shard_map/ppermute | solution.py:95
  62.1 21.9 %collective-permute-start.7 = (bf16[512,1024]{1,0:T(8,128)(2,1)S(1)}, bf16[512,1024]{1,0:T(8,128)(2,1)S(1)}, u32[]{:S(2)}, u32[]{:S(2)}) collective-permute-start(bf16[512,1024]{1,0:T(8,128)(2,1)S(1)} %collective-permute-done.4), channel_id=1, source_target_pairs={{2,0},{4,2},{6,4},{7,6},{5,7},{3,5},{1,3},{0,1},{10,8},{12,10},{14... | collective-permute-start | bytes 3145736 | tf_op jit(solution)/shard_map/ppermute | solution.py:95
  62.5 21.6 %collective-permute-start.8 = (bf16[2048,256]{1,0:T(8,128)(2,1)S(1)}, bf16[2048,256]{1,0:T(8,128)(2,1)S(1)}, u32[]{:S(2)}, u32[]{:S(2)}) collective-permute-start(bf16[2048,256]{1,0:T(8,128)(2,1)S(1)} %get-tuple-element.108), channel_id=1, source_target_pairs={{0,16},{8,24},{16,0},{24,8},{1,17},{9,25},{17,1},{25,9},{2,18},{10... | collective-permute-start | bytes 3145736 | tf_op jit(solution)/shard_map/ppermute | solution.py:23
  96.5 17.7 %collective-permute-start.15 = (bf16[2048,1024]{1,0:T(8,128)(2,1)}, bf16[2048,1024]{1,0:T(8,128)(2,1)}, u32[]{:S(2)}, u32[]{:S(2)}) collective-permute-start(bf16[2048,1024]{1,0:T(8,128)(2,1)} %refs_0_.1), channel_id=1, source_target_pairs={{0,8},{8,0},{16,24},{24,16},{1,9},{9,1},{17,25},{25,17},{2,10},{10... | collective-permute-start | bytes 12582920 | tf_op jit(solution)/shard_map/ppermute | solution.py:23
  97.0 17.2 %collective-permute-start.17 = (bf16[2048,256]{1,0:T(8,128)(2,1)S(1)}, bf16[2048,256]{1,0:T(8,128)(2,1)}, u32[]{:S(2)}, u32[]{:S(2)}) collective-permute-start(bf16[2048,256]{1,0:T(8,128)(2,1)S(1)} %collective-permute-done.8.refs_3_), channel_id=1, source_target_pairs={{0,8},{8,0},{16,24},{24,16},{1,9},{9,1},{17,25},{25,17},{2,10},{10... | collective-permute-start | bytes 3145736 | tf_op jit(solution)/shard_map/ppermute | solution.py:23
  97.5 30.9 %collective-permute-start.19 = (bf16[2048,256]{1,0:T(8,128)(2,1)}, bf16[2048,256]{1,0:T(8,128)(2,1)}, u32[]{:S(2)}, u32[]{:S(2)}) collective-permute-start(bf16[2048,256]{1,0:T(8,128)(2,1)} %get-tuple-element.137), channel_id=1, source_target_pairs={{0,16},{8,24},{16,0},{24,8},{1,17},{9,25},{17,1},{25,9},{2,18},{10... | collective-permute-start | bytes 3145736 | tf_op jit(solution)/shard_map/ppermute | solution.py:23
  108.6 19.8 %collective-permute-start.14 = (bf16[512,256]{1,0:T(8,128)(2,1)}, bf16[512,256]{1,0:T(8,128)(2,1)S(1)}, u32[]{:S(2)}, u32[]{:S(2)}) collective-permute-start(bf16[512,256]{1,0:T(8,128)(2,1)} %shard_map.65.refs_1_), channel_id=1, source_target_pairs={{0,16},{8,24},{16,0},{24,8},{1,17},{9,25},{17,1},{25,9},{2,18},{10... | collective-permute-start | bytes 786440 | tf_op jit(solution)/shard_map/ppermute | solution.py:23
  109.9 18.5 %collective-permute-start.18 = (bf16[512,256]{1,0:T(8,128)(2,1)}, bf16[512,256]{1,0:T(8,128)(2,1)S(1)}, u32[]{:S(2)}, u32[]{:S(2)}) collective-permute-start(bf16[512,256]{1,0:T(8,128)(2,1)} %shard_map.65.refs_1_), channel_id=1, source_target_pairs={{0,8},{8,0},{16,24},{24,16},{1,9},{9,1},{17,25},{25,17},{2,10},{10... | collective-permute-start | bytes 786440 | tf_op jit(solution)/shard_map/ppermute | solution.py:23
  128.5 16.5 %collective-permute-start.23 = (bf16[2048,128]{1,0:T(8,128)(2,1)}, bf16[2048,128]{1,0:T(8,128)(2,1)}, u32[]{:S(2)}, u32[]{:S(2)}) collective-permute-start(bf16[2048,128]{1,0:T(8,128)(2,1)} %get-tuple-element.142), channel_id=1, source_target_pairs={{0,16},{8,24},{16,0},{24,8},{1,17},{9,25},{17,1},{25,9},{2,18},{10... | collective-permute-start | bytes 1572872 | tf_op jit(solution)/shard_map/ppermute | solution.py:23
  138.2 13.5 %collective-permute-start.21 = (bf16[512,512]{1,0:T(8,128)(2,1)S(1)}, bf16[512,512]{1,0:T(8,128)(2,1)}, u32[]{:S(2)}, u32[]{:S(2)}) collective-permute-start(bf16[512,512]{1,0:T(8,128)(2,1)S(1)} %shard_map.67), channel_id=1, source_target_pairs={{0,2},{2,4},{4,6},{6,7},{7,5},{5,3},{3,1},{1,0},{8,10},{10,12},{12... | collective-permute-start | bytes 1572872 | tf_op jit(solution)/shard_map/ppermute | solution.py:95
  139.8 13.7 %collective-permute-start.22 = (bf16[512,512]{1,0:T(8,128)(2,1)S(1)}, bf16[512,512]{1,0:T(8,128)(2,1)}, u32[]{:S(2)}, u32[]{:S(2)}) collective-permute-start(bf16[512,512]{1,0:T(8,128)(2,1)S(1)} %shard_map.67), channel_id=1, source_target_pairs={{2,0},{4,2},{6,4},{7,6},{5,7},{3,5},{1,3},{0,1},{10,8},{12,10},{14... | collective-permute-start | bytes 1572872 | tf_op jit(solution)/shard_map/ppermute | solution.py:95
  140.2 20.4 %collective-permute-start.27 = (bf16[2048,256]{1,0:T(8,128)(2,1)}, bf16[2048,256]{1,0:T(8,128)(2,1)S(1)}, u32[]{:S(2)}, u32[]{:S(2)}) collective-permute-start(bf16[2048,256]{1,0:T(8,128)(2,1)} %collective-permute-done.19.refs_3_), channel_id=1, source_target_pairs={{0,8},{8,0},{16,24},{24,16},{1,9},{9,1},{17,25},{25,17},{2,10},{10... | collective-permute-start | bytes 3145736 | tf_op jit(solution)/shard_map/ppermute | solution.py:23
  142.1 18.6 %collective-permute-start.26 = (bf16[2048,128]{1,0:T(8,128)(2,1)S(1)}, bf16[2048,128]{1,0:T(8,128)(2,1)S(1)}, u32[]{:S(2)}, u32[]{:S(2)}) collective-permute-start(bf16[2048,128]{1,0:T(8,128)(2,1)S(1)} %copy-done.12), channel_id=1, source_target_pairs={{0,8},{8,0},{16,24},{24,16},{1,9},{9,1},{17,25},{25,17},{2,10},{10... | collective-permute-start | bytes 1572872 | tf_op jit(solution)/shard_map/ppermute | solution.py:23
  154.8 18.8 %collective-permute-start.24 = (bf16[512,512]{1,0:T(8,128)(2,1)}, bf16[512,512]{1,0:T(8,128)(2,1)}, u32[]{:S(2)}, u32[]{:S(2)}) collective-permute-start(bf16[512,512]{1,0:T(8,128)(2,1)} %collective-permute-done.21), channel_id=1, source_target_pairs={{0,2},{2,4},{4,6},{6,7},{7,5},{5,3},{3,1},{1,0},{8,10},{10,12},{12... | collective-permute-start | bytes 1572872 | tf_op jit(solution)/shard_map/ppermute | solution.py:95
  156.5 17.2 %collective-permute-start.25 = (bf16[512,512]{1,0:T(8,128)(2,1)}, bf16[512,512]{1,0:T(8,128)(2,1)}, u32[]{:S(2)}, u32[]{:S(2)}) collective-permute-start(bf16[512,512]{1,0:T(8,128)(2,1)} %collective-permute-done.22), channel_id=1, source_target_pairs={{2,0},{4,2},{6,4},{7,6},{5,7},{3,5},{1,3},{0,1},{10,8},{12,10},{14... | collective-permute-start | bytes 1572872 | tf_op jit(solution)/shard_map/ppermute | solution.py:95
  173.7 14.0 %collective-permute-start.29 = (bf16[512,512]{1,0:T(8,128)(2,1)}, bf16[512,512]{1,0:T(8,128)(2,1)S(1)}, u32[]{:S(2)}, u32[]{:S(2)}) collective-permute-start(bf16[512,512]{1,0:T(8,128)(2,1)} %collective-permute-done.24), channel_id=1, source_target_pairs={{0,2},{2,4},{4,6},{6,7},{7,5},{5,3},{3,1},{1,0},{8,10},{10,12},{12... | collective-permute-start | bytes 1572872 | tf_op jit(solution)/shard_map/ppermute | solution.py:95
  188.5 14.0 %collective-permute-start.31 = (bf16[512,512]{1,0:T(8,128)(2,1)S(1)}, bf16[512,512]{1,0:T(8,128)(2,1)S(1)}, u32[]{:S(2)}, u32[]{:S(2)}) collective-permute-start(bf16[512,512]{1,0:T(8,128)(2,1)S(1)} %shard_map.71), channel_id=1, source_target_pairs={{0,2},{2,4},{4,6},{6,7},{7,5},{5,3},{3,1},{1,0},{8,10},{10,12},{12... | collective-permute-start | bytes 1572872 | tf_op jit(solution)/shard_map/ppermute | solution.py:95
  190.1 13.8 %collective-permute-start.32 = (bf16[512,512]{1,0:T(8,128)(2,1)S(1)}, bf16[512,512]{1,0:T(8,128)(2,1)S(1)}, u32[]{:S(2)}, u32[]{:S(2)}) collective-permute-start(bf16[512,512]{1,0:T(8,128)(2,1)S(1)} %shard_map.71), channel_id=1, source_target_pairs={{2,0},{4,2},{6,4},{7,6},{5,7},{3,5},{1,3},{0,1},{10,8},{12,10},{14... | collective-permute-start | bytes 1572872 | tf_op jit(solution)/shard_map/ppermute | solution.py:95
  218.9 23.6 %collective-permute-start.37 = (bf16[512,1024]{1,0:T(8,128)(2,1)S(1)}, bf16[512,1024]{1,0:T(8,128)(2,1)S(1)}, u32[]{:S(2)}, u32[]{:S(2)}) collective-permute-start(bf16[512,1024]{1,0:T(8,128)(2,1)S(1)} %bitcast.91), channel_id=1, source_target_pairs={{0,16},{8,24},{16,0},{24,8},{1,17},{9,25},{17,1},{25,9},{2,18},{10... | collective-permute-start | bytes 3145736 | tf_op jit(solution)/shard_map/ppermute | solution.py:23
  218.9 24.5 %collective-permute-start.42 = (bf16[256,512]{1,0:T(8,128)(2,1)S(1)}, bf16[256,512]{1,0:T(8,128)(2,1)S(1)}, u32[]{:S(2)}, u32[]{:S(2)}) collective-permute-start(bf16[256,512]{1,0:T(8,128)(2,1)S(1)} %slice.105), channel_id=1, source_target_pairs={{0,2},{2,4},{4,6},{6,7},{7,5},{5,3},{3,1},{1,0},{8,10},{10,12},{12... | collective-permute-start | bytes 786440 | tf_op jit(solution)/shard_map/ppermute | solution.py:95
  220.7 22.7 %collective-permute-start.43 = (bf16[256,512]{1,0:T(8,128)(2,1)S(1)}, bf16[256,512]{1,0:T(8,128)(2,1)S(1)}, u32[]{:S(2)}, u32[]{:S(2)}) collective-permute-start(bf16[256,512]{1,0:T(8,128)(2,1)S(1)} %slice.106), channel_id=1, source_target_pairs={{2,0},{4,2},{6,4},{7,6},{5,7},{3,5},{1,3},{0,1},{10,8},{12,10},{14... | collective-permute-start | bytes 786440 | tf_op jit(solution)/shard_map/ppermute | solution.py:95
  221.0 15.9 %collective-permute-start.35 = (bf16[512,512]{1,0:T(8,128)(2,1)S(1)}, bf16[512,512]{1,0:T(8,128)(2,1)S(1)}, u32[]{:S(2)}, u32[]{:S(2)}) collective-permute-start(bf16[512,512]{1,0:T(8,128)(2,1)S(1)} %collective-permute-done.33), channel_id=1, source_target_pairs={{0,2},{2,4},{4,6},{6,7},{7,5},{5,3},{3,1},{1,0},{8,10},{10,12},{12... | collective-permute-start | bytes 1572872 | tf_op jit(solution)/shard_map/ppermute | solution.py:95
  222.8 16.0 %collective-permute-start.36 = (bf16[512,512]{1,0:T(8,128)(2,1)S(1)}, bf16[512,512]{1,0:T(8,128)(2,1)S(1)}, u32[]{:S(2)}, u32[]{:S(2)}) collective-permute-start(bf16[512,512]{1,0:T(8,128)(2,1)S(1)} %collective-permute-done.34), channel_id=1, source_target_pairs={{2,0},{4,2},{6,4},{7,6},{5,7},{3,5},{1,3},{0,1},{10,8},{12,10},{14... | collective-permute-start | bytes 1572872 | tf_op jit(solution)/shard_map/ppermute | solution.py:95
  236.9 21.8 %collective-permute-start.40 = (bf16[512,1024]{1,0:T(8,128)(2,1)S(1)}, bf16[512,1024]{1,0:T(8,128)(2,1)}, u32[]{:S(2)}, u32[]{:S(2)}) collective-permute-start(bf16[512,1024]{1,0:T(8,128)(2,1)S(1)} %bitcast.92), channel_id=1, source_target_pairs={{0,8},{8,0},{16,24},{24,16},{1,9},{9,1},{17,25},{25,17},{2,10},{10... | collective-permute-start | bytes 3145736 | tf_op jit(solution)/shard_map/ppermute | solution.py:23
  242.5 16.2 %collective-permute-start.41 = (bf16[512,1024]{1,0:T(8,128)(2,1)S(1)}, bf16[512,1024]{1,0:T(8,128)(2,1)}, u32[]{:S(2)}, u32[]{:S(2)}) collective-permute-start(bf16[512,1024]{1,0:T(8,128)(2,1)S(1)} %collective-permute-done.37.refs_2_), channel_id=1, source_target_pairs={{0,8},{8,0},{16,24},{24,16},{1,9},{9,1},{17,25},{25,17},{2,10},{10... | collective-permute-start | bytes 3145736 | tf_op jit(solution)/shard_map/ppermute | solution.py:23
  (29 other events, 233.4 us)
Sparse Core Ops, SparseCore 0:
  128.5 83.8 all-gather.2

commit v9 on v8

--- a/solution.py
+++ b/solution.py
@@ -157,7 +157,7 @@
     for h in range(cols // HD):
         at = pl.ds(h * HD, HD)
         x = acc[:, at] * scale
-        if h < heads:
+        if heads < 0 or h < heads:
             x = x * cos_ref[...] + pltpu.roll(x, HD // 2, 1) * sin_ref[...]
         o_ref[:, at] = x.astype(o_ref.dtype)
 
@@ -275,52 +275,48 @@
     )(r.reshape(1), *queries, *pieces)
 
 
-def finish_kernel(most, per, first, depth, count, r_ref, panel_ref, gathered_ref, *refs):
-    pieces, (*old, o_ref, a_buf, w_buf, acc, a_sem, w_sem) = take(refs, count)
+def finish_kernel(slots, per, count, r_ref, first_ref, second_ref, *refs):
+    weights, (*old, o_ref, a_buf, w_buf, acc, a_sem, w_sem) = take(refs, count)
     steps = []
-    slots, _, wide = panel_ref.shape
-    stride = gathered_ref.shape[1] // per
-    for k in range(slots):
-        block = jnp.bitwise_xor(r_ref[0], k // per)
-        for at in range(0, wide, depth):
-            if at < most:
-                row = k % per * stride + first + at
-                right = gathered_ref.at[block, pl.ds(row, depth), :]
+    depth = first_ref.shape[2]
+    rows = depth + second_ref.shape[2]
+    for k in range(*slots):
+        for g, panel_ref in enumerate((first_ref, second_ref)):
+            at = pl.ds(k % per * rows + g * depth, depth)
+            if len(weights[0].shape) == 3:
+                right = weights[0].at[jnp.bitwise_xor(r_ref[0], k // per), at, :]
             else:
-                row = k % per * (wide - most) + at - most
-                right = pieces[k // per].at[pl.ds(row, depth), :]
-            steps.append((panel_ref.at[k, :, pl.ds(at, depth)], [[right]]))
+                right = weights[k // per].at[at, :]
+            steps.append((panel_ref.at[k], [[right]]))
     acc[...] = old[0][...] if old else jnp.zeros_like(acc)
     multiply(steps, a_buf, [w_buf], [acc], a_sem, w_sem)
     o_ref[...] = acc[...].astype(o_ref.dtype)
 
 
-def finish(r, panel, most, gathered, per, first, pieces, dtype, total=None):
-    n, tok, wide = panel.shape
-    cols = gathered.shape[2]
-    most = most or wide
-    depth = math.gcd(most, wide)
-    count = n * wide // depth
+def finish(r, panels, slots, weights, per, dtype, total=None):
+    _, tok, wide = panels[0].shape
+    cols = weights[0].shape[-1]
+    count = 2 * (slots[1] - slots[0])
     hbm = pl.BlockSpec(memory_space=pl.ANY)
     vmem = pl.BlockSpec(memory_space=pltpu.VMEM)
     old = [] if total is None else [total]
     return pl.pallas_call(
-        functools.partial(finish_kernel, most, per, first, depth, len(pieces)),
+        functools.partial(finish_kernel, slots, per, len(weights)),
         in_specs=[pl.BlockSpec(memory_space=pltpu.SMEM)]
-        + [hbm] * (2 + len(pieces))
+        + [hbm] * (2 + len(weights))
         + [vmem] * len(old),
         out_specs=vmem,
         out_shape=jax.ShapeDtypeStruct((tok, cols), dtype),
         scratch_shapes=[
-            pltpu.VMEM((count, tok, depth), jnp.bfloat16),
-            pltpu.VMEM((count, depth, cols), jnp.bfloat16),
+            pltpu.VMEM((count, tok, wide), jnp.bfloat16),
+            pltpu.VMEM((count, wide, cols), jnp.bfloat16),
             pltpu.VMEM((tok, cols), jnp.float32),
             pltpu.SemaphoreType.DMA((count,)),
             pltpu.SemaphoreType.DMA((1, count)),
         ],
         compiler_params=pltpu.CompilerParams(vmem_limit_bytes=60 * MIB),
         cost_estimate=SHORT,
-    )(r.reshape(1), panel, gathered, *pieces, *old)
+    )(r.reshape(1), *panels, *weights, *old)
 
 
 def per_device(hidden, norm_gain, wq, wk, wv, wo):
@@ -343,9 +339,9 @@
     first_heads = n_heads // 2
     late_heads = n_heads - first_heads
     if n_heads >= 4:
-        eighth = max(1, n_heads // 8)
-        sizes = [first_heads // 2, first_heads - first_heads // 2, eighth]
-        sizes += [n for n in (late_heads - 2 * eighth, eighth) if n > 0]
+        quarter = late_heads // 2
+        sizes = [first_heads // 2, first_heads - first_heads // 2]
+        sizes += [n for n in (quarter // 2, quarter - quarter // 2, late_heads - quarter) if n > 0]
     else:
         sizes = [first_heads, late_heads]
     early = 2 if n_heads >= 4 else 1
@@ -426,52 +422,41 @@
     kv_pieces, arrived = take(beside, blocks_near)
     kv_pieces = [*kv_pieces, *gather_near(kv_other)]
     late_far = [gather_near(piece) for piece in (*got_x[1 + early :], *arrived)]
+    late_far = [list(far) for far in late_far]
     last_other = exchange(last_chunk)
-    split = cols - rest // 2 if rest >= 2 * HD else cols
-
-    def o_rows(first, last):
-        return wo.reshape(-1, cols, wo.shape[1])[:, first:last].reshape(-1, wo.shape[1])
-
-    o_most = lax.all_gather(after(o_rows(0, split), kv_other), "row")
-    o_last = [o_rows(split, cols)] if split < cols else []
+    o_weights = lax.all_gather(after(wo, kv_other), "row")
     heads = attend(r, [queries], kv_pieces)
 
     ring = Ring(heads, 1)
     panels = [put(blank((n_col, tok, wide)), ring.found), blank((n_col, tok, rest))]
-    found, (last_other, *panels) = ring.hop([last_other, *panels])
+    tables = scale, cosine, sine
+    late, first = [], wide
+    if late_far:
+        late_far = by_block(late_far)
+        late.append(project(panel, q_near, late_far, first, -1, factor, *tables))
+        first += late[0].shape[1]
+    found, (last_other, *rest_of) = ring.hop([last_other, *panels, *late])
+    panels, late = take(rest_of, 2)
     panels[0] = put(panels[0], found)
-    late_far = by_block([*late_far, gather_near(last_other)])
-    queries = project(
-        panel, q_near, late_far, wide, late_heads, factor, scale, cosine, sine
-    )
-    found, (queries, panels[0]) = ring.hop([queries, panels[0]])
+    last_far = by_block([gather_near(last_other)])
+    late = [*late, project(panel, q_near, last_far, first, -1, factor, *tables)]
+    found, (panels[0], *late) = ring.hop([panels[0], *late])
     panels[0] = put(panels[0], found)
-    heads = attend(r, [queries], kv_pieces)
-    found, (heads, panels[0]) = ring.hop([heads, panels[0]])
+    heads = attend(r, late, kv_pieces)
+    o_near = gather_near(after(wo, late[-1]))
+    found, (heads, panels[0], *o_near) = ring.hop([heads, panels[0], *o_near])
     panels[0] = put(panels[0], found)
     second = Ring(heads, 1)
     panels[1] = put(panels[1], second.found)
     for i in range(hops):
         found, (panels[0],) = ring.hop([panels[0]])
         panels[0] = put(panels[0], found)
-        beside = [panels[1]]
-        if i == hops - 3:
-            beside += o_last
-        if i == hops - 2:
-            beside += [exchange(w) for w in o_last]
-        if i == hops - 1:
-            for w in o_last:
-                beside += [*gather_near(w), *gather_near(o_other)]
-            beside.append(finish(r, panels[0], 0, o_most, per, 0, [], jnp.float32))
-        found, (panels[1], *beside) = second.hop(beside)
+        found, (panels[1],) = second.hop([panels[1]])
         panels[1] = put(panels[1], found)
-        if i == hops - 3:
-            o_last = beside
-        if i == hops - 2 and o_last:
-            (o_other,) = beside
-    *pieces, total = beside
-
-    return finish(r, panels[1], split - wide, o_most, per, wide, pieces, jnp.bfloat16, total)
+
+    half = n_col // 2
+    total = finish(r, panels, (0, half), o_near, per, jnp.float32)
+    return finish(r, panels, (half, n_col), [after(o_weights, total)], per, jnp.bfloat16, total)
 
 
 def solution(mesh):

time: 281 us -> 278 us (0.989)
  local copies, waits for them, and re-layouts: 39.8 us -> 29.5 us
  waiting for transfers between devices: 110 us -> 116 us
  Pallas kernels: 62.9 us -> 68.1 us
    ppermute x20 -> x18, waiting for transfers between devices: 13.3 us -> 27.6 us  [swap(): lax.ppermute(array, axis, [(i, i ^ mask) for i in range(lax.axis_size(axi...]
    ppermute x24, waiting for transfers between devices: 96.4 us -> 88 us  [hop(): lax.ppermute(s[0], 'col', s[1])]
    pallas_call x3 -> x4, Pallas kernels: 28.9 us -> 35.3 us  [project(): pl.pallas_call(functools.partial(project_kernel, len(near), len(far), chu...]
    slice x2 -> x0, local copies, waits for them, and re-layouts: 5.58 us -> none  [o_rows(): wo.reshape(-1, cols, wo.shape[1])[:, first:last].reshape(-1, wo.shape[1])]
    ppermute x20 -> x18, starting transfers between devices: 9.07 us -> 6.84 us  [swap(): lax.ppermute(array, axis, [(i, i ^ mask) for i in range(lax.axis_size(axi...]
    unnamed x32 -> x30, local copies, waits for them, and re-layouts: 6.56 us -> 5.46 us
  transfers between devices with their start and end apart: 45 -> 43, of which waited for: 25 -> 26; matrix products, arithmetic and copies ran while one was open for 18% -> 16% of each run, Pallas kernels for 19% -> 21%
where the time goes in v9:
time: 278 us
  waiting for transfers between devices  116 us (42%)
  Pallas kernels  68.1 us (24%)
  starting transfers between devices  31.7 us (11%)
  local copies, waits for them, and re-layouts  29.5 us (11%)
  other arithmetic  19.2 us (7%)
  between operations  13.8 us (5%)
    ppermute x24, waiting for transfers between devices, hop(): lax.ppermute(s[0], 'col', s[1])  88 us
    pallas_call x4, Pallas kernels, project(): pl.pallas_call(functools.partial(project_kernel, len(near), len(far), chu...  35.3 us
    ppermute x18, waiting for transfers between devices, swap(): lax.ppermute(array, axis, [(i, i ^ mask) for i in range(lax.axis_size(axi...  27.6 us
    ppermute x24, starting transfers between devices, hop(): lax.ppermute(s[0], 'col', s[1])  24.8 us
    pallas_call x2, Pallas kernels, finish(): pl.pallas_call(functools.partial(finish_kernel, slots, per, len(weights))...  18.7 us
    dynamic_update_slice x18, local copies, waits for them, and re-layouts, put(): panel = lax.dynamic_update_slice(panel, piece[None], (slot, first, 0))  17.8 us
    pallas_call x2, Pallas kernels, attend(): pl.pallas_call(functools.partial(attend_kernel, parts, chunks, pair), gri...  14.1 us
    dynamic_update_slice x9, other arithmetic, put(): panel = lax.dynamic_update_slice(panel, piece[None], (slot, first, 0))  10.6 us
  transfers between devices with their start and end apart: 43, of which 26 were waited for; matrix products, arithmetic and copies ran while one was open for 16% of the time, Pallas kernels for 21%

profile of v9, /device:TPU:2, one launch (start us, length us, event | category | flops | bytes accessed | tf_op | source)
XLA Modules:
  0.0 277.9 jit_solution(12862765359555796012)
XLA Ops:
  8.6 2.3 copy_bitcast_fusion.refs_0_
  12.6 1.8 fusion.36
  15.7 2.1 pad_maximum_fusion
  17.8 2.1 fusion.39
  19.9 3.1 %fusion.38 = (bf16[2048,256]{1,0:T(8,128)(2,1)}, bf16[2048,256]{1,0:T(8,128)(2,1)S(1)}, bf16[2048,256]{1,0:T(8,128)(2,1)S(1)}) fusion(bf16[2048,1024]{1,0:T(8,128)(2,1)} %refs_0_.2), kind=kLoop, calls=%fused_computation.89 | loop fusion | bytes 6291456 | tf_op jit(solution)/shard_map/slice | solution.py:350
  23.0 12.5 %collective-permute-done.2.refs_2_ = bf16[2048,256]{1,0:T(8,128)(2,1)} collective-permute-done((bf16[2048,256]{1,0:T(8,128)(2,1)}, bf16[2048,256]{1,0:T(8,128)(2,1)}, u32[]{:S(2)}, u32[]{:S(2)}) %collective-permute-start.2) | collective-permute-done | bytes 1048608 | tf_op jit(solution)/shard_map/ppermute | solution.py:23
  35.5 1.6 collective-permute-start.3
  41.0 18.0 %collective-permute-done.3 = bf16[512,1024]{1,0:T(8,128)(2,1)S(1)} collective-permute-done((bf16[512,1024]{1,0:T(8,128)(2,1)S(1)}, bf16[512,1024]{1,0:T(8,128)(2,1)S(1)}, u32[]{:S(2)}, u32[]{:S(2)}) %collective-permute-start.3) | collective-permute-done | bytes 1048608 | tf_op jit(solution)/shard_map/ppermute | solution.py:95
  67.2 16.2 %collective-permute-done.6 = bf16[512,1024]{1,0:T(8,128)(2,1)S(1)} collective-permute-done((bf16[512,1024]{1,0:T(8,128)(2,1)S(1)}, bf16[512,1024]{1,0:T(8,128)(2,1)S(1)}, u32[]{:S(2)}, u32[]{:S(2)}) %collective-permute-start.6) | collective-permute-done | bytes 1048608 | tf_op jit(solution)/shard_map/ppermute | solution.py:95
  91.7 7.7 %collective-permute-done.10 = bf16[256,1024]{1,0:T(8,128)(2,1)S(1)} collective-permute-done((bf16[256,1024]{1,0:T(8,128)(2,1)S(1)}, bf16[256,1024]{1,0:T(8,128)(2,1)S(1)}, u32[]{:S(2)}, u32[]{:S(2)}) %collective-permute-start.10) | collective-permute-done | bytes 524320 | tf_op jit(solution)/shard_map/ppermute | solution.py:95
  107.2 7.2 %shard_map.65.refs_1_.refs_2_ = bf16[512,256]{1,0:T(8,128)(2,1)} custom-call(bf16[8,512,1024]{2,1,0:T(8,128)(2,1)} %fusion.33.panel_ref, bf16[2048,256]{1,0:T(8,128)(2,1)} %copy_bitcast_fusion.refs_0_, bf16[2048,256]{1,0:T(8,128)(2,1)} %copy-done.12, bf16[2048,256]{1,0:T(8,128)(2,1)} %collective-permute-done.2.refs_2_, bf16[2048,256]{1,0:T(8,128)(2,1)} %copy-done.11, ...), custom_call_target="tpu_custom_call" | custom-call | flops 1 | bytes 1 | tf_op jit(solution)/shard_map/pallas_call | solution.py:171
  115.8 10.6 %shard_map.66.refs_0_ = bf16[512,512]{1,0:T(8,128)(2,1)} custom-call(bf16[8,512,1024]{2,1,0:T(8,128)(2,1)} %fusion.33.panel_ref, bf16[2048,1024]{1,0:T(8,128)(2,1)} %refs_0_.2, bf16[2048,1024]{1,0:T(8,128)(2,1)} %collective-permute-done.15.refs_1_, bf16[2048,256]{1,0:T(8,128)(2,1)} %copy-done.6, bf16[2048,256]{1,0:T(8,128)(2,1)} %copy-done.8, ...), custom_call_target="tpu_custom_call" | custom-call | flops 1 | bytes 1 | tf_op jit(solution)/shard_map/pallas_call | solution.py:171
  128.8 7.1 %shard_map.67 = bf16[512,512]{1,0:T(8,128)(2,1)S(1)} custom-call(s32[1]{0:T(128)} %bitcast.r_ref, bf16[512,512]{1,0:T(8,128)(2,1)S(1)} %copy-done.1, bf16[512,256]{1,0:T(8,128)(2,1)S(1)} %copy-done, bf16[512,256]{1,0:T(8,128)(2,1)S(1)} %collective-permute-done.18.refs_2_.refs_3_, bf16[512,256]{1,0:T(8,128)(2,1)S(1)} %collective-permute-done.14.refs_3_.refs_4_, ...), custom_call_target="tpu_custom_call" | custom-call | flops 1 | bytes 1 | tf_op jit(solution)/shard_map/pallas_call | solution.py:254
  138.8 10.1 %shard_map.70.refs_0_ = bf16[512,256]{1,0:T(8,128)(2,1)} custom-call(bf16[8,512,1024]{2,1,0:T(8,128)(2,1)} %fusion.33.panel_ref, bf16[2048,1024]{1,0:T(8,128)(2,1)} %refs_0_.2, bf16[2048,1024]{1,0:T(8,128)(2,1)} %collective-permute-done.15.refs_1_, bf16[2048,128]{1,0:T(8,128)(2,1)} %collective-permute-done.11.refs_2_, ...), custom_call_target="tpu_custom_call" | custom-call | flops 1 | bytes 1 | tf_op jit(solution)/shard_map/pallas_call | solution.py:171
  149.2 1.7 collective-permute-done.22
  150.9 13.5 %collective-permute-done.23.refs_2_ = bf16[2048,256]{1,0:T(8,128)(2,1)S(1)} collective-permute-done((bf16[2048,256]{1,0:T(8,128)(2,1)}, bf16[2048,256]{1,0:T(8,128)(2,1)S(1)}, u32[]{:S(2)}, u32[]{:S(2)}) %collective-permute-start.23) | collective-permute-done | bytes 1048608 | tf_op jit(solution)/shard_map/ppermute | solution.py:23
  166.4 1.9 bitcast_dynamic-update-slice_fusion.12
  168.3 1.9 bitcast_dynamic-update-slice_fusion.11
  171.1 7.4 %shard_map.71.refs_1_ = bf16[512,256]{1,0:T(8,128)(2,1)} custom-call(bf16[8,512,1024]{2,1,0:T(8,128)(2,1)} %fusion.33.panel_ref, bf16[2048,1024]{1,0:T(8,128)(2,1)} %refs_0_.2, bf16[2048,1024]{1,0:T(8,128)(2,1)} %collective-permute-done.15.refs_1_, bf16[2048,256]{1,0:T(8,128)(2,1)} %copy-done.9, bf16[2048,256]{1,0:T(8,128)(2,1)} %copy-done.10, ...), custom_call_target="tpu_custom_call" | custom-call | flops 1 | bytes 1 | tf_op jit(solution)/shard_map/pallas_call | solution.py:171
  180.0 1.6 collective-permute-start.29
  183.0 7.0 %shard_map.72 = bf16[512,512]{1,0:T(8,128)(2,1)S(1)} custom-call(s32[1]{0:T(128)} %bitcast.r_ref, bf16[512,256]{1,0:T(8,128)(2,1)S(1)} %copy-done.2, bf16[512,256]{1,0:T(8,128)(2,1)S(1)} %copy-done.3, bf16[512,256]{1,0:T(8,128)(2,1)S(1)} %copy-done, bf16[512,256]{1,0:T(8,128)(2,1)S(1)} %collective-permute-done.18.refs_2_.refs_3_, ...), custom_call_target="tpu_custom_call" | custom-call | flops 1 | bytes 1 | tf_op jit(solution)/shard_map/pallas_call | solution.py:254
  190.8 1.9 bitcast_dynamic-update-slice_fusion.9
  192.7 1.6 collective-permute-done.29
  198.8 1.6 collective-permute-start.32
  202.6 12.2 %collective-permute-done.32 = bf16[256,512]{1,0:T(8,128)(2,1)S(1)} collective-permute-done((bf16[256,512]{1,0:T(8,128)(2,1)S(1)}, bf16[256,512]{1,0:T(8,128)(2,1)S(1)}, u32[]{:S(2)}, u32[]{:S(2)}) %collective-permute-start.32) | collective-permute-done | bytes 262176 | tf_op jit(solution)/shard_map/ppermute | solution.py:95
  220.6 7.8 %collective-permute-done.36 = bf16[512,512]{1,0:T(8,128)(2,1)S(1)} collective-permute-done((bf16[512,512]{1,0:T(8,128)(2,1)S(1)}, bf16[512,512]{1,0:T(8,128)(2,1)S(1)}, u32[]{:S(2)}, u32[]{:S(2)}) %collective-permute-start.36) | collective-permute-done | bytes 524320 | tf_op jit(solution)/shard_map/ppermute | solution.py:95
  229.9 1.7 collective-permute-start.38
  234.4 7.0 %collective-permute-done.38 = bf16[512,512]{1,0:T(8,128)(2,1)S(1)} collective-permute-done((bf16[512,512]{1,0:T(8,128)(2,1)S(1)}, bf16[512,512]{1,0:T(8,128)(2,1)S(1)}, u32[]{:S(2)}, u32[]{:S(2)}) %collective-permute-start.38) | collective-permute-done | bytes 524320 | tf_op jit(solution)/shard_map/ppermute | solution.py:95
  241.4 2.0 collective-permute-done.39
  247.3 2.6 collective-permute-done.40
  252.3 8.8 %shard_map.73.refs_1_ = f32[512,1024]{1,0:T(8,128)} custom-call(s32[1]{0:T(128)} %bitcast.r_ref, bf16[8,512,512]{2,1,0:T(8,128)(2,1)} %bitcast_dynamic-update-slice_fusion.16.first_ref, bf16[8,512,512]{2,1,0:T(8,128)(2,1)} %bitcast_dynamic-update-slice_fusion.14.second_ref, bf16[2048,1024]{1,0:T(8,128)(2,1)} %refs_0_.3, bf16[2048,1024]{1,0:T(8,128)(2,1)} %copy-done.5), custom_call_target="tpu_custom_call" | custom-call | flops 1 | bytes 1 | tf_op jit(solution)/shard_map/pallas_call | solution.py:303
  261.1 9.9 %shard_map.74 = bf16[512,1024]{1,0:T(8,128)(2,1)} custom-call(s32[1]{0:T(128)} %bitcast.r_ref, bf16[8,512,512]{2,1,0:T(8,128)(2,1)} %bitcast_dynamic-update-slice_fusion.16.first_ref, bf16[8,512,512]{2,1,0:T(8,128)(2,1)} %bitcast_dynamic-update-slice_fusion.14.second_ref, bf16[4,2048,1024]{2,1,0:T(8,128)(2,1)} %bitcast.83, f32[512,1024]{1,0:T(8,128)} %shard_map.73.refs_1_), custom_call_target="tpu_custom_call" | custom-call | flops 1 | bytes 1 | tf_op jit(solution)/shard_map/pallas_call | solution.py:303
  (155 shorter events, 69.5 us)
Async XLA Ops:
  6.5 254.6 %all-gather.3.cloned.1.call-start = ((), (), s32[]{:S(2)}) async-start(), calls=%async_computation | async-start | bytes 20971520 | tf_op jit(solution)/shard_map/all_gather | solution.py:427
  6.5 29.0 %collective-permute-start = (bf16[512,1024]{1,0:T(8,128)(2,1)}, bf16[512,1024]{1,0:T(8,128)(2,1)S(1)}, u32[]{:S(2)}, u32[]{:S(2)}) collective-permute-start(bf16[512,1024]{1,0:T(8,128)(2,1)} %param.6), channel_id=1, source_target_pairs={{0,2},{2,4},{4,6},{6,7},{7,5},{5,3},{3,1},{1,0},{8,10},{10,12},{12... | collective-permute-start | bytes 3145736 | tf_op jit(solution)/shard_map/ppermute | solution.py:95
  8.1 27.4 %collective-permute-start.1 = (bf16[512,1024]{1,0:T(8,128)(2,1)}, bf16[512,1024]{1,0:T(8,128)(2,1)S(1)}, u32[]{:S(2)}, u32[]{:S(2)}) collective-permute-start(bf16[512,1024]{1,0:T(8,128)(2,1)} %param.6), channel_id=1, source_target_pairs={{2,0},{4,2},{6,4},{7,6},{5,7},{3,5},{1,3},{0,1},{10,8},{12,10},{14... | collective-permute-start | bytes 3145736 | tf_op jit(solution)/shard_map/ppermute | solution.py:95
  10.9 24.7 %collective-permute-start.2 = (bf16[2048,256]{1,0:T(8,128)(2,1)}, bf16[2048,256]{1,0:T(8,128)(2,1)}, u32[]{:S(2)}, u32[]{:S(2)}) collective-permute-start(bf16[2048,256]{1,0:T(8,128)(2,1)} %copy_bitcast_fusion.refs_0_), channel_id=1, source_target_pairs={{0,16},{8,24},{16,0},{24,8},{1,17},{9,25},{17,1},{25,9},{2,18},{10... | collective-permute-start | bytes 3145736 | tf_op jit(solution)/shard_map/ppermute | solution.py:23
  35.5 23.4 %collective-permute-start.3 = (bf16[512,1024]{1,0:T(8,128)(2,1)S(1)}, bf16[512,1024]{1,0:T(8,128)(2,1)S(1)}, u32[]{:S(2)}, u32[]{:S(2)}) collective-permute-start(bf16[512,1024]{1,0:T(8,128)(2,1)S(1)} %collective-permute-done), channel_id=1, source_target_pairs={{0,2},{2,4},{4,6},{6,7},{7,5},{5,3},{3,1},{1,0},{8,10},{10,12},{12... | collective-permute-start | bytes 3145736 | tf_op jit(solution)/shard_map/ppermute | solution.py:95
  37.1 23.1 %collective-permute-start.4 = (bf16[512,1024]{1,0:T(8,128)(2,1)S(1)}, bf16[512,1024]{1,0:T(8,128)(2,1)S(1)}, u32[]{:S(2)}, u32[]{:S(2)}) collective-permute-start(bf16[512,1024]{1,0:T(8,128)(2,1)S(1)} %collective-permute-done.1), channel_id=1, source_target_pairs={{2,0},{4,2},{6,4},{7,6},{5,7},{3,5},{1,3},{0,1},{10,8},{12,10},{14... | collective-permute-start | bytes 3145736 | tf_op jit(solution)/shard_map/ppermute | solution.py:95
  37.6 22.9 %collective-permute-start.5 = (bf16[2048,256]{1,0:T(8,128)(2,1)S(1)}, bf16[2048,256]{1,0:T(8,128)(2,1)S(1)}, u32[]{:S(2)}, u32[]{:S(2)}) collective-permute-start(bf16[2048,256]{1,0:T(8,128)(2,1)S(1)} %get-tuple-element.99), channel_id=1, source_target_pairs={{0,16},{8,24},{16,0},{24,8},{1,17},{9,25},{17,1},{25,9},{2,18},{10... | collective-permute-start | bytes 3145736 | tf_op jit(solution)/shard_map/ppermute | solution.py:23
  61.4 22.0 %collective-permute-start.6 = (bf16[512,1024]{1,0:T(8,128)(2,1)S(1)}, bf16[512,1024]{1,0:T(8,128)(2,1)S(1)}, u32[]{:S(2)}, u32[]{:S(2)}) collective-permute-start(bf16[512,1024]{1,0:T(8,128)(2,1)S(1)} %collective-permute-done.3), channel_id=1, source_target_pairs={{0,2},{2,4},{4,6},{6,7},{7,5},{5,3},{3,1},{1,0},{8,10},{10,12},{12... | collective-permute-start | bytes 3145736 | tf_op jit(solution)/shard_map/ppermute | solution.py:95
  63.0 21.8 %collective-permute-start.7 = (bf16[512,1024]{1,0:T(8,128)(2,1)S(1)}, bf16[512,1024]{1,0:T(8,128)(2,1)S(1)}, u32[]{:S(2)}, u32[]{:S(2)}) collective-permute-start(bf16[512,1024]{1,0:T(8,128)(2,1)S(1)} %collective-permute-done.4), channel_id=1, source_target_pairs={{2,0},{4,2},{6,4},{7,6},{5,7},{3,5},{1,3},{0,1},{10,8},{12,10},{14... | collective-permute-start | bytes 3145736 | tf_op jit(solution)/shard_map/ppermute | solution.py:95
  63.4 21.5 %collective-permute-start.8 = (bf16[2048,256]{1,0:T(8,128)(2,1)S(1)}, bf16[2048,256]{1,0:T(8,128)(2,1)S(1)}, u32[]{:S(2)}, u32[]{:S(2)}) collective-permute-start(bf16[2048,256]{1,0:T(8,128)(2,1)S(1)} %get-tuple-element.107), channel_id=1, source_target_pairs={{0,16},{8,24},{16,0},{24,8},{1,17},{9,25},{17,1},{25,9},{2,18},{10... | collective-permute-start | bytes 3145736 | tf_op jit(solution)/shard_map/ppermute | solution.py:23
  85.0 16.3 %collective-permute-start.13 = (bf16[2048,256]{1,0:T(8,128)(2,1)}, bf16[2048,256]{1,0:T(8,128)(2,1)S(1)}, u32[]{:S(2)}, u32[]{:S(2)}) collective-permute-start(bf16[2048,256]{1,0:T(8,128)(2,1)} %collective-permute-done.2.refs_2_), channel_id=1, source_target_pairs={{0,8},{8,0},{16,24},{24,16},{1,9},{9,1},{17,25},{25,17},{2,10},{10... | collective-permute-start | bytes 3145736 | tf_op jit(solution)/shard_map/ppermute | solution.py:23
  85.1 16.3 %collective-permute-start.12 = (bf16[2048,256]{1,0:T(8,128)(2,1)}, bf16[2048,256]{1,0:T(8,128)(2,1)S(1)}, u32[]{:S(2)}, u32[]{:S(2)}) collective-permute-start(bf16[2048,256]{1,0:T(8,128)(2,1)} %copy_bitcast_fusion.refs_0_), channel_id=1, source_target_pairs={{0,8},{8,0},{16,24},{24,16},{1,9},{9,1},{17,25},{25,17},{2,10},{10... | collective-permute-start | bytes 3145736 | tf_op jit(solution)/shard_map/ppermute | solution.py:23
  85.5 13.9 %collective-permute-start.10 = (bf16[256,1024]{1,0:T(8,128)(2,1)S(1)}, bf16[256,1024]{1,0:T(8,128)(2,1)S(1)}, u32[]{:S(2)}, u32[]{:S(2)}) collective-permute-start(bf16[256,1024]{1,0:T(8,128)(2,1)S(1)} %slice.89), channel_id=1, source_target_pairs={{2,0},{4,2},{6,4},{7,6},{5,7},{3,5},{1,3},{0,1},{10,8},{12,10},{14... | collective-permute-start | bytes 1572872 | tf_op jit(solution)/shard_map/ppermute | solution.py:95
  87.0 13.9 %collective-permute-start.9 = (bf16[256,1024]{1,0:T(8,128)(2,1)S(1)}, bf16[256,1024]{1,0:T(8,128)(2,1)S(1)}, u32[]{:S(2)}, u32[]{:S(2)}) collective-permute-start(bf16[256,1024]{1,0:T(8,128)(2,1)S(1)} %slice.88), channel_id=1, source_target_pairs={{0,2},{2,4},{4,6},{6,7},{7,5},{5,3},{3,1},{1,0},{8,10},{10,12},{12... | collective-permute-start | bytes 1572872 | tf_op jit(solution)/shard_map/ppermute | solution.py:95
  87.8 13.5 %collective-permute-start.11 = (bf16[2048,128]{1,0:T(8,128)(2,1)S(1)}, bf16[2048,128]{1,0:T(8,128)(2,1)}, u32[]{:S(2)}, u32[]{:S(2)}) collective-permute-start(bf16[2048,128]{1,0:T(8,128)(2,1)S(1)} %get-tuple-element.115), channel_id=1, source_target_pairs={{0,16},{8,24},{16,0},{24,8},{1,17},{9,25},{17,1},{25,9},{2,18},{10... | collective-permute-start | bytes 1572872 | tf_op jit(solution)/shard_map/ppermute | solution.py:23
  102.4 13.4 %collective-permute-start.15 = (bf16[2048,1024]{1,0:T(8,128)(2,1)}, bf16[2048,1024]{1,0:T(8,128)(2,1)}, u32[]{:S(2)}, u32[]{:S(2)}) collective-permute-start(bf16[2048,1024]{1,0:T(8,128)(2,1)} %refs_0_.2), channel_id=1, source_target_pairs={{0,8},{8,0},{16,24},{24,16},{1,9},{9,1},{17,25},{25,17},{2,10},{10... | collective-permute-start | bytes 12582920 | tf_op jit(solution)/shard_map/ppermute | solution.py:23
  102.6 13.1 %collective-permute-start.17 = (bf16[2048,256]{1,0:T(8,128)(2,1)S(1)}, bf16[2048,256]{1,0:T(8,128)(2,1)}, u32[]{:S(2)}, u32[]{:S(2)}) collective-permute-start(bf16[2048,256]{1,0:T(8,128)(2,1)S(1)} %collective-permute-done.8.refs_3_), channel_id=1, source_target_pairs={{0,8},{8,0},{16,24},{24,16},{1,9},{9,1},{17,25},{25,17},{2,10},{10... | collective-permute-start | bytes 3145736 | tf_op jit(solution)/shard_map/ppermute | solution.py:23
  102.9 12.8 %collective-permute-start.16 = (bf16[2048,256]{1,0:T(8,128)(2,1)S(1)}, bf16[2048,256]{1,0:T(8,128)(2,1)}, u32[]{:S(2)}, u32[]{:S(2)}) collective-permute-start(bf16[2048,256]{1,0:T(8,128)(2,1)S(1)} %copy-done.7), channel_id=1, source_target_pairs={{0,8},{8,0},{16,24},{24,16},{1,9},{9,1},{17,25},{25,17},{2,10},{10... | collective-permute-start | bytes 3145736 | tf_op jit(solution)/shard_map/ppermute | solution.py:23
  103.3 23.1 %collective-permute-start.19 = (bf16[2048,128]{1,0:T(8,128)(2,1)}, bf16[2048,128]{1,0:T(8,128)(2,1)}, u32[]{:S(2)}, u32[]{:S(2)}) collective-permute-start(bf16[2048,128]{1,0:T(8,128)(2,1)} %get-tuple-element.136), channel_id=1, source_target_pairs={{0,16},{8,24},{16,0},{24,8},{1,17},{9,25},{17,1},{25,9},{2,18},{10... | collective-permute-start | bytes 1572872 | tf_op jit(solution)/shard_map/ppermute | solution.py:23
  126.5 37.9 %collective-permute-start.23 = (bf16[2048,256]{1,0:T(8,128)(2,1)}, bf16[2048,256]{1,0:T(8,128)(2,1)S(1)}, u32[]{:S(2)}, u32[]{:S(2)}) collective-permute-start(bf16[2048,256]{1,0:T(8,128)(2,1)} %get-tuple-element.141), channel_id=1, source_target_pairs={{0,16},{8,24},{16,0},{24,8},{1,17},{9,25},{17,1},{25,9},{2,18},{10... | collective-permute-start | bytes 3145736 | tf_op jit(solution)/shard_map/ppermute | solution.py:23
  135.9 13.3 %collective-permute-start.21 = (bf16[512,512]{1,0:T(8,128)(2,1)S(1)}, bf16[512,512]{1,0:T(8,128)(2,1)S(1)}, u32[]{:S(2)}, u32[]{:S(2)}) collective-permute-start(bf16[512,512]{1,0:T(8,128)(2,1)S(1)} %shard_map.67), channel_id=1, source_target_pairs={{0,2},{2,4},{4,6},{6,7},{7,5},{5,3},{3,1},{1,0},{8,10},{10,12},{12... | collective-permute-start | bytes 1572872 | tf_op jit(solution)/shard_map/ppermute | solution.py:95
  137.2 13.7 %collective-permute-start.22 = (bf16[512,512]{1,0:T(8,128)(2,1)S(1)}, bf16[512,512]{1,0:T(8,128)(2,1)}, u32[]{:S(2)}, u32[]{:S(2)}) collective-permute-start(bf16[512,512]{1,0:T(8,128)(2,1)S(1)} %shard_map.67), channel_id=1, source_target_pairs={{2,0},{4,2},{6,4},{7,6},{5,7},{3,5},{1,3},{0,1},{10,8},{12,10},{14... | collective-permute-start | bytes 1572872 | tf_op jit(solution)/shard_map/ppermute | solution.py:95
  164.3 14.5 %collective-permute-start.26 = (bf16[512,512]{1,0:T(8,128)(2,1)}, bf16[512,512]{1,0:T(8,128)(2,1)S(1)}, u32[]{:S(2)}, u32[]{:S(2)}) collective-permute-start(bf16[512,512]{1,0:T(8,128)(2,1)} %copy-done.13), channel_id=1, source_target_pairs={{0,2},{2,4},{4,6},{6,7},{7,5},{5,3},{3,1},{1,0},{8,10},{10,12},{12... | collective-permute-start | bytes 1572872 | tf_op jit(solution)/shard_map/ppermute | solution.py:95
  165.6 14.4 %collective-permute-start.27 = (bf16[512,512]{1,0:T(8,128)(2,1)}, bf16[512,512]{1,0:T(8,128)(2,1)}, u32[]{:S(2)}, u32[]{:S(2)}) collective-permute-start(bf16[512,512]{1,0:T(8,128)(2,1)} %collective-permute-done.22), channel_id=1, source_target_pairs={{2,0},{4,2},{6,4},{7,6},{5,7},{3,5},{1,3},{0,1},{10,8},{12,10},{14... | collective-permute-start | bytes 1572872 | tf_op jit(solution)/shard_map/ppermute | solution.py:95
  180.0 15.9 %collective-permute-start.31 = (bf16[2048,1024]{1,0:T(8,128)(2,1)}, bf16[2048,1024]{1,0:T(8,128)(2,1)S(1)}, u32[]{:S(2)}, u32[]{:S(2)}) collective-permute-start(bf16[2048,1024]{1,0:T(8,128)(2,1)} %refs_0_.3), channel_id=1, source_target_pairs={{0,8},{8,0},{16,24},{24,16},{1,9},{9,1},{17,25},{25,17},{2,10},{10... | collective-permute-start | bytes 12582920 | tf_op jit(solution)/shard_map/ppermute | solution.py:23
  180.0 14.3 %collective-permute-start.29 = (bf16[512,512]{1,0:T(8,128)(2,1)S(1)}, bf16[512,512]{1,0:T(8,128)(2,1)S(1)}, u32[]{:S(2)}, u32[]{:S(2)}) collective-permute-start(bf16[512,512]{1,0:T(8,128)(2,1)S(1)} %collective-permute-done.26), channel_id=1, source_target_pairs={{0,2},{2,4},{4,6},{6,7},{7,5},{5,3},{3,1},{1,0},{8,10},{10,12},{12... | collective-permute-start | bytes 1572872 | tf_op jit(solution)/shard_map/ppermute | solution.py:95
  181.6 14.3 %collective-permute-start.30 = (bf16[512,512]{1,0:T(8,128)(2,1)}, bf16[512,512]{1,0:T(8,128)(2,1)S(1)}, u32[]{:S(2)}, u32[]{:S(2)}) collective-permute-start(bf16[512,512]{1,0:T(8,128)(2,1)} %collective-permute-done.27), channel_id=1, source_target_pairs={{2,0},{4,2},{6,4},{7,6},{5,7},{3,5},{1,3},{0,1},{10,8},{12,10},{14... | collective-permute-start | bytes 1572872 | tf_op jit(solution)/shard_map/ppermute | solution.py:95
  195.9 20.2 %collective-permute-start.34 = (bf16[512,512]{1,0:T(8,128)(2,1)S(1)}, bf16[512,512]{1,0:T(8,128)(2,1)S(1)}, u32[]{:S(2)}, u32[]{:S(2)}) collective-permute-start(bf16[512,512]{1,0:T(8,128)(2,1)S(1)} %shard_map.72), channel_id=1, source_target_pairs={{0,2},{2,4},{4,6},{6,7},{7,5},{5,3},{3,1},{1,0},{8,10},{10,12},{12... | collective-permute-start | bytes 1572872 | tf_op jit(solution)/shard_map/ppermute | solution.py:95
  197.4 18.7 %collective-permute-start.35 = (bf16[512,512]{1,0:T(8,128)(2,1)S(1)}, bf16[512,512]{1,0:T(8,128)(2,1)S(1)}, u32[]{:S(2)}, u32[]{:S(2)}) collective-permute-start(bf16[512,512]{1,0:T(8,128)(2,1)S(1)} %shard_map.72), channel_id=1, source_target_pairs={{2,0},{4,2},{6,4},{7,6},{5,7},{3,5},{1,3},{0,1},{10,8},{12,10},{14... | collective-permute-start | bytes 1572872 | tf_op jit(solution)/shard_map/ppermute | solution.py:95
  198.8 16.1 %collective-permute-start.32 = (bf16[256,512]{1,0:T(8,128)(2,1)S(1)}, bf16[256,512]{1,0:T(8,128)(2,1)S(1)}, u32[]{:S(2)}, u32[]{:S(2)}) collective-permute-start(bf16[256,512]{1,0:T(8,128)(2,1)S(1)} %slice.96), channel_id=1, source_target_pairs={{0,2},{2,4},{4,6},{6,7},{7,5},{5,3},{3,1},{1,0},{8,10},{10,12},{12... | collective-permute-start | bytes 786440 | tf_op jit(solution)/shard_map/ppermute | solution.py:95
  200.4 15.7 %collective-permute-start.33 = (bf16[256,512]{1,0:T(8,128)(2,1)S(1)}, bf16[256,512]{1,0:T(8,128)(2,1)S(1)}, u32[]{:S(2)}, u32[]{:S(2)}) collective-permute-start(bf16[256,512]{1,0:T(8,128)(2,1)S(1)} %slice.97), channel_id=1, source_target_pairs={{2,0},{4,2},{6,4},{7,6},{5,7},{3,5},{1,3},{0,1},{10,8},{12,10},{14... | collective-permute-start | bytes 786440 | tf_op jit(solution)/shard_map/ppermute | solution.py:95
  217.6 12.3 %collective-permute-start.37 = (bf16[512,512]{1,0:T(8,128)(2,1)S(1)}, bf16[512,512]{1,0:T(8,128)(2,1)S(1)}, u32[]{:S(2)}, u32[]{:S(2)}) collective-permute-start(bf16[512,512]{1,0:T(8,128)(2,1)S(1)} %collective-permute-done.35), channel_id=1, source_target_pairs={{2,0},{4,2},{6,4},{7,6},{5,7},{3,5},{1,3},{0,1},{10,8},{12,10},{14... | collective-permute-start | bytes 1572872 | tf_op jit(solution)/shard_map/ppermute | solution.py:95
  (26 other events, 208.0 us)
Sparse Core Ops, SparseCore 0:
  126.6 117.7 all-gather.2

commit v10 on v9

--- a/solution.py
+++ b/solution.py
@@ -115,30 +115,22 @@
     )()
 
 
-def multiply(steps, a_buf, w_bufs, accs, a_sem, w_sem):
-    for i, (left, rights) in enumerate(steps):
-        pltpu.make_async_copy(left, a_buf.at[i], a_sem.at[i]).start()
-        for g, chunks in enumerate(rights):
-            at = 0
-            for chunk in chunks:
-                wide = chunk.shape[1]
-                into = w_bufs[g].at[i, :, pl.ds(at, wide)]
-                pltpu.make_async_copy(chunk, into, w_sem.at[g, i]).start()
-                at += wide
-
-    def body(i, carry):
-        pltpu.make_async_copy(a_buf.at[i], a_buf.at[i], a_sem.at[i]).wait()
-        for g, acc in enumerate(accs):
-            pltpu.make_async_copy(w_bufs[g].at[i], w_bufs[g].at[i], w_sem.at[g, i]).wait()
-            acc[...] += jnp.dot(a_buf[i], w_bufs[g][i], preferred_element_type=jnp.float32)
-        return carry
-
-    lax.fori_loop(0, len(steps), body, 0)
+def multiply(steps, w_buf, acc, sems):
+    for i, (_, chunks) in enumerate(steps):
+        at = 0
+        for chunk in chunks:
+            wide = chunk.shape[1]
+            into = w_buf.at[i, :, pl.ds(at, wide)]
+            pltpu.make_async_copy(chunk, into, sems.at[i]).start()
+            at += wide
+    for i, (left, _) in enumerate(steps):
+        pltpu.make_async_copy(w_buf.at[i], w_buf.at[i], sems.at[i]).wait()
+        acc[...] += jnp.dot(left(), w_buf[i], preferred_element_type=jnp.float32)
 
 
 def project_kernel(near, far, chunks, first, heads, factor, panel_ref, *refs):
     near_refs, far_refs, (scale_ref, cos_ref, sin_ref), rest = take(refs, near, far * chunks, 3)
-    o_ref, a_buf, w_buf, acc, a_sem, w_sem = rest
+    o_ref, w_buf, acc, sems = rest
     slots, _, depth = panel_ref.shape
     per = slots // (near + far)
     cols = acc.shape[1]
@@ -150,9 +142,9 @@
         else:
             at = (p - near) * chunks
             right = [ref.at[rows, :] for ref in far_refs[at : at + chunks]]
-        steps.append((panel_ref.at[k], [right]))
+        steps.append((functools.partial(panel_ref.__getitem__, k), right))
     acc[...] = jnp.zeros_like(acc)
-    multiply(steps, a_buf, [w_buf], [acc], a_sem, w_sem)
+    multiply(steps, w_buf, acc, sems)
     scale = scale_ref[...] * factor
     for h in range(cols // HD):
         at = pl.ds(h * HD, HD)
@@ -170,17 +162,15 @@
     vmem = pl.BlockSpec(memory_space=pltpu.VMEM)
     return pl.pallas_call(
         functools.partial(project_kernel, len(near), len(far), chunks, first, heads, factor),
-        in_specs=[hbm] * (1 + len(near) + len(far) * chunks) + [vmem] * 3,
+        in_specs=[vmem] + [hbm] * (len(near) + len(far) * chunks) + [vmem] * 3,
         out_specs=vmem,
         out_shape=jax.ShapeDtypeStruct((tok, cols), jnp.bfloat16),
         scratch_shapes=[
-            pltpu.VMEM((slots, tok, depth), jnp.bfloat16),
             pltpu.VMEM((slots, depth, cols), jnp.bfloat16),
             pltpu.VMEM((tok, cols), jnp.float32),
             pltpu.SemaphoreType.DMA((slots,)),
-            pltpu.SemaphoreType.DMA((1, slots)),
         ],
-        compiler_params=pltpu.CompilerParams(vmem_limit_bytes=60 * MIB),
+        compiler_params=pltpu.CompilerParams(vmem_limit_bytes=18 * MIB),
         cost_estimate=SHORT,
     )(panel, *near, *[w for pieces in far for w in pieces], scale, cos, sin)
 
@@ -269,14 +259,14 @@
         ),
         out_shape=jax.ShapeDtypeStruct((tok, chunks * cols), jnp.bfloat16),
         compiler_params=pltpu.CompilerParams(
-            dimension_semantics=("arbitrary",), vmem_limit_bytes=32 * MIB
+            dimension_semantics=("arbitrary",), vmem_limit_bytes=18 * MIB
         ),
         cost_estimate=SHORT,
     )(r.reshape(1), *queries, *pieces)
 
 
 def finish_kernel(slots, per, count, r_ref, first_ref, second_ref, *refs):
-    weights, (*old, o_ref, a_buf, w_buf, acc, a_sem, w_sem) = take(refs, count)
+    weights, (*old, o_ref, w_buf, acc, sems) = take(refs, count)
     steps = []
     depth = first_ref.shape[2]
     rows = depth + second_ref.shape[2]
@@ -287,13 +277,13 @@
                 right = weights[0].at[jnp.bitwise_xor(r_ref[0], k // per), at, :]
             else:
                 right = weights[k // per].at[at, :]
-            steps.append((panel_ref.at[k], [[right]]))
+            steps.append((functools.partial(panel_ref.__getitem__, k), [right]))
     acc[...] = old[0][...] if old else jnp.zeros_like(acc)
-    multiply(steps, a_buf, [w_buf], [acc], a_sem, w_sem)
+    multiply(steps, w_buf, acc, sems)
     o_ref[...] = acc[...].astype(o_ref.dtype)
 
 
-def finish(r, panels, slots, weights, per, dtype, total=None):
+def finish(r, panels, slots, weights, per, dtype, limit, total=None):
     _, tok, wide = panels[0].shape
     cols = weights[0].shape[-1]
     count = 2 * (slots[1] - slots[0])
@@ -303,18 +293,17 @@
     return pl.pallas_call(
         functools.partial(finish_kernel, slots, per, len(weights)),
         in_specs=[pl.BlockSpec(memory_space=pltpu.SMEM)]
-        + [hbm] * (2 + len(weights))
+        + [vmem] * 2
+        + [hbm] * len(weights)
         + [vmem] * len(old),
         out_specs=vmem,
         out_shape=jax.ShapeDtypeStruct((tok, cols), dtype),
         scratch_shapes=[
-            pltpu.VMEM((count, tok, wide), jnp.bfloat16),
             pltpu.VMEM((count, wide, cols), jnp.bfloat16),
             pltpu.VMEM((tok, cols), jnp.float32),
             pltpu.SemaphoreType.DMA((count,)),
-            pltpu.SemaphoreType.DMA((1, count)),
         ],
-        compiler_params=pltpu.CompilerParams(vmem_limit_bytes=60 * MIB),
+        compiler_params=pltpu.CompilerParams(vmem_limit_bytes=limit * MIB),
         cost_estimate=SHORT,
     )(r.reshape(1), *panels, *weights, *old)
 
@@ -455,8 +444,8 @@
         panels[1] = put(panels[1], found)
 
     half = n_col // 2
-    total = finish(r, panels, (0, half), o_near, per, jnp.float32)
-    return finish(r, panels, (half, n_col), [after(o_weights, total)], per, jnp.bfloat16, total)
+    total = finish(r, panels, (0, half), o_near, per, jnp.float32, 18)
+    return finish(r, panels, (half, n_col), [o_weights], per, jnp.bfloat16, 44, total)
 
 
 def solution(mesh):

time: 278 us -> 284 us (1.022)
  local copies, waits for them, and re-layouts: 29.5 us -> 19.9 us
  other arithmetic: 19.2 us -> 26.9 us
  waiting for transfers between devices: 116 us -> 120 us
    dynamic_update_slice x18, local copies, waits for them, and re-layouts: 17.8 us -> 3.51 us  [put(): panel = lax.dynamic_update_slice(panel, piece[None], (slot, first, 0))]
    reduce_sum x9, other arithmetic: 2.31 us -> 8.07 us  [put_hidden(): sums = jnp.sum(wider * wider, axis=1)]
    dynamic_update_slice x9, other arithmetic: 10.6 us -> 16.3 us  [put(): panel = lax.dynamic_update_slice(panel, piece[None], (slot, first, 0))]
    unnamed x30 -> x40, local copies, waits for them, and re-layouts: 5.46 us -> 10.9 us
    pallas_call x4, Pallas kernels: 35.3 us -> 40.6 us  [project(): pl.pallas_call(functools.partial(project_kernel, len(near), len(far), chu...]
    pallas_call x2, Pallas kernels: 18.7 us -> 15 us  [finish(): pl.pallas_call(functools.partial(finish_kernel, slots, per, len(weights))...]
    ppermute x24, waiting for transfers between devices: 88 us -> 91.2 us  [hop(): lax.ppermute(s[0], 'col', s[1])]
  transfers between devices with their start and end apart: 43 -> 43, of which waited for: 26 -> 24; matrix products, arithmetic and copies ran while one was open for 16% -> 13% of each run, Pallas kernels for 21% -> 21%
where the time goes in v10:
time: 284 us; the launch traced here: 283 us
  waiting for transfers between devices  120 us (42%)
  Pallas kernels  69.6 us (25%)
  starting transfers between devices  31.9 us (11%)
  other arithmetic  26.9 us (9%)
  local copies, waits for them, and re-layouts  19.9 us (7%)
  between operations  14.4 us (5%)
    ppermute x24, waiting for transfers between devices, hop(): lax.ppermute(s[0], 'col', s[1])  91.2 us
    pallas_call x4, Pallas kernels, project(): pl.pallas_call(functools.partial(project_kernel, len(near), len(far), chu...  40.6 us
    ppermute x18, waiting for transfers between devices, swap(): lax.ppermute(array, axis, [(i, i ^ mask) for i in range(lax.axis_size(axi...  28.7 us
    ppermute x24, starting transfers between devices, hop(): lax.ppermute(s[0], 'col', s[1])  25.6 us
    dynamic_update_slice x9, other arithmetic, put(): panel = lax.dynamic_update_slice(panel, piece[None], (slot, first, 0))  16.3 us
    pallas_call x2, Pallas kernels, finish(): pl.pallas_call(functools.partial(finish_kernel, slots, per, len(weights))...  15 us
    pallas_call x2, Pallas kernels, attend(): pl.pallas_call(functools.partial(attend_kernel, parts, chunks, pair), gri...  14 us
    unnamed x40, local copies, waits for them, and re-layouts  10.9 us
  transfers between devices with their start and end apart: 43, of which 24 were waited for; matrix products, arithmetic and copies ran while one was open for 13% of the time, Pallas kernels for 21%

profile of v10, /device:TPU:2, one launch (start us, length us, event | category | flops | bytes accessed | tf_op | source)
XLA Modules:
  0.0 282.6 jit_solution(4842286601031511243)
XLA Ops:
  12.9 2.5 fusion.31
  15.8 2.1 fusion.39
  17.9 3.1 %fusion.38 = (bf16[2048,256]{1,0:T(8,128)(2,1)}, bf16[2048,256]{1,0:T(8,128)(2,1)S(1)}, bf16[2048,256]{1,0:T(8,128)(2,1)S(1)}) fusion(bf16[2048,1024]{1,0:T(8,128)(2,1)} %refs_0_.2), kind=kLoop, calls=%fused_computation.89 | loop fusion | bytes 6291456 | tf_op jit(solution)/shard_map/slice | solution.py:339
  20.9 13.4 %collective-permute-done.2.refs_2_ = bf16[2048,256]{1,0:T(8,128)(2,1)S(1)} collective-permute-done((bf16[2048,256]{1,0:T(8,128)(2,1)S(1)}, bf16[2048,256]{1,0:T(8,128)(2,1)S(1)}, u32[]{:S(2)}, u32[]{:S(2)}) %collective-permute-start.2) | collective-permute-done | bytes 1048608 | tf_op jit(solution)/shard_map/ppermute | solution.py:23
  34.3 1.6 collective-permute-start.3
  40.4 2.5 fusion.29
  42.8 2.4 fusion.27
  45.3 12.8 %collective-permute-done.3 = bf16[512,1024]{1,0:T(8,128)(2,1)S(1)} collective-permute-done((bf16[512,1024]{1,0:T(8,128)(2,1)}, bf16[512,1024]{1,0:T(8,128)(2,1)S(1)}, u32[]{:S(2)}, u32[]{:S(2)}) %collective-permute-start.3) | collective-permute-done | bytes 1048608 | tf_op jit(solution)/shard_map/ppermute | solution.py:95
  65.6 16.5 %collective-permute-done.6 = bf16[512,1024]{1,0:T(8,128)(2,1)S(1)} collective-permute-done((bf16[512,1024]{1,0:T(8,128)(2,1)S(1)}, bf16[512,1024]{1,0:T(8,128)(2,1)S(1)}, u32[]{:S(2)}, u32[]{:S(2)}) %collective-permute-start.6) | collective-permute-done | bytes 1048608 | tf_op jit(solution)/shard_map/ppermute | solution.py:95
  90.2 8.2 %collective-permute-done.10 = bf16[256,1024]{1,0:T(8,128)(2,1)} collective-permute-done((bf16[256,1024]{1,0:T(8,128)(2,1)S(1)}, bf16[256,1024]{1,0:T(8,128)(2,1)}, u32[]{:S(2)}, u32[]{:S(2)}) %collective-permute-start.10) | collective-permute-done | bytes 524320 | tf_op jit(solution)/shard_map/ppermute | solution.py:95
  105.7 2.0 fusion.35
  107.8 2.0 fusion.33.panel_ref
  113.5 8.7 %shard_map.65.refs_1_.refs_2_ = bf16[512,256]{1,0:T(8,128)(2,1)S(1)} custom-call(bf16[8,512,1024]{2,1,0:T(8,128)(2,1)} %fusion.33.panel_ref, bf16[2048,256]{1,0:T(8,128)(2,1)S(1)} %copy_bitcast_fusion.refs_0_, bf16[2048,256]{1,0:T(8,128)(2,1)S(1)} %copy-done.17, bf16[2048,256]{1,0:T(8,128)(2,1)S(1)} %copy-done.13, bf16[2048,256]{1,0:T(8,128)(2,1)S(1)} %copy-done.15, ...), custom_call_target="tpu_custom_call" | custom-call | flops 1 | bytes 1 | tf_op jit(solution)/shard_map/pallas_call | solution.py:163
  122.1 1.6 collective-permute-start.14
  123.8 9.7 %shard_map.66.refs_0_ = bf16[512,512]{1,0:T(8,128)(2,1)S(1)} custom-call(bf16[8,512,1024]{2,1,0:T(8,128)(2,1)} %fusion.33.panel_ref, bf16[2048,1024]{1,0:T(8,128)(2,1)} %refs_0_.2, bf16[2048,1024]{1,0:T(8,128)(2,1)} %collective-permute-done.15.refs_1_, bf16[2048,256]{1,0:T(8,128)(2,1)S(1)} %collective-permute-done.5.refs_2_, ...), custom_call_target="tpu_custom_call" | custom-call | flops 1 | bytes 1 | tf_op jit(solution)/shard_map/pallas_call | solution.py:163
  136.7 7.1 %shard_map.67 = bf16[512,512]{1,0:T(8,128)(2,1)S(1)} custom-call(s32[1]{0:T(128)} %bitcast.r_ref, bf16[512,512]{1,0:T(8,128)(2,1)S(1)} %shard_map.66.refs_0_, bf16[512,256]{1,0:T(8,128)(2,1)S(1)} %shard_map.65.refs_1_.refs_2_, bf16[512,256]{1,0:T(8,128)(2,1)S(1)} %copy-done.7, bf16[512,256]{1,0:T(8,128)(2,1)S(1)} %collective-permute-done.14.refs_3_.refs_4_, ...), custom_call_target="tpu_custom_call" | custom-call | flops 1 | bytes 1 | tf_op jit(solution)/shard_map/pallas_call | solution.py:244
  146.7 12.4 %shard_map.70.refs_0_ = bf16[512,256]{1,0:T(8,128)(2,1)S(1)} custom-call(bf16[8,512,1024]{2,1,0:T(8,128)(2,1)} %fusion.33.panel_ref, bf16[2048,1024]{1,0:T(8,128)(2,1)} %refs_0_.2, bf16[2048,1024]{1,0:T(8,128)(2,1)} %collective-permute-done.15.refs_1_, bf16[2048,128]{1,0:T(8,128)(2,1)} %collective-permute-done.11.refs_2_, ...), custom_call_target="tpu_custom_call" | custom-call | flops 1 | bytes 1 | tf_op jit(solution)/shard_map/pallas_call | solution.py:163
  159.1 13.0 %collective-permute-done.23.refs_2_ = bf16[2048,256]{1,0:T(8,128)(2,1)S(1)} collective-permute-done((bf16[2048,256]{1,0:T(8,128)(2,1)}, bf16[2048,256]{1,0:T(8,128)(2,1)S(1)}, u32[]{:S(2)}, u32[]{:S(2)}) %collective-permute-start.23) | collective-permute-done | bytes 1048608 | tf_op jit(solution)/shard_map/ppermute | solution.py:23
  172.5 1.6 collective-permute-start.27
  176.3 9.8 %shard_map.71.refs_1_ = bf16[512,256]{1,0:T(8,128)(2,1)S(1)} custom-call(bf16[8,512,1024]{2,1,0:T(8,128)(2,1)} %fusion.33.panel_ref, bf16[2048,1024]{1,0:T(8,128)(2,1)} %refs_0_.2, bf16[2048,1024]{1,0:T(8,128)(2,1)} %collective-permute-done.15.refs_1_, bf16[2048,256]{1,0:T(8,128)(2,1)S(1)} %collective-permute-done.23.refs_2_, ...), custom_call_target="tpu_custom_call" | custom-call | flops 1 | bytes 1 | tf_op jit(solution)/shard_map/pallas_call | solution.py:163
  188.8 7.0 %shard_map.72 = bf16[512,512]{1,0:T(8,128)(2,1)S(1)} custom-call(s32[1]{0:T(128)} %bitcast.r_ref, bf16[512,256]{1,0:T(8,128)(2,1)S(1)} %shard_map.70.refs_0_, bf16[512,256]{1,0:T(8,128)(2,1)S(1)} %shard_map.71.refs_1_, bf16[512,256]{1,0:T(8,128)(2,1)S(1)} %shard_map.65.refs_1_.refs_2_, bf16[512,256]{1,0:T(8,128)(2,1)S(1)} %copy-done.8, ...), custom_call_target="tpu_custom_call" | custom-call | flops 1 | bytes 1 | tf_op jit(solution)/shard_map/pallas_call | solution.py:244
  195.9 5.2 %collective-permute-done.29 = bf16[512,512]{1,0:T(8,128)(2,1)S(1)} collective-permute-done((bf16[512,512]{1,0:T(8,128)(2,1)S(1)}, bf16[512,512]{1,0:T(8,128)(2,1)S(1)}, u32[]{:S(2)}, u32[]{:S(2)}) %collective-permute-start.29) | collective-permute-done | bytes 524320 | tf_op jit(solution)/shard_map/ppermute | solution.py:95
  206.8 14.6 %collective-permute-done.32 = bf16[256,512]{1,0:T(8,128)(2,1)S(1)} collective-permute-done((bf16[256,512]{1,0:T(8,128)(2,1)S(1)}, bf16[256,512]{1,0:T(8,128)(2,1)S(1)}, u32[]{:S(2)}, u32[]{:S(2)}) %collective-permute-start.32) | collective-permute-done | bytes 262176 | tf_op jit(solution)/shard_map/ppermute | solution.py:95
  222.3 1.7 collective-permute-start.36
  224.5 10.1 %collective-permute-done.36 = bf16[512,512]{1,0:T(8,128)(2,1)S(1)} collective-permute-done((bf16[512,512]{1,0:T(8,128)(2,1)S(1)}, bf16[512,512]{1,0:T(8,128)(2,1)S(1)}, u32[]{:S(2)}, u32[]{:S(2)}) %collective-permute-start.36) | collective-permute-done | bytes 524320 | tf_op jit(solution)/shard_map/ppermute | solution.py:95
  236.0 1.7 collective-permute-start.38
  238.2 9.0 %collective-permute-done.38 = bf16[512,512]{1,0:T(8,128)(2,1)S(1)} collective-permute-done((bf16[512,512]{1,0:T(8,128)(2,1)S(1)}, bf16[512,512]{1,0:T(8,128)(2,1)S(1)}, u32[]{:S(2)}, u32[]{:S(2)}) %collective-permute-start.38) | collective-permute-done | bytes 524320 | tf_op jit(solution)/shard_map/ppermute | solution.py:95
  251.2 3.9 %collective-permute-done.40 = bf16[256,512]{1,0:T(8,128)(2,1)S(1)} collective-permute-done((bf16[256,512]{1,0:T(8,128)(2,1)S(1)}, bf16[256,512]{1,0:T(8,128)(2,1)S(1)}, u32[]{:S(2)}, u32[]{:S(2)}) %collective-permute-start.40) | collective-permute-done | bytes 262176 | tf_op jit(solution)/shard_map/ppermute | solution.py:95
  256.5 5.7 %shard_map.73.refs_1_ = f32[512,1024]{1,0:T(8,128)S(1)} custom-call(s32[1]{0:T(128)} %bitcast.r_ref, bf16[8,512,512]{2,1,0:T(8,128)(2,1)S(1)} %bitcast_dynamic-update-slice_fusion.16.first_ref, bf16[8,512,512]{2,1,0:T(8,128)(2,1)S(1)} %bitcast_dynamic-update-slice_fusion.14.second_ref, bf16[2048,1024]{1,0:T(8,128)(2,1)S(1)} %copy-done.5, ...), custom_call_target="tpu_custom_call" | custom-call | flops 1 | bytes 1 | tf_op jit(solution)/shard_map/pallas_call | solution.py:293
  262.2 2.0 copy-done.1
  264.2 2.2 copy-done.4
  266.4 9.3 %shard_map.74 = bf16[512,1024]{1,0:T(8,128)(2,1)} custom-call(s32[1]{0:T(128)} %bitcast.r_ref, bf16[8,512,512]{2,1,0:T(8,128)(2,1)S(1)} %copy-done.4, bf16[8,512,512]{2,1,0:T(8,128)(2,1)} %copy-done.1, bf16[4,2048,1024]{2,1,0:T(8,128)(2,1)} %bitcast.83, f32[512,1024]{1,0:T(8,128)S(1)} %shard_map.73.refs_1_), custom_call_target="tpu_custom_call" | custom-call | flops 1 | bytes 1 | tf_op jit(solution)/shard_map/pallas_call | solution.py:293
  (165 shorter events, 63.0 us)
Async XLA Ops:
  6.5 257.6 %all-gather.3.cloned.1.call-start = ((), (), s32[]{:S(2)}) async-start(), calls=%async_computation | async-start | bytes 20971520 | tf_op jit(solution)/shard_map/all_gather | solution.py:416
  6.5 27.8 %collective-permute-start = (bf16[512,1024]{1,0:T(8,128)(2,1)}, bf16[512,1024]{1,0:T(8,128)(2,1)}, u32[]{:S(2)}, u32[]{:S(2)}) collective-permute-start(bf16[512,1024]{1,0:T(8,128)(2,1)} %param.6), channel_id=1, source_target_pairs={{0,2},{2,4},{4,6},{6,7},{7,5},{5,3},{3,1},{1,0},{8,10},{10,12},{12... | collective-permute-start | bytes 3145736 | tf_op jit(solution)/shard_map/ppermute | solution.py:95
  8.1 26.2 %collective-permute-start.1 = (bf16[512,1024]{1,0:T(8,128)(2,1)}, bf16[512,1024]{1,0:T(8,128)(2,1)}, u32[]{:S(2)}, u32[]{:S(2)}) collective-permute-start(bf16[512,1024]{1,0:T(8,128)(2,1)} %param.6), channel_id=1, source_target_pairs={{2,0},{4,2},{6,4},{7,6},{5,7},{3,5},{1,3},{0,1},{10,8},{12,10},{14... | collective-permute-start | bytes 3145736 | tf_op jit(solution)/shard_map/ppermute | solution.py:95
  9.9 24.4 %collective-permute-start.2 = (bf16[2048,256]{1,0:T(8,128)(2,1)S(1)}, bf16[2048,256]{1,0:T(8,128)(2,1)S(1)}, u32[]{:S(2)}, u32[]{:S(2)}) collective-permute-start(bf16[2048,256]{1,0:T(8,128)(2,1)S(1)} %copy_bitcast_fusion.refs_0_), channel_id=1, source_target_pairs={{0,16},{8,24},{16,0},{24,8},{1,17},{9,25},{17,1},{25,9},{2,18},{10... | collective-permute-start | bytes 3145736 | tf_op jit(solution)/shard_map/ppermute | solution.py:23
  34.3 23.8 %collective-permute-start.3 = (bf16[512,1024]{1,0:T(8,128)(2,1)}, bf16[512,1024]{1,0:T(8,128)(2,1)S(1)}, u32[]{:S(2)}, u32[]{:S(2)}) collective-permute-start(bf16[512,1024]{1,0:T(8,128)(2,1)} %collective-permute-done), channel_id=1, source_target_pairs={{0,2},{2,4},{4,6},{6,7},{7,5},{5,3},{3,1},{1,0},{8,10},{10,12},{12... | collective-permute-start | bytes 3145736 | tf_op jit(solution)/shard_map/ppermute | solution.py:95
  35.9 23.4 %collective-permute-start.4 = (bf16[512,1024]{1,0:T(8,128)(2,1)}, bf16[512,1024]{1,0:T(8,128)(2,1)S(1)}, u32[]{:S(2)}, u32[]{:S(2)}) collective-permute-start(bf16[512,1024]{1,0:T(8,128)(2,1)} %collective-permute-done.1), channel_id=1, source_target_pairs={{2,0},{4,2},{6,4},{7,6},{5,7},{3,5},{1,3},{0,1},{10,8},{12,10},{14... | collective-permute-start | bytes 3145736 | tf_op jit(solution)/shard_map/ppermute | solution.py:95
  36.8 23.1 %collective-permute-start.5 = (bf16[2048,256]{1,0:T(8,128)(2,1)S(1)}, bf16[2048,256]{1,0:T(8,128)(2,1)S(1)}, u32[]{:S(2)}, u32[]{:S(2)}) collective-permute-start(bf16[2048,256]{1,0:T(8,128)(2,1)S(1)} %get-tuple-element.98), channel_id=1, source_target_pairs={{0,16},{8,24},{16,0},{24,8},{1,17},{9,25},{17,1},{25,9},{2,18},{10... | collective-permute-start | bytes 3145736 | tf_op jit(solution)/shard_map/ppermute | solution.py:23
  59.9 22.2 %collective-permute-start.6 = (bf16[512,1024]{1,0:T(8,128)(2,1)S(1)}, bf16[512,1024]{1,0:T(8,128)(2,1)S(1)}, u32[]{:S(2)}, u32[]{:S(2)}) collective-permute-start(bf16[512,1024]{1,0:T(8,128)(2,1)S(1)} %collective-permute-done.3), channel_id=1, source_target_pairs={{0,2},{2,4},{4,6},{6,7},{7,5},{5,3},{3,1},{1,0},{8,10},{10,12},{12... | collective-permute-start | bytes 3145736 | tf_op jit(solution)/shard_map/ppermute | solution.py:95
  61.0 22.0 %collective-permute-start.7 = (bf16[512,1024]{1,0:T(8,128)(2,1)S(1)}, bf16[512,1024]{1,0:T(8,128)(2,1)S(1)}, u32[]{:S(2)}, u32[]{:S(2)}) collective-permute-start(bf16[512,1024]{1,0:T(8,128)(2,1)S(1)} %collective-permute-done.4), channel_id=1, source_target_pairs={{2,0},{4,2},{6,4},{7,6},{5,7},{3,5},{1,3},{0,1},{10,8},{12,10},{14... | collective-permute-start | bytes 3145736 | tf_op jit(solution)/shard_map/ppermute | solution.py:95
  62.0 21.8 %collective-permute-start.8 = (bf16[2048,256]{1,0:T(8,128)(2,1)S(1)}, bf16[2048,256]{1,0:T(8,128)(2,1)}, u32[]{:S(2)}, u32[]{:S(2)}) collective-permute-start(bf16[2048,256]{1,0:T(8,128)(2,1)S(1)} %get-tuple-element.106), channel_id=1, source_target_pairs={{0,16},{8,24},{16,0},{24,8},{1,17},{9,25},{17,1},{25,9},{2,18},{10... | collective-permute-start | bytes 3145736 | tf_op jit(solution)/shard_map/ppermute | solution.py:23
  83.8 16.3 %collective-permute-start.13 = (bf16[2048,256]{1,0:T(8,128)(2,1)S(1)}, bf16[2048,256]{1,0:T(8,128)(2,1)S(1)}, u32[]{:S(2)}, u32[]{:S(2)}) collective-permute-start(bf16[2048,256]{1,0:T(8,128)(2,1)S(1)} %copy-done.12), channel_id=1, source_target_pairs={{0,8},{8,0},{16,24},{24,16},{1,9},{9,1},{17,25},{25,17},{2,10},{10... | collective-permute-start | bytes 3145736 | tf_op jit(solution)/shard_map/ppermute | solution.py:23
  83.9 17.2 %collective-permute-start.12 = (bf16[2048,256]{1,0:T(8,128)(2,1)S(1)}, bf16[2048,256]{1,0:T(8,128)(2,1)S(1)}, u32[]{:S(2)}, u32[]{:S(2)}) collective-permute-start(bf16[2048,256]{1,0:T(8,128)(2,1)S(1)} %copy_bitcast_fusion.refs_0_), channel_id=1, source_target_pairs={{0,8},{8,0},{16,24},{24,16},{1,9},{9,1},{17,25},{25,17},{2,10},{10... | collective-permute-start | bytes 3145736 | tf_op jit(solution)/shard_map/ppermute | solution.py:23
  84.4 14.0 %collective-permute-start.10 = (bf16[256,1024]{1,0:T(8,128)(2,1)S(1)}, bf16[256,1024]{1,0:T(8,128)(2,1)}, u32[]{:S(2)}, u32[]{:S(2)}) collective-permute-start(bf16[256,1024]{1,0:T(8,128)(2,1)S(1)} %slice.89), channel_id=1, source_target_pairs={{2,0},{4,2},{6,4},{7,6},{5,7},{3,5},{1,3},{0,1},{10,8},{12,10},{14... | collective-permute-start | bytes 1572872 | tf_op jit(solution)/shard_map/ppermute | solution.py:95
  86.0 13.9 %collective-permute-start.9 = (bf16[256,1024]{1,0:T(8,128)(2,1)S(1)}, bf16[256,1024]{1,0:T(8,128)(2,1)S(1)}, u32[]{:S(2)}, u32[]{:S(2)}) collective-permute-start(bf16[256,1024]{1,0:T(8,128)(2,1)S(1)} %slice.88), channel_id=1, source_target_pairs={{0,2},{2,4},{4,6},{6,7},{7,5},{5,3},{3,1},{1,0},{8,10},{10,12},{12... | collective-permute-start | bytes 1572872 | tf_op jit(solution)/shard_map/ppermute | solution.py:95
  86.7 13.5 %collective-permute-start.11 = (bf16[2048,128]{1,0:T(8,128)(2,1)S(1)}, bf16[2048,128]{1,0:T(8,128)(2,1)}, u32[]{:S(2)}, u32[]{:S(2)}) collective-permute-start(bf16[2048,128]{1,0:T(8,128)(2,1)S(1)} %get-tuple-element.114), channel_id=1, source_target_pairs={{0,16},{8,24},{16,0},{24,8},{1,17},{9,25},{17,1},{25,9},{2,18},{10... | collective-permute-start | bytes 1572872 | tf_op jit(solution)/shard_map/ppermute | solution.py:23
  102.1 21.7 %collective-permute-start.15 = (bf16[2048,1024]{1,0:T(8,128)(2,1)}, bf16[2048,1024]{1,0:T(8,128)(2,1)}, u32[]{:S(2)}, u32[]{:S(2)}) collective-permute-start(bf16[2048,1024]{1,0:T(8,128)(2,1)} %refs_0_.2), channel_id=1, source_target_pairs={{0,8},{8,0},{16,24},{24,16},{1,9},{9,1},{17,25},{25,17},{2,10},{10... | collective-permute-start | bytes 12582920 | tf_op jit(solution)/shard_map/ppermute | solution.py:23
  102.1 21.7 %collective-permute-start.17 = (bf16[2048,256]{1,0:T(8,128)(2,1)}, bf16[2048,256]{1,0:T(8,128)(2,1)}, u32[]{:S(2)}, u32[]{:S(2)}) collective-permute-start(bf16[2048,256]{1,0:T(8,128)(2,1)} %collective-permute-done.8.refs_3_), channel_id=1, source_target_pairs={{0,8},{8,0},{16,24},{24,16},{1,9},{9,1},{17,25},{25,17},{2,10},{10... | collective-permute-start | bytes 3145736 | tf_op jit(solution)/shard_map/ppermute | solution.py:23
  102.6 21.2 %collective-permute-start.16 = (bf16[2048,256]{1,0:T(8,128)(2,1)S(1)}, bf16[2048,256]{1,0:T(8,128)(2,1)}, u32[]{:S(2)}, u32[]{:S(2)}) collective-permute-start(bf16[2048,256]{1,0:T(8,128)(2,1)S(1)} %collective-permute-done.5.refs_2_), channel_id=1, source_target_pairs={{0,8},{8,0},{16,24},{24,16},{1,9},{9,1},{17,25},{25,17},{2,10},{10... | collective-permute-start | bytes 3145736 | tf_op jit(solution)/shard_map/ppermute | solution.py:23
  103.8 29.8 %collective-permute-start.19 = (bf16[2048,128]{1,0:T(8,128)(2,1)}, bf16[2048,128]{1,0:T(8,128)(2,1)}, u32[]{:S(2)}, u32[]{:S(2)}) collective-permute-start(bf16[2048,128]{1,0:T(8,128)(2,1)} %get-tuple-element.135), channel_id=1, source_target_pairs={{0,16},{8,24},{16,0},{24,8},{1,17},{9,25},{17,1},{25,9},{2,18},{10... | collective-permute-start | bytes 1572872 | tf_op jit(solution)/shard_map/ppermute | solution.py:23
  133.6 38.5 %collective-permute-start.23 = (bf16[2048,256]{1,0:T(8,128)(2,1)}, bf16[2048,256]{1,0:T(8,128)(2,1)S(1)}, u32[]{:S(2)}, u32[]{:S(2)}) collective-permute-start(bf16[2048,256]{1,0:T(8,128)(2,1)} %get-tuple-element.140), channel_id=1, source_target_pairs={{0,16},{8,24},{16,0},{24,8},{1,17},{9,25},{17,1},{25,9},{2,18},{10... | collective-permute-start | bytes 3145736 | tf_op jit(solution)/shard_map/ppermute | solution.py:23
  134.3 12.4 %collective-permute-start.24 = (bf16[2048,128]{1,0:T(8,128)(2,1)}, bf16[2048,128]{1,0:T(8,128)(2,1)}, u32[]{:S(2)}, u32[]{:S(2)}) collective-permute-start(bf16[2048,128]{1,0:T(8,128)(2,1)} %collective-permute-done.11.refs_2_), channel_id=1, source_target_pairs={{0,8},{8,0},{16,24},{24,16},{1,9},{9,1},{17,25},{25,17},{2,10},{10... | collective-permute-start | bytes 1572872 | tf_op jit(solution)/shard_map/ppermute | solution.py:23
  143.8 15.3 %collective-permute-start.21 = (bf16[512,512]{1,0:T(8,128)(2,1)S(1)}, bf16[512,512]{1,0:T(8,128)(2,1)}, u32[]{:S(2)}, u32[]{:S(2)}) collective-permute-start(bf16[512,512]{1,0:T(8,128)(2,1)S(1)} %shard_map.67), channel_id=1, source_target_pairs={{0,2},{2,4},{4,6},{6,7},{7,5},{5,3},{3,1},{1,0},{8,10},{10,12},{12... | collective-permute-start | bytes 1572872 | tf_op jit(solution)/shard_map/ppermute | solution.py:95
  145.0 14.1 %collective-permute-start.22 = (bf16[512,512]{1,0:T(8,128)(2,1)S(1)}, bf16[512,512]{1,0:T(8,128)(2,1)}, u32[]{:S(2)}, u32[]{:S(2)}) collective-permute-start(bf16[512,512]{1,0:T(8,128)(2,1)S(1)} %shard_map.67), channel_id=1, source_target_pairs={{2,0},{4,2},{6,4},{7,6},{5,7},{3,5},{1,3},{0,1},{10,8},{12,10},{14... | collective-permute-start | bytes 1572872 | tf_op jit(solution)/shard_map/ppermute | solution.py:95
  172.1 14.5 %collective-permute-start.26 = (bf16[512,512]{1,0:T(8,128)(2,1)}, bf16[512,512]{1,0:T(8,128)(2,1)S(1)}, u32[]{:S(2)}, u32[]{:S(2)}) collective-permute-start(bf16[512,512]{1,0:T(8,128)(2,1)} %collective-permute-done.21), channel_id=1, source_target_pairs={{0,2},{2,4},{4,6},{6,7},{7,5},{5,3},{3,1},{1,0},{8,10},{10,12},{12... | collective-permute-start | bytes 1572872 | tf_op jit(solution)/shard_map/ppermute | solution.py:95
  172.5 14.3 %collective-permute-start.27 = (bf16[512,512]{1,0:T(8,128)(2,1)}, bf16[512,512]{1,0:T(8,128)(2,1)S(1)}, u32[]{:S(2)}, u32[]{:S(2)}) collective-permute-start(bf16[512,512]{1,0:T(8,128)(2,1)} %collective-permute-done.22), channel_id=1, source_target_pairs={{2,0},{4,2},{6,4},{7,6},{5,7},{3,5},{1,3},{0,1},{10,8},{12,10},{14... | collective-permute-start | bytes 1572872 | tf_op jit(solution)/shard_map/ppermute | solution.py:95
  186.7 15.7 %collective-permute-start.31 = (bf16[2048,1024]{1,0:T(8,128)(2,1)S(1)}, bf16[2048,1024]{1,0:T(8,128)(2,1)S(1)}, u32[]{:S(2)}, u32[]{:S(2)}) collective-permute-start(bf16[2048,1024]{1,0:T(8,128)(2,1)S(1)} %copy-done.5), channel_id=1, source_target_pairs={{0,8},{8,0},{16,24},{24,16},{1,9},{9,1},{17,25},{25,17},{2,10},{10... | collective-permute-start | bytes 12582920 | tf_op jit(solution)/shard_map/ppermute | solution.py:23
  186.7 14.3 %collective-permute-start.29 = (bf16[512,512]{1,0:T(8,128)(2,1)S(1)}, bf16[512,512]{1,0:T(8,128)(2,1)S(1)}, u32[]{:S(2)}, u32[]{:S(2)}) collective-permute-start(bf16[512,512]{1,0:T(8,128)(2,1)S(1)} %collective-permute-done.26), channel_id=1, source_target_pairs={{0,2},{2,4},{4,6},{6,7},{7,5},{5,3},{3,1},{1,0},{8,10},{10,12},{12... | collective-permute-start | bytes 1572872 | tf_op jit(solution)/shard_map/ppermute | solution.py:95
  188.4 14.1 %collective-permute-start.30 = (bf16[512,512]{1,0:T(8,128)(2,1)S(1)}, bf16[512,512]{1,0:T(8,128)(2,1)S(1)}, u32[]{:S(2)}, u32[]{:S(2)}) collective-permute-start(bf16[512,512]{1,0:T(8,128)(2,1)S(1)} %collective-permute-done.27), channel_id=1, source_target_pairs={{2,0},{4,2},{6,4},{7,6},{5,7},{3,5},{1,3},{0,1},{10,8},{12,10},{14... | collective-permute-start | bytes 1572872 | tf_op jit(solution)/shard_map/ppermute | solution.py:95
  202.4 19.9 %collective-permute-start.34 = (bf16[512,512]{1,0:T(8,128)(2,1)S(1)}, bf16[512,512]{1,0:T(8,128)(2,1)S(1)}, u32[]{:S(2)}, u32[]{:S(2)}) collective-permute-start(bf16[512,512]{1,0:T(8,128)(2,1)S(1)} %shard_map.72), channel_id=1, source_target_pairs={{0,2},{2,4},{4,6},{6,7},{7,5},{5,3},{3,1},{1,0},{8,10},{10,12},{12... | collective-permute-start | bytes 1572872 | tf_op jit(solution)/shard_map/ppermute | solution.py:95
  203.6 18.7 %collective-permute-start.35 = (bf16[512,512]{1,0:T(8,128)(2,1)S(1)}, bf16[512,512]{1,0:T(8,128)(2,1)S(1)}, u32[]{:S(2)}, u32[]{:S(2)}) collective-permute-start(bf16[512,512]{1,0:T(8,128)(2,1)S(1)} %shard_map.72), channel_id=1, source_target_pairs={{2,0},{4,2},{6,4},{7,6},{5,7},{3,5},{1,3},{0,1},{10,8},{12,10},{14... | collective-permute-start | bytes 1572872 | tf_op jit(solution)/shard_map/ppermute | solution.py:95
  204.5 16.9 %collective-permute-start.32 = (bf16[256,512]{1,0:T(8,128)(2,1)S(1)}, bf16[256,512]{1,0:T(8,128)(2,1)S(1)}, u32[]{:S(2)}, u32[]{:S(2)}) collective-permute-start(bf16[256,512]{1,0:T(8,128)(2,1)S(1)} %slice.96), channel_id=1, source_target_pairs={{0,2},{2,4},{4,6},{6,7},{7,5},{5,3},{3,1},{1,0},{8,10},{10,12},{12... | collective-permute-start | bytes 786440 | tf_op jit(solution)/shard_map/ppermute | solution.py:95
  205.8 16.5 %collective-permute-start.33 = (bf16[256,512]{1,0:T(8,128)(2,1)S(1)}, bf16[256,512]{1,0:T(8,128)(2,1)S(1)}, u32[]{:S(2)}, u32[]{:S(2)}) collective-permute-start(bf16[256,512]{1,0:T(8,128)(2,1)S(1)} %slice.97), channel_id=1, source_target_pairs={{2,0},{4,2},{6,4},{7,6},{5,7},{3,5},{1,3},{0,1},{10,8},{12,10},{14... | collective-permute-start | bytes 786440 | tf_op jit(solution)/shard_map/ppermute | solution.py:95
  (31 other events, 263.2 us)
Sparse Core Ops, SparseCore 0:
  133.7 117.7 all-gather.2

commit v11 on v10

--- a/solution.py
+++ b/solution.py
@@ -115,17 +115,23 @@
     )()
 
 
-def multiply(steps, w_buf, acc, sems):
-    for i, (_, chunks) in enumerate(steps):
+def multiply(lefts, rights, w_buf, acc, sems):
+    for i, chunks in enumerate(rights):
         at = 0
         for chunk in chunks:
             wide = chunk.shape[1]
             into = w_buf.at[i, :, pl.ds(at, wide)]
             pltpu.make_async_copy(chunk, into, sems.at[i]).start()
             at += wide
-    for i, (left, _) in enumerate(steps):
-        pltpu.make_async_copy(w_buf.at[i], w_buf.at[i], sems.at[i]).wait()
-        acc[...] += jnp.dot(left(), w_buf[i], preferred_element_type=jnp.float32)
+
+    def body(k, carry):
+        for g, left in enumerate(lefts):
+            i = k * len(lefts) + g
+            pltpu.make_async_copy(w_buf.at[i], w_buf.at[i], sems.at[i]).wait()
+            acc[...] += jnp.dot(left[k], w_buf[i], preferred_element_type=jnp.float32)
+        return carry
+
+    lax.fori_loop(0, len(rights) // len(lefts), body, 0)
 
 
 def project_kernel(near, far, chunks, first, heads, factor, panel_ref, *refs):
@@ -134,7 +140,7 @@
     slots, _, depth = panel_ref.shape
     per = slots // (near + far)
     cols = acc.shape[1]
-    steps = []
+    rights = []
     for k in range(slots):
         p, rows = k // per, pl.ds(k % per * depth, depth)
         if p < near:
@@ -142,9 +148,9 @@
         else:
             at = (p - near) * chunks
             right = [ref.at[rows, :] for ref in far_refs[at : at + chunks]]
-        steps.append((functools.partial(panel_ref.__getitem__, k), right))
+        rights.append(right)
     acc[...] = jnp.zeros_like(acc)
-    multiply(steps, w_buf, acc, sems)
+    multiply([panel_ref], rights, w_buf, acc, sems)
     scale = scale_ref[...] * factor
     for h in range(cols // HD):
         at = pl.ds(h * HD, HD)
@@ -170,96 +176,88 @@
             pltpu.VMEM((tok, cols), jnp.float32),
             pltpu.SemaphoreType.DMA((slots,)),
         ],
-        compiler_params=pltpu.CompilerParams(vmem_limit_bytes=18 * MIB),
+        compiler_params=pltpu.CompilerParams(vmem_limit_bytes=24 * MIB),
         cost_estimate=SHORT,
     )(panel, *near, *[w for pieces in far for w in pieces], scale, cos, sin)
 
 
-def attend_kernel(parts, chunks, pair, r_ref, *refs):
-    chunk_refs, pieces = refs[:chunks], refs[chunks : chunks + parts]
-    o_ref, q_ref, turned, top, total, acc = refs[chunks + parts :]
+def attend_kernel(parts, chunks, r_ref, *refs):
+    chunk_refs, pieces, (o_ref, q, keys, values, top, total, acc) = take(refs, chunks, parts)
     r = r_ref[0]
-    tok = q_ref.shape[0]
+    tok = q.shape[0]
     step = pl.program_id(0)
     per = pl.num_programs(0) // chunks
     for i in range(chunks):
 
         @pl.when(step // per == i)
         def _():
-            q_ref[...] = chunk_refs[i][...]
-
-    dims = (((1,), (1,)), ((), ()))
+            q[...] = chunk_refs[i][...]
 
     @pl.when(step == 0)
     def _():
         for j in range(parts):
-            turned[j] = pieces[j][:, HD:].T
-
-    def scores(j, g):
-        return lax.dot_general(
-            pieces[j][:, :HD],
-            q_ref[:, g * HD : (g + 1) * HD],
-            dims,
-            preferred_element_type=jnp.float32,
-        )
+            keys[j] = pieces[j][:, :HD]
+            values[j] = pieces[j][:, HD:].T
+
+    def scores(j):
+        dims = (((1,), (1,)), ((), ()))
+        return lax.dot_general(keys[j], q[...], dims, preferred_element_type=jnp.float32)
+
+    def weigh(j, p):
+        return jnp.dot(values[j], p.astype(jnp.bfloat16), preferred_element_type=jnp.float32)
 
     key = lax.broadcasted_iota(jnp.int32, (tok, tok), 0)
     query = lax.broadcasted_iota(jnp.int32, (tok, tok), 1)
-    for g in range(pair):
-        s = jnp.where(key <= query, scores(0, g), -jnp.inf)
-        m = jnp.max(s, axis=0, keepdims=True)
+    s = jnp.where(key <= query, scores(0), -jnp.inf)
+    m = jnp.max(s, axis=0, keepdims=True)
+    p = jnp.exp2(s - m)
+    top[...] = m
+    total[...] = jnp.sum(p, axis=0, keepdims=True)
+    acc[...] = weigh(0, p)
+
+    def body(t, carry):
+        j = jnp.bitwise_xor(r, t)
+        s = scores(j)
+        m = jnp.maximum(top[...], jnp.max(s, axis=0, keepdims=True))
+        keep = jnp.exp2(top[...] - m)
         p = jnp.exp2(s - m)
-        top[g] = m
-        total[g] = jnp.sum(p, axis=0, keepdims=True)
-        acc[g] = jnp.dot(turned[0], p.astype(jnp.bfloat16), preferred_element_type=jnp.float32)
-    for j in range(1, parts):
-
-        @pl.when(jnp.bitwise_xor(r, j) < r)
-        def _():
-            for g in range(pair):
-                s = scores(j, g)
-                m = jnp.maximum(top[g], jnp.max(s, axis=0, keepdims=True))
-                keep = jnp.exp2(top[g] - m)
-                p = jnp.exp2(s - m)
-                top[g] = m
-                total[g] = total[g] * keep + jnp.sum(p, axis=0, keepdims=True)
-                acc[g] = acc[g] * keep + jnp.dot(
-                    turned[j], p.astype(jnp.bfloat16), preferred_element_type=jnp.float32
-                )
-
-    for g in range(pair):
-        o_ref[:, g * HD : (g + 1) * HD] = (acc[g] / total[g]).T.astype(o_ref.dtype)
+        top[...] = m
+        total[...] = total[...] * keep + jnp.sum(p, axis=0, keepdims=True)
+        acc[...] = acc[...] * keep + weigh(j, p)
+        return carry
+
+    lax.fori_loop(0, r, body, 0)
+    o_ref[...] = (acc[...] / total[...]).T.astype(o_ref.dtype)
 
 
 def attend(r, queries, pieces):
     tok, cols = queries[0].shape
     chunks, parts = len(queries), len(pieces)
-    pair = 2 if cols // HD % 2 == 0 else 1
-    per = cols // (HD * pair)
-    heads = chunks * cols // HD
+    per = cols // HD
 
     def query_spec(i):
-        return pl.BlockSpec((tok, pair * HD), lambda h, r: (0, jnp.clip(h - i * per, 0, per - 1)))
+        return pl.BlockSpec((tok, HD), lambda h, r: (0, jnp.clip(h - i * per, 0, per - 1)))
 
     return pl.pallas_call(
-        functools.partial(attend_kernel, parts, chunks, pair),
+        functools.partial(attend_kernel, parts, chunks),
         grid_spec=pltpu.PrefetchScalarGridSpec(
             num_scalar_prefetch=1,
             grid=(chunks * per,),
             in_specs=[query_spec(i) for i in range(chunks)]
             + [pl.BlockSpec((tok, 2 * HD), lambda h, r: (0, 0)) for _ in pieces],
-            out_specs=pl.BlockSpec((tok, pair * HD), lambda h, r: (0, h)),
+            out_specs=pl.BlockSpec((tok, HD), lambda h, r: (0, h)),
             scratch_shapes=[
-                pltpu.VMEM((tok, pair * HD), jnp.bfloat16),
+                pltpu.VMEM((tok, HD), jnp.bfloat16),
+                pltpu.VMEM((parts, tok, HD), jnp.bfloat16),
                 pltpu.VMEM((parts, HD, tok), jnp.bfloat16),
-                pltpu.VMEM((pair, 1, tok), jnp.float32),
-                pltpu.VMEM((pair, 1, tok), jnp.float32),
-                pltpu.VMEM((pair, HD, tok), jnp.float32),
+                pltpu.VMEM((1, tok), jnp.float32),
+                pltpu.VMEM((1, tok), jnp.float32),
+                pltpu.VMEM((HD, tok), jnp.float32),
             ],
         ),
         out_shape=jax.ShapeDtypeStruct((tok, chunks * cols), jnp.bfloat16),
         compiler_params=pltpu.CompilerParams(
-            dimension_semantics=("arbitrary",), vmem_limit_bytes=18 * MIB
+            dimension_semantics=("arbitrary",), vmem_limit_bytes=24 * MIB
         ),
         cost_estimate=SHORT,
     )(r.reshape(1), *queries, *pieces)
@@ -267,19 +265,20 @@
 
 def finish_kernel(slots, per, count, r_ref, first_ref, second_ref, *refs):
     weights, (*old, o_ref, w_buf, acc, sems) = take(refs, count)
-    steps = []
+    rights = []
     depth = first_ref.shape[2]
     rows = depth + second_ref.shape[2]
     for k in range(*slots):
-        for g, panel_ref in enumerate((first_ref, second_ref)):
+        for g in range(2):
             at = pl.ds(k % per * rows + g * depth, depth)
             if len(weights[0].shape) == 3:
                 right = weights[0].at[jnp.bitwise_xor(r_ref[0], k // per), at, :]
             else:
                 right = weights[k // per].at[at, :]
-            steps.append((functools.partial(panel_ref.__getitem__, k), [right]))
+            rights.append([right])
     acc[...] = old[0][...] if old else jnp.zeros_like(acc)
-    multiply(steps, w_buf, acc, sems)
+    lefts = [ref.at[pl.ds(slots[0], slots[1] - slots[0])] for ref in (first_ref, second_ref)]
+    multiply(lefts, rights, w_buf, acc, sems)
     o_ref[...] = acc[...].astype(o_ref.dtype)
 
 
@@ -444,8 +443,8 @@
         panels[1] = put(panels[1], found)
 
     half = n_col // 2
-    total = finish(r, panels, (0, half), o_near, per, jnp.float32, 18)
-    return finish(r, panels, (half, n_col), [o_weights], per, jnp.bfloat16, 44, total)
+    total = finish(r, panels, (0, half), o_near, per, jnp.float32, 52)
+    return finish(r, panels, (half, n_col), [o_weights], per, jnp.bfloat16, 52, total)
 
 
 def solution(mesh):

time: 284 us -> 290 us (1.021)
  Pallas kernels: 69.6 us -> 77.1 us
  local copies, waits for them, and re-layouts: 19.9 us -> 24 us
  waiting for transfers between devices: 120 us -> 116 us
    pallas_call x2, Pallas kernels: 15 us -> 23.1 us  [finish(): pl.pallas_call(functools.partial(finish_kernel, slots, per, len(weights))...]
    dynamic_update_slice x18, local copies, waits for them, and re-layouts: 3.51 us -> 9.75 us  [put(): panel = lax.dynamic_update_slice(panel, piece[None], (slot, first, 0))]
    ppermute x24, waiting for transfers between devices: 91.2 us -> 87.3 us  [hop(): lax.ppermute(s[0], 'col', s[1])]
    pallas_call x4, Pallas kernels: 40.6 us -> 37.4 us  [project(): pl.pallas_call(functools.partial(project_kernel, len(near), len(far), chu...]
    unnamed x40 -> x36, local copies, waits for them, and re-layouts: 10.9 us -> 8.76 us
  transfers between devices with their start and end apart: 43 -> 43, of which waited for: 24 -> 24; matrix products, arithmetic and copies ran while one was open for 13% -> 15% of each run, Pallas kernels for 21% -> 23%
where the time goes in v11:
time: 290 us
  waiting for transfers between devices  116 us (40%)
  Pallas kernels  77.1 us (27%)
  starting transfers between devices  31.5 us (11%)
  other arithmetic  26.9 us (9%)
  local copies, waits for them, and re-layouts  24 us (8%)
  between operations  14.3 us (5%)
    ppermute x24, waiting for transfers between devices, hop(): lax.ppermute(s[0], 'col', s[1])  87.3 us
    pallas_call x4, Pallas kernels, project(): pl.pallas_call(functools.partial(project_kernel, len(near), len(far), chu...  37.4 us
    ppermute x18, waiting for transfers between devices, swap(): lax.ppermute(array, axis, [(i, i ^ mask) for i in range(lax.axis_size(axi...  28.4 us
    ppermute x24, starting transfers between devices, hop(): lax.ppermute(s[0], 'col', s[1])  25.1 us
    pallas_call x2, Pallas kernels, finish(): pl.pallas_call(functools.partial(finish_kernel, slots, per, len(weights))...  23.1 us
    pallas_call x2, Pallas kernels, attend(): pl.pallas_call(functools.partial(attend_kernel, parts, chunks), grid_spec...  16.6 us
    dynamic_update_slice x9, other arithmetic, put(): panel = lax.dynamic_update_slice(panel, piece[None], (slot, first, 0))  16.3 us
    dynamic_update_slice x18, local copies, waits for them, and re-layouts, put(): panel = lax.dynamic_update_slice(panel, piece[None], (slot, first, 0))  9.75 us
  transfers between devices with their start and end apart: 43, of which 24 were waited for; matrix products, arithmetic and copies ran while one was open for 15% of the time, Pallas kernels for 23%

profile of v11, /device:TPU:2, one launch (start us, length us, event | category | flops | bytes accessed | tf_op | source)
XLA Modules:
  0.0 289.5 jit_solution(10032115344858807682)
XLA Ops:
  12.9 2.5 fusion.31
  15.8 2.1 fusion.39
  17.9 3.1 %fusion.38 = (bf16[2048,256]{1,0:T(8,128)(2,1)}, bf16[2048,256]{1,0:T(8,128)(2,1)S(1)}, bf16[2048,256]{1,0:T(8,128)(2,1)S(1)}) fusion(bf16[2048,1024]{1,0:T(8,128)(2,1)} %refs_0_.2), kind=kLoop, calls=%fused_computation.89 | loop fusion | bytes 6291456 | tf_op jit(solution)/shard_map/slice | solution.py:338
  20.9 13.4 %collective-permute-done.2.refs_2_ = bf16[2048,256]{1,0:T(8,128)(2,1)S(1)} collective-permute-done((bf16[2048,256]{1,0:T(8,128)(2,1)S(1)}, bf16[2048,256]{1,0:T(8,128)(2,1)S(1)}, u32[]{:S(2)}, u32[]{:S(2)}) %collective-permute-start.2) | collective-permute-done | bytes 1048608 | tf_op jit(solution)/shard_map/ppermute | solution.py:23
  40.4 2.5 fusion.29
  42.8 2.5 fusion.27
  45.3 12.8 %collective-permute-done.3 = bf16[512,1024]{1,0:T(8,128)(2,1)S(1)} collective-permute-done((bf16[512,1024]{1,0:T(8,128)(2,1)}, bf16[512,1024]{1,0:T(8,128)(2,1)S(1)}, u32[]{:S(2)}, u32[]{:S(2)}) %collective-permute-start.3) | collective-permute-done | bytes 1048608 | tf_op jit(solution)/shard_map/ppermute | solution.py:95
  65.6 16.5 %collective-permute-done.6 = bf16[512,1024]{1,0:T(8,128)(2,1)S(1)} collective-permute-done((bf16[512,1024]{1,0:T(8,128)(2,1)S(1)}, bf16[512,1024]{1,0:T(8,128)(2,1)S(1)}, u32[]{:S(2)}, u32[]{:S(2)}) %collective-permute-start.6) | collective-permute-done | bytes 1048608 | tf_op jit(solution)/shard_map/ppermute | solution.py:95
  90.0 8.3 %collective-permute-done.10 = bf16[256,1024]{1,0:T(8,128)(2,1)} collective-permute-done((bf16[256,1024]{1,0:T(8,128)(2,1)S(1)}, bf16[256,1024]{1,0:T(8,128)(2,1)}, u32[]{:S(2)}, u32[]{:S(2)}) %collective-permute-start.10) | collective-permute-done | bytes 524320 | tf_op jit(solution)/shard_map/ppermute | solution.py:95
  105.5 1.9 fusion.35
  107.6 1.9 fusion.33.panel_ref
  113.3 7.5 %shard_map.65.refs_1_.refs_2_ = bf16[512,256]{1,0:T(8,128)(2,1)S(1)} custom-call(bf16[8,512,1024]{2,1,0:T(8,128)(2,1)} %fusion.33.panel_ref, bf16[2048,256]{1,0:T(8,128)(2,1)S(1)} %copy_bitcast_fusion.refs_0_, bf16[2048,256]{1,0:T(8,128)(2,1)S(1)} %copy-done.11, bf16[2048,256]{1,0:T(8,128)(2,1)S(1)} %copy-done.7, bf16[2048,256]{1,0:T(8,128)(2,1)S(1)} %copy-done.9, ...), custom_call_target="tpu_custom_call" | custom-call | flops 1 | bytes 1 | tf_op jit(solution)/shard_map/pallas_call | solution.py:169
  122.4 10.8 %shard_map.66.refs_0_ = bf16[512,512]{1,0:T(8,128)(2,1)S(1)} custom-call(bf16[8,512,1024]{2,1,0:T(8,128)(2,1)} %fusion.33.panel_ref, bf16[2048,1024]{1,0:T(8,128)(2,1)} %refs_0_.2, bf16[2048,1024]{1,0:T(8,128)(2,1)} %collective-permute-done.15.refs_1_, bf16[2048,256]{1,0:T(8,128)(2,1)S(1)} %collective-permute-done.5.refs_2_, ...), custom_call_target="tpu_custom_call" | custom-call | flops 1 | bytes 1 | tf_op jit(solution)/shard_map/pallas_call | solution.py:169
  136.3 8.3 %shard_map.67 = bf16[512,512]{1,0:T(8,128)(2,1)S(1)} custom-call(s32[1]{0:T(128)} %bitcast.r_ref, bf16[512,512]{1,0:T(8,128)(2,1)S(1)} %shard_map.66.refs_0_, bf16[512,256]{1,0:T(8,128)(2,1)S(1)} %shard_map.65.refs_1_.refs_2_, bf16[512,256]{1,0:T(8,128)(2,1)S(1)} %copy-done.1, bf16[512,256]{1,0:T(8,128)(2,1)S(1)} %collective-permute-done.14.refs_3_.refs_4_, ...), custom_call_target="tpu_custom_call" | custom-call | flops 1 | bytes 1 | tf_op jit(solution)/shard_map/pallas_call | solution.py:241
  147.5 10.4 %shard_map.70.refs_0_ = bf16[512,256]{1,0:T(8,128)(2,1)S(1)} custom-call(bf16[8,512,1024]{2,1,0:T(8,128)(2,1)} %fusion.33.panel_ref, bf16[2048,1024]{1,0:T(8,128)(2,1)} %refs_0_.2, bf16[2048,1024]{1,0:T(8,128)(2,1)} %collective-permute-done.15.refs_1_, bf16[2048,128]{1,0:T(8,128)(2,1)} %collective-permute-done.11.refs_2_, ...), custom_call_target="tpu_custom_call" | custom-call | flops 1 | bytes 1 | tf_op jit(solution)/shard_map/pallas_call | solution.py:169
  159.1 12.6 %collective-permute-done.23.refs_2_ = bf16[2048,256]{1,0:T(8,128)(2,1)S(1)} collective-permute-done((bf16[2048,256]{1,0:T(8,128)(2,1)}, bf16[2048,256]{1,0:T(8,128)(2,1)S(1)}, u32[]{:S(2)}, u32[]{:S(2)}) %collective-permute-start.23) | collective-permute-done | bytes 1048608 | tf_op jit(solution)/shard_map/ppermute | solution.py:23
  173.8 1.9 bitcast_dynamic-update-slice_fusion.12
  175.7 1.9 bitcast_dynamic-update-slice_fusion.11
  177.6 8.7 %shard_map.71.refs_1_ = bf16[512,256]{1,0:T(8,128)(2,1)S(1)} custom-call(bf16[8,512,1024]{2,1,0:T(8,128)(2,1)} %fusion.33.panel_ref, bf16[2048,1024]{1,0:T(8,128)(2,1)} %refs_0_.2, bf16[2048,1024]{1,0:T(8,128)(2,1)} %collective-permute-done.15.refs_1_, bf16[2048,256]{1,0:T(8,128)(2,1)S(1)} %collective-permute-done.23.refs_2_, ...), custom_call_target="tpu_custom_call" | custom-call | flops 1 | bytes 1 | tf_op jit(solution)/shard_map/pallas_call | solution.py:169
  188.5 8.4 %shard_map.72 = bf16[512,512]{1,0:T(8,128)(2,1)S(1)} custom-call(s32[1]{0:T(128)} %bitcast.r_ref, bf16[512,256]{1,0:T(8,128)(2,1)S(1)} %shard_map.70.refs_0_, bf16[512,256]{1,0:T(8,128)(2,1)S(1)} %shard_map.71.refs_1_, bf16[512,256]{1,0:T(8,128)(2,1)S(1)} %shard_map.65.refs_1_.refs_2_, bf16[512,256]{1,0:T(8,128)(2,1)S(1)} %copy-done.2, ...), custom_call_target="tpu_custom_call" | custom-call | flops 1 | bytes 1 | tf_op jit(solution)/shard_map/pallas_call | solution.py:241
  198.5 2.2 collective-permute-done.29
  208.0 13.0 %collective-permute-done.32 = bf16[256,512]{1,0:T(8,128)(2,1)S(1)} collective-permute-done((bf16[256,512]{1,0:T(8,128)(2,1)S(1)}, bf16[256,512]{1,0:T(8,128)(2,1)S(1)}, u32[]{:S(2)}, u32[]{:S(2)}) %collective-permute-start.32) | collective-permute-done | bytes 262176 | tf_op jit(solution)/shard_map/ppermute | solution.py:95
  224.8 9.4 %collective-permute-done.36 = bf16[512,512]{1,0:T(8,128)(2,1)S(1)} collective-permute-done((bf16[512,512]{1,0:T(8,128)(2,1)S(1)}, bf16[512,512]{1,0:T(8,128)(2,1)S(1)}, u32[]{:S(2)}, u32[]{:S(2)}) %collective-permute-start.36) | collective-permute-done | bytes 524320 | tf_op jit(solution)/shard_map/ppermute | solution.py:95
  235.6 1.9 collective-permute-start.38
  238.5 8.3 %collective-permute-done.38 = bf16[512,512]{1,0:T(8,128)(2,1)S(1)} collective-permute-done((bf16[512,512]{1,0:T(8,128)(2,1)S(1)}, bf16[512,512]{1,0:T(8,128)(2,1)S(1)}, u32[]{:S(2)}, u32[]{:S(2)}) %collective-permute-start.38) | collective-permute-done | bytes 524320 | tf_op jit(solution)/shard_map/ppermute | solution.py:95
  246.8 2.3 collective-permute-done.39
  249.2 1.8 collective-permute-start.40
  251.4 4.2 %collective-permute-done.40 = bf16[256,512]{1,0:T(8,128)(2,1)S(1)} collective-permute-done((bf16[256,512]{1,0:T(8,128)(2,1)S(1)}, bf16[256,512]{1,0:T(8,128)(2,1)S(1)}, u32[]{:S(2)}, u32[]{:S(2)}) %collective-permute-start.40) | collective-permute-done | bytes 262176 | tf_op jit(solution)/shard_map/ppermute | solution.py:95
  255.6 1.8 collective-permute-done.41
  257.5 2.0 copy-done.13
  259.5 11.5 %shard_map.73.refs_1_ = f32[512,1024]{1,0:T(8,128)} custom-call(s32[1]{0:T(128)} %bitcast.r_ref, bf16[8,512,512]{2,1,0:T(8,128)(2,1)} %bitcast_dynamic-update-slice_fusion.16.first_ref, bf16[8,512,512]{2,1,0:T(8,128)(2,1)} %copy-done.13, bf16[2048,1024]{1,0:T(8,128)(2,1)} %refs_0_.3, bf16[2048,1024]{1,0:T(8,128)(2,1)} %copy-done.15), custom_call_target="tpu_custom_call" | custom-call | flops 1 | bytes 1 | tf_op jit(solution)/shard_map/pallas_call | solution.py:292
  271.0 11.7 %shard_map.74 = bf16[512,1024]{1,0:T(8,128)(2,1)} custom-call(s32[1]{0:T(128)} %bitcast.r_ref, bf16[8,512,512]{2,1,0:T(8,128)(2,1)} %bitcast_dynamic-update-slice_fusion.16.first_ref, bf16[8,512,512]{2,1,0:T(8,128)(2,1)} %copy-done.13, bf16[4,2048,1024]{2,1,0:T(8,128)(2,1)} %bitcast.83, f32[512,1024]{1,0:T(8,128)} %shard_map.73.refs_1_), custom_call_target="tpu_custom_call" | custom-call | flops 1 | bytes 1 | tf_op jit(solution)/shard_map/pallas_call | solution.py:292
  (161 shorter events, 67.3 us)
Async XLA Ops:
  6.5 264.4 %all-gather.3.cloned.1.call-start = ((), (), s32[]{:S(2)}) async-start(), calls=%async_computation | async-start | bytes 20971520 | tf_op jit(solution)/shard_map/all_gather | solution.py:415
  6.5 27.8 %collective-permute-start = (bf16[512,1024]{1,0:T(8,128)(2,1)}, bf16[512,1024]{1,0:T(8,128)(2,1)}, u32[]{:S(2)}, u32[]{:S(2)}) collective-permute-start(bf16[512,1024]{1,0:T(8,128)(2,1)} %param.6), channel_id=1, source_target_pairs={{0,2},{2,4},{4,6},{6,7},{7,5},{5,3},{3,1},{1,0},{8,10},{10,12},{12... | collective-permute-start | bytes 3145736 | tf_op jit(solution)/shard_map/ppermute | solution.py:95
  8.1 26.2 %collective-permute-start.1 = (bf16[512,1024]{1,0:T(8,128)(2,1)}, bf16[512,1024]{1,0:T(8,128)(2,1)}, u32[]{:S(2)}, u32[]{:S(2)}) collective-permute-start(bf16[512,1024]{1,0:T(8,128)(2,1)} %param.6), channel_id=1, source_target_pairs={{2,0},{4,2},{6,4},{7,6},{5,7},{3,5},{1,3},{0,1},{10,8},{12,10},{14... | collective-permute-start | bytes 3145736 | tf_op jit(solution)/shard_map/ppermute | solution.py:95
  9.9 24.4 %collective-permute-start.2 = (bf16[2048,256]{1,0:T(8,128)(2,1)S(1)}, bf16[2048,256]{1,0:T(8,128)(2,1)S(1)}, u32[]{:S(2)}, u32[]{:S(2)}) collective-permute-start(bf16[2048,256]{1,0:T(8,128)(2,1)S(1)} %copy_bitcast_fusion.refs_0_), channel_id=1, source_target_pairs={{0,16},{8,24},{16,0},{24,8},{1,17},{9,25},{17,1},{25,9},{2,18},{10... | collective-permute-start | bytes 3145736 | tf_op jit(solution)/shard_map/ppermute | solution.py:23
  34.3 23.8 %collective-permute-start.3 = (bf16[512,1024]{1,0:T(8,128)(2,1)}, bf16[512,1024]{1,0:T(8,128)(2,1)S(1)}, u32[]{:S(2)}, u32[]{:S(2)}) collective-permute-start(bf16[512,1024]{1,0:T(8,128)(2,1)} %collective-permute-done), channel_id=1, source_target_pairs={{0,2},{2,4},{4,6},{6,7},{7,5},{5,3},{3,1},{1,0},{8,10},{10,12},{12... | collective-permute-start | bytes 3145736 | tf_op jit(solution)/shard_map/ppermute | solution.py:95
  35.9 23.4 %collective-permute-start.4 = (bf16[512,1024]{1,0:T(8,128)(2,1)}, bf16[512,1024]{1,0:T(8,128)(2,1)S(1)}, u32[]{:S(2)}, u32[]{:S(2)}) collective-permute-start(bf16[512,1024]{1,0:T(8,128)(2,1)} %collective-permute-done.1), channel_id=1, source_target_pairs={{2,0},{4,2},{6,4},{7,6},{5,7},{3,5},{1,3},{0,1},{10,8},{12,10},{14... | collective-permute-start | bytes 3145736 | tf_op jit(solution)/shard_map/ppermute | solution.py:95
  36.8 23.1 %collective-permute-start.5 = (bf16[2048,256]{1,0:T(8,128)(2,1)S(1)}, bf16[2048,256]{1,0:T(8,128)(2,1)S(1)}, u32[]{:S(2)}, u32[]{:S(2)}) collective-permute-start(bf16[2048,256]{1,0:T(8,128)(2,1)S(1)} %get-tuple-element.98), channel_id=1, source_target_pairs={{0,16},{8,24},{16,0},{24,8},{1,17},{9,25},{17,1},{25,9},{2,18},{10... | collective-permute-start | bytes 3145736 | tf_op jit(solution)/shard_map/ppermute | solution.py:23
  59.9 22.2 %collective-permute-start.6 = (bf16[512,1024]{1,0:T(8,128)(2,1)S(1)}, bf16[512,1024]{1,0:T(8,128)(2,1)S(1)}, u32[]{:S(2)}, u32[]{:S(2)}) collective-permute-start(bf16[512,1024]{1,0:T(8,128)(2,1)S(1)} %collective-permute-done.3), channel_id=1, source_target_pairs={{0,2},{2,4},{4,6},{6,7},{7,5},{5,3},{3,1},{1,0},{8,10},{10,12},{12... | collective-permute-start | bytes 3145736 | tf_op jit(solution)/shard_map/ppermute | solution.py:95
  61.0 22.0 %collective-permute-start.7 = (bf16[512,1024]{1,0:T(8,128)(2,1)S(1)}, bf16[512,1024]{1,0:T(8,128)(2,1)S(1)}, u32[]{:S(2)}, u32[]{:S(2)}) collective-permute-start(bf16[512,1024]{1,0:T(8,128)(2,1)S(1)} %collective-permute-done.4), channel_id=1, source_target_pairs={{2,0},{4,2},{6,4},{7,6},{5,7},{3,5},{1,3},{0,1},{10,8},{12,10},{14... | collective-permute-start | bytes 3145736 | tf_op jit(solution)/shard_map/ppermute | solution.py:95
  62.0 21.8 %collective-permute-start.8 = (bf16[2048,256]{1,0:T(8,128)(2,1)S(1)}, bf16[2048,256]{1,0:T(8,128)(2,1)}, u32[]{:S(2)}, u32[]{:S(2)}) collective-permute-start(bf16[2048,256]{1,0:T(8,128)(2,1)S(1)} %get-tuple-element.106), channel_id=1, source_target_pairs={{0,16},{8,24},{16,0},{24,8},{1,17},{9,25},{17,1},{25,9},{2,18},{10... | collective-permute-start | bytes 3145736 | tf_op jit(solution)/shard_map/ppermute | solution.py:23
  83.8 16.1 %collective-permute-start.13 = (bf16[2048,256]{1,0:T(8,128)(2,1)S(1)}, bf16[2048,256]{1,0:T(8,128)(2,1)S(1)}, u32[]{:S(2)}, u32[]{:S(2)}) collective-permute-start(bf16[2048,256]{1,0:T(8,128)(2,1)S(1)} %copy-done.6), channel_id=1, source_target_pairs={{0,8},{8,0},{16,24},{24,16},{1,9},{9,1},{17,25},{25,17},{2,10},{10... | collective-permute-start | bytes 3145736 | tf_op jit(solution)/shard_map/ppermute | solution.py:23
  83.8 17.1 %collective-permute-start.12 = (bf16[2048,256]{1,0:T(8,128)(2,1)S(1)}, bf16[2048,256]{1,0:T(8,128)(2,1)S(1)}, u32[]{:S(2)}, u32[]{:S(2)}) collective-permute-start(bf16[2048,256]{1,0:T(8,128)(2,1)S(1)} %copy_bitcast_fusion.refs_0_), channel_id=1, source_target_pairs={{0,8},{8,0},{16,24},{24,16},{1,9},{9,1},{17,25},{25,17},{2,10},{10... | collective-permute-start | bytes 3145736 | tf_op jit(solution)/shard_map/ppermute | solution.py:23
  84.3 14.0 %collective-permute-start.10 = (bf16[256,1024]{1,0:T(8,128)(2,1)S(1)}, bf16[256,1024]{1,0:T(8,128)(2,1)}, u32[]{:S(2)}, u32[]{:S(2)}) collective-permute-start(bf16[256,1024]{1,0:T(8,128)(2,1)S(1)} %slice.89), channel_id=1, source_target_pairs={{2,0},{4,2},{6,4},{7,6},{5,7},{3,5},{1,3},{0,1},{10,8},{12,10},{14... | collective-permute-start | bytes 1572872 | tf_op jit(solution)/shard_map/ppermute | solution.py:95
  86.0 13.7 %collective-permute-start.9 = (bf16[256,1024]{1,0:T(8,128)(2,1)S(1)}, bf16[256,1024]{1,0:T(8,128)(2,1)S(1)}, u32[]{:S(2)}, u32[]{:S(2)}) collective-permute-start(bf16[256,1024]{1,0:T(8,128)(2,1)S(1)} %slice.88), channel_id=1, source_target_pairs={{0,2},{2,4},{4,6},{6,7},{7,5},{5,3},{3,1},{1,0},{8,10},{10,12},{12... | collective-permute-start | bytes 1572872 | tf_op jit(solution)/shard_map/ppermute | solution.py:95
  86.5 13.5 %collective-permute-start.11 = (bf16[2048,128]{1,0:T(8,128)(2,1)S(1)}, bf16[2048,128]{1,0:T(8,128)(2,1)}, u32[]{:S(2)}, u32[]{:S(2)}) collective-permute-start(bf16[2048,128]{1,0:T(8,128)(2,1)S(1)} %get-tuple-element.114), channel_id=1, source_target_pairs={{0,16},{8,24},{16,0},{24,8},{1,17},{9,25},{17,1},{25,9},{2,18},{10... | collective-permute-start | bytes 1572872 | tf_op jit(solution)/shard_map/ppermute | solution.py:23
  101.9 20.5 %collective-permute-start.15 = (bf16[2048,1024]{1,0:T(8,128)(2,1)}, bf16[2048,1024]{1,0:T(8,128)(2,1)}, u32[]{:S(2)}, u32[]{:S(2)}) collective-permute-start(bf16[2048,1024]{1,0:T(8,128)(2,1)} %refs_0_.2), channel_id=1, source_target_pairs={{0,8},{8,0},{16,24},{24,16},{1,9},{9,1},{17,25},{25,17},{2,10},{10... | collective-permute-start | bytes 12582920 | tf_op jit(solution)/shard_map/ppermute | solution.py:23
  101.9 20.5 %collective-permute-start.17 = (bf16[2048,256]{1,0:T(8,128)(2,1)}, bf16[2048,256]{1,0:T(8,128)(2,1)}, u32[]{:S(2)}, u32[]{:S(2)}) collective-permute-start(bf16[2048,256]{1,0:T(8,128)(2,1)} %collective-permute-done.8.refs_3_), channel_id=1, source_target_pairs={{0,8},{8,0},{16,24},{24,16},{1,9},{9,1},{17,25},{25,17},{2,10},{10... | collective-permute-start | bytes 3145736 | tf_op jit(solution)/shard_map/ppermute | solution.py:23
  102.4 20.0 %collective-permute-start.16 = (bf16[2048,256]{1,0:T(8,128)(2,1)S(1)}, bf16[2048,256]{1,0:T(8,128)(2,1)}, u32[]{:S(2)}, u32[]{:S(2)}) collective-permute-start(bf16[2048,256]{1,0:T(8,128)(2,1)S(1)} %collective-permute-done.5.refs_2_), channel_id=1, source_target_pairs={{0,8},{8,0},{16,24},{24,16},{1,9},{9,1},{17,25},{25,17},{2,10},{10... | collective-permute-start | bytes 3145736 | tf_op jit(solution)/shard_map/ppermute | solution.py:23
  103.7 29.6 %collective-permute-start.19 = (bf16[2048,128]{1,0:T(8,128)(2,1)}, bf16[2048,128]{1,0:T(8,128)(2,1)}, u32[]{:S(2)}, u32[]{:S(2)}) collective-permute-start(bf16[2048,128]{1,0:T(8,128)(2,1)} %get-tuple-element.135), channel_id=1, source_target_pairs={{0,16},{8,24},{16,0},{24,8},{1,17},{9,25},{17,1},{25,9},{2,18},{10... | collective-permute-start | bytes 1572872 | tf_op jit(solution)/shard_map/ppermute | solution.py:23
  133.3 38.5 %collective-permute-start.23 = (bf16[2048,256]{1,0:T(8,128)(2,1)}, bf16[2048,256]{1,0:T(8,128)(2,1)S(1)}, u32[]{:S(2)}, u32[]{:S(2)}) collective-permute-start(bf16[2048,256]{1,0:T(8,128)(2,1)} %get-tuple-element.140), channel_id=1, source_target_pairs={{0,16},{8,24},{16,0},{24,8},{1,17},{9,25},{17,1},{25,9},{2,18},{10... | collective-permute-start | bytes 3145736 | tf_op jit(solution)/shard_map/ppermute | solution.py:23
  134.0 13.6 %collective-permute-start.24 = (bf16[2048,128]{1,0:T(8,128)(2,1)}, bf16[2048,128]{1,0:T(8,128)(2,1)}, u32[]{:S(2)}, u32[]{:S(2)}) collective-permute-start(bf16[2048,128]{1,0:T(8,128)(2,1)} %collective-permute-done.11.refs_2_), channel_id=1, source_target_pairs={{0,8},{8,0},{16,24},{24,16},{1,9},{9,1},{17,25},{25,17},{2,10},{10... | collective-permute-start | bytes 1572872 | tf_op jit(solution)/shard_map/ppermute | solution.py:23
  144.6 13.3 %collective-permute-start.21 = (bf16[512,512]{1,0:T(8,128)(2,1)S(1)}, bf16[512,512]{1,0:T(8,128)(2,1)}, u32[]{:S(2)}, u32[]{:S(2)}) collective-permute-start(bf16[512,512]{1,0:T(8,128)(2,1)S(1)} %shard_map.67), channel_id=1, source_target_pairs={{0,2},{2,4},{4,6},{6,7},{7,5},{5,3},{3,1},{1,0},{8,10},{10,12},{12... | collective-permute-start | bytes 1572872 | tf_op jit(solution)/shard_map/ppermute | solution.py:95
  145.8 13.3 %collective-permute-start.22 = (bf16[512,512]{1,0:T(8,128)(2,1)S(1)}, bf16[512,512]{1,0:T(8,128)(2,1)}, u32[]{:S(2)}, u32[]{:S(2)}) collective-permute-start(bf16[512,512]{1,0:T(8,128)(2,1)S(1)} %shard_map.67), channel_id=1, source_target_pairs={{2,0},{4,2},{6,4},{7,6},{5,7},{3,5},{1,3},{0,1},{10,8},{12,10},{14... | collective-permute-start | bytes 1572872 | tf_op jit(solution)/shard_map/ppermute | solution.py:95
  171.7 14.5 %collective-permute-start.26 = (bf16[512,512]{1,0:T(8,128)(2,1)}, bf16[512,512]{1,0:T(8,128)(2,1)S(1)}, u32[]{:S(2)}, u32[]{:S(2)}) collective-permute-start(bf16[512,512]{1,0:T(8,128)(2,1)} %collective-permute-done.21), channel_id=1, source_target_pairs={{0,2},{2,4},{4,6},{6,7},{7,5},{5,3},{3,1},{1,0},{8,10},{10,12},{12... | collective-permute-start | bytes 1572872 | tf_op jit(solution)/shard_map/ppermute | solution.py:95
  172.1 14.3 %collective-permute-start.27 = (bf16[512,512]{1,0:T(8,128)(2,1)}, bf16[512,512]{1,0:T(8,128)(2,1)S(1)}, u32[]{:S(2)}, u32[]{:S(2)}) collective-permute-start(bf16[512,512]{1,0:T(8,128)(2,1)} %collective-permute-done.22), channel_id=1, source_target_pairs={{2,0},{4,2},{6,4},{7,6},{5,7},{3,5},{1,3},{0,1},{10,8},{12,10},{14... | collective-permute-start | bytes 1572872 | tf_op jit(solution)/shard_map/ppermute | solution.py:95
  186.4 15.7 %collective-permute-start.31 = (bf16[2048,1024]{1,0:T(8,128)(2,1)S(1)}, bf16[2048,1024]{1,0:T(8,128)(2,1)S(1)}, u32[]{:S(2)}, u32[]{:S(2)}) collective-permute-start(bf16[2048,1024]{1,0:T(8,128)(2,1)S(1)} %copy-done.14), channel_id=1, source_target_pairs={{0,8},{8,0},{16,24},{24,16},{1,9},{9,1},{17,25},{25,17},{2,10},{10... | collective-permute-start | bytes 12582920 | tf_op jit(solution)/shard_map/ppermute | solution.py:23
  186.4 14.3 %collective-permute-start.29 = (bf16[512,512]{1,0:T(8,128)(2,1)S(1)}, bf16[512,512]{1,0:T(8,128)(2,1)S(1)}, u32[]{:S(2)}, u32[]{:S(2)}) collective-permute-start(bf16[512,512]{1,0:T(8,128)(2,1)S(1)} %collective-permute-done.26), channel_id=1, source_target_pairs={{0,2},{2,4},{4,6},{6,7},{7,5},{5,3},{3,1},{1,0},{8,10},{10,12},{12... | collective-permute-start | bytes 1572872 | tf_op jit(solution)/shard_map/ppermute | solution.py:95
  188.0 14.1 %collective-permute-start.30 = (bf16[512,512]{1,0:T(8,128)(2,1)S(1)}, bf16[512,512]{1,0:T(8,128)(2,1)S(1)}, u32[]{:S(2)}, u32[]{:S(2)}) collective-permute-start(bf16[512,512]{1,0:T(8,128)(2,1)S(1)} %collective-permute-done.27), channel_id=1, source_target_pairs={{2,0},{4,2},{6,4},{7,6},{5,7},{3,5},{1,3},{0,1},{10,8},{12,10},{14... | collective-permute-start | bytes 1572872 | tf_op jit(solution)/shard_map/ppermute | solution.py:95
  202.1 19.8 %collective-permute-start.34 = (bf16[512,512]{1,0:T(8,128)(2,1)S(1)}, bf16[512,512]{1,0:T(8,128)(2,1)S(1)}, u32[]{:S(2)}, u32[]{:S(2)}) collective-permute-start(bf16[512,512]{1,0:T(8,128)(2,1)S(1)} %shard_map.72), channel_id=1, source_target_pairs={{0,2},{2,4},{4,6},{6,7},{7,5},{5,3},{3,1},{1,0},{8,10},{10,12},{12... | collective-permute-start | bytes 1572872 | tf_op jit(solution)/shard_map/ppermute | solution.py:95
  203.2 18.7 %collective-permute-start.35 = (bf16[512,512]{1,0:T(8,128)(2,1)S(1)}, bf16[512,512]{1,0:T(8,128)(2,1)S(1)}, u32[]{:S(2)}, u32[]{:S(2)}) collective-permute-start(bf16[512,512]{1,0:T(8,128)(2,1)S(1)} %shard_map.72), channel_id=1, source_target_pairs={{2,0},{4,2},{6,4},{7,6},{5,7},{3,5},{1,3},{0,1},{10,8},{12,10},{14... | collective-permute-start | bytes 1572872 | tf_op jit(solution)/shard_map/ppermute | solution.py:95
  204.2 16.9 %collective-permute-start.32 = (bf16[256,512]{1,0:T(8,128)(2,1)S(1)}, bf16[256,512]{1,0:T(8,128)(2,1)S(1)}, u32[]{:S(2)}, u32[]{:S(2)}) collective-permute-start(bf16[256,512]{1,0:T(8,128)(2,1)S(1)} %slice.96), channel_id=1, source_target_pairs={{0,2},{2,4},{4,6},{6,7},{7,5},{5,3},{3,1},{1,0},{8,10},{10,12},{12... | collective-permute-start | bytes 786440 | tf_op jit(solution)/shard_map/ppermute | solution.py:95
  205.4 16.5 %collective-permute-start.33 = (bf16[256,512]{1,0:T(8,128)(2,1)S(1)}, bf16[256,512]{1,0:T(8,128)(2,1)S(1)}, u32[]{:S(2)}, u32[]{:S(2)}) collective-permute-start(bf16[256,512]{1,0:T(8,128)(2,1)S(1)} %slice.97), channel_id=1, source_target_pairs={{2,0},{4,2},{6,4},{7,6},{5,7},{3,5},{1,3},{0,1},{10,8},{12,10},{14... | collective-permute-start | bytes 786440 | tf_op jit(solution)/shard_map/ppermute | solution.py:95
  (29 other events, 252.8 us)
Sparse Core Ops, SparseCore 0:
  133.4 117.7 all-gather.2

commit v12 on v9

--- a/solution.py
+++ b/solution.py
@@ -275,35 +275,37 @@
     )(r.reshape(1), *queries, *pieces)
 
 
-def finish_kernel(slots, per, count, r_ref, first_ref, second_ref, *refs):
-    weights, (*old, o_ref, a_buf, w_buf, acc, a_sem, w_sem) = take(refs, count)
-    steps = []
-    depth = first_ref.shape[2]
-    rows = depth + second_ref.shape[2]
-    for k in range(*slots):
-        for g, panel_ref in enumerate((first_ref, second_ref)):
-            at = pl.ds(k % per * rows + g * depth, depth)
-            if len(weights[0].shape) == 3:
-                right = weights[0].at[jnp.bitwise_xor(r_ref[0], k // per), at, :]
-            else:
-                right = weights[k // per].at[at, :]
-            steps.append((panel_ref.at[k], [[right]]))
+def finish_kernel(steps, per, rows, n_panels, near, others, r_ref, *refs):
+    panels, near_refs, rest = take(refs, n_panels, near)
+    gathered, (*old, o_ref, a_buf, w_buf, acc, a_sem, w_sem) = take(rest, others)
+    depth = a_buf.shape[2]
+    plan = []
+    for g, k in steps:
+        at = pl.ds(k % per * rows + g * depth, depth)
+        if k // per < near:
+            right = near_refs[k // per].at[at, :]
+        else:
+            right = gathered[0].at[jnp.bitwise_xor(r_ref[0], k // per), at, :]
+        plan.append((panels[g].at[k], [[right]]))
     acc[...] = old[0][...] if old else jnp.zeros_like(acc)
-    multiply(steps, a_buf, [w_buf], [acc], a_sem, w_sem)
+    multiply(plan, a_buf, [w_buf], [acc], a_sem, w_sem)
     o_ref[...] = acc[...].astype(o_ref.dtype)
 
 
-def finish(r, panels, slots, weights, per, dtype, total=None):
+def finish(r, panels, steps, near, gathered, per, rows, dtype, total=None):
     _, tok, wide = panels[0].shape
-    cols = weights[0].shape[-1]
-    count = 2 * (slots[1] - slots[0])
+    cols = near[0].shape[1]
+    count = len(steps)
+    others = [] if gathered is None else [gathered]
+    old = [] if total is None else [total]
     hbm = pl.BlockSpec(memory_space=pl.ANY)
     vmem = pl.BlockSpec(memory_space=pltpu.VMEM)
-    old = [] if total is None else [total]
     return pl.pallas_call(
-        functools.partial(finish_kernel, slots, per, len(weights)),
+        functools.partial(
+            finish_kernel, steps, per, rows, len(panels), len(near), len(others)
+        ),
         in_specs=[pl.BlockSpec(memory_space=pltpu.SMEM)]
-        + [hbm] * (2 + len(weights))
+        + [hbm] * (len(panels) + len(near) + len(others))
         + [vmem] * len(old),
         out_specs=vmem,
         out_shape=jax.ShapeDtypeStruct((tok, cols), dtype),
@@ -316,7 +318,7 @@
         ],
         compiler_params=pltpu.CompilerParams(vmem_limit_bytes=60 * MIB),
         cost_estimate=SHORT,
-    )(r.reshape(1), *panels, *weights, *old)
+    )(r.reshape(1), *panels, *near, *others, *old)
 
 
 def per_device(hidden, norm_gain, wq, wk, wv, wo):
@@ -339,9 +341,8 @@
     first_heads = n_heads // 2
     late_heads = n_heads - first_heads
     if n_heads >= 4:
-        quarter = late_heads // 2
         sizes = [first_heads // 2, first_heads - first_heads // 2]
-        sizes += [n for n in (quarter // 2, quarter - quarter // 2, late_heads - quarter) if n > 0]
+        sizes += [n for n in (late_heads // 4, late_heads - late_heads // 4) if n > 0]
     else:
         sizes = [first_heads, late_heads]
     early = 2 if n_heads >= 4 else 1
@@ -392,7 +393,7 @@
         last_hop = i == hops - 1
         tie = ring.last[0][1]
         sent = [] if x_sent is None else [x_sent]
-        ahead = chunks[i : i + 1] if i < len(sizes) - 1 else []
+        ahead = chunks[i : i + 1]
         beside = [panel, *squares, cosine, sine, *sent, *ahead]
         if last_hop:
             near = gather_near(after(stacked, tie))
@@ -415,48 +416,43 @@
     queries = project(
         panel, q_near, by_block(q_far[:early]), 0, first_heads, factor, scale, cosine, sine
     )
-    beside = [exchange(kv), queries, chunks[-1], *gather_near(kv)]
+    beside = [exchange(kv), queries, *gather_near(kv)]
     if x_sent is not None:
         beside.append(x_sent)
-    kv_other, queries, last_chunk, *beside = lax.optimization_barrier(tuple(beside))
+    kv_other, queries, *beside = lax.optimization_barrier(tuple(beside))
     kv_pieces, arrived = take(beside, blocks_near)
     kv_pieces = [*kv_pieces, *gather_near(kv_other)]
-    late_far = [gather_near(piece) for piece in (*got_x[1 + early :], *arrived)]
-    late_far = [list(far) for far in late_far]
-    last_other = exchange(last_chunk)
+    late_far = [list(gather_near(piece)) for piece in (*got_x[1 + early :], *arrived)]
     o_weights = lax.all_gather(after(wo, kv_other), "row")
     heads = attend(r, [queries], kv_pieces)
 
     ring = Ring(heads, 1)
     panels = [put(blank((n_col, tok, wide)), ring.found), blank((n_col, tok, rest))]
-    tables = scale, cosine, sine
-    late, first = [], wide
-    if late_far:
-        late_far = by_block(late_far)
-        late.append(project(panel, q_near, late_far, first, -1, factor, *tables))
-        first += late[0].shape[1]
-    found, (last_other, *rest_of) = ring.hop([last_other, *panels, *late])
-    panels, late = take(rest_of, 2)
+    late = project(
+        panel, q_near, by_block(late_far), wide, -1, factor, scale, cosine, sine
+    )
+    found, (late, *panels) = ring.hop([late, *panels])
     panels[0] = put(panels[0], found)
-    last_far = by_block([gather_near(last_other)])
-    late = [*late, project(panel, q_near, last_far, first, -1, factor, *tables)]
-    found, (panels[0], *late) = ring.hop([panels[0], *late])
-    panels[0] = put(panels[0], found)
-    heads = attend(r, late, kv_pieces)
-    o_near = gather_near(after(wo, late[-1]))
+    heads = attend(r, [late], kv_pieces)
+    o_near = gather_near(after(wo, late))
     found, (heads, panels[0], *o_near) = ring.hop([heads, panels[0], *o_near])
     panels[0] = put(panels[0], found)
     second = Ring(heads, 1)
     panels[1] = put(panels[1], second.found)
+    half = n_col // 2
     for i in range(hops):
         found, (panels[0],) = ring.hop([panels[0]])
         panels[0] = put(panels[0], found)
-        found, (panels[1],) = second.hop([panels[1]])
+        beside = [panels[1]]
+        if i == hops - 1:
+            steps = [(0, k) for k in range(half)]
+            beside.append(finish(r, panels[:1], steps, o_near, None, per, cols, jnp.float32))
+        found, (panels[1], *beside) = second.hop(beside)
         panels[1] = put(panels[1], found)
-
-    half = n_col // 2
-    total = finish(r, panels, (0, half), o_near, per, jnp.float32)
-    return finish(r, panels, (half, n_col), [after(o_weights, total)], per, jnp.bfloat16, total)
+    (total,) = beside
+
+    steps = [(1, k) for k in range(half)] + [(g, k) for k in range(half, n_col) for g in (0, 1)]
+    return finish(r, panels, steps, o_near, o_weights, per, cols, jnp.bfloat16, total)
 
 
 def solution(mesh):

time: 278 us -> 274 us (0.986)
  Pallas kernels: 68.1 us -> 62.7 us
  waiting for transfers between devices: 116 us -> 121 us
  local copies, waits for them, and re-layouts: 29.5 us -> 25.3 us
    ppermute x18 -> x16, waiting for transfers between devices: 27.6 us -> 35.7 us  [swap(): lax.ppermute(array, axis, [(i, i ^ mask) for i in range(lax.axis_size(axi...]
    pallas_call x4 -> x3, Pallas kernels: 35.3 us -> 29.9 us  [project(): pl.pallas_call(functools.partial(project_kernel, len(near), len(far), chu...]
    dynamic_update_slice x18, local copies, waits for them, and re-layouts: 17.8 us -> 14.6 us  [put(): panel = lax.dynamic_update_slice(panel, piece[None], (slot, first, 0))]
    ppermute x24, waiting for transfers between devices: 88 us -> 85.1 us  [hop(): lax.ppermute(s[0], 'col', s[1])]
    slice x2 -> x3, local copies, waits for them, and re-layouts: 5.19 us -> 6.45 us  [per_device(): wq[:, sum(sizes[:i]) * HD:sum(sizes[:i + 1]) * HD]]
    ppermute x18 -> x16, starting transfers between devices: 6.84 us -> 7.04 us  [swap(): lax.ppermute(array, axis, [(i, i ^ mask) for i in range(lax.axis_size(axi...]
  transfers between devices with their start and end apart: 43 -> 41, of which waited for: 26 -> 24; matrix products, arithmetic and copies ran while one was open for 16% -> 15% of each run, Pallas kernels for 21% -> 18%
where the time goes in v12:
time: 274 us; the launch traced here: 273 us
  waiting for transfers between devices  121 us (44%)
  Pallas kernels  62.7 us (23%)
  starting transfers between devices  31.9 us (12%)
  local copies, waits for them, and re-layouts  25.3 us (9%)
  other arithmetic  18.4 us (7%)
  between operations  14 us (5%)
    ppermute x24, waiting for transfers between devices, hop(): lax.ppermute(s[0], 'col', s[1])  85.1 us
    ppermute x16, waiting for transfers between devices, swap(): lax.ppermute(array, axis, [(i, i ^ mask) for i in range(lax.axis_size(axi...  35.7 us
    pallas_call x3, Pallas kernels, project(): pl.pallas_call(functools.partial(project_kernel, len(near), len(far), chu...  29.9 us
    ppermute x24, starting transfers between devices, hop(): lax.ppermute(s[0], 'col', s[1])  24.9 us
    pallas_call x2, Pallas kernels, finish(): pl.pallas_call(functools.partial(finish_kernel, steps, per, rows, len(pan...  18.7 us
    dynamic_update_slice x18, local copies, waits for them, and re-layouts, put(): panel = lax.dynamic_update_slice(panel, piece[None], (slot, first, 0))  14.6 us
    pallas_call x2, Pallas kernels, attend(): pl.pallas_call(functools.partial(attend_kernel, parts, chunks, pair), gri...  14.1 us
    dynamic_update_slice x9, other arithmetic, put(): panel = lax.dynamic_update_slice(panel, piece[None], (slot, first, 0))  10.5 us
  transfers between devices with their start and end apart: 41, of which 24 were waited for; matrix products, arithmetic and copies ran while one was open for 15% of the time, Pallas kernels for 18%

profile of v12, /device:TPU:2, one launch (start us, length us, event | category | flops | bytes accessed | tf_op | source)
XLA Modules:
  0.0 273.2 jit_solution(6328300573485844718)
XLA Ops:
  6.5 1.6 collective-permute-start
  8.6 2.3 copy_bitcast_fusion.refs_0_
  14.8 2.0 slice.84
  16.8 2.7 %slice.91 = bf16[2048,384]{1,0:T(8,128)(2,1)} slice(bf16[2048,1024]{1,0:T(8,128)(2,1)} %refs_0_.1), slice={[0:2048], [640:1024]} | slice | bytes 3145728 | tf_op jit(solution)/shard_map/slice | solution.py:351
  20.8 1.7 fusion.38
  22.5 13.0 %collective-permute-done.2.refs_2_ = bf16[2048,256]{1,0:T(8,128)(2,1)} collective-permute-done((bf16[2048,256]{1,0:T(8,128)(2,1)}, bf16[2048,256]{1,0:T(8,128)(2,1)}, u32[]{:S(2)}, u32[]{:S(2)}) %collective-permute-start.2) | collective-permute-done | bytes 1048608 | tf_op jit(solution)/shard_map/ppermute | solution.py:23
  35.5 1.6 collective-permute-start.3
  40.9 18.0 %collective-permute-done.3 = bf16[512,1024]{1,0:T(8,128)(2,1)S(1)} collective-permute-done((bf16[512,1024]{1,0:T(8,128)(2,1)S(1)}, bf16[512,1024]{1,0:T(8,128)(2,1)S(1)}, u32[]{:S(2)}, u32[]{:S(2)}) %collective-permute-start.3) | collective-permute-done | bytes 1048608 | tf_op jit(solution)/shard_map/ppermute | solution.py:95
  61.4 1.6 collective-permute-start.6
  67.2 16.3 %collective-permute-done.6 = bf16[512,1024]{1,0:T(8,128)(2,1)S(1)} collective-permute-done((bf16[512,1024]{1,0:T(8,128)(2,1)S(1)}, bf16[512,1024]{1,0:T(8,128)(2,1)S(1)}, u32[]{:S(2)}, u32[]{:S(2)}) %collective-permute-start.6) | collective-permute-done | bytes 1048608 | tf_op jit(solution)/shard_map/ppermute | solution.py:95
  91.8 7.7 %collective-permute-done.10 = bf16[256,1024]{1,0:T(8,128)(2,1)S(1)} collective-permute-done((bf16[256,1024]{1,0:T(8,128)(2,1)S(1)}, bf16[256,1024]{1,0:T(8,128)(2,1)S(1)}, u32[]{:S(2)}, u32[]{:S(2)}) %collective-permute-start.10) | collective-permute-done | bytes 524320 | tf_op jit(solution)/shard_map/ppermute | solution.py:95
  106.3 7.1 %shard_map.65.refs_1_ = bf16[512,256]{1,0:T(8,128)(2,1)} custom-call(bf16[8,512,1024]{2,1,0:T(8,128)(2,1)} %fusion.33.panel_ref, bf16[2048,256]{1,0:T(8,128)(2,1)} %copy_bitcast_fusion.refs_0_, bf16[2048,256]{1,0:T(8,128)(2,1)} %copy-done.8, bf16[2048,256]{1,0:T(8,128)(2,1)} %collective-permute-done.2.refs_2_, bf16[2048,256]{1,0:T(8,128)(2,1)} %copy-done.7, ...), custom_call_target="tpu_custom_call" | custom-call | flops 1 | bytes 1 | tf_op jit(solution)/shard_map/pallas_call | solution.py:171
  114.4 10.6 %shard_map.66.refs_0_ = bf16[512,512]{1,0:T(8,128)(2,1)} custom-call(bf16[8,512,1024]{2,1,0:T(8,128)(2,1)} %fusion.33.panel_ref, bf16[2048,1024]{1,0:T(8,128)(2,1)} %refs_0_.1, bf16[2048,1024]{1,0:T(8,128)(2,1)} %collective-permute-done.15.refs_1_, bf16[2048,256]{1,0:T(8,128)(2,1)} %copy-done.6, bf16[2048,256]{1,0:T(8,128)(2,1)} %collective-permute-done.8.refs_3_, ...), custom_call_target="tpu_custom_call" | custom-call | flops 1 | bytes 1 | tf_op jit(solution)/shard_map/pallas_call | solution.py:171
  125.1 18.7 %collective-permute-done.14.refs_3_ = bf16[512,256]{1,0:T(8,128)(2,1)S(1)} collective-permute-done((bf16[512,256]{1,0:T(8,128)(2,1)}, bf16[512,256]{1,0:T(8,128)(2,1)S(1)}, u32[]{:S(2)}, u32[]{:S(2)}) %collective-permute-start.14) | collective-permute-done | bytes 262176 | tf_op jit(solution)/shard_map/ppermute | solution.py:23
  144.5 3.2 %collective-permute-done.20.refs_4_ = bf16[512,256]{1,0:T(8,128)(2,1)S(1)} collective-permute-done((bf16[512,256]{1,0:T(8,128)(2,1)S(1)}, bf16[512,256]{1,0:T(8,128)(2,1)S(1)}, u32[]{:S(2)}, u32[]{:S(2)}) %collective-permute-start.20) | collective-permute-done | bytes 262176 | tf_op jit(solution)/shard_map/ppermute | solution.py:23
  147.7 7.1 %shard_map.67 = bf16[512,512]{1,0:T(8,128)(2,1)S(1)} custom-call(s32[1]{0:T(128)} %bitcast.r_ref, bf16[512,512]{1,0:T(8,128)(2,1)S(1)} %copy-done.1, bf16[512,256]{1,0:T(8,128)(2,1)S(1)} %copy-done, bf16[512,256]{1,0:T(8,128)(2,1)S(1)} %collective-permute-done.18.refs_2_, bf16[512,256]{1,0:T(8,128)(2,1)S(1)} %collective-permute-done.14.refs_3_, ...), custom_call_target="tpu_custom_call" | custom-call | flops 1 | bytes 1 | tf_op jit(solution)/shard_map/pallas_call | solution.py:254
  154.8 1.6 collective-permute-start.21
  158.5 12.1 %shard_map.68.refs_0_ = bf16[512,512]{1,0:T(8,128)(2,1)} custom-call(bf16[8,512,1024]{2,1,0:T(8,128)(2,1)} %fusion.33.panel_ref, bf16[2048,1024]{1,0:T(8,128)(2,1)} %refs_0_.1, bf16[2048,1024]{1,0:T(8,128)(2,1)} %collective-permute-done.15.refs_1_, bf16[2048,128]{1,0:T(8,128)(2,1)} %copy-done.9, bf16[2048,384]{1,0:T(8,128)(2,1)} %collective-permute-done.19.refs_3_, ...), custom_call_target="tpu_custom_call" | custom-call | flops 1 | bytes 1 | tf_op jit(solution)/shard_map/pallas_call | solution.py:171
  175.0 7.1 %shard_map.71 = bf16[512,512]{1,0:T(8,128)(2,1)S(1)} custom-call(s32[1]{0:T(128)} %bitcast.r_ref, bf16[512,512]{1,0:T(8,128)(2,1)S(1)} %copy-done.2, bf16[512,256]{1,0:T(8,128)(2,1)S(1)} %copy-done, bf16[512,256]{1,0:T(8,128)(2,1)S(1)} %collective-permute-done.18.refs_2_, bf16[512,256]{1,0:T(8,128)(2,1)S(1)} %collective-permute-done.14.refs_3_, ...), custom_call_target="tpu_custom_call" | custom-call | flops 1 | bytes 1 | tf_op jit(solution)/shard_map/pallas_call | solution.py:254
  183.8 2.1 collective-permute-done.25
  187.1 1.6 collective-permute-start.32
  189.2 1.6 collective-permute-start.28
  193.7 17.5 %collective-permute-done.28 = bf16[512,512]{1,0:T(8,128)(2,1)S(1)} collective-permute-done((bf16[512,512]{1,0:T(8,128)(2,1)S(1)}, bf16[512,512]{1,0:T(8,128)(2,1)S(1)}, u32[]{:S(2)}, u32[]{:S(2)}) %collective-permute-start.28) | collective-permute-done | bytes 524320 | tf_op jit(solution)/shard_map/ppermute | solution.py:95
  212.5 1.6 collective-permute-start.30
  220.0 1.8 collective-permute-done.30
  221.8 1.6 collective-permute-done.31
  224.2 5.8 %collective-permute-done.34 = bf16[512,512]{1,0:T(8,128)(2,1)S(1)} collective-permute-done((bf16[512,512]{1,0:T(8,128)(2,1)S(1)}, bf16[512,512]{1,0:T(8,128)(2,1)S(1)}, u32[]{:S(2)}, u32[]{:S(2)}) %collective-permute-start.34) | collective-permute-done | bytes 524320 | tf_op jit(solution)/shard_map/ppermute | solution.py:95
  234.0 5.8 %shard_map.72.refs_5_ = f32[512,1024]{1,0:T(8,128)} custom-call(s32[1]{0:T(128)} %bitcast.r_ref, bf16[8,512,512]{2,1,0:T(8,128)(2,1)} %bitcast_dynamic-update-slice_fusion.16.refs_0_, bf16[2048,1024]{1,0:T(8,128)(2,1)} %refs_2_, bf16[2048,1024]{1,0:T(8,128)(2,1)} %copy-done.3), custom_call_target="tpu_custom_call" | custom-call | flops 1 | bytes 1 | tf_op jit(solution)/shard_map/pallas_call | solution.py:303
  243.4 2.2 collective-permute-start.38
  247.3 2.5 collective-permute-done.38
  249.8 2.2 collective-permute-done.39
  253.4 12.8 %shard_map.73 = bf16[512,1024]{1,0:T(8,128)(2,1)} custom-call(s32[1]{0:T(128)} %bitcast.r_ref, bf16[8,512,512]{2,1,0:T(8,128)(2,1)} %bitcast_dynamic-update-slice_fusion.16.refs_0_, bf16[8,512,512]{2,1,0:T(8,128)(2,1)} %bitcast_dynamic-update-slice_fusion.14.refs_1_, bf16[2048,1024]{1,0:T(8,128)(2,1)} %refs_2_, bf16[2048,1024]{1,0:T(8,128)(2,1)} %copy-done.3, ...), custom_call_target="tpu_custom_call" | custom-call | flops 1 | bytes 1 | tf_op jit(solution)/shard_map/pallas_call | solution.py:303
  (147 shorter events, 64.2 us)
Async XLA Ops:
  6.5 246.9 %all-gather.3.cloned.1.call-start = ((), (), s32[]{:S(2)}) async-start(), calls=%async_computation | async-start | bytes 20971520 | tf_op jit(solution)/shard_map/all_gather | solution.py:426
  6.5 29.0 %collective-permute-start = (bf16[512,1024]{1,0:T(8,128)(2,1)}, bf16[512,1024]{1,0:T(8,128)(2,1)S(1)}, u32[]{:S(2)}, u32[]{:S(2)}) collective-permute-start(bf16[512,1024]{1,0:T(8,128)(2,1)} %param.6), channel_id=1, source_target_pairs={{0,2},{2,4},{4,6},{6,7},{7,5},{5,3},{3,1},{1,0},{8,10},{10,12},{12... | collective-permute-start | bytes 3145736 | tf_op jit(solution)/shard_map/ppermute | solution.py:95
  8.1 27.4 %collective-permute-start.1 = (bf16[512,1024]{1,0:T(8,128)(2,1)}, bf16[512,1024]{1,0:T(8,128)(2,1)S(1)}, u32[]{:S(2)}, u32[]{:S(2)}) collective-permute-start(bf16[512,1024]{1,0:T(8,128)(2,1)} %param.6), channel_id=1, source_target_pairs={{2,0},{4,2},{6,4},{7,6},{5,7},{3,5},{1,3},{0,1},{10,8},{12,10},{14... | collective-permute-start | bytes 3145736 | tf_op jit(solution)/shard_map/ppermute | solution.py:95
  10.9 24.7 %collective-permute-start.2 = (bf16[2048,256]{1,0:T(8,128)(2,1)}, bf16[2048,256]{1,0:T(8,128)(2,1)}, u32[]{:S(2)}, u32[]{:S(2)}) collective-permute-start(bf16[2048,256]{1,0:T(8,128)(2,1)} %copy_bitcast_fusion.refs_0_), channel_id=1, source_target_pairs={{0,16},{8,24},{16,0},{24,8},{1,17},{9,25},{17,1},{25,9},{2,18},{10... | collective-permute-start | bytes 3145736 | tf_op jit(solution)/shard_map/ppermute | solution.py:23
  35.5 23.4 %collective-permute-start.3 = (bf16[512,1024]{1,0:T(8,128)(2,1)S(1)}, bf16[512,1024]{1,0:T(8,128)(2,1)S(1)}, u32[]{:S(2)}, u32[]{:S(2)}) collective-permute-start(bf16[512,1024]{1,0:T(8,128)(2,1)S(1)} %collective-permute-done), channel_id=1, source_target_pairs={{0,2},{2,4},{4,6},{6,7},{7,5},{5,3},{3,1},{1,0},{8,10},{10,12},{12... | collective-permute-start | bytes 3145736 | tf_op jit(solution)/shard_map/ppermute | solution.py:95
  37.1 23.1 %collective-permute-start.4 = (bf16[512,1024]{1,0:T(8,128)(2,1)S(1)}, bf16[512,1024]{1,0:T(8,128)(2,1)S(1)}, u32[]{:S(2)}, u32[]{:S(2)}) collective-permute-start(bf16[512,1024]{1,0:T(8,128)(2,1)S(1)} %collective-permute-done.1), channel_id=1, source_target_pairs={{2,0},{4,2},{6,4},{7,6},{5,7},{3,5},{1,3},{0,1},{10,8},{12,10},{14... | collective-permute-start | bytes 3145736 | tf_op jit(solution)/shard_map/ppermute | solution.py:95
  37.5 22.9 %collective-permute-start.5 = (bf16[2048,256]{1,0:T(8,128)(2,1)S(1)}, bf16[2048,256]{1,0:T(8,128)(2,1)S(1)}, u32[]{:S(2)}, u32[]{:S(2)}) collective-permute-start(bf16[2048,256]{1,0:T(8,128)(2,1)S(1)} %get-tuple-element.95), channel_id=1, source_target_pairs={{0,16},{8,24},{16,0},{24,8},{1,17},{9,25},{17,1},{25,9},{2,18},{10... | collective-permute-start | bytes 3145736 | tf_op jit(solution)/shard_map/ppermute | solution.py:23
  61.4 22.0 %collective-permute-start.6 = (bf16[512,1024]{1,0:T(8,128)(2,1)S(1)}, bf16[512,1024]{1,0:T(8,128)(2,1)S(1)}, u32[]{:S(2)}, u32[]{:S(2)}) collective-permute-start(bf16[512,1024]{1,0:T(8,128)(2,1)S(1)} %collective-permute-done.3), channel_id=1, source_target_pairs={{0,2},{2,4},{4,6},{6,7},{7,5},{5,3},{3,1},{1,0},{8,10},{10,12},{12... | collective-permute-start | bytes 3145736 | tf_op jit(solution)/shard_map/ppermute | solution.py:95
  62.9 21.8 %collective-permute-start.7 = (bf16[512,1024]{1,0:T(8,128)(2,1)S(1)}, bf16[512,1024]{1,0:T(8,128)(2,1)S(1)}, u32[]{:S(2)}, u32[]{:S(2)}) collective-permute-start(bf16[512,1024]{1,0:T(8,128)(2,1)S(1)} %collective-permute-done.4), channel_id=1, source_target_pairs={{2,0},{4,2},{6,4},{7,6},{5,7},{3,5},{1,3},{0,1},{10,8},{12,10},{14... | collective-permute-start | bytes 3145736 | tf_op jit(solution)/shard_map/ppermute | solution.py:95
  63.4 21.6 %collective-permute-start.8 = (bf16[2048,256]{1,0:T(8,128)(2,1)S(1)}, bf16[2048,256]{1,0:T(8,128)(2,1)}, u32[]{:S(2)}, u32[]{:S(2)}) collective-permute-start(bf16[2048,256]{1,0:T(8,128)(2,1)S(1)} %get-tuple-element.103), channel_id=1, source_target_pairs={{0,16},{8,24},{16,0},{24,8},{1,17},{9,25},{17,1},{25,9},{2,18},{10... | collective-permute-start | bytes 3145736 | tf_op jit(solution)/shard_map/ppermute | solution.py:23
  85.0 16.2 %collective-permute-start.13 = (bf16[2048,256]{1,0:T(8,128)(2,1)}, bf16[2048,256]{1,0:T(8,128)(2,1)S(1)}, u32[]{:S(2)}, u32[]{:S(2)}) collective-permute-start(bf16[2048,256]{1,0:T(8,128)(2,1)} %collective-permute-done.2.refs_2_), channel_id=1, source_target_pairs={{0,8},{8,0},{16,24},{24,16},{1,9},{9,1},{17,25},{25,17},{2,10},{10... | collective-permute-start | bytes 3145736 | tf_op jit(solution)/shard_map/ppermute | solution.py:23
  85.1 16.2 %collective-permute-start.12 = (bf16[2048,256]{1,0:T(8,128)(2,1)}, bf16[2048,256]{1,0:T(8,128)(2,1)S(1)}, u32[]{:S(2)}, u32[]{:S(2)}) collective-permute-start(bf16[2048,256]{1,0:T(8,128)(2,1)} %copy_bitcast_fusion.refs_0_), channel_id=1, source_target_pairs={{0,8},{8,0},{16,24},{24,16},{1,9},{9,1},{17,25},{25,17},{2,10},{10... | collective-permute-start | bytes 3145736 | tf_op jit(solution)/shard_map/ppermute | solution.py:23
  85.6 13.9 %collective-permute-start.10 = (bf16[256,1024]{1,0:T(8,128)(2,1)S(1)}, bf16[256,1024]{1,0:T(8,128)(2,1)S(1)}, u32[]{:S(2)}, u32[]{:S(2)}) collective-permute-start(bf16[256,1024]{1,0:T(8,128)(2,1)S(1)} %slice.86), channel_id=1, source_target_pairs={{2,0},{4,2},{6,4},{7,6},{5,7},{3,5},{1,3},{0,1},{10,8},{12,10},{14... | collective-permute-start | bytes 1572872 | tf_op jit(solution)/shard_map/ppermute | solution.py:95
  87.0 13.9 %collective-permute-start.9 = (bf16[256,1024]{1,0:T(8,128)(2,1)S(1)}, bf16[256,1024]{1,0:T(8,128)(2,1)S(1)}, u32[]{:S(2)}, u32[]{:S(2)}) collective-permute-start(bf16[256,1024]{1,0:T(8,128)(2,1)S(1)} %slice.85), channel_id=1, source_target_pairs={{0,2},{2,4},{4,6},{6,7},{7,5},{5,3},{3,1},{1,0},{8,10},{10,12},{12... | collective-permute-start | bytes 1572872 | tf_op jit(solution)/shard_map/ppermute | solution.py:95
  87.9 13.3 %collective-permute-start.11 = (bf16[2048,128]{1,0:T(8,128)(2,1)S(1)}, bf16[2048,128]{1,0:T(8,128)(2,1)S(1)}, u32[]{:S(2)}, u32[]{:S(2)}) collective-permute-start(bf16[2048,128]{1,0:T(8,128)(2,1)S(1)} %copy-done.11), channel_id=1, source_target_pairs={{0,16},{8,24},{16,0},{24,8},{1,17},{9,25},{17,1},{25,9},{2,18},{10... | collective-permute-start | bytes 1572872 | tf_op jit(solution)/shard_map/ppermute | solution.py:23
  101.3 13.1 %collective-permute-start.15 = (bf16[2048,1024]{1,0:T(8,128)(2,1)}, bf16[2048,1024]{1,0:T(8,128)(2,1)}, u32[]{:S(2)}, u32[]{:S(2)}) collective-permute-start(bf16[2048,1024]{1,0:T(8,128)(2,1)} %refs_0_.1), channel_id=1, source_target_pairs={{0,8},{8,0},{16,24},{24,16},{1,9},{9,1},{17,25},{25,17},{2,10},{10... | collective-permute-start | bytes 12582920 | tf_op jit(solution)/shard_map/ppermute | solution.py:23
  101.4 42.4 %collective-permute-start.19 = (bf16[2048,384]{1,0:T(8,128)(2,1)S(1)}, bf16[2048,384]{1,0:T(8,128)(2,1)}, u32[]{:S(2)}, u32[]{:S(2)}) collective-permute-start(bf16[2048,384]{1,0:T(8,128)(2,1)S(1)} %copy-done.5), channel_id=1, source_target_pairs={{0,16},{8,24},{16,0},{24,8},{1,17},{9,25},{17,1},{25,9},{2,18},{10... | collective-permute-start | bytes 4718600 | tf_op jit(solution)/shard_map/ppermute | solution.py:23
  113.4 30.4 %collective-permute-start.14 = (bf16[512,256]{1,0:T(8,128)(2,1)}, bf16[512,256]{1,0:T(8,128)(2,1)S(1)}, u32[]{:S(2)}, u32[]{:S(2)}) collective-permute-start(bf16[512,256]{1,0:T(8,128)(2,1)} %shard_map.65.refs_1_), channel_id=1, source_target_pairs={{0,16},{8,24},{16,0},{24,8},{1,17},{9,25},{17,1},{25,9},{2,18},{10... | collective-permute-start | bytes 786440 | tf_op jit(solution)/shard_map/ppermute | solution.py:23
  114.4 29.4 %collective-permute-start.18 = (bf16[512,256]{1,0:T(8,128)(2,1)}, bf16[512,256]{1,0:T(8,128)(2,1)S(1)}, u32[]{:S(2)}, u32[]{:S(2)}) collective-permute-start(bf16[512,256]{1,0:T(8,128)(2,1)} %shard_map.65.refs_1_), channel_id=1, source_target_pairs={{0,8},{8,0},{16,24},{24,16},{1,9},{9,1},{17,25},{25,17},{2,10},{10... | collective-permute-start | bytes 786440 | tf_op jit(solution)/shard_map/ppermute | solution.py:23
  143.8 13.9 %collective-permute-start.24 = (bf16[2048,384]{1,0:T(8,128)(2,1)}, bf16[2048,384]{1,0:T(8,128)(2,1)}, u32[]{:S(2)}, u32[]{:S(2)}) collective-permute-start(bf16[2048,384]{1,0:T(8,128)(2,1)} %collective-permute-done.19.refs_3_), channel_id=1, source_target_pairs={{0,8},{8,0},{16,24},{24,16},{1,9},{9,1},{17,25},{25,17},{2,10},{10... | collective-permute-start | bytes 4718600 | tf_op jit(solution)/shard_map/ppermute | solution.py:23
  144.4 13.3 %collective-permute-start.23 = (bf16[2048,128]{1,0:T(8,128)(2,1)}, bf16[2048,128]{1,0:T(8,128)(2,1)S(1)}, u32[]{:S(2)}, u32[]{:S(2)}) collective-permute-start(bf16[2048,128]{1,0:T(8,128)(2,1)} %copy-done.9), channel_id=1, source_target_pairs={{0,8},{8,0},{16,24},{24,16},{1,9},{9,1},{17,25},{25,17},{2,10},{10... | collective-permute-start | bytes 1572872 | tf_op jit(solution)/shard_map/ppermute | solution.py:23
  154.8 15.8 %collective-permute-start.21 = (bf16[512,512]{1,0:T(8,128)(2,1)S(1)}, bf16[512,512]{1,0:T(8,128)(2,1)S(1)}, u32[]{:S(2)}, u32[]{:S(2)}) collective-permute-start(bf16[512,512]{1,0:T(8,128)(2,1)S(1)} %shard_map.67), channel_id=1, source_target_pairs={{0,2},{2,4},{4,6},{6,7},{7,5},{5,3},{3,1},{1,0},{8,10},{10,12},{12... | collective-permute-start | bytes 1572872 | tf_op jit(solution)/shard_map/ppermute | solution.py:95
  156.4 14.2 %collective-permute-start.22 = (bf16[512,512]{1,0:T(8,128)(2,1)S(1)}, bf16[512,512]{1,0:T(8,128)(2,1)S(1)}, u32[]{:S(2)}, u32[]{:S(2)}) collective-permute-start(bf16[512,512]{1,0:T(8,128)(2,1)S(1)} %shard_map.67), channel_id=1, source_target_pairs={{2,0},{4,2},{6,4},{7,6},{5,7},{3,5},{1,3},{0,1},{10,8},{12,10},{14... | collective-permute-start | bytes 1572872 | tf_op jit(solution)/shard_map/ppermute | solution.py:95
  170.6 16.5 %collective-permute-start.27 = (bf16[2048,1024]{1,0:T(8,128)(2,1)}, bf16[2048,1024]{1,0:T(8,128)(2,1)S(1)}, u32[]{:S(2)}, u32[]{:S(2)}) collective-permute-start(bf16[2048,1024]{1,0:T(8,128)(2,1)} %refs_2_), channel_id=1, source_target_pairs={{0,8},{8,0},{16,24},{24,16},{1,9},{9,1},{17,25},{25,17},{2,10},{10... | collective-permute-start | bytes 12582920 | tf_op jit(solution)/shard_map/ppermute | solution.py:23
  172.0 13.9 %collective-permute-start.25 = (bf16[512,512]{1,0:T(8,128)(2,1)S(1)}, bf16[512,512]{1,0:T(8,128)(2,1)S(1)}, u32[]{:S(2)}, u32[]{:S(2)}) collective-permute-start(bf16[512,512]{1,0:T(8,128)(2,1)S(1)} %collective-permute-done.21), channel_id=1, source_target_pairs={{0,2},{2,4},{4,6},{6,7},{7,5},{5,3},{3,1},{1,0},{8,10},{10,12},{12... | collective-permute-start | bytes 1572872 | tf_op jit(solution)/shard_map/ppermute | solution.py:95
  173.5 13.6 %collective-permute-start.26 = (bf16[512,512]{1,0:T(8,128)(2,1)S(1)}, bf16[512,512]{1,0:T(8,128)(2,1)S(1)}, u32[]{:S(2)}, u32[]{:S(2)}) collective-permute-start(bf16[512,512]{1,0:T(8,128)(2,1)S(1)} %collective-permute-done.22), channel_id=1, source_target_pairs={{2,0},{4,2},{6,4},{7,6},{5,7},{3,5},{1,3},{0,1},{10,8},{12,10},{14... | collective-permute-start | bytes 1572872 | tf_op jit(solution)/shard_map/ppermute | solution.py:95
  187.1 27.5 %collective-permute-start.32 = (bf16[512,512]{1,0:T(8,128)(2,1)S(1)}, bf16[512,512]{1,0:T(8,128)(2,1)S(1)}, u32[]{:S(2)}, u32[]{:S(2)}) collective-permute-start(bf16[512,512]{1,0:T(8,128)(2,1)S(1)} %shard_map.71), channel_id=1, source_target_pairs={{0,2},{2,4},{4,6},{6,7},{7,5},{5,3},{3,1},{1,0},{8,10},{10,12},{12... | collective-permute-start | bytes 1572872 | tf_op jit(solution)/shard_map/ppermute | solution.py:95
  188.7 26.0 %collective-permute-start.33 = (bf16[512,512]{1,0:T(8,128)(2,1)S(1)}, bf16[512,512]{1,0:T(8,128)(2,1)S(1)}, u32[]{:S(2)}, u32[]{:S(2)}) collective-permute-start(bf16[512,512]{1,0:T(8,128)(2,1)S(1)} %shard_map.71), channel_id=1, source_target_pairs={{2,0},{4,2},{6,4},{7,6},{5,7},{3,5},{1,3},{0,1},{10,8},{12,10},{14... | collective-permute-start | bytes 1572872 | tf_op jit(solution)/shard_map/ppermute | solution.py:95
  189.2 22.1 %collective-permute-start.28 = (bf16[512,512]{1,0:T(8,128)(2,1)S(1)}, bf16[512,512]{1,0:T(8,128)(2,1)S(1)}, u32[]{:S(2)}, u32[]{:S(2)}) collective-permute-start(bf16[512,512]{1,0:T(8,128)(2,1)S(1)} %collective-permute-done.25), channel_id=1, source_target_pairs={{0,2},{2,4},{4,6},{6,7},{7,5},{5,3},{3,1},{1,0},{8,10},{10,12},{12... | collective-permute-start | bytes 1572872 | tf_op jit(solution)/shard_map/ppermute | solution.py:95
  190.7 21.8 %collective-permute-start.29 = (bf16[512,512]{1,0:T(8,128)(2,1)S(1)}, bf16[512,512]{1,0:T(8,128)(2,1)S(1)}, u32[]{:S(2)}, u32[]{:S(2)}) collective-permute-start(bf16[512,512]{1,0:T(8,128)(2,1)S(1)} %collective-permute-done.26), channel_id=1, source_target_pairs={{2,0},{4,2},{6,4},{7,6},{5,7},{3,5},{1,3},{0,1},{10,8},{12,10},{14... | collective-permute-start | bytes 1572872 | tf_op jit(solution)/shard_map/ppermute | solution.py:95
  214.7 15.3 %collective-permute-start.34 = (bf16[512,512]{1,0:T(8,128)(2,1)S(1)}, bf16[512,512]{1,0:T(8,128)(2,1)S(1)}, u32[]{:S(2)}, u32[]{:S(2)}) collective-permute-start(bf16[512,512]{1,0:T(8,128)(2,1)S(1)} %collective-permute-done.32), channel_id=1, source_target_pairs={{0,2},{2,4},{4,6},{6,7},{7,5},{5,3},{3,1},{1,0},{8,10},{10,12},{12... | collective-permute-start | bytes 1572872 | tf_op jit(solution)/shard_map/ppermute | solution.py:95
  216.2 15.0 %collective-permute-start.35 = (bf16[512,512]{1,0:T(8,128)(2,1)S(1)}, bf16[512,512]{1,0:T(8,128)(2,1)S(1)}, u32[]{:S(2)}, u32[]{:S(2)}) collective-permute-start(bf16[512,512]{1,0:T(8,128)(2,1)S(1)} %collective-permute-done.33), channel_id=1, source_target_pairs={{2,0},{4,2},{6,4},{7,6},{5,7},{3,5},{1,3},{0,1},{10,8},{12,10},{14... | collective-permute-start | bytes 1572872 | tf_op jit(solution)/shard_map/ppermute | solution.py:95
  (22 other events, 221.5 us)
Sparse Core Ops, SparseCore 0:
  143.9 105.8 all-gather.2

commit v13 on v12

--- a/solution.py
+++ b/solution.py
@@ -342,7 +342,8 @@
     late_heads = n_heads - first_heads
     if n_heads >= 4:
         sizes = [first_heads // 2, first_heads - first_heads // 2]
-        sizes += [n for n in (late_heads // 4, late_heads - late_heads // 4) if n > 0]
+        eighth = late_heads // 4
+        sizes += [n for n in (eighth, late_heads - 2 * eighth, eighth) if n > 0]
     else:
         sizes = [first_heads, late_heads]
     early = 2 if n_heads >= 4 else 1
@@ -393,7 +394,7 @@
         last_hop = i == hops - 1
         tie = ring.last[0][1]
         sent = [] if x_sent is None else [x_sent]
-        ahead = chunks[i : i + 1]
+        ahead = chunks[i : i + 1] if i < len(sizes) - 1 else []
         beside = [panel, *squares, cosine, sine, *sent, *ahead]
         if last_hop:
             near = gather_near(after(stacked, tie))
@@ -416,25 +417,32 @@
     queries = project(
         panel, q_near, by_block(q_far[:early]), 0, first_heads, factor, scale, cosine, sine
     )
-    beside = [exchange(kv), queries, *gather_near(kv)]
+    beside = [exchange(kv), queries, chunks[-1], *gather_near(kv)]
     if x_sent is not None:
         beside.append(x_sent)
-    kv_other, queries, *beside = lax.optimization_barrier(tuple(beside))
+    kv_other, queries, last_chunk, *beside = lax.optimization_barrier(tuple(beside))
     kv_pieces, arrived = take(beside, blocks_near)
     kv_pieces = [*kv_pieces, *gather_near(kv_other)]
     late_far = [list(gather_near(piece)) for piece in (*got_x[1 + early :], *arrived)]
+    last_other = exchange(last_chunk)
     o_weights = lax.all_gather(after(wo, kv_other), "row")
     heads = attend(r, [queries], kv_pieces)
 
     ring = Ring(heads, 1)
     panels = [put(blank((n_col, tok, wide)), ring.found), blank((n_col, tok, rest))]
-    late = project(
-        panel, q_near, by_block(late_far), wide, -1, factor, scale, cosine, sine
-    )
-    found, (late, *panels) = ring.hop([late, *panels])
+    tables = scale, cosine, sine
+    late, first = [], wide
+    if late_far:
+        late.append(project(panel, q_near, by_block(late_far), first, -1, factor, *tables))
+        first += late[0].shape[1]
+    found, (last_other, *beside) = ring.hop([last_other, *panels, *late])
+    panels, late = take(beside, 2)
     panels[0] = put(panels[0], found)
+    last_far = by_block([gather_near(last_other)])
+    late = [*late, project(panel, q_near, last_far, first, -1, factor, *tables)]
+    late = jnp.concatenate(late, axis=1)
     heads = attend(r, [late], kv_pieces)
-    o_near = gather_near(after(wo, late))
+    o_near = gather_near(after(wo, last_other))
     found, (heads, panels[0], *o_near) = ring.hop([heads, panels[0], *o_near])
     panels[0] = put(panels[0], found)
     second = Ring(heads, 1)

time: 274 us -> 277 us (1.011)
  waiting for transfers between devices: 121 us -> 112 us
  Pallas kernels: 62.7 us -> 69.4 us
  local copies, waits for them, and re-layouts: 25.3 us -> 28.3 us
    ppermute x16 -> x18, waiting for transfers between devices: 35.7 us -> 22.8 us  [swap(): lax.ppermute(array, axis, [(i, i ^ mask) for i in range(lax.axis_size(axi...]
    pallas_call x3 -> x4, Pallas kernels: 29.9 us -> 36.6 us  [project(): pl.pallas_call(functools.partial(project_kernel, len(near), len(far), chu...]
    ppermute x24, waiting for transfers between devices: 85.1 us -> 89.2 us  [hop(): lax.ppermute(s[0], 'col', s[1])]
    slice x3 -> x2, local copies, waits for them, and re-layouts: 6.45 us -> 5.16 us  [per_device(): wq[:, sum(sizes[:i]) * HD:sum(sizes[:i + 1]) * HD]]
    ppermute x16 -> x18, starting transfers between devices: 7.04 us -> 7.98 us  [swap(): lax.ppermute(array, axis, [(i, i ^ mask) for i in range(lax.axis_size(axi...]
  transfers between devices with their start and end apart: 41 -> 43, of which waited for: 24 -> 22; matrix products, arithmetic and copies ran while one was open for 15% -> 16% of each run, Pallas kernels for 18% -> 20%
where the time goes in v13:
time: 277 us
  waiting for transfers between devices  112 us (40%)
  Pallas kernels  69.4 us (25%)
  starting transfers between devices  32.8 us (12%)
  local copies, waits for them, and re-layouts  28.3 us (10%)
  other arithmetic  20.1 us (7%)
  between operations  13.8 us (5%)
    ppermute x24, waiting for transfers between devices, hop(): lax.ppermute(s[0], 'col', s[1])  89.2 us
    pallas_call x4, Pallas kernels, project(): pl.pallas_call(functools.partial(project_kernel, len(near), len(far), chu...  36.6 us
    ppermute x24, starting transfers between devices, hop(): lax.ppermute(s[0], 'col', s[1])  24.9 us
    ppermute x18, waiting for transfers between devices, swap(): lax.ppermute(array, axis, [(i, i ^ mask) for i in range(lax.axis_size(axi...  22.8 us
    pallas_call x2, Pallas kernels, finish(): pl.pallas_call(functools.partial(finish_kernel, steps, per, rows, len(pan...  18.7 us
    dynamic_update_slice x18, local copies, waits for them, and re-layouts, put(): panel = lax.dynamic_update_slice(panel, piece[None], (slot, first, 0))  16.7 us
    pallas_call x2, Pallas kernels, attend(): pl.pallas_call(functools.partial(attend_kernel, parts, chunks, pair), gri...  14.1 us
    dynamic_update_slice x9, other arithmetic, put(): panel = lax.dynamic_update_slice(panel, piece[None], (slot, first, 0))  10.6 us
  transfers between devices with their start and end apart: 43, of which 22 were waited for; matrix products, arithmetic and copies ran while one was open for 16% of the time, Pallas kernels for 20%

profile of v13, /device:TPU:2, one launch (start us, length us, event | category | flops | bytes accessed | tf_op | source)
XLA Modules:
  0.0 276.5 jit_solution(5003773987959765309)
XLA Ops:
  8.6 2.3 copy_bitcast_fusion.refs_0_
  12.6 1.8 fusion.36
  15.7 2.1 pad_maximum_fusion.1
  17.8 2.1 fusion.38
  19.9 3.1 %fusion.39 = (bf16[2048,256]{1,0:T(8,128)(2,1)}, bf16[2048,256]{1,0:T(8,128)(2,1)S(1)}, bf16[2048,256]{1,0:T(8,128)(2,1)S(1)}) fusion(bf16[2048,1024]{1,0:T(8,128)(2,1)} %refs_0_.2), kind=kLoop, calls=%fused_computation.91 | loop fusion | bytes 6291456 | tf_op jit(solution)/shard_map/slice | solution.py:352
  22.9 12.6 %collective-permute-done.2.refs_2_ = bf16[2048,256]{1,0:T(8,128)(2,1)} collective-permute-done((bf16[2048,256]{1,0:T(8,128)(2,1)}, bf16[2048,256]{1,0:T(8,128)(2,1)}, u32[]{:S(2)}, u32[]{:S(2)}) %collective-permute-start.2) | collective-permute-done | bytes 1048608 | tf_op jit(solution)/shard_map/ppermute | solution.py:23
  41.0 18.0 %collective-permute-done.3 = bf16[512,1024]{1,0:T(8,128)(2,1)S(1)} collective-permute-done((bf16[512,1024]{1,0:T(8,128)(2,1)S(1)}, bf16[512,1024]{1,0:T(8,128)(2,1)S(1)}, u32[]{:S(2)}, u32[]{:S(2)}) %collective-permute-start.3) | collective-permute-done | bytes 1048608 | tf_op jit(solution)/shard_map/ppermute | solution.py:95
  67.2 16.2 %collective-permute-done.6 = bf16[512,1024]{1,0:T(8,128)(2,1)S(1)} collective-permute-done((bf16[512,1024]{1,0:T(8,128)(2,1)S(1)}, bf16[512,1024]{1,0:T(8,128)(2,1)S(1)}, u32[]{:S(2)}, u32[]{:S(2)}) %collective-permute-start.6) | collective-permute-done | bytes 1048608 | tf_op jit(solution)/shard_map/ppermute | solution.py:95
  91.7 7.8 %collective-permute-done.10 = bf16[256,1024]{1,0:T(8,128)(2,1)S(1)} collective-permute-done((bf16[256,1024]{1,0:T(8,128)(2,1)S(1)}, bf16[256,1024]{1,0:T(8,128)(2,1)S(1)}, u32[]{:S(2)}, u32[]{:S(2)}) %collective-permute-start.10) | collective-permute-done | bytes 524320 | tf_op jit(solution)/shard_map/ppermute | solution.py:95
  107.2 7.2 %shard_map.65.refs_1_ = bf16[512,256]{1,0:T(8,128)(2,1)} custom-call(bf16[8,512,1024]{2,1,0:T(8,128)(2,1)} %fusion.33.panel_ref, bf16[2048,256]{1,0:T(8,128)(2,1)} %copy_bitcast_fusion.refs_0_, bf16[2048,256]{1,0:T(8,128)(2,1)} %copy-done.9, bf16[2048,256]{1,0:T(8,128)(2,1)} %collective-permute-done.2.refs_2_, bf16[2048,256]{1,0:T(8,128)(2,1)} %copy-done.8, ...), custom_call_target="tpu_custom_call" | custom-call | flops 1 | bytes 1 | tf_op jit(solution)/shard_map/pallas_call | solution.py:171
  115.7 10.7 %shard_map.66.refs_0_ = bf16[512,512]{1,0:T(8,128)(2,1)} custom-call(bf16[8,512,1024]{2,1,0:T(8,128)(2,1)} %fusion.33.panel_ref, bf16[2048,1024]{1,0:T(8,128)(2,1)} %refs_0_.2, bf16[2048,1024]{1,0:T(8,128)(2,1)} %collective-permute-done.15.refs_1_, bf16[2048,256]{1,0:T(8,128)(2,1)} %copy-done.4, bf16[2048,256]{1,0:T(8,128)(2,1)} %copy-done.6, ...), custom_call_target="tpu_custom_call" | custom-call | flops 1 | bytes 1 | tf_op jit(solution)/shard_map/pallas_call | solution.py:171
  126.4 7.8 %collective-permute-done.14.refs_3_ = bf16[512,256]{1,0:T(8,128)(2,1)S(1)} collective-permute-done((bf16[512,256]{1,0:T(8,128)(2,1)}, bf16[512,256]{1,0:T(8,128)(2,1)S(1)}, u32[]{:S(2)}, u32[]{:S(2)}) %collective-permute-start.14) | collective-permute-done | bytes 262176 | tf_op jit(solution)/shard_map/ppermute | solution.py:23
  135.7 1.6 collective-permute-done.20.refs_4_
  137.3 7.1 %shard_map.67 = bf16[512,512]{1,0:T(8,128)(2,1)S(1)} custom-call(s32[1]{0:T(128)} %bitcast.r_ref, bf16[512,512]{1,0:T(8,128)(2,1)S(1)} %copy-done.1, bf16[512,256]{1,0:T(8,128)(2,1)S(1)} %copy-done, bf16[512,256]{1,0:T(8,128)(2,1)S(1)} %collective-permute-done.18.refs_2_, bf16[512,256]{1,0:T(8,128)(2,1)S(1)} %collective-permute-done.14.refs_3_, ...), custom_call_target="tpu_custom_call" | custom-call | flops 1 | bytes 1 | tf_op jit(solution)/shard_map/pallas_call | solution.py:254
  144.4 1.6 collective-permute-start.21
  148.3 11.9 %shard_map.70 = bf16[512,384]{1,0:T(8,128)(2,1)} custom-call(bf16[8,512,1024]{2,1,0:T(8,128)(2,1)} %fusion.33.panel_ref, bf16[2048,1024]{1,0:T(8,128)(2,1)} %refs_0_.2, bf16[2048,1024]{1,0:T(8,128)(2,1)} %collective-permute-done.15.refs_1_, bf16[2048,128]{1,0:T(8,128)(2,1)} %collective-permute-done.11.refs_2_, ...), custom_call_target="tpu_custom_call" | custom-call | flops 1 | bytes 1 | tf_op jit(solution)/shard_map/pallas_call | solution.py:171
  163.5 1.9 bitcast_dynamic-update-slice_fusion.12
  166.2 6.9 %shard_map.71 = bf16[512,128]{1,0:T(8,128)(2,1)} custom-call(bf16[8,512,1024]{2,1,0:T(8,128)(2,1)} %fusion.33.panel_ref, bf16[2048,1024]{1,0:T(8,128)(2,1)} %refs_0_.2, bf16[2048,1024]{1,0:T(8,128)(2,1)} %collective-permute-done.15.refs_1_, bf16[2048,128]{1,0:T(8,128)(2,1)} %collective-permute-done.23.refs_2_, bf16[2048,128]{1,0:T(8,128)(2,1)} %copy-done.10, ...), custom_call_target="tpu_custom_call" | custom-call | flops 1 | bytes 1 | tf_op jit(solution)/shard_map/pallas_call | solution.py:171
  174.1 1.9 bitcast_dynamic-update-slice_fusion.11
  176.0 7.1 %shard_map.72 = bf16[512,512]{1,0:T(8,128)(2,1)S(1)} custom-call(s32[1]{0:T(128)} %bitcast.r_ref, bf16[512,512]{1,0:T(8,128)(2,1)S(1)} %pad_maximum_fusion.refs_0_, bf16[512,256]{1,0:T(8,128)(2,1)S(1)} %copy-done, bf16[512,256]{1,0:T(8,128)(2,1)S(1)} %collective-permute-done.18.refs_2_, bf16[512,256]{1,0:T(8,128)(2,1)S(1)} %collective-permute-done.14.refs_3_, ...), custom_call_target="tpu_custom_call" | custom-call | flops 1 | bytes 1 | tf_op jit(solution)/shard_map/pallas_call | solution.py:254
  183.1 1.6 collective-permute-start.34
  189.7 18.3 %collective-permute-done.30 = bf16[512,512]{1,0:T(8,128)(2,1)S(1)} collective-permute-done((bf16[512,512]{1,0:T(8,128)(2,1)S(1)}, bf16[512,512]{1,0:T(8,128)(2,1)S(1)}, u32[]{:S(2)}, u32[]{:S(2)}) %collective-permute-start.30) | collective-permute-done | bytes 524320 | tf_op jit(solution)/shard_map/ppermute | solution.py:95
  208.0 1.8 collective-permute-done.31
  209.9 1.7 collective-permute-start.32
  212.0 1.6 collective-permute-start.36
  218.9 1.8 collective-permute-done.33
  221.5 8.7 %collective-permute-done.36 = bf16[512,512]{1,0:T(8,128)(2,1)S(1)} collective-permute-done((bf16[512,512]{1,0:T(8,128)(2,1)S(1)}, bf16[512,512]{1,0:T(8,128)(2,1)S(1)}, u32[]{:S(2)}, u32[]{:S(2)}) %collective-permute-start.36) | collective-permute-done | bytes 524320 | tf_op jit(solution)/shard_map/ppermute | solution.py:95
  230.2 1.7 collective-permute-done.37
  234.6 5.8 %shard_map.73.refs_5_ = f32[512,1024]{1,0:T(8,128)} custom-call(s32[1]{0:T(128)} %bitcast.r_ref, bf16[8,512,512]{2,1,0:T(8,128)(2,1)} %bitcast_dynamic-update-slice_fusion.16.refs_0_, bf16[2048,1024]{1,0:T(8,128)(2,1)} %refs_2_, bf16[2048,1024]{1,0:T(8,128)(2,1)} %collective-permute-done.29.refs_2_.refs_3_), custom_call_target="tpu_custom_call" | custom-call | flops 1 | bytes 1 | tf_op jit(solution)/shard_map/pallas_call | solution.py:303
  242.2 3.6 %collective-permute-done.38 = bf16[512,512]{1,0:T(8,128)(2,1)S(1)} collective-permute-done((bf16[512,512]{1,0:T(8,128)(2,1)S(1)}, bf16[512,512]{1,0:T(8,128)(2,1)S(1)}, u32[]{:S(2)}, u32[]{:S(2)}) %collective-permute-start.38) | collective-permute-done | bytes 524320 | tf_op jit(solution)/shard_map/ppermute | solution.py:95
  250.8 3.4 %collective-permute-done.40 = bf16[256,512]{1,0:T(8,128)(2,1)S(1)} collective-permute-done((bf16[256,512]{1,0:T(8,128)(2,1)S(1)}, bf16[256,512]{1,0:T(8,128)(2,1)S(1)}, u32[]{:S(2)}, u32[]{:S(2)}) %collective-permute-start.40) | collective-permute-done | bytes 262176 | tf_op jit(solution)/shard_map/ppermute | solution.py:95
  256.8 12.9 %shard_map.74 = bf16[512,1024]{1,0:T(8,128)(2,1)} custom-call(s32[1]{0:T(128)} %bitcast.r_ref, bf16[8,512,512]{2,1,0:T(8,128)(2,1)} %bitcast_dynamic-update-slice_fusion.16.refs_0_, bf16[8,512,512]{2,1,0:T(8,128)(2,1)} %bitcast_dynamic-update-slice_fusion.14.refs_1_, bf16[2048,1024]{1,0:T(8,128)(2,1)} %refs_2_, ...), custom_call_target="tpu_custom_call" | custom-call | flops 1 | bytes 1 | tf_op jit(solution)/shard_map/pallas_call | solution.py:303
  (150 shorter events, 68.4 us)
Async XLA Ops:
  6.5 250.3 %all-gather.3.cloned.1.call-start = ((), (), s32[]{:S(2)}) async-start(), calls=%async_computation | async-start | bytes 20971520 | tf_op jit(solution)/shard_map/all_gather | solution.py:428
  6.5 29.0 %collective-permute-start = (bf16[512,1024]{1,0:T(8,128)(2,1)}, bf16[512,1024]{1,0:T(8,128)(2,1)S(1)}, u32[]{:S(2)}, u32[]{:S(2)}) collective-permute-start(bf16[512,1024]{1,0:T(8,128)(2,1)} %param.6), channel_id=1, source_target_pairs={{0,2},{2,4},{4,6},{6,7},{7,5},{5,3},{3,1},{1,0},{8,10},{10,12},{12... | collective-permute-start | bytes 3145736 | tf_op jit(solution)/shard_map/ppermute | solution.py:95
  8.1 27.4 %collective-permute-start.1 = (bf16[512,1024]{1,0:T(8,128)(2,1)}, bf16[512,1024]{1,0:T(8,128)(2,1)S(1)}, u32[]{:S(2)}, u32[]{:S(2)}) collective-permute-start(bf16[512,1024]{1,0:T(8,128)(2,1)} %param.6), channel_id=1, source_target_pairs={{2,0},{4,2},{6,4},{7,6},{5,7},{3,5},{1,3},{0,1},{10,8},{12,10},{14... | collective-permute-start | bytes 3145736 | tf_op jit(solution)/shard_map/ppermute | solution.py:95
  10.9 24.7 %collective-permute-start.2 = (bf16[2048,256]{1,0:T(8,128)(2,1)}, bf16[2048,256]{1,0:T(8,128)(2,1)}, u32[]{:S(2)}, u32[]{:S(2)}) collective-permute-start(bf16[2048,256]{1,0:T(8,128)(2,1)} %copy_bitcast_fusion.refs_0_), channel_id=1, source_target_pairs={{0,16},{8,24},{16,0},{24,8},{1,17},{9,25},{17,1},{25,9},{2,18},{10... | collective-permute-start | bytes 3145736 | tf_op jit(solution)/shard_map/ppermute | solution.py:23
  35.5 23.4 %collective-permute-start.3 = (bf16[512,1024]{1,0:T(8,128)(2,1)S(1)}, bf16[512,1024]{1,0:T(8,128)(2,1)S(1)}, u32[]{:S(2)}, u32[]{:S(2)}) collective-permute-start(bf16[512,1024]{1,0:T(8,128)(2,1)S(1)} %collective-permute-done), channel_id=1, source_target_pairs={{0,2},{2,4},{4,6},{6,7},{7,5},{5,3},{3,1},{1,0},{8,10},{10,12},{12... | collective-permute-start | bytes 3145736 | tf_op jit(solution)/shard_map/ppermute | solution.py:95
  37.1 23.1 %collective-permute-start.4 = (bf16[512,1024]{1,0:T(8,128)(2,1)S(1)}, bf16[512,1024]{1,0:T(8,128)(2,1)S(1)}, u32[]{:S(2)}, u32[]{:S(2)}) collective-permute-start(bf16[512,1024]{1,0:T(8,128)(2,1)S(1)} %collective-permute-done.1), channel_id=1, source_target_pairs={{2,0},{4,2},{6,4},{7,6},{5,7},{3,5},{1,3},{0,1},{10,8},{12,10},{14... | collective-permute-start | bytes 3145736 | tf_op jit(solution)/shard_map/ppermute | solution.py:95
  37.5 22.9 %collective-permute-start.5 = (bf16[2048,256]{1,0:T(8,128)(2,1)S(1)}, bf16[2048,256]{1,0:T(8,128)(2,1)S(1)}, u32[]{:S(2)}, u32[]{:S(2)}) collective-permute-start(bf16[2048,256]{1,0:T(8,128)(2,1)S(1)} %get-tuple-element.97), channel_id=1, source_target_pairs={{0,16},{8,24},{16,0},{24,8},{1,17},{9,25},{17,1},{25,9},{2,18},{10... | collective-permute-start | bytes 3145736 | tf_op jit(solution)/shard_map/ppermute | solution.py:23
  61.4 22.0 %collective-permute-start.6 = (bf16[512,1024]{1,0:T(8,128)(2,1)S(1)}, bf16[512,1024]{1,0:T(8,128)(2,1)S(1)}, u32[]{:S(2)}, u32[]{:S(2)}) collective-permute-start(bf16[512,1024]{1,0:T(8,128)(2,1)S(1)} %collective-permute-done.3), channel_id=1, source_target_pairs={{0,2},{2,4},{4,6},{6,7},{7,5},{5,3},{3,1},{1,0},{8,10},{10,12},{12... | collective-permute-start | bytes 3145736 | tf_op jit(solution)/shard_map/ppermute | solution.py:95
  63.0 21.8 %collective-permute-start.7 = (bf16[512,1024]{1,0:T(8,128)(2,1)S(1)}, bf16[512,1024]{1,0:T(8,128)(2,1)S(1)}, u32[]{:S(2)}, u32[]{:S(2)}) collective-permute-start(bf16[512,1024]{1,0:T(8,128)(2,1)S(1)} %collective-permute-done.4), channel_id=1, source_target_pairs={{2,0},{4,2},{6,4},{7,6},{5,7},{3,5},{1,3},{0,1},{10,8},{12,10},{14... | collective-permute-start | bytes 3145736 | tf_op jit(solution)/shard_map/ppermute | solution.py:95
  63.4 21.5 %collective-permute-start.8 = (bf16[2048,256]{1,0:T(8,128)(2,1)S(1)}, bf16[2048,256]{1,0:T(8,128)(2,1)S(1)}, u32[]{:S(2)}, u32[]{:S(2)}) collective-permute-start(bf16[2048,256]{1,0:T(8,128)(2,1)S(1)} %get-tuple-element.105), channel_id=1, source_target_pairs={{0,16},{8,24},{16,0},{24,8},{1,17},{9,25},{17,1},{25,9},{2,18},{10... | collective-permute-start | bytes 3145736 | tf_op jit(solution)/shard_map/ppermute | solution.py:23
  84.9 16.3 %collective-permute-start.13 = (bf16[2048,256]{1,0:T(8,128)(2,1)}, bf16[2048,256]{1,0:T(8,128)(2,1)S(1)}, u32[]{:S(2)}, u32[]{:S(2)}) collective-permute-start(bf16[2048,256]{1,0:T(8,128)(2,1)} %collective-permute-done.2.refs_2_), channel_id=1, source_target_pairs={{0,8},{8,0},{16,24},{24,16},{1,9},{9,1},{17,25},{25,17},{2,10},{10... | collective-permute-start | bytes 3145736 | tf_op jit(solution)/shard_map/ppermute | solution.py:23
  85.0 16.3 %collective-permute-start.12 = (bf16[2048,256]{1,0:T(8,128)(2,1)}, bf16[2048,256]{1,0:T(8,128)(2,1)S(1)}, u32[]{:S(2)}, u32[]{:S(2)}) collective-permute-start(bf16[2048,256]{1,0:T(8,128)(2,1)} %copy_bitcast_fusion.refs_0_), channel_id=1, source_target_pairs={{0,8},{8,0},{16,24},{24,16},{1,9},{9,1},{17,25},{25,17},{2,10},{10... | collective-permute-start | bytes 3145736 | tf_op jit(solution)/shard_map/ppermute | solution.py:23
  85.5 13.9 %collective-permute-start.10 = (bf16[256,1024]{1,0:T(8,128)(2,1)S(1)}, bf16[256,1024]{1,0:T(8,128)(2,1)S(1)}, u32[]{:S(2)}, u32[]{:S(2)}) collective-permute-start(bf16[256,1024]{1,0:T(8,128)(2,1)S(1)} %slice.89), channel_id=1, source_target_pairs={{2,0},{4,2},{6,4},{7,6},{5,7},{3,5},{1,3},{0,1},{10,8},{12,10},{14... | collective-permute-start | bytes 1572872 | tf_op jit(solution)/shard_map/ppermute | solution.py:95
  87.0 13.9 %collective-permute-start.9 = (bf16[256,1024]{1,0:T(8,128)(2,1)S(1)}, bf16[256,1024]{1,0:T(8,128)(2,1)S(1)}, u32[]{:S(2)}, u32[]{:S(2)}) collective-permute-start(bf16[256,1024]{1,0:T(8,128)(2,1)S(1)} %slice.88), channel_id=1, source_target_pairs={{0,2},{2,4},{4,6},{6,7},{7,5},{5,3},{3,1},{1,0},{8,10},{10,12},{12... | collective-permute-start | bytes 1572872 | tf_op jit(solution)/shard_map/ppermute | solution.py:95
  87.8 13.5 %collective-permute-start.11 = (bf16[2048,128]{1,0:T(8,128)(2,1)S(1)}, bf16[2048,128]{1,0:T(8,128)(2,1)}, u32[]{:S(2)}, u32[]{:S(2)}) collective-permute-start(bf16[2048,128]{1,0:T(8,128)(2,1)S(1)} %get-tuple-element.113), channel_id=1, source_target_pairs={{0,16},{8,24},{16,0},{24,8},{1,17},{9,25},{17,1},{25,9},{2,18},{10... | collective-permute-start | bytes 1572872 | tf_op jit(solution)/shard_map/ppermute | solution.py:23
  103.2 31.0 %collective-permute-start.19 = (bf16[2048,256]{1,0:T(8,128)(2,1)}, bf16[2048,256]{1,0:T(8,128)(2,1)}, u32[]{:S(2)}, u32[]{:S(2)}) collective-permute-start(bf16[2048,256]{1,0:T(8,128)(2,1)} %get-tuple-element.134), channel_id=1, source_target_pairs={{0,16},{8,24},{16,0},{24,8},{1,17},{9,25},{17,1},{25,9},{2,18},{10... | collective-permute-start | bytes 3145736 | tf_op jit(solution)/shard_map/ppermute | solution.py:23
  114.3 19.8 %collective-permute-start.14 = (bf16[512,256]{1,0:T(8,128)(2,1)}, bf16[512,256]{1,0:T(8,128)(2,1)S(1)}, u32[]{:S(2)}, u32[]{:S(2)}) collective-permute-start(bf16[512,256]{1,0:T(8,128)(2,1)} %shard_map.65.refs_1_), channel_id=1, source_target_pairs={{0,16},{8,24},{16,0},{24,8},{1,17},{9,25},{17,1},{25,9},{2,18},{10... | collective-permute-start | bytes 786440 | tf_op jit(solution)/shard_map/ppermute | solution.py:23
  115.7 18.5 %collective-permute-start.18 = (bf16[512,256]{1,0:T(8,128)(2,1)}, bf16[512,256]{1,0:T(8,128)(2,1)S(1)}, u32[]{:S(2)}, u32[]{:S(2)}) collective-permute-start(bf16[512,256]{1,0:T(8,128)(2,1)} %shard_map.65.refs_1_), channel_id=1, source_target_pairs={{0,8},{8,0},{16,24},{24,16},{1,9},{9,1},{17,25},{25,17},{2,10},{10... | collective-permute-start | bytes 786440 | tf_op jit(solution)/shard_map/ppermute | solution.py:23
  134.9 25.3 %collective-permute-start.23 = (bf16[2048,128]{1,0:T(8,128)(2,1)}, bf16[2048,128]{1,0:T(8,128)(2,1)}, u32[]{:S(2)}, u32[]{:S(2)}) collective-permute-start(bf16[2048,128]{1,0:T(8,128)(2,1)} %get-tuple-element.139), channel_id=1, source_target_pairs={{0,16},{8,24},{16,0},{24,8},{1,17},{9,25},{17,1},{25,9},{2,18},{10... | collective-permute-start | bytes 1572872 | tf_op jit(solution)/shard_map/ppermute | solution.py:23
  144.4 15.8 %collective-permute-start.21 = (bf16[512,512]{1,0:T(8,128)(2,1)S(1)}, bf16[512,512]{1,0:T(8,128)(2,1)}, u32[]{:S(2)}, u32[]{:S(2)}) collective-permute-start(bf16[512,512]{1,0:T(8,128)(2,1)S(1)} %shard_map.67), channel_id=1, source_target_pairs={{0,2},{2,4},{4,6},{6,7},{7,5},{5,3},{3,1},{1,0},{8,10},{10,12},{12... | collective-permute-start | bytes 1572872 | tf_op jit(solution)/shard_map/ppermute | solution.py:95
  146.0 14.2 %collective-permute-start.22 = (bf16[512,512]{1,0:T(8,128)(2,1)S(1)}, bf16[512,512]{1,0:T(8,128)(2,1)}, u32[]{:S(2)}, u32[]{:S(2)}) collective-permute-start(bf16[512,512]{1,0:T(8,128)(2,1)S(1)} %shard_map.67), channel_id=1, source_target_pairs={{2,0},{4,2},{6,4},{7,6},{5,7},{3,5},{1,3},{0,1},{10,8},{12,10},{14... | collective-permute-start | bytes 1572872 | tf_op jit(solution)/shard_map/ppermute | solution.py:95
  160.2 22.9 %collective-permute-start.29 = (bf16[2048,1024]{1,0:T(8,128)(2,1)}, bf16[2048,1024]{1,0:T(8,128)(2,1)}, u32[]{:S(2)}, u32[]{:S(2)}) collective-permute-start(bf16[2048,1024]{1,0:T(8,128)(2,1)} %refs_2_), channel_id=1, source_target_pairs={{0,8},{8,0},{16,24},{24,16},{1,9},{9,1},{17,25},{25,17},{2,10},{10... | collective-permute-start | bytes 12582920 | tf_op jit(solution)/shard_map/ppermute | solution.py:23
  161.5 21.6 %collective-permute-start.26 = (bf16[512,512]{1,0:T(8,128)(2,1)}, bf16[512,512]{1,0:T(8,128)(2,1)S(1)}, u32[]{:S(2)}, u32[]{:S(2)}) collective-permute-start(bf16[512,512]{1,0:T(8,128)(2,1)} %collective-permute-done.21), channel_id=1, source_target_pairs={{0,2},{2,4},{4,6},{6,7},{7,5},{5,3},{3,1},{1,0},{8,10},{10,12},{12... | collective-permute-start | bytes 1572872 | tf_op jit(solution)/shard_map/ppermute | solution.py:95
  163.1 20.0 %collective-permute-start.27 = (bf16[512,512]{1,0:T(8,128)(2,1)}, bf16[512,512]{1,0:T(8,128)(2,1)S(1)}, u32[]{:S(2)}, u32[]{:S(2)}) collective-permute-start(bf16[512,512]{1,0:T(8,128)(2,1)} %collective-permute-done.22), channel_id=1, source_target_pairs={{2,0},{4,2},{6,4},{7,6},{5,7},{3,5},{1,3},{0,1},{10,8},{12,10},{14... | collective-permute-start | bytes 1572872 | tf_op jit(solution)/shard_map/ppermute | solution.py:95
  183.1 28.9 %collective-permute-start.34 = (bf16[512,512]{1,0:T(8,128)(2,1)S(1)}, bf16[512,512]{1,0:T(8,128)(2,1)S(1)}, u32[]{:S(2)}, u32[]{:S(2)}) collective-permute-start(bf16[512,512]{1,0:T(8,128)(2,1)S(1)} %shard_map.72), channel_id=1, source_target_pairs={{0,2},{2,4},{4,6},{6,7},{7,5},{5,3},{3,1},{1,0},{8,10},{10,12},{12... | collective-permute-start | bytes 1572872 | tf_op jit(solution)/shard_map/ppermute | solution.py:95
  184.7 27.3 %collective-permute-start.35 = (bf16[512,512]{1,0:T(8,128)(2,1)S(1)}, bf16[512,512]{1,0:T(8,128)(2,1)S(1)}, u32[]{:S(2)}, u32[]{:S(2)}) collective-permute-start(bf16[512,512]{1,0:T(8,128)(2,1)S(1)} %shard_map.72), channel_id=1, source_target_pairs={{2,0},{4,2},{6,4},{7,6},{5,7},{3,5},{1,3},{0,1},{10,8},{12,10},{14... | collective-permute-start | bytes 1572872 | tf_op jit(solution)/shard_map/ppermute | solution.py:95
  185.2 22.8 %collective-permute-start.30 = (bf16[512,512]{1,0:T(8,128)(2,1)S(1)}, bf16[512,512]{1,0:T(8,128)(2,1)S(1)}, u32[]{:S(2)}, u32[]{:S(2)}) collective-permute-start(bf16[512,512]{1,0:T(8,128)(2,1)S(1)} %collective-permute-done.26), channel_id=1, source_target_pairs={{0,2},{2,4},{4,6},{6,7},{7,5},{5,3},{3,1},{1,0},{8,10},{10,12},{12... | collective-permute-start | bytes 1572872 | tf_op jit(solution)/shard_map/ppermute | solution.py:95
  186.7 23.1 %collective-permute-start.31 = (bf16[512,512]{1,0:T(8,128)(2,1)S(1)}, bf16[512,512]{1,0:T(8,128)(2,1)S(1)}, u32[]{:S(2)}, u32[]{:S(2)}) collective-permute-start(bf16[512,512]{1,0:T(8,128)(2,1)S(1)} %collective-permute-done.27), channel_id=1, source_target_pairs={{2,0},{4,2},{6,4},{7,6},{5,7},{3,5},{1,3},{0,1},{10,8},{12,10},{14... | collective-permute-start | bytes 1572872 | tf_op jit(solution)/shard_map/ppermute | solution.py:95
  212.0 18.2 %collective-permute-start.36 = (bf16[512,512]{1,0:T(8,128)(2,1)S(1)}, bf16[512,512]{1,0:T(8,128)(2,1)S(1)}, u32[]{:S(2)}, u32[]{:S(2)}) collective-permute-start(bf16[512,512]{1,0:T(8,128)(2,1)S(1)} %collective-permute-done.34), channel_id=1, source_target_pairs={{0,2},{2,4},{4,6},{6,7},{7,5},{5,3},{3,1},{1,0},{8,10},{10,12},{12... | collective-permute-start | bytes 1572872 | tf_op jit(solution)/shard_map/ppermute | solution.py:95
  213.6 18.2 %collective-permute-start.37 = (bf16[512,512]{1,0:T(8,128)(2,1)S(1)}, bf16[512,512]{1,0:T(8,128)(2,1)S(1)}, u32[]{:S(2)}, u32[]{:S(2)}) collective-permute-start(bf16[512,512]{1,0:T(8,128)(2,1)S(1)} %collective-permute-done.35), channel_id=1, source_target_pairs={{2,0},{4,2},{6,4},{7,6},{5,7},{3,5},{1,3},{0,1},{10,8},{12,10},{14... | collective-permute-start | bytes 1572872 | tf_op jit(solution)/shard_map/ppermute | solution.py:95
  231.8 13.9 %collective-permute-start.38 = (bf16[512,512]{1,0:T(8,128)(2,1)S(1)}, bf16[512,512]{1,0:T(8,128)(2,1)S(1)}, u32[]{:S(2)}, u32[]{:S(2)}) collective-permute-start(bf16[512,512]{1,0:T(8,128)(2,1)S(1)} %collective-permute-done.36), channel_id=1, source_target_pairs={{0,2},{2,4},{4,6},{6,7},{7,5},{5,3},{3,1},{1,0},{8,10},{10,12},{12... | collective-permute-start | bytes 1572872 | tf_op jit(solution)/shard_map/ppermute | solution.py:95
  233.3 13.6 %collective-permute-start.39 = (bf16[512,512]{1,0:T(8,128)(2,1)S(1)}, bf16[512,512]{1,0:T(8,128)(2,1)S(1)}, u32[]{:S(2)}, u32[]{:S(2)}) collective-permute-start(bf16[512,512]{1,0:T(8,128)(2,1)S(1)} %collective-permute-done.37), channel_id=1, source_target_pairs={{2,0},{4,2},{6,4},{7,6},{5,7},{3,5},{1,3},{0,1},{10,8},{12,10},{14... | collective-permute-start | bytes 1572872 | tf_op jit(solution)/shard_map/ppermute | solution.py:95
  (23 other events, 179.1 us)
Sparse Core Ops, SparseCore 0:
  134.3 107.0 all-gather.2

commit v14 on v13

--- a/solution.py
+++ b/solution.py
@@ -441,8 +441,10 @@
     last_far = by_block([gather_near(last_other)])
     late = [*late, project(panel, q_near, last_far, first, -1, factor, *tables)]
     late = jnp.concatenate(late, axis=1)
+    found, (late, panels[0]) = ring.hop([late, panels[0]])
+    panels[0] = put(panels[0], found)
     heads = attend(r, [late], kv_pieces)
-    o_near = gather_near(after(wo, last_other))
+    o_near = gather_near(after(wo, late))
     found, (heads, panels[0], *o_near) = ring.hop([heads, panels[0], *o_near])
     panels[0] = put(panels[0], found)
     second = Ring(heads, 1)

time: 277 us -> 268 us (0.968)
  waiting for transfers between devices: 112 us -> 102 us
    ppermute x24, waiting for transfers between devices: 89.2 us -> 79.3 us  [hop(): lax.ppermute(s[0], 'col', s[1])]
    unnamed x24 -> x28, local copies, waits for them, and re-layouts: 5.35 us -> 6.14 us
  transfers between devices with their start and end apart: 43 -> 43, of which waited for: 22 -> 22; matrix products, arithmetic and copies ran while one was open for 16% -> 16% of each run, Pallas kernels for 20% -> 21%
where the time goes in v14:
time: 268 us; the launch traced here: 267 us
  waiting for transfers between devices  102 us (38%)
  Pallas kernels  69.4 us (26%)
  starting transfers between devices  32.7 us (12%)
  local copies, waits for them, and re-layouts  29 us (11%)
  other arithmetic  20.1 us (8%)
  between operations  13.8 us (5%)
    ppermute x24, waiting for transfers between devices, hop(): lax.ppermute(s[0], 'col', s[1])  79.3 us
    pallas_call x4, Pallas kernels, project(): pl.pallas_call(functools.partial(project_kernel, len(near), len(far), chu...  36.6 us
    ppermute x24, starting transfers between devices, hop(): lax.ppermute(s[0], 'col', s[1])  24.9 us
    ppermute x18, waiting for transfers between devices, swap(): lax.ppermute(array, axis, [(i, i ^ mask) for i in range(lax.axis_size(axi...  23 us
    pallas_call x2, Pallas kernels, finish(): pl.pallas_call(functools.partial(finish_kernel, steps, per, rows, len(pan...  18.7 us
    dynamic_update_slice x18, local copies, waits for them, and re-layouts, put(): panel = lax.dynamic_update_slice(panel, piece[None], (slot, first, 0))  16.7 us
    pallas_call x2, Pallas kernels, attend(): pl.pallas_call(functools.partial(attend_kernel, parts, chunks, pair), gri...  14.1 us
    dynamic_update_slice x9, other arithmetic, put(): panel = lax.dynamic_update_slice(panel, piece[None], (slot, first, 0))  10.6 us
  transfers between devices with their start and end apart: 43, of which 22 were waited for; matrix products, arithmetic and copies ran while one was open for 16% of the time, Pallas kernels for 21%

profile of v14, /device:TPU:2, one launch (start us, length us, event | category | flops | bytes accessed | tf_op | source)
XLA Modules:
  0.0 267.3 jit_solution(12359989657833603174)
XLA Ops:
  6.5 1.6 collective-permute-start
  8.6 2.3 copy_bitcast_fusion.refs_0_
  12.6 1.8 fusion.36
  15.7 2.1 pad_maximum_fusion.1
  17.8 2.0 fusion.38
  19.8 3.1 %fusion.39 = (bf16[2048,256]{1,0:T(8,128)(2,1)}, bf16[2048,256]{1,0:T(8,128)(2,1)S(1)}, bf16[2048,256]{1,0:T(8,128)(2,1)S(1)}) fusion(bf16[2048,1024]{1,0:T(8,128)(2,1)} %refs_0_.2), kind=kLoop, calls=%fused_computation.91 | loop fusion | bytes 6291456 | tf_op jit(solution)/shard_map/slice | solution.py:352
  22.9 12.6 %collective-permute-done.2.refs_2_ = bf16[2048,256]{1,0:T(8,128)(2,1)} collective-permute-done((bf16[2048,256]{1,0:T(8,128)(2,1)}, bf16[2048,256]{1,0:T(8,128)(2,1)}, u32[]{:S(2)}, u32[]{:S(2)}) %collective-permute-start.2) | collective-permute-done | bytes 1048608 | tf_op jit(solution)/shard_map/ppermute | solution.py:23
  35.5 1.6 collective-permute-start.3
  41.0 18.0 %collective-permute-done.3 = bf16[512,1024]{1,0:T(8,128)(2,1)S(1)} collective-permute-done((bf16[512,1024]{1,0:T(8,128)(2,1)S(1)}, bf16[512,1024]{1,0:T(8,128)(2,1)S(1)}, u32[]{:S(2)}, u32[]{:S(2)}) %collective-permute-start.3) | collective-permute-done | bytes 1048608 | tf_op jit(solution)/shard_map/ppermute | solution.py:95
  61.4 1.6 collective-permute-start.6
  67.2 16.2 %collective-permute-done.6 = bf16[512,1024]{1,0:T(8,128)(2,1)S(1)} collective-permute-done((bf16[512,1024]{1,0:T(8,128)(2,1)S(1)}, bf16[512,1024]{1,0:T(8,128)(2,1)S(1)}, u32[]{:S(2)}, u32[]{:S(2)}) %collective-permute-start.6) | collective-permute-done | bytes 1048608 | tf_op jit(solution)/shard_map/ppermute | solution.py:95
  91.7 7.8 %collective-permute-done.10 = bf16[256,1024]{1,0:T(8,128)(2,1)S(1)} collective-permute-done((bf16[256,1024]{1,0:T(8,128)(2,1)S(1)}, bf16[256,1024]{1,0:T(8,128)(2,1)S(1)}, u32[]{:S(2)}, u32[]{:S(2)}) %collective-permute-start.10) | collective-permute-done | bytes 524320 | tf_op jit(solution)/shard_map/ppermute | solution.py:95
  107.1 7.2 %shard_map.65.refs_1_ = bf16[512,256]{1,0:T(8,128)(2,1)} custom-call(bf16[8,512,1024]{2,1,0:T(8,128)(2,1)} %fusion.33.panel_ref, bf16[2048,256]{1,0:T(8,128)(2,1)} %copy_bitcast_fusion.refs_0_, bf16[2048,256]{1,0:T(8,128)(2,1)} %copy-done.10, bf16[2048,256]{1,0:T(8,128)(2,1)} %collective-permute-done.2.refs_2_, bf16[2048,256]{1,0:T(8,128)(2,1)} %copy-done.9, ...), custom_call_target="tpu_custom_call" | custom-call | flops 1 | bytes 1 | tf_op jit(solution)/shard_map/pallas_call | solution.py:171
  115.6 10.6 %shard_map.66.refs_0_ = bf16[512,512]{1,0:T(8,128)(2,1)} custom-call(bf16[8,512,1024]{2,1,0:T(8,128)(2,1)} %fusion.33.panel_ref, bf16[2048,1024]{1,0:T(8,128)(2,1)} %refs_0_.2, bf16[2048,1024]{1,0:T(8,128)(2,1)} %collective-permute-done.15.refs_1_, bf16[2048,256]{1,0:T(8,128)(2,1)} %copy-done.5, bf16[2048,256]{1,0:T(8,128)(2,1)} %copy-done.7, ...), custom_call_target="tpu_custom_call" | custom-call | flops 1 | bytes 1 | tf_op jit(solution)/shard_map/pallas_call | solution.py:171
  126.3 7.9 %collective-permute-done.14.refs_3_ = bf16[512,256]{1,0:T(8,128)(2,1)S(1)} collective-permute-done((bf16[512,256]{1,0:T(8,128)(2,1)}, bf16[512,256]{1,0:T(8,128)(2,1)S(1)}, u32[]{:S(2)}, u32[]{:S(2)}) %collective-permute-start.14) | collective-permute-done | bytes 262176 | tf_op jit(solution)/shard_map/ppermute | solution.py:23
  135.7 1.6 collective-permute-done.20.refs_4_
  137.3 7.1 %shard_map.67 = bf16[512,512]{1,0:T(8,128)(2,1)S(1)} custom-call(s32[1]{0:T(128)} %bitcast.r_ref, bf16[512,512]{1,0:T(8,128)(2,1)S(1)} %copy-done.1, bf16[512,256]{1,0:T(8,128)(2,1)S(1)} %copy-done, bf16[512,256]{1,0:T(8,128)(2,1)S(1)} %collective-permute-done.18.refs_2_, bf16[512,256]{1,0:T(8,128)(2,1)S(1)} %collective-permute-done.14.refs_3_, ...), custom_call_target="tpu_custom_call" | custom-call | flops 1 | bytes 1 | tf_op jit(solution)/shard_map/pallas_call | solution.py:254
  144.4 1.6 collective-permute-start.21
  148.3 11.9 %shard_map.70 = bf16[512,384]{1,0:T(8,128)(2,1)} custom-call(bf16[8,512,1024]{2,1,0:T(8,128)(2,1)} %fusion.33.panel_ref, bf16[2048,1024]{1,0:T(8,128)(2,1)} %refs_0_.2, bf16[2048,1024]{1,0:T(8,128)(2,1)} %collective-permute-done.15.refs_1_, bf16[2048,128]{1,0:T(8,128)(2,1)} %collective-permute-done.11.refs_2_, ...), custom_call_target="tpu_custom_call" | custom-call | flops 1 | bytes 1 | tf_op jit(solution)/shard_map/pallas_call | solution.py:171
  162.1 1.6 collective-permute-start.26
  164.2 1.9 bitcast_dynamic-update-slice_fusion.12
  166.0 1.9 bitcast_dynamic-update-slice_fusion.11
  168.8 6.9 %shard_map.71 = bf16[512,128]{1,0:T(8,128)(2,1)} custom-call(bf16[8,512,1024]{2,1,0:T(8,128)(2,1)} %fusion.33.panel_ref, bf16[2048,1024]{1,0:T(8,128)(2,1)} %refs_0_.2, bf16[2048,1024]{1,0:T(8,128)(2,1)} %collective-permute-done.15.refs_1_, bf16[2048,128]{1,0:T(8,128)(2,1)} %collective-permute-done.23.refs_2_, bf16[2048,128]{1,0:T(8,128)(2,1)} %copy-done.11, ...), custom_call_target="tpu_custom_call" | custom-call | flops 1 | bytes 1 | tf_op jit(solution)/shard_map/pallas_call | solution.py:171
  177.5 1.6 collective-permute-start.29
  179.5 7.0 %shard_map.72 = bf16[512,512]{1,0:T(8,128)(2,1)S(1)} custom-call(s32[1]{0:T(128)} %bitcast.r_ref, bf16[512,512]{1,0:T(8,128)(2,1)S(1)} %pad_maximum_fusion.refs_0_, bf16[512,256]{1,0:T(8,128)(2,1)S(1)} %copy-done, bf16[512,256]{1,0:T(8,128)(2,1)S(1)} %collective-permute-done.18.refs_2_, bf16[512,256]{1,0:T(8,128)(2,1)S(1)} %collective-permute-done.14.refs_3_, ...), custom_call_target="tpu_custom_call" | custom-call | flops 1 | bytes 1 | tf_op jit(solution)/shard_map/pallas_call | solution.py:254
  188.3 3.5 %collective-permute-done.29 = bf16[512,512]{1,0:T(8,128)(2,1)S(1)} collective-permute-done((bf16[512,512]{1,0:T(8,128)(2,1)S(1)}, bf16[512,512]{1,0:T(8,128)(2,1)S(1)}, u32[]{:S(2)}, u32[]{:S(2)}) %collective-permute-start.29) | collective-permute-done | bytes 524320 | tf_op jit(solution)/shard_map/ppermute | solution.py:95
  199.8 12.2 %collective-permute-done.32 = bf16[256,512]{1,0:T(8,128)(2,1)S(1)} collective-permute-done((bf16[256,512]{1,0:T(8,128)(2,1)S(1)}, bf16[256,512]{1,0:T(8,128)(2,1)S(1)}, u32[]{:S(2)}, u32[]{:S(2)}) %collective-permute-start.32) | collective-permute-done | bytes 262176 | tf_op jit(solution)/shard_map/ppermute | solution.py:95
  217.8 7.8 %collective-permute-done.36 = bf16[512,512]{1,0:T(8,128)(2,1)S(1)} collective-permute-done((bf16[512,512]{1,0:T(8,128)(2,1)S(1)}, bf16[512,512]{1,0:T(8,128)(2,1)S(1)}, u32[]{:S(2)}, u32[]{:S(2)}) %collective-permute-start.36) | collective-permute-done | bytes 524320 | tf_op jit(solution)/shard_map/ppermute | solution.py:95
  229.6 5.8 %shard_map.73.refs_5_ = f32[512,1024]{1,0:T(8,128)} custom-call(s32[1]{0:T(128)} %bitcast.r_ref, bf16[8,512,512]{2,1,0:T(8,128)(2,1)} %bitcast_dynamic-update-slice_fusion.16.refs_0_, bf16[2048,1024]{1,0:T(8,128)(2,1)} %refs_2_, bf16[2048,1024]{1,0:T(8,128)(2,1)} %copy-done.2), custom_call_target="tpu_custom_call" | custom-call | flops 1 | bytes 1 | tf_op jit(solution)/shard_map/pallas_call | solution.py:303
  237.1 1.6 collective-permute-done.38
  242.5 2.6 collective-permute-done.40
  247.6 12.9 %shard_map.74 = bf16[512,1024]{1,0:T(8,128)(2,1)} custom-call(s32[1]{0:T(128)} %bitcast.r_ref, bf16[8,512,512]{2,1,0:T(8,128)(2,1)} %bitcast_dynamic-update-slice_fusion.16.refs_0_, bf16[8,512,512]{2,1,0:T(8,128)(2,1)} %bitcast_dynamic-update-slice_fusion.14.refs_1_, bf16[2048,1024]{1,0:T(8,128)(2,1)} %refs_2_, bf16[2048,1024]{1,0:T(8,128)(2,1)} %copy-done.2, ...), custom_call_target="tpu_custom_call" | custom-call | flops 1 | bytes 1 | tf_op jit(solution)/shard_map/pallas_call | solution.py:303
  (154 shorter events, 67.6 us)
Async XLA Ops:
  6.5 241.0 %all-gather.3.cloned.1.call-start = ((), (), s32[]{:S(2)}) async-start(), calls=%async_computation | async-start | bytes 20971520 | tf_op jit(solution)/shard_map/all_gather | solution.py:428
  6.5 29.0 %collective-permute-start = (bf16[512,1024]{1,0:T(8,128)(2,1)}, bf16[512,1024]{1,0:T(8,128)(2,1)S(1)}, u32[]{:S(2)}, u32[]{:S(2)}) collective-permute-start(bf16[512,1024]{1,0:T(8,128)(2,1)} %param.6), channel_id=1, source_target_pairs={{0,2},{2,4},{4,6},{6,7},{7,5},{5,3},{3,1},{1,0},{8,10},{10,12},{12... | collective-permute-start | bytes 3145736 | tf_op jit(solution)/shard_map/ppermute | solution.py:95
  8.1 27.4 %collective-permute-start.1 = (bf16[512,1024]{1,0:T(8,128)(2,1)}, bf16[512,1024]{1,0:T(8,128)(2,1)S(1)}, u32[]{:S(2)}, u32[]{:S(2)}) collective-permute-start(bf16[512,1024]{1,0:T(8,128)(2,1)} %param.6), channel_id=1, source_target_pairs={{2,0},{4,2},{6,4},{7,6},{5,7},{3,5},{1,3},{0,1},{10,8},{12,10},{14... | collective-permute-start | bytes 3145736 | tf_op jit(solution)/shard_map/ppermute | solution.py:95
  10.9 24.7 %collective-permute-start.2 = (bf16[2048,256]{1,0:T(8,128)(2,1)}, bf16[2048,256]{1,0:T(8,128)(2,1)}, u32[]{:S(2)}, u32[]{:S(2)}) collective-permute-start(bf16[2048,256]{1,0:T(8,128)(2,1)} %copy_bitcast_fusion.refs_0_), channel_id=1, source_target_pairs={{0,16},{8,24},{16,0},{24,8},{1,17},{9,25},{17,1},{25,9},{2,18},{10... | collective-permute-start | bytes 3145736 | tf_op jit(solution)/shard_map/ppermute | solution.py:23
  35.5 23.4 %collective-permute-start.3 = (bf16[512,1024]{1,0:T(8,128)(2,1)S(1)}, bf16[512,1024]{1,0:T(8,128)(2,1)S(1)}, u32[]{:S(2)}, u32[]{:S(2)}) collective-permute-start(bf16[512,1024]{1,0:T(8,128)(2,1)S(1)} %collective-permute-done), channel_id=1, source_target_pairs={{0,2},{2,4},{4,6},{6,7},{7,5},{5,3},{3,1},{1,0},{8,10},{10,12},{12... | collective-permute-start | bytes 3145736 | tf_op jit(solution)/shard_map/ppermute | solution.py:95
  37.1 23.1 %collective-permute-start.4 = (bf16[512,1024]{1,0:T(8,128)(2,1)S(1)}, bf16[512,1024]{1,0:T(8,128)(2,1)S(1)}, u32[]{:S(2)}, u32[]{:S(2)}) collective-permute-start(bf16[512,1024]{1,0:T(8,128)(2,1)S(1)} %collective-permute-done.1), channel_id=1, source_target_pairs={{2,0},{4,2},{6,4},{7,6},{5,7},{3,5},{1,3},{0,1},{10,8},{12,10},{14... | collective-permute-start | bytes 3145736 | tf_op jit(solution)/shard_map/ppermute | solution.py:95
  37.6 22.9 %collective-permute-start.5 = (bf16[2048,256]{1,0:T(8,128)(2,1)S(1)}, bf16[2048,256]{1,0:T(8,128)(2,1)S(1)}, u32[]{:S(2)}, u32[]{:S(2)}) collective-permute-start(bf16[2048,256]{1,0:T(8,128)(2,1)S(1)} %get-tuple-element.98), channel_id=1, source_target_pairs={{0,16},{8,24},{16,0},{24,8},{1,17},{9,25},{17,1},{25,9},{2,18},{10... | collective-permute-start | bytes 3145736 | tf_op jit(solution)/shard_map/ppermute | solution.py:23
  61.4 22.0 %collective-permute-start.6 = (bf16[512,1024]{1,0:T(8,128)(2,1)S(1)}, bf16[512,1024]{1,0:T(8,128)(2,1)S(1)}, u32[]{:S(2)}, u32[]{:S(2)}) collective-permute-start(bf16[512,1024]{1,0:T(8,128)(2,1)S(1)} %collective-permute-done.3), channel_id=1, source_target_pairs={{0,2},{2,4},{4,6},{6,7},{7,5},{5,3},{3,1},{1,0},{8,10},{10,12},{12... | collective-permute-start | bytes 3145736 | tf_op jit(solution)/shard_map/ppermute | solution.py:95
  63.0 21.8 %collective-permute-start.7 = (bf16[512,1024]{1,0:T(8,128)(2,1)S(1)}, bf16[512,1024]{1,0:T(8,128)(2,1)S(1)}, u32[]{:S(2)}, u32[]{:S(2)}) collective-permute-start(bf16[512,1024]{1,0:T(8,128)(2,1)S(1)} %collective-permute-done.4), channel_id=1, source_target_pairs={{2,0},{4,2},{6,4},{7,6},{5,7},{3,5},{1,3},{0,1},{10,8},{12,10},{14... | collective-permute-start | bytes 3145736 | tf_op jit(solution)/shard_map/ppermute | solution.py:95
  63.4 21.5 %collective-permute-start.8 = (bf16[2048,256]{1,0:T(8,128)(2,1)S(1)}, bf16[2048,256]{1,0:T(8,128)(2,1)S(1)}, u32[]{:S(2)}, u32[]{:S(2)}) collective-permute-start(bf16[2048,256]{1,0:T(8,128)(2,1)S(1)} %get-tuple-element.106), channel_id=1, source_target_pairs={{0,16},{8,24},{16,0},{24,8},{1,17},{9,25},{17,1},{25,9},{2,18},{10... | collective-permute-start | bytes 3145736 | tf_op jit(solution)/shard_map/ppermute | solution.py:23
  85.0 16.3 %collective-permute-start.13 = (bf16[2048,256]{1,0:T(8,128)(2,1)}, bf16[2048,256]{1,0:T(8,128)(2,1)S(1)}, u32[]{:S(2)}, u32[]{:S(2)}) collective-permute-start(bf16[2048,256]{1,0:T(8,128)(2,1)} %collective-permute-done.2.refs_2_), channel_id=1, source_target_pairs={{0,8},{8,0},{16,24},{24,16},{1,9},{9,1},{17,25},{25,17},{2,10},{10... | collective-permute-start | bytes 3145736 | tf_op jit(solution)/shard_map/ppermute | solution.py:23
  85.0 16.3 %collective-permute-start.12 = (bf16[2048,256]{1,0:T(8,128)(2,1)}, bf16[2048,256]{1,0:T(8,128)(2,1)S(1)}, u32[]{:S(2)}, u32[]{:S(2)}) collective-permute-start(bf16[2048,256]{1,0:T(8,128)(2,1)} %copy_bitcast_fusion.refs_0_), channel_id=1, source_target_pairs={{0,8},{8,0},{16,24},{24,16},{1,9},{9,1},{17,25},{25,17},{2,10},{10... | collective-permute-start | bytes 3145736 | tf_op jit(solution)/shard_map/ppermute | solution.py:23
  85.5 13.9 %collective-permute-start.10 = (bf16[256,1024]{1,0:T(8,128)(2,1)S(1)}, bf16[256,1024]{1,0:T(8,128)(2,1)S(1)}, u32[]{:S(2)}, u32[]{:S(2)}) collective-permute-start(bf16[256,1024]{1,0:T(8,128)(2,1)S(1)} %slice.89), channel_id=1, source_target_pairs={{2,0},{4,2},{6,4},{7,6},{5,7},{3,5},{1,3},{0,1},{10,8},{12,10},{14... | collective-permute-start | bytes 1572872 | tf_op jit(solution)/shard_map/ppermute | solution.py:95
  87.0 13.9 %collective-permute-start.9 = (bf16[256,1024]{1,0:T(8,128)(2,1)S(1)}, bf16[256,1024]{1,0:T(8,128)(2,1)S(1)}, u32[]{:S(2)}, u32[]{:S(2)}) collective-permute-start(bf16[256,1024]{1,0:T(8,128)(2,1)S(1)} %slice.88), channel_id=1, source_target_pairs={{0,2},{2,4},{4,6},{6,7},{7,5},{5,3},{3,1},{1,0},{8,10},{10,12},{12... | collective-permute-start | bytes 1572872 | tf_op jit(solution)/shard_map/ppermute | solution.py:95
  87.8 13.5 %collective-permute-start.11 = (bf16[2048,128]{1,0:T(8,128)(2,1)S(1)}, bf16[2048,128]{1,0:T(8,128)(2,1)}, u32[]{:S(2)}, u32[]{:S(2)}) collective-permute-start(bf16[2048,128]{1,0:T(8,128)(2,1)S(1)} %get-tuple-element.114), channel_id=1, source_target_pairs={{0,16},{8,24},{16,0},{24,8},{1,17},{9,25},{17,1},{25,9},{2,18},{10... | collective-permute-start | bytes 1572872 | tf_op jit(solution)/shard_map/ppermute | solution.py:23
  102.3 13.3 %collective-permute-start.15 = (bf16[2048,1024]{1,0:T(8,128)(2,1)}, bf16[2048,1024]{1,0:T(8,128)(2,1)}, u32[]{:S(2)}, u32[]{:S(2)}) collective-permute-start(bf16[2048,1024]{1,0:T(8,128)(2,1)} %refs_0_.2), channel_id=1, source_target_pairs={{0,8},{8,0},{16,24},{24,16},{1,9},{9,1},{17,25},{25,17},{2,10},{10... | collective-permute-start | bytes 12582920 | tf_op jit(solution)/shard_map/ppermute | solution.py:23
  103.1 31.1 %collective-permute-start.19 = (bf16[2048,256]{1,0:T(8,128)(2,1)}, bf16[2048,256]{1,0:T(8,128)(2,1)}, u32[]{:S(2)}, u32[]{:S(2)}) collective-permute-start(bf16[2048,256]{1,0:T(8,128)(2,1)} %get-tuple-element.135), channel_id=1, source_target_pairs={{0,16},{8,24},{16,0},{24,8},{1,17},{9,25},{17,1},{25,9},{2,18},{10... | collective-permute-start | bytes 3145736 | tf_op jit(solution)/shard_map/ppermute | solution.py:23
  114.3 19.9 %collective-permute-start.14 = (bf16[512,256]{1,0:T(8,128)(2,1)}, bf16[512,256]{1,0:T(8,128)(2,1)S(1)}, u32[]{:S(2)}, u32[]{:S(2)}) collective-permute-start(bf16[512,256]{1,0:T(8,128)(2,1)} %shard_map.65.refs_1_), channel_id=1, source_target_pairs={{0,16},{8,24},{16,0},{24,8},{1,17},{9,25},{17,1},{25,9},{2,18},{10... | collective-permute-start | bytes 786440 | tf_op jit(solution)/shard_map/ppermute | solution.py:23
  115.6 18.6 %collective-permute-start.18 = (bf16[512,256]{1,0:T(8,128)(2,1)}, bf16[512,256]{1,0:T(8,128)(2,1)S(1)}, u32[]{:S(2)}, u32[]{:S(2)}) collective-permute-start(bf16[512,256]{1,0:T(8,128)(2,1)} %shard_map.65.refs_1_), channel_id=1, source_target_pairs={{0,8},{8,0},{16,24},{24,16},{1,9},{9,1},{17,25},{25,17},{2,10},{10... | collective-permute-start | bytes 786440 | tf_op jit(solution)/shard_map/ppermute | solution.py:23
  134.2 13.1 %collective-permute-start.25 = (bf16[2048,256]{1,0:T(8,128)(2,1)}, bf16[2048,256]{1,0:T(8,128)(2,1)S(1)}, u32[]{:S(2)}, u32[]{:S(2)}) collective-permute-start(bf16[2048,256]{1,0:T(8,128)(2,1)} %collective-permute-done.19.refs_3_), channel_id=1, source_target_pairs={{0,8},{8,0},{16,24},{24,16},{1,9},{9,1},{17,25},{25,17},{2,10},{10... | collective-permute-start | bytes 3145736 | tf_op jit(solution)/shard_map/ppermute | solution.py:23
  134.9 25.3 %collective-permute-start.23 = (bf16[2048,128]{1,0:T(8,128)(2,1)}, bf16[2048,128]{1,0:T(8,128)(2,1)}, u32[]{:S(2)}, u32[]{:S(2)}) collective-permute-start(bf16[2048,128]{1,0:T(8,128)(2,1)} %get-tuple-element.140), channel_id=1, source_target_pairs={{0,16},{8,24},{16,0},{24,8},{1,17},{9,25},{17,1},{25,9},{2,18},{10... | collective-permute-start | bytes 1572872 | tf_op jit(solution)/shard_map/ppermute | solution.py:23
  144.4 15.8 %collective-permute-start.21 = (bf16[512,512]{1,0:T(8,128)(2,1)S(1)}, bf16[512,512]{1,0:T(8,128)(2,1)S(1)}, u32[]{:S(2)}, u32[]{:S(2)}) collective-permute-start(bf16[512,512]{1,0:T(8,128)(2,1)S(1)} %shard_map.67), channel_id=1, source_target_pairs={{0,2},{2,4},{4,6},{6,7},{7,5},{5,3},{3,1},{1,0},{8,10},{10,12},{12... | collective-permute-start | bytes 1572872 | tf_op jit(solution)/shard_map/ppermute | solution.py:95
  146.0 15.0 %collective-permute-start.22 = (bf16[512,512]{1,0:T(8,128)(2,1)S(1)}, bf16[512,512]{1,0:T(8,128)(2,1)}, u32[]{:S(2)}, u32[]{:S(2)}) collective-permute-start(bf16[512,512]{1,0:T(8,128)(2,1)S(1)} %shard_map.67), channel_id=1, source_target_pairs={{2,0},{4,2},{6,4},{7,6},{5,7},{3,5},{1,3},{0,1},{10,8},{12,10},{14... | collective-permute-start | bytes 1572872 | tf_op jit(solution)/shard_map/ppermute | solution.py:95
  162.1 14.5 %collective-permute-start.26 = (bf16[512,512]{1,0:T(8,128)(2,1)}, bf16[512,512]{1,0:T(8,128)(2,1)S(1)}, u32[]{:S(2)}, u32[]{:S(2)}) collective-permute-start(bf16[512,512]{1,0:T(8,128)(2,1)} %copy-done.12), channel_id=1, source_target_pairs={{0,2},{2,4},{4,6},{6,7},{7,5},{5,3},{3,1},{1,0},{8,10},{10,12},{12... | collective-permute-start | bytes 1572872 | tf_op jit(solution)/shard_map/ppermute | solution.py:95
  163.7 13.8 %collective-permute-start.27 = (bf16[512,512]{1,0:T(8,128)(2,1)}, bf16[512,512]{1,0:T(8,128)(2,1)S(1)}, u32[]{:S(2)}, u32[]{:S(2)}) collective-permute-start(bf16[512,512]{1,0:T(8,128)(2,1)} %collective-permute-done.22), channel_id=1, source_target_pairs={{2,0},{4,2},{6,4},{7,6},{5,7},{3,5},{1,3},{0,1},{10,8},{12,10},{14... | collective-permute-start | bytes 1572872 | tf_op jit(solution)/shard_map/ppermute | solution.py:95
  177.5 15.7 %collective-permute-start.31 = (bf16[2048,1024]{1,0:T(8,128)(2,1)}, bf16[2048,1024]{1,0:T(8,128)(2,1)S(1)}, u32[]{:S(2)}, u32[]{:S(2)}) collective-permute-start(bf16[2048,1024]{1,0:T(8,128)(2,1)} %refs_2_), channel_id=1, source_target_pairs={{0,8},{8,0},{16,24},{24,16},{1,9},{9,1},{17,25},{25,17},{2,10},{10... | collective-permute-start | bytes 12582920 | tf_op jit(solution)/shard_map/ppermute | solution.py:23
  177.5 14.3 %collective-permute-start.29 = (bf16[512,512]{1,0:T(8,128)(2,1)S(1)}, bf16[512,512]{1,0:T(8,128)(2,1)S(1)}, u32[]{:S(2)}, u32[]{:S(2)}) collective-permute-start(bf16[512,512]{1,0:T(8,128)(2,1)S(1)} %collective-permute-done.26), channel_id=1, source_target_pairs={{0,2},{2,4},{4,6},{6,7},{7,5},{5,3},{3,1},{1,0},{8,10},{10,12},{12... | collective-permute-start | bytes 1572872 | tf_op jit(solution)/shard_map/ppermute | solution.py:95
  179.1 14.1 %collective-permute-start.30 = (bf16[512,512]{1,0:T(8,128)(2,1)S(1)}, bf16[512,512]{1,0:T(8,128)(2,1)S(1)}, u32[]{:S(2)}, u32[]{:S(2)}) collective-permute-start(bf16[512,512]{1,0:T(8,128)(2,1)S(1)} %collective-permute-done.27), channel_id=1, source_target_pairs={{2,0},{4,2},{6,4},{7,6},{5,7},{3,5},{1,3},{0,1},{10,8},{12,10},{14... | collective-permute-start | bytes 1572872 | tf_op jit(solution)/shard_map/ppermute | solution.py:95
  193.1 20.2 %collective-permute-start.34 = (bf16[512,512]{1,0:T(8,128)(2,1)S(1)}, bf16[512,512]{1,0:T(8,128)(2,1)S(1)}, u32[]{:S(2)}, u32[]{:S(2)}) collective-permute-start(bf16[512,512]{1,0:T(8,128)(2,1)S(1)} %shard_map.72), channel_id=1, source_target_pairs={{0,2},{2,4},{4,6},{6,7},{7,5},{5,3},{3,1},{1,0},{8,10},{10,12},{12... | collective-permute-start | bytes 1572872 | tf_op jit(solution)/shard_map/ppermute | solution.py:95
  194.6 18.7 %collective-permute-start.35 = (bf16[512,512]{1,0:T(8,128)(2,1)S(1)}, bf16[512,512]{1,0:T(8,128)(2,1)S(1)}, u32[]{:S(2)}, u32[]{:S(2)}) collective-permute-start(bf16[512,512]{1,0:T(8,128)(2,1)S(1)} %shard_map.72), channel_id=1, source_target_pairs={{2,0},{4,2},{6,4},{7,6},{5,7},{3,5},{1,3},{0,1},{10,8},{12,10},{14... | collective-permute-start | bytes 1572872 | tf_op jit(solution)/shard_map/ppermute | solution.py:95
  196.0 16.1 %collective-permute-start.32 = (bf16[256,512]{1,0:T(8,128)(2,1)S(1)}, bf16[256,512]{1,0:T(8,128)(2,1)S(1)}, u32[]{:S(2)}, u32[]{:S(2)}) collective-permute-start(bf16[256,512]{1,0:T(8,128)(2,1)S(1)} %slice.96), channel_id=1, source_target_pairs={{0,2},{2,4},{4,6},{6,7},{7,5},{5,3},{3,1},{1,0},{8,10},{10,12},{12... | collective-permute-start | bytes 786440 | tf_op jit(solution)/shard_map/ppermute | solution.py:95
  197.6 15.7 %collective-permute-start.33 = (bf16[256,512]{1,0:T(8,128)(2,1)S(1)}, bf16[256,512]{1,0:T(8,128)(2,1)S(1)}, u32[]{:S(2)}, u32[]{:S(2)}) collective-permute-start(bf16[256,512]{1,0:T(8,128)(2,1)S(1)} %slice.97), channel_id=1, source_target_pairs={{2,0},{4,2},{6,4},{7,6},{5,7},{3,5},{1,3},{0,1},{10,8},{12,10},{14... | collective-permute-start | bytes 786440 | tf_op jit(solution)/shard_map/ppermute | solution.py:95
  (25 other events, 204.4 us)
Sparse Core Ops, SparseCore 0:
  134.3 107.0 all-gather.2

commit v15 on v14

--- a/solution.py
+++ b/solution.py
@@ -435,33 +435,40 @@
     if late_far:
         late.append(project(panel, q_near, by_block(late_far), first, -1, factor, *tables))
         first += late[0].shape[1]
-    found, (last_other, *beside) = ring.hop([last_other, *panels, *late])
+    pending, (last_other, *beside) = ring.hop([last_other, *panels, *late])
     panels, late = take(beside, 2)
-    panels[0] = put(panels[0], found)
     last_far = by_block([gather_near(last_other)])
     late = [*late, project(panel, q_near, last_far, first, -1, factor, *tables)]
     late = jnp.concatenate(late, axis=1)
-    found, (late, panels[0]) = ring.hop([late, panels[0]])
-    panels[0] = put(panels[0], found)
+    found, (late,) = ring.hop([late])
+    pending += found
     heads = attend(r, [late], kv_pieces)
     o_near = gather_near(after(wo, late))
-    found, (heads, panels[0], *o_near) = ring.hop([heads, panels[0], *o_near])
-    panels[0] = put(panels[0], found)
+    found, (heads, *o_near) = ring.hop([heads, *o_near])
+    pending += found
     second = Ring(heads, 1)
     panels[1] = put(panels[1], second.found)
     half = n_col // 2
     for i in range(hops):
-        found, (panels[0],) = ring.hop([panels[0]])
-        panels[0] = put(panels[0], found)
-        beside = [panels[1]]
-        if i == hops - 1:
+        found, _ = ring.hop()
+        if i > 0:
+            panels[0] = put(panels[0], pending)
+            pending = []
+        pending += found
+        beside = panels
+        if i == hops - 2:
             steps = [(0, k) for k in range(half)]
-            beside.append(finish(r, panels[:1], steps, o_near, None, per, cols, jnp.float32))
-        found, (panels[1], *beside) = second.hop(beside)
+            total = finish(r, panels[:1], steps, o_near, None, per, cols, jnp.float32)
+            beside = [*panels, total]
+        found, beside = second.hop(beside)
+        panels, beside = take(beside, 2)
         panels[1] = put(panels[1], found)
-    (total,) = beside
-
-    steps = [(1, k) for k in range(half)] + [(g, k) for k in range(half, n_col) for g in (0, 1)]
+        if beside:
+            (total,) = beside
+
+    steps = [(1, k) for k in range(half)]
+    total = finish(r, panels, steps, o_near, None, per, cols, jnp.float32, total)
+    steps = [(g, k) for k in range(half, n_col) for g in (0, 1)]
     return finish(r, panels, steps, o_near, o_weights, per, cols, jnp.bfloat16, total)
 
 

time: 268 us -> 272 us (1.015)
  Pallas kernels: 69.4 us -> 74 us
    pallas_call x2 -> x3, Pallas kernels: 18.7 us -> 23.3 us  [finish(): pl.pallas_call(functools.partial(finish_kernel, steps, per, rows, len(pan...]
    unnamed x28 -> x26, local copies, waits for them, and re-layouts: 6.14 us -> 5.26 us
  transfers between devices with their start and end apart: 43 -> 43, of which waited for: 22 -> 23; matrix products, arithmetic and copies ran while one was open for 16% -> 16% of each run, Pallas kernels for 21% -> 24%
where the time goes in v15:
time: 272 us; the launch traced here: 271 us
  waiting for transfers between devices  101 us (37%)
  Pallas kernels  74 us (27%)
  starting transfers between devices  32.7 us (12%)
  local copies, waits for them, and re-layouts  29.2 us (11%)
  other arithmetic  20.1 us (7%)
  between operations  13.8 us (5%)
    ppermute x24, waiting for transfers between devices, hop(): lax.ppermute(s[0], 'col', s[1])  78.3 us
    pallas_call x4, Pallas kernels, project(): pl.pallas_call(functools.partial(project_kernel, len(near), len(far), chu...  36.6 us
    ppermute x24, starting transfers between devices, hop(): lax.ppermute(s[0], 'col', s[1])  24.8 us
    pallas_call x3, Pallas kernels, finish(): pl.pallas_call(functools.partial(finish_kernel, steps, per, rows, len(pan...  23.3 us
    ppermute x18, waiting for transfers between devices, swap(): lax.ppermute(array, axis, [(i, i ^ mask) for i in range(lax.axis_size(axi...  23 us
    dynamic_update_slice x18, local copies, waits for them, and re-layouts, put(): panel = lax.dynamic_update_slice(panel, piece[None], (slot, first, 0))  17.8 us
    pallas_call x2, Pallas kernels, attend(): pl.pallas_call(functools.partial(attend_kernel, parts, chunks, pair), gri...  14.1 us
    dynamic_update_slice x9, other arithmetic, put(): panel = lax.dynamic_update_slice(panel, piece[None], (slot, first, 0))  10.6 us
  transfers between devices with their start and end apart: 43, of which 23 were waited for; matrix products, arithmetic and copies ran while one was open for 16% of the time, Pallas kernels for 24%

profile of v15, /device:TPU:2, one launch (start us, length us, event | category | flops | bytes accessed | tf_op | source)
XLA Modules:
  0.0 271.1 jit_solution(8234611728046713693)
XLA Ops:
  6.5 1.6 collective-permute-start
  8.6 2.3 copy_bitcast_fusion.refs_0_
  12.6 1.8 fusion.36
  15.7 2.1 pad_maximum_fusion.1
  17.8 2.1 fusion.38
  19.8 3.1 %fusion.39 = (bf16[2048,256]{1,0:T(8,128)(2,1)}, bf16[2048,256]{1,0:T(8,128)(2,1)S(1)}, bf16[2048,256]{1,0:T(8,128)(2,1)S(1)}) fusion(bf16[2048,1024]{1,0:T(8,128)(2,1)} %refs_0_.2), kind=kLoop, calls=%fused_computation.91 | loop fusion | bytes 6291456 | tf_op jit(solution)/shard_map/slice | solution.py:352
  22.9 12.6 %collective-permute-done.2.refs_2_ = bf16[2048,256]{1,0:T(8,128)(2,1)} collective-permute-done((bf16[2048,256]{1,0:T(8,128)(2,1)}, bf16[2048,256]{1,0:T(8,128)(2,1)}, u32[]{:S(2)}, u32[]{:S(2)}) %collective-permute-start.2) | collective-permute-done | bytes 1048608 | tf_op jit(solution)/shard_map/ppermute | solution.py:23
  35.5 1.6 collective-permute-start.3
  41.0 18.0 %collective-permute-done.3 = bf16[512,1024]{1,0:T(8,128)(2,1)S(1)} collective-permute-done((bf16[512,1024]{1,0:T(8,128)(2,1)S(1)}, bf16[512,1024]{1,0:T(8,128)(2,1)S(1)}, u32[]{:S(2)}, u32[]{:S(2)}) %collective-permute-start.3) | collective-permute-done | bytes 1048608 | tf_op jit(solution)/shard_map/ppermute | solution.py:95
  61.4 1.6 collective-permute-start.6
  67.2 16.2 %collective-permute-done.6 = bf16[512,1024]{1,0:T(8,128)(2,1)S(1)} collective-permute-done((bf16[512,1024]{1,0:T(8,128)(2,1)S(1)}, bf16[512,1024]{1,0:T(8,128)(2,1)S(1)}, u32[]{:S(2)}, u32[]{:S(2)}) %collective-permute-start.6) | collective-permute-done | bytes 1048608 | tf_op jit(solution)/shard_map/ppermute | solution.py:95
  91.6 7.8 %collective-permute-done.10 = bf16[256,1024]{1,0:T(8,128)(2,1)S(1)} collective-permute-done((bf16[256,1024]{1,0:T(8,128)(2,1)S(1)}, bf16[256,1024]{1,0:T(8,128)(2,1)S(1)}, u32[]{:S(2)}, u32[]{:S(2)}) %collective-permute-start.10) | collective-permute-done | bytes 524320 | tf_op jit(solution)/shard_map/ppermute | solution.py:95
  107.1 7.1 %shard_map.65.refs_1_ = bf16[512,256]{1,0:T(8,128)(2,1)} custom-call(bf16[8,512,1024]{2,1,0:T(8,128)(2,1)} %fusion.33.panel_ref, bf16[2048,256]{1,0:T(8,128)(2,1)} %copy_bitcast_fusion.refs_0_, bf16[2048,256]{1,0:T(8,128)(2,1)} %copy-done.10, bf16[2048,256]{1,0:T(8,128)(2,1)} %collective-permute-done.2.refs_2_, bf16[2048,256]{1,0:T(8,128)(2,1)} %copy-done.9, ...), custom_call_target="tpu_custom_call" | custom-call | flops 1 | bytes 1 | tf_op jit(solution)/shard_map/pallas_call | solution.py:171
  115.6 10.6 %shard_map.66.refs_0_ = bf16[512,512]{1,0:T(8,128)(2,1)} custom-call(bf16[8,512,1024]{2,1,0:T(8,128)(2,1)} %fusion.33.panel_ref, bf16[2048,1024]{1,0:T(8,128)(2,1)} %refs_0_.2, bf16[2048,1024]{1,0:T(8,128)(2,1)} %collective-permute-done.15.refs_1_, bf16[2048,256]{1,0:T(8,128)(2,1)} %copy-done.5, bf16[2048,256]{1,0:T(8,128)(2,1)} %copy-done.7, ...), custom_call_target="tpu_custom_call" | custom-call | flops 1 | bytes 1 | tf_op jit(solution)/shard_map/pallas_call | solution.py:171
  126.2 7.9 %collective-permute-done.14.refs_3_ = bf16[512,256]{1,0:T(8,128)(2,1)S(1)} collective-permute-done((bf16[512,256]{1,0:T(8,128)(2,1)}, bf16[512,256]{1,0:T(8,128)(2,1)S(1)}, u32[]{:S(2)}, u32[]{:S(2)}) %collective-permute-start.14) | collective-permute-done | bytes 262176 | tf_op jit(solution)/shard_map/ppermute | solution.py:23
  135.7 1.6 collective-permute-done.20.refs_4_
  137.3 7.1 %shard_map.67 = bf16[512,512]{1,0:T(8,128)(2,1)S(1)} custom-call(s32[1]{0:T(128)} %bitcast.r_ref, bf16[512,512]{1,0:T(8,128)(2,1)S(1)} %copy-done.1, bf16[512,256]{1,0:T(8,128)(2,1)S(1)} %copy-done, bf16[512,256]{1,0:T(8,128)(2,1)S(1)} %collective-permute-done.18.refs_2_, bf16[512,256]{1,0:T(8,128)(2,1)S(1)} %collective-permute-done.14.refs_3_, ...), custom_call_target="tpu_custom_call" | custom-call | flops 1 | bytes 1 | tf_op jit(solution)/shard_map/pallas_call | solution.py:254
  144.4 1.6 collective-permute-start.21
  148.3 11.9 %shard_map.70 = bf16[512,384]{1,0:T(8,128)(2,1)} custom-call(bf16[8,512,1024]{2,1,0:T(8,128)(2,1)} %fusion.33.panel_ref, bf16[2048,1024]{1,0:T(8,128)(2,1)} %refs_0_.2, bf16[2048,1024]{1,0:T(8,128)(2,1)} %collective-permute-done.15.refs_1_, bf16[2048,128]{1,0:T(8,128)(2,1)} %collective-permute-done.11.refs_2_, ...), custom_call_target="tpu_custom_call" | custom-call | flops 1 | bytes 1 | tf_op jit(solution)/shard_map/pallas_call | solution.py:171
  164.3 6.9 %shard_map.71 = bf16[512,128]{1,0:T(8,128)(2,1)} custom-call(bf16[8,512,1024]{2,1,0:T(8,128)(2,1)} %fusion.33.panel_ref, bf16[2048,1024]{1,0:T(8,128)(2,1)} %refs_0_.2, bf16[2048,1024]{1,0:T(8,128)(2,1)} %collective-permute-done.15.refs_1_, bf16[2048,128]{1,0:T(8,128)(2,1)} %collective-permute-done.23.refs_2_, bf16[2048,128]{1,0:T(8,128)(2,1)} %copy-done.11, ...), custom_call_target="tpu_custom_call" | custom-call | flops 1 | bytes 1 | tf_op jit(solution)/shard_map/pallas_call | solution.py:171
  172.1 3.4 %collective-permute-done.26 = bf16[512,512]{1,0:T(8,128)(2,1)S(1)} collective-permute-done((bf16[512,512]{1,0:T(8,128)(2,1)}, bf16[512,512]{1,0:T(8,128)(2,1)S(1)}, u32[]{:S(2)}, u32[]{:S(2)}) %collective-permute-start.26) | collective-permute-done | bytes 524320 | tf_op jit(solution)/shard_map/ppermute | solution.py:95
  178.8 7.1 %shard_map.72 = bf16[512,512]{1,0:T(8,128)(2,1)S(1)} custom-call(s32[1]{0:T(128)} %bitcast.r_ref, bf16[512,512]{1,0:T(8,128)(2,1)S(1)} %pad_maximum_fusion.refs_0_, bf16[512,256]{1,0:T(8,128)(2,1)S(1)} %copy-done, bf16[512,256]{1,0:T(8,128)(2,1)S(1)} %collective-permute-done.18.refs_2_, bf16[512,256]{1,0:T(8,128)(2,1)S(1)} %collective-permute-done.14.refs_3_, ...), custom_call_target="tpu_custom_call" | custom-call | flops 1 | bytes 1 | tf_op jit(solution)/shard_map/pallas_call | solution.py:254
  185.9 5.2 %collective-permute-done.29 = bf16[512,512]{1,0:T(8,128)(2,1)S(1)} collective-permute-done((bf16[512,512]{1,0:T(8,128)(2,1)S(1)}, bf16[512,512]{1,0:T(8,128)(2,1)S(1)}, u32[]{:S(2)}, u32[]{:S(2)}) %collective-permute-start.29) | collective-permute-done | bytes 524320 | tf_op jit(solution)/shard_map/ppermute | solution.py:95
  194.5 1.6 collective-permute-start.36
  197.5 13.9 %collective-permute-done.36 = bf16[256,512]{1,0:T(8,128)(2,1)S(1)} collective-permute-done((bf16[256,512]{1,0:T(8,128)(2,1)S(1)}, bf16[256,512]{1,0:T(8,128)(2,1)S(1)}, u32[]{:S(2)}, u32[]{:S(2)}) %collective-permute-start.36) | collective-permute-done | bytes 262176 | tf_op jit(solution)/shard_map/ppermute | solution.py:95
  214.7 1.9 bitcast_dynamic-update-slice_fusion.11
  216.5 1.9 bitcast_dynamic-update-slice_fusion.10
  228.2 5.9 %shard_map.73.refs_4_ = f32[512,1024]{1,0:T(8,128)} custom-call(s32[1]{0:T(128)} %bitcast.r_ref, bf16[8,512,512]{2,1,0:T(8,128)(2,1)} %bitcast_dynamic-update-slice_fusion.16.refs_0_, bf16[2048,1024]{1,0:T(8,128)(2,1)} %refs_2_.1, bf16[2048,1024]{1,0:T(8,128)(2,1)} %copy-done.2), custom_call_target="tpu_custom_call" | custom-call | flops 1 | bytes 1 | tf_op jit(solution)/shard_map/pallas_call | solution.py:303
  235.0 1.9 bitcast_dynamic-update-slice_fusion.2
  242.2 2.6 collective-permute-done.40
  246.9 7.4 %shard_map.74.refs_5_ = f32[512,1024]{1,0:T(8,128)} custom-call(s32[1]{0:T(128)} %bitcast.r_ref, bf16[8,512,512]{2,1,0:T(8,128)(2,1)} %bitcast_dynamic-update-slice_fusion.16.refs_0_, bf16[8,512,512]{2,1,0:T(8,128)(2,1)} %bitcast_dynamic-update-slice_fusion.14.refs_1_, bf16[2048,1024]{1,0:T(8,128)(2,1)} %refs_2_.1, bf16[2048,1024]{1,0:T(8,128)(2,1)} %copy-done.2, ...), custom_call_target="tpu_custom_call" | custom-call | flops 1 | bytes 1 | tf_op jit(solution)/shard_map/pallas_call | solution.py:303
  254.3 9.9 %shard_map.75 = bf16[512,1024]{1,0:T(8,128)(2,1)} custom-call(s32[1]{0:T(128)} %bitcast.r_ref, bf16[8,512,512]{2,1,0:T(8,128)(2,1)} %bitcast_dynamic-update-slice_fusion.16.refs_0_, bf16[8,512,512]{2,1,0:T(8,128)(2,1)} %bitcast_dynamic-update-slice_fusion.14.refs_1_, bf16[2048,1024]{1,0:T(8,128)(2,1)} %refs_2_.1, bf16[2048,1024]{1,0:T(8,128)(2,1)} %copy-done.2, ...), custom_call_target="tpu_custom_call" | custom-call | flops 1 | bytes 1 | tf_op jit(solution)/shard_map/pallas_call | solution.py:303
  (153 shorter events, 69.1 us)
Async XLA Ops:
  6.5 247.8 %all-gather.3.cloned.1.call-start = ((), (), s32[]{:S(2)}) async-start(), calls=%async_computation | async-start | bytes 20971520 | tf_op jit(solution)/shard_map/all_gather | solution.py:428
  6.5 29.0 %collective-permute-start = (bf16[512,1024]{1,0:T(8,128)(2,1)}, bf16[512,1024]{1,0:T(8,128)(2,1)S(1)}, u32[]{:S(2)}, u32[]{:S(2)}) collective-permute-start(bf16[512,1024]{1,0:T(8,128)(2,1)} %param.6), channel_id=1, source_target_pairs={{0,2},{2,4},{4,6},{6,7},{7,5},{5,3},{3,1},{1,0},{8,10},{10,12},{12... | collective-permute-start | bytes 3145736 | tf_op jit(solution)/shard_map/ppermute | solution.py:95
  8.1 27.4 %collective-permute-start.1 = (bf16[512,1024]{1,0:T(8,128)(2,1)}, bf16[512,1024]{1,0:T(8,128)(2,1)S(1)}, u32[]{:S(2)}, u32[]{:S(2)}) collective-permute-start(bf16[512,1024]{1,0:T(8,128)(2,1)} %param.6), channel_id=1, source_target_pairs={{2,0},{4,2},{6,4},{7,6},{5,7},{3,5},{1,3},{0,1},{10,8},{12,10},{14... | collective-permute-start | bytes 3145736 | tf_op jit(solution)/shard_map/ppermute | solution.py:95
  10.9 24.7 %collective-permute-start.2 = (bf16[2048,256]{1,0:T(8,128)(2,1)}, bf16[2048,256]{1,0:T(8,128)(2,1)}, u32[]{:S(2)}, u32[]{:S(2)}) collective-permute-start(bf16[2048,256]{1,0:T(8,128)(2,1)} %copy_bitcast_fusion.refs_0_), channel_id=1, source_target_pairs={{0,16},{8,24},{16,0},{24,8},{1,17},{9,25},{17,1},{25,9},{2,18},{10... | collective-permute-start | bytes 3145736 | tf_op jit(solution)/shard_map/ppermute | solution.py:23
  35.5 23.4 %collective-permute-start.3 = (bf16[512,1024]{1,0:T(8,128)(2,1)S(1)}, bf16[512,1024]{1,0:T(8,128)(2,1)S(1)}, u32[]{:S(2)}, u32[]{:S(2)}) collective-permute-start(bf16[512,1024]{1,0:T(8,128)(2,1)S(1)} %collective-permute-done), channel_id=1, source_target_pairs={{0,2},{2,4},{4,6},{6,7},{7,5},{5,3},{3,1},{1,0},{8,10},{10,12},{12... | collective-permute-start | bytes 3145736 | tf_op jit(solution)/shard_map/ppermute | solution.py:95
  37.1 23.1 %collective-permute-start.4 = (bf16[512,1024]{1,0:T(8,128)(2,1)S(1)}, bf16[512,1024]{1,0:T(8,128)(2,1)S(1)}, u32[]{:S(2)}, u32[]{:S(2)}) collective-permute-start(bf16[512,1024]{1,0:T(8,128)(2,1)S(1)} %collective-permute-done.1), channel_id=1, source_target_pairs={{2,0},{4,2},{6,4},{7,6},{5,7},{3,5},{1,3},{0,1},{10,8},{12,10},{14... | collective-permute-start | bytes 3145736 | tf_op jit(solution)/shard_map/ppermute | solution.py:95
  37.5 22.9 %collective-permute-start.5 = (bf16[2048,256]{1,0:T(8,128)(2,1)S(1)}, bf16[2048,256]{1,0:T(8,128)(2,1)S(1)}, u32[]{:S(2)}, u32[]{:S(2)}) collective-permute-start(bf16[2048,256]{1,0:T(8,128)(2,1)S(1)} %get-tuple-element.99), channel_id=1, source_target_pairs={{0,16},{8,24},{16,0},{24,8},{1,17},{9,25},{17,1},{25,9},{2,18},{10... | collective-permute-start | bytes 3145736 | tf_op jit(solution)/shard_map/ppermute | solution.py:23
  61.4 22.0 %collective-permute-start.6 = (bf16[512,1024]{1,0:T(8,128)(2,1)S(1)}, bf16[512,1024]{1,0:T(8,128)(2,1)S(1)}, u32[]{:S(2)}, u32[]{:S(2)}) collective-permute-start(bf16[512,1024]{1,0:T(8,128)(2,1)S(1)} %collective-permute-done.3), channel_id=1, source_target_pairs={{0,2},{2,4},{4,6},{6,7},{7,5},{5,3},{3,1},{1,0},{8,10},{10,12},{12... | collective-permute-start | bytes 3145736 | tf_op jit(solution)/shard_map/ppermute | solution.py:95
  62.9 21.8 %collective-permute-start.7 = (bf16[512,1024]{1,0:T(8,128)(2,1)S(1)}, bf16[512,1024]{1,0:T(8,128)(2,1)S(1)}, u32[]{:S(2)}, u32[]{:S(2)}) collective-permute-start(bf16[512,1024]{1,0:T(8,128)(2,1)S(1)} %collective-permute-done.4), channel_id=1, source_target_pairs={{2,0},{4,2},{6,4},{7,6},{5,7},{3,5},{1,3},{0,1},{10,8},{12,10},{14... | collective-permute-start | bytes 3145736 | tf_op jit(solution)/shard_map/ppermute | solution.py:95
  63.4 21.5 %collective-permute-start.8 = (bf16[2048,256]{1,0:T(8,128)(2,1)S(1)}, bf16[2048,256]{1,0:T(8,128)(2,1)S(1)}, u32[]{:S(2)}, u32[]{:S(2)}) collective-permute-start(bf16[2048,256]{1,0:T(8,128)(2,1)S(1)} %get-tuple-element.107), channel_id=1, source_target_pairs={{0,16},{8,24},{16,0},{24,8},{1,17},{9,25},{17,1},{25,9},{2,18},{10... | collective-permute-start | bytes 3145736 | tf_op jit(solution)/shard_map/ppermute | solution.py:23
  84.9 16.3 %collective-permute-start.13 = (bf16[2048,256]{1,0:T(8,128)(2,1)}, bf16[2048,256]{1,0:T(8,128)(2,1)S(1)}, u32[]{:S(2)}, u32[]{:S(2)}) collective-permute-start(bf16[2048,256]{1,0:T(8,128)(2,1)} %collective-permute-done.2.refs_2_), channel_id=1, source_target_pairs={{0,8},{8,0},{16,24},{24,16},{1,9},{9,1},{17,25},{25,17},{2,10},{10... | collective-permute-start | bytes 3145736 | tf_op jit(solution)/shard_map/ppermute | solution.py:23
  85.0 16.3 %collective-permute-start.12 = (bf16[2048,256]{1,0:T(8,128)(2,1)}, bf16[2048,256]{1,0:T(8,128)(2,1)S(1)}, u32[]{:S(2)}, u32[]{:S(2)}) collective-permute-start(bf16[2048,256]{1,0:T(8,128)(2,1)} %copy_bitcast_fusion.refs_0_), channel_id=1, source_target_pairs={{0,8},{8,0},{16,24},{24,16},{1,9},{9,1},{17,25},{25,17},{2,10},{10... | collective-permute-start | bytes 3145736 | tf_op jit(solution)/shard_map/ppermute | solution.py:23
  85.5 13.9 %collective-permute-start.10 = (bf16[256,1024]{1,0:T(8,128)(2,1)S(1)}, bf16[256,1024]{1,0:T(8,128)(2,1)S(1)}, u32[]{:S(2)}, u32[]{:S(2)}) collective-permute-start(bf16[256,1024]{1,0:T(8,128)(2,1)S(1)} %slice.89), channel_id=1, source_target_pairs={{2,0},{4,2},{6,4},{7,6},{5,7},{3,5},{1,3},{0,1},{10,8},{12,10},{14... | collective-permute-start | bytes 1572872 | tf_op jit(solution)/shard_map/ppermute | solution.py:95
  86.9 13.9 %collective-permute-start.9 = (bf16[256,1024]{1,0:T(8,128)(2,1)S(1)}, bf16[256,1024]{1,0:T(8,128)(2,1)S(1)}, u32[]{:S(2)}, u32[]{:S(2)}) collective-permute-start(bf16[256,1024]{1,0:T(8,128)(2,1)S(1)} %slice.88), channel_id=1, source_target_pairs={{0,2},{2,4},{4,6},{6,7},{7,5},{5,3},{3,1},{1,0},{8,10},{10,12},{12... | collective-permute-start | bytes 1572872 | tf_op jit(solution)/shard_map/ppermute | solution.py:95
  87.8 13.5 %collective-permute-start.11 = (bf16[2048,128]{1,0:T(8,128)(2,1)S(1)}, bf16[2048,128]{1,0:T(8,128)(2,1)}, u32[]{:S(2)}, u32[]{:S(2)}) collective-permute-start(bf16[2048,128]{1,0:T(8,128)(2,1)S(1)} %get-tuple-element.115), channel_id=1, source_target_pairs={{0,16},{8,24},{16,0},{24,8},{1,17},{9,25},{17,1},{25,9},{2,18},{10... | collective-permute-start | bytes 1572872 | tf_op jit(solution)/shard_map/ppermute | solution.py:23
  102.2 13.3 %collective-permute-start.15 = (bf16[2048,1024]{1,0:T(8,128)(2,1)}, bf16[2048,1024]{1,0:T(8,128)(2,1)}, u32[]{:S(2)}, u32[]{:S(2)}) collective-permute-start(bf16[2048,1024]{1,0:T(8,128)(2,1)} %refs_0_.2), channel_id=1, source_target_pairs={{0,8},{8,0},{16,24},{24,16},{1,9},{9,1},{17,25},{25,17},{2,10},{10... | collective-permute-start | bytes 12582920 | tf_op jit(solution)/shard_map/ppermute | solution.py:23
  103.1 31.1 %collective-permute-start.19 = (bf16[2048,256]{1,0:T(8,128)(2,1)}, bf16[2048,256]{1,0:T(8,128)(2,1)}, u32[]{:S(2)}, u32[]{:S(2)}) collective-permute-start(bf16[2048,256]{1,0:T(8,128)(2,1)} %get-tuple-element.136), channel_id=1, source_target_pairs={{0,16},{8,24},{16,0},{24,8},{1,17},{9,25},{17,1},{25,9},{2,18},{10... | collective-permute-start | bytes 3145736 | tf_op jit(solution)/shard_map/ppermute | solution.py:23
  114.2 19.9 %collective-permute-start.14 = (bf16[512,256]{1,0:T(8,128)(2,1)}, bf16[512,256]{1,0:T(8,128)(2,1)S(1)}, u32[]{:S(2)}, u32[]{:S(2)}) collective-permute-start(bf16[512,256]{1,0:T(8,128)(2,1)} %shard_map.65.refs_1_), channel_id=1, source_target_pairs={{0,16},{8,24},{16,0},{24,8},{1,17},{9,25},{17,1},{25,9},{2,18},{10... | collective-permute-start | bytes 786440 | tf_op jit(solution)/shard_map/ppermute | solution.py:23
  115.6 18.6 %collective-permute-start.18 = (bf16[512,256]{1,0:T(8,128)(2,1)}, bf16[512,256]{1,0:T(8,128)(2,1)S(1)}, u32[]{:S(2)}, u32[]{:S(2)}) collective-permute-start(bf16[512,256]{1,0:T(8,128)(2,1)} %shard_map.65.refs_1_), channel_id=1, source_target_pairs={{0,8},{8,0},{16,24},{24,16},{1,9},{9,1},{17,25},{25,17},{2,10},{10... | collective-permute-start | bytes 786440 | tf_op jit(solution)/shard_map/ppermute | solution.py:23
  134.2 13.1 %collective-permute-start.25 = (bf16[2048,256]{1,0:T(8,128)(2,1)}, bf16[2048,256]{1,0:T(8,128)(2,1)S(1)}, u32[]{:S(2)}, u32[]{:S(2)}) collective-permute-start(bf16[2048,256]{1,0:T(8,128)(2,1)} %collective-permute-done.19.refs_3_), channel_id=1, source_target_pairs={{0,8},{8,0},{16,24},{24,16},{1,9},{9,1},{17,25},{25,17},{2,10},{10... | collective-permute-start | bytes 3145736 | tf_op jit(solution)/shard_map/ppermute | solution.py:23
  134.8 25.3 %collective-permute-start.23 = (bf16[2048,128]{1,0:T(8,128)(2,1)}, bf16[2048,128]{1,0:T(8,128)(2,1)}, u32[]{:S(2)}, u32[]{:S(2)}) collective-permute-start(bf16[2048,128]{1,0:T(8,128)(2,1)} %get-tuple-element.141), channel_id=1, source_target_pairs={{0,16},{8,24},{16,0},{24,8},{1,17},{9,25},{17,1},{25,9},{2,18},{10... | collective-permute-start | bytes 1572872 | tf_op jit(solution)/shard_map/ppermute | solution.py:23
  144.4 15.8 %collective-permute-start.21 = (bf16[512,512]{1,0:T(8,128)(2,1)S(1)}, bf16[512,512]{1,0:T(8,128)(2,1)}, u32[]{:S(2)}, u32[]{:S(2)}) collective-permute-start(bf16[512,512]{1,0:T(8,128)(2,1)S(1)} %shard_map.67), channel_id=1, source_target_pairs={{0,2},{2,4},{4,6},{6,7},{7,5},{5,3},{3,1},{1,0},{8,10},{10,12},{12... | collective-permute-start | bytes 1572872 | tf_op jit(solution)/shard_map/ppermute | solution.py:95
  146.0 14.2 %collective-permute-start.22 = (bf16[512,512]{1,0:T(8,128)(2,1)S(1)}, bf16[512,512]{1,0:T(8,128)(2,1)}, u32[]{:S(2)}, u32[]{:S(2)}) collective-permute-start(bf16[512,512]{1,0:T(8,128)(2,1)S(1)} %shard_map.67), channel_id=1, source_target_pairs={{2,0},{4,2},{6,4},{7,6},{5,7},{3,5},{1,3},{0,1},{10,8},{12,10},{14... | collective-permute-start | bytes 1572872 | tf_op jit(solution)/shard_map/ppermute | solution.py:95
  161.4 14.1 %collective-permute-start.26 = (bf16[512,512]{1,0:T(8,128)(2,1)}, bf16[512,512]{1,0:T(8,128)(2,1)S(1)}, u32[]{:S(2)}, u32[]{:S(2)}) collective-permute-start(bf16[512,512]{1,0:T(8,128)(2,1)} %collective-permute-done.21), channel_id=1, source_target_pairs={{0,2},{2,4},{4,6},{6,7},{7,5},{5,3},{3,1},{1,0},{8,10},{10,12},{12... | collective-permute-start | bytes 1572872 | tf_op jit(solution)/shard_map/ppermute | solution.py:95
  163.0 13.8 %collective-permute-start.27 = (bf16[512,512]{1,0:T(8,128)(2,1)}, bf16[512,512]{1,0:T(8,128)(2,1)S(1)}, u32[]{:S(2)}, u32[]{:S(2)}) collective-permute-start(bf16[512,512]{1,0:T(8,128)(2,1)} %collective-permute-done.22), channel_id=1, source_target_pairs={{2,0},{4,2},{6,4},{7,6},{5,7},{3,5},{1,3},{0,1},{10,8},{12,10},{14... | collective-permute-start | bytes 1572872 | tf_op jit(solution)/shard_map/ppermute | solution.py:95
  176.8 15.6 %collective-permute-start.31 = (bf16[2048,1024]{1,0:T(8,128)(2,1)}, bf16[2048,1024]{1,0:T(8,128)(2,1)S(1)}, u32[]{:S(2)}, u32[]{:S(2)}) collective-permute-start(bf16[2048,1024]{1,0:T(8,128)(2,1)} %refs_2_.1), channel_id=1, source_target_pairs={{0,8},{8,0},{16,24},{24,16},{1,9},{9,1},{17,25},{25,17},{2,10},{10... | collective-permute-start | bytes 12582920 | tf_op jit(solution)/shard_map/ppermute | solution.py:23
  176.8 14.3 %collective-permute-start.29 = (bf16[512,512]{1,0:T(8,128)(2,1)S(1)}, bf16[512,512]{1,0:T(8,128)(2,1)S(1)}, u32[]{:S(2)}, u32[]{:S(2)}) collective-permute-start(bf16[512,512]{1,0:T(8,128)(2,1)S(1)} %collective-permute-done.26), channel_id=1, source_target_pairs={{0,2},{2,4},{4,6},{6,7},{7,5},{5,3},{3,1},{1,0},{8,10},{10,12},{12... | collective-permute-start | bytes 1572872 | tf_op jit(solution)/shard_map/ppermute | solution.py:95
  178.4 14.1 %collective-permute-start.30 = (bf16[512,512]{1,0:T(8,128)(2,1)S(1)}, bf16[512,512]{1,0:T(8,128)(2,1)S(1)}, u32[]{:S(2)}, u32[]{:S(2)}) collective-permute-start(bf16[512,512]{1,0:T(8,128)(2,1)S(1)} %collective-permute-done.27), channel_id=1, source_target_pairs={{2,0},{4,2},{6,4},{7,6},{5,7},{3,5},{1,3},{0,1},{10,8},{12,10},{14... | collective-permute-start | bytes 1572872 | tf_op jit(solution)/shard_map/ppermute | solution.py:95
  192.4 20.2 %collective-permute-start.32 = (bf16[512,512]{1,0:T(8,128)(2,1)S(1)}, bf16[512,512]{1,0:T(8,128)(2,1)S(1)}, u32[]{:S(2)}, u32[]{:S(2)}) collective-permute-start(bf16[512,512]{1,0:T(8,128)(2,1)S(1)} %shard_map.72), channel_id=1, source_target_pairs={{0,2},{2,4},{4,6},{6,7},{7,5},{5,3},{3,1},{1,0},{8,10},{10,12},{12... | collective-permute-start | bytes 1572872 | tf_op jit(solution)/shard_map/ppermute | solution.py:95
  193.9 18.7 %collective-permute-start.33 = (bf16[512,512]{1,0:T(8,128)(2,1)S(1)}, bf16[512,512]{1,0:T(8,128)(2,1)S(1)}, u32[]{:S(2)}, u32[]{:S(2)}) collective-permute-start(bf16[512,512]{1,0:T(8,128)(2,1)S(1)} %shard_map.72), channel_id=1, source_target_pairs={{2,0},{4,2},{6,4},{7,6},{5,7},{3,5},{1,3},{0,1},{10,8},{12,10},{14... | collective-permute-start | bytes 1572872 | tf_op jit(solution)/shard_map/ppermute | solution.py:95
  194.5 16.9 %collective-permute-start.36 = (bf16[256,512]{1,0:T(8,128)(2,1)S(1)}, bf16[256,512]{1,0:T(8,128)(2,1)S(1)}, u32[]{:S(2)}, u32[]{:S(2)}) collective-permute-start(bf16[256,512]{1,0:T(8,128)(2,1)S(1)} %slice.96), channel_id=1, source_target_pairs={{0,2},{2,4},{4,6},{6,7},{7,5},{5,3},{3,1},{1,0},{8,10},{10,12},{12... | collective-permute-start | bytes 786440 | tf_op jit(solution)/shard_map/ppermute | solution.py:95
  196.1 16.6 %collective-permute-start.37 = (bf16[256,512]{1,0:T(8,128)(2,1)S(1)}, bf16[256,512]{1,0:T(8,128)(2,1)S(1)}, u32[]{:S(2)}, u32[]{:S(2)}) collective-permute-start(bf16[256,512]{1,0:T(8,128)(2,1)S(1)} %slice.97), channel_id=1, source_target_pairs={{2,0},{4,2},{6,4},{7,6},{5,7},{3,5},{1,3},{0,1},{10,8},{12,10},{14... | collective-permute-start | bytes 786440 | tf_op jit(solution)/shard_map/ppermute | solution.py:95
  (24 other events, 211.9 us)
Sparse Core Ops, SparseCore 0:
  134.3 107.0 all-gather.2

commit v16 on v14

--- a/solution.py
+++ b/solution.py
@@ -316,7 +316,7 @@
             pltpu.SemaphoreType.DMA((count,)),
             pltpu.SemaphoreType.DMA((1, count)),
         ],
-        compiler_params=pltpu.CompilerParams(vmem_limit_bytes=60 * MIB),
+        compiler_params=pltpu.CompilerParams(vmem_limit_bytes=40 * MIB),
         cost_estimate=SHORT,
     )(r.reshape(1), *panels, *near, *others, *old)
 

time: 268 us -> 270 us (level)
  waiting for transfers between devices: 102 us -> 109 us
  Pallas kernels: 69.4 us -> 65.4 us
    unnamed x28 -> x34, local copies, waits for them, and re-layouts: 6.14 us -> 13.4 us
    dynamic_update_slice x18, local copies, waits for them, and re-layouts: 16.7 us -> 9.76 us  [put(): panel = lax.dynamic_update_slice(panel, piece[None], (slot, first, 0))]
    ppermute x24, waiting for transfers between devices: 79.3 us -> 84.9 us  [hop(): lax.ppermute(s[0], 'col', s[1])]
    pallas_call x2, Pallas kernels: 18.7 us -> 14.7 us  [finish(): pl.pallas_call(functools.partial(finish_kernel, steps, per, rows, len(pan...]
  transfers between devices with their start and end apart: 43 -> 43, of which waited for: 22 -> 23; matrix products, arithmetic and copies ran while one was open for 16% -> 13% of each run, Pallas kernels for 21% -> 20%
where the time goes in v16:
time: 270 us
  waiting for transfers between devices  109 us (40%)
  Pallas kernels  65.4 us (24%)
  starting transfers between devices  32.7 us (12%)
  local copies, waits for them, and re-layouts  28.3 us (10%)
  other arithmetic  20.2 us (7%)
  between operations  13.9 us (5%)
    ppermute x24, waiting for transfers between devices, hop(): lax.ppermute(s[0], 'col', s[1])  84.9 us
    pallas_call x4, Pallas kernels, project(): pl.pallas_call(functools.partial(project_kernel, len(near), len(far), chu...  36.6 us
    ppermute x24, starting transfers between devices, hop(): lax.ppermute(s[0], 'col', s[1])  24.8 us
    ppermute x18, waiting for transfers between devices, swap(): lax.ppermute(array, axis, [(i, i ^ mask) for i in range(lax.axis_size(axi...  24.1 us
    pallas_call x2, Pallas kernels, finish(): pl.pallas_call(functools.partial(finish_kernel, steps, per, rows, len(pan...  14.7 us
    pallas_call x2, Pallas kernels, attend(): pl.pallas_call(functools.partial(attend_kernel, parts, chunks, pair), gri...  14.1 us
    unnamed x34, local copies, waits for them, and re-layouts  13.4 us
    dynamic_update_slice x9, other arithmetic, put(): panel = lax.dynamic_update_slice(panel, piece[None], (slot, first, 0))  10.5 us
  transfers between devices with their start and end apart: 43, of which 23 were waited for; matrix products, arithmetic and copies ran while one was open for 13% of the time, Pallas kernels for 20%

profile of v16, /device:TPU:2, one launch (start us, length us, event | category | flops | bytes accessed | tf_op | source)
XLA Modules:
  0.0 269.6 jit_solution(2272270673613478743)
XLA Ops:
  8.6 2.3 copy_bitcast_fusion.refs_0_
  12.6 1.8 fusion.36
  15.7 2.1 pad_maximum_fusion.1
  17.8 2.1 fusion.38
  19.9 2.1 fusion.39
  22.0 13.6 %collective-permute-done.2.refs_2_ = bf16[2048,256]{1,0:T(8,128)(2,1)} collective-permute-done((bf16[2048,256]{1,0:T(8,128)(2,1)}, bf16[2048,256]{1,0:T(8,128)(2,1)}, u32[]{:S(2)}, u32[]{:S(2)}) %collective-permute-start.2) | collective-permute-done | bytes 1048608 | tf_op jit(solution)/shard_map/ppermute | solution.py:23
  41.0 18.0 %collective-permute-done.3 = bf16[512,1024]{1,0:T(8,128)(2,1)S(1)} collective-permute-done((bf16[512,1024]{1,0:T(8,128)(2,1)S(1)}, bf16[512,1024]{1,0:T(8,128)(2,1)S(1)}, u32[]{:S(2)}, u32[]{:S(2)}) %collective-permute-start.3) | collective-permute-done | bytes 1048608 | tf_op jit(solution)/shard_map/ppermute | solution.py:95
  67.2 16.3 %collective-permute-done.6 = bf16[512,1024]{1,0:T(8,128)(2,1)S(1)} collective-permute-done((bf16[512,1024]{1,0:T(8,128)(2,1)S(1)}, bf16[512,1024]{1,0:T(8,128)(2,1)S(1)}, u32[]{:S(2)}, u32[]{:S(2)}) %collective-permute-start.6) | collective-permute-done | bytes 1048608 | tf_op jit(solution)/shard_map/ppermute | solution.py:95
  91.8 7.7 %collective-permute-done.10 = bf16[256,1024]{1,0:T(8,128)(2,1)S(1)} collective-permute-done((bf16[256,1024]{1,0:T(8,128)(2,1)S(1)}, bf16[256,1024]{1,0:T(8,128)(2,1)S(1)}, u32[]{:S(2)}, u32[]{:S(2)}) %collective-permute-start.10) | collective-permute-done | bytes 524320 | tf_op jit(solution)/shard_map/ppermute | solution.py:95
  105.9 7.1 %shard_map.65.refs_1_ = bf16[512,256]{1,0:T(8,128)(2,1)} custom-call(bf16[8,512,1024]{2,1,0:T(8,128)(2,1)} %fusion.33.panel_ref, bf16[2048,256]{1,0:T(8,128)(2,1)} %copy_bitcast_fusion.refs_0_, bf16[2048,256]{1,0:T(8,128)(2,1)} %collective-permute-done.12.refs_1_, bf16[2048,256]{1,0:T(8,128)(2,1)} %collective-permute-done.2.refs_2_, ...), custom_call_target="tpu_custom_call" | custom-call | flops 1 | bytes 1 | tf_op jit(solution)/shard_map/pallas_call | solution.py:171
  114.4 10.6 %shard_map.66.refs_0_ = bf16[512,512]{1,0:T(8,128)(2,1)} custom-call(bf16[8,512,1024]{2,1,0:T(8,128)(2,1)} %fusion.33.panel_ref, bf16[2048,1024]{1,0:T(8,128)(2,1)} %refs_0_.2, bf16[2048,1024]{1,0:T(8,128)(2,1)} %collective-permute-done.15.refs_1_, bf16[2048,256]{1,0:T(8,128)(2,1)} %copy-done.11, bf16[2048,256]{1,0:T(8,128)(2,1)} %collective-permute-done.8.refs_3_, ...), custom_call_target="tpu_custom_call" | custom-call | flops 1 | bytes 1 | tf_op jit(solution)/shard_map/pallas_call | solution.py:171
  125.1 8.0 %collective-permute-done.14.refs_3_ = bf16[512,256]{1,0:T(8,128)(2,1)S(1)} collective-permute-done((bf16[512,256]{1,0:T(8,128)(2,1)}, bf16[512,256]{1,0:T(8,128)(2,1)S(1)}, u32[]{:S(2)}, u32[]{:S(2)}) %collective-permute-start.14) | collective-permute-done | bytes 262176 | tf_op jit(solution)/shard_map/ppermute | solution.py:23
  134.6 1.6 collective-permute-done.20.refs_4_
  136.2 7.1 %shard_map.67 = bf16[512,512]{1,0:T(8,128)(2,1)S(1)} custom-call(s32[1]{0:T(128)} %bitcast.r_ref, bf16[512,512]{1,0:T(8,128)(2,1)S(1)} %copy-done.7, bf16[512,256]{1,0:T(8,128)(2,1)S(1)} %copy-done.6, bf16[512,256]{1,0:T(8,128)(2,1)S(1)} %collective-permute-done.18.refs_2_, bf16[512,256]{1,0:T(8,128)(2,1)S(1)} %collective-permute-done.14.refs_3_, ...), custom_call_target="tpu_custom_call" | custom-call | flops 1 | bytes 1 | tf_op jit(solution)/shard_map/pallas_call | solution.py:254
  143.3 1.6 collective-permute-start.21
  147.2 11.9 %shard_map.70 = bf16[512,384]{1,0:T(8,128)(2,1)} custom-call(bf16[8,512,1024]{2,1,0:T(8,128)(2,1)} %fusion.33.panel_ref, bf16[2048,1024]{1,0:T(8,128)(2,1)} %refs_0_.2, bf16[2048,1024]{1,0:T(8,128)(2,1)} %collective-permute-done.15.refs_1_, bf16[2048,128]{1,0:T(8,128)(2,1)} %collective-permute-done.11.refs_2_, ...), custom_call_target="tpu_custom_call" | custom-call | flops 1 | bytes 1 | tf_op jit(solution)/shard_map/pallas_call | solution.py:171
  163.1 1.9 bitcast_dynamic-update-slice_fusion.12
  165.0 1.9 bitcast_dynamic-update-slice_fusion.11
  167.7 6.9 %shard_map.71 = bf16[512,128]{1,0:T(8,128)(2,1)} custom-call(bf16[8,512,1024]{2,1,0:T(8,128)(2,1)} %fusion.33.panel_ref, bf16[2048,1024]{1,0:T(8,128)(2,1)} %refs_0_.2, bf16[2048,1024]{1,0:T(8,128)(2,1)} %collective-permute-done.15.refs_1_, bf16[2048,128]{1,0:T(8,128)(2,1)} %collective-permute-done.23.refs_2_, bf16[2048,128]{1,0:T(8,128)(2,1)} %copy-done.14, ...), custom_call_target="tpu_custom_call" | custom-call | flops 1 | bytes 1 | tf_op jit(solution)/shard_map/pallas_call | solution.py:171
  176.4 1.6 collective-permute-start.29
  178.4 7.1 %shard_map.72 = bf16[512,512]{1,0:T(8,128)(2,1)S(1)} custom-call(s32[1]{0:T(128)} %bitcast.r_ref, bf16[512,512]{1,0:T(8,128)(2,1)S(1)} %pad_maximum_fusion.refs_0_, bf16[512,256]{1,0:T(8,128)(2,1)S(1)} %copy-done.6, bf16[512,256]{1,0:T(8,128)(2,1)S(1)} %collective-permute-done.18.refs_2_, bf16[512,256]{1,0:T(8,128)(2,1)S(1)} %collective-permute-done.14.refs_3_, ...), custom_call_target="tpu_custom_call" | custom-call | flops 1 | bytes 1 | tf_op jit(solution)/shard_map/pallas_call | solution.py:254
  187.2 3.5 %collective-permute-done.29 = bf16[512,512]{1,0:T(8,128)(2,1)S(1)} collective-permute-done((bf16[512,512]{1,0:T(8,128)(2,1)S(1)}, bf16[512,512]{1,0:T(8,128)(2,1)S(1)}, u32[]{:S(2)}, u32[]{:S(2)}) %collective-permute-start.29) | collective-permute-done | bytes 524320 | tf_op jit(solution)/shard_map/ppermute | solution.py:95
  197.9 13.0 %collective-permute-done.32 = bf16[256,512]{1,0:T(8,128)(2,1)S(1)} collective-permute-done((bf16[256,512]{1,0:T(8,128)(2,1)S(1)}, bf16[256,512]{1,0:T(8,128)(2,1)S(1)}, u32[]{:S(2)}, u32[]{:S(2)}) %collective-permute-start.32) | collective-permute-done | bytes 262176 | tf_op jit(solution)/shard_map/ppermute | solution.py:95
  215.0 9.4 %collective-permute-done.36 = bf16[512,512]{1,0:T(8,128)(2,1)S(1)} collective-permute-done((bf16[512,512]{1,0:T(8,128)(2,1)S(1)}, bf16[512,512]{1,0:T(8,128)(2,1)S(1)}, u32[]{:S(2)}, u32[]{:S(2)}) %collective-permute-start.36) | collective-permute-done | bytes 524320 | tf_op jit(solution)/shard_map/ppermute | solution.py:95
  228.4 2.2 copy-done.1
  230.6 3.5 %shard_map.73.refs_5_ = f32[512,1024]{1,0:T(8,128)S(1)} custom-call(s32[1]{0:T(128)} %bitcast.r_ref, bf16[8,512,512]{2,1,0:T(8,128)(2,1)S(1)} %copy-done.1, bf16[2048,1024]{1,0:T(8,128)(2,1)S(1)} %copy-done, bf16[2048,1024]{1,0:T(8,128)(2,1)} %copy-done.8), custom_call_target="tpu_custom_call" | custom-call | flops 1 | bytes 1 | tf_op jit(solution)/shard_map/pallas_call | solution.py:303
  234.2 3.2 %collective-permute-done.38 = bf16[512,512]{1,0:T(8,128)(2,1)S(1)} collective-permute-done((bf16[512,512]{1,0:T(8,128)(2,1)S(1)}, bf16[512,512]{1,0:T(8,128)(2,1)S(1)}, u32[]{:S(2)}, u32[]{:S(2)}) %collective-permute-start.38) | collective-permute-done | bytes 524320 | tf_op jit(solution)/shard_map/ppermute | solution.py:95
  239.8 4.2 %collective-permute-done.40 = bf16[256,512]{1,0:T(8,128)(2,1)S(1)} collective-permute-done((bf16[256,512]{1,0:T(8,128)(2,1)S(1)}, bf16[256,512]{1,0:T(8,128)(2,1)S(1)}, u32[]{:S(2)}, u32[]{:S(2)}) %collective-permute-start.40) | collective-permute-done | bytes 262176 | tf_op jit(solution)/shard_map/ppermute | solution.py:95
  245.1 2.0 copy-done.4
  247.1 2.2 copy-done.2
  249.3 2.2 copy-done.5
  251.5 11.3 %shard_map.74 = bf16[512,1024]{1,0:T(8,128)(2,1)} custom-call(s32[1]{0:T(128)} %bitcast.r_ref, bf16[8,512,512]{2,1,0:T(8,128)(2,1)S(1)} %copy-done.2, bf16[8,512,512]{2,1,0:T(8,128)(2,1)S(1)} %copy-done.5, bf16[2048,1024]{1,0:T(8,128)(2,1)} %refs_2_, bf16[2048,1024]{1,0:T(8,128)(2,1)} %copy-done.8, bf16[4,2048,1024]{2,1,0:T(8,128)(2,1)} %bitcast.83, ...), custom_call_target="tpu_custom_call" | custom-call | flops 1 | bytes 1 | tf_op jit(solution)/shard_map/pallas_call | solution.py:303
  (160 shorter events, 65.8 us)
Async XLA Ops:
  6.5 240.6 %all-gather.3.cloned.1.call-start = ((), (), s32[]{:S(2)}) async-start(), calls=%async_computation | async-start | bytes 20971520 | tf_op jit(solution)/shard_map/all_gather | solution.py:428
  6.5 29.0 %collective-permute-start = (bf16[512,1024]{1,0:T(8,128)(2,1)}, bf16[512,1024]{1,0:T(8,128)(2,1)S(1)}, u32[]{:S(2)}, u32[]{:S(2)}) collective-permute-start(bf16[512,1024]{1,0:T(8,128)(2,1)} %param.6), channel_id=1, source_target_pairs={{0,2},{2,4},{4,6},{6,7},{7,5},{5,3},{3,1},{1,0},{8,10},{10,12},{12... | collective-permute-start | bytes 3145736 | tf_op jit(solution)/shard_map/ppermute | solution.py:95
  8.1 27.4 %collective-permute-start.1 = (bf16[512,1024]{1,0:T(8,128)(2,1)}, bf16[512,1024]{1,0:T(8,128)(2,1)S(1)}, u32[]{:S(2)}, u32[]{:S(2)}) collective-permute-start(bf16[512,1024]{1,0:T(8,128)(2,1)} %param.6), channel_id=1, source_target_pairs={{2,0},{4,2},{6,4},{7,6},{5,7},{3,5},{1,3},{0,1},{10,8},{12,10},{14... | collective-permute-start | bytes 3145736 | tf_op jit(solution)/shard_map/ppermute | solution.py:95
  10.9 24.7 %collective-permute-start.2 = (bf16[2048,256]{1,0:T(8,128)(2,1)}, bf16[2048,256]{1,0:T(8,128)(2,1)}, u32[]{:S(2)}, u32[]{:S(2)}) collective-permute-start(bf16[2048,256]{1,0:T(8,128)(2,1)} %copy_bitcast_fusion.refs_0_), channel_id=1, source_target_pairs={{0,16},{8,24},{16,0},{24,8},{1,17},{9,25},{17,1},{25,9},{2,18},{10... | collective-permute-start | bytes 3145736 | tf_op jit(solution)/shard_map/ppermute | solution.py:23
  35.5 23.4 %collective-permute-start.3 = (bf16[512,1024]{1,0:T(8,128)(2,1)S(1)}, bf16[512,1024]{1,0:T(8,128)(2,1)S(1)}, u32[]{:S(2)}, u32[]{:S(2)}) collective-permute-start(bf16[512,1024]{1,0:T(8,128)(2,1)S(1)} %collective-permute-done), channel_id=1, source_target_pairs={{0,2},{2,4},{4,6},{6,7},{7,5},{5,3},{3,1},{1,0},{8,10},{10,12},{12... | collective-permute-start | bytes 3145736 | tf_op jit(solution)/shard_map/ppermute | solution.py:95
  37.1 23.1 %collective-permute-start.4 = (bf16[512,1024]{1,0:T(8,128)(2,1)S(1)}, bf16[512,1024]{1,0:T(8,128)(2,1)S(1)}, u32[]{:S(2)}, u32[]{:S(2)}) collective-permute-start(bf16[512,1024]{1,0:T(8,128)(2,1)S(1)} %collective-permute-done.1), channel_id=1, source_target_pairs={{2,0},{4,2},{6,4},{7,6},{5,7},{3,5},{1,3},{0,1},{10,8},{12,10},{14... | collective-permute-start | bytes 3145736 | tf_op jit(solution)/shard_map/ppermute | solution.py:95
  37.6 22.9 %collective-permute-start.5 = (bf16[2048,256]{1,0:T(8,128)(2,1)S(1)}, bf16[2048,256]{1,0:T(8,128)(2,1)S(1)}, u32[]{:S(2)}, u32[]{:S(2)}) collective-permute-start(bf16[2048,256]{1,0:T(8,128)(2,1)S(1)} %get-tuple-element.98), channel_id=1, source_target_pairs={{0,16},{8,24},{16,0},{24,8},{1,17},{9,25},{17,1},{25,9},{2,18},{10... | collective-permute-start | bytes 3145736 | tf_op jit(solution)/shard_map/ppermute | solution.py:23
  61.4 22.0 %collective-permute-start.6 = (bf16[512,1024]{1,0:T(8,128)(2,1)S(1)}, bf16[512,1024]{1,0:T(8,128)(2,1)S(1)}, u32[]{:S(2)}, u32[]{:S(2)}) collective-permute-start(bf16[512,1024]{1,0:T(8,128)(2,1)S(1)} %collective-permute-done.3), channel_id=1, source_target_pairs={{0,2},{2,4},{4,6},{6,7},{7,5},{5,3},{3,1},{1,0},{8,10},{10,12},{12... | collective-permute-start | bytes 3145736 | tf_op jit(solution)/shard_map/ppermute | solution.py:95
  63.0 21.8 %collective-permute-start.7 = (bf16[512,1024]{1,0:T(8,128)(2,1)S(1)}, bf16[512,1024]{1,0:T(8,128)(2,1)S(1)}, u32[]{:S(2)}, u32[]{:S(2)}) collective-permute-start(bf16[512,1024]{1,0:T(8,128)(2,1)S(1)} %collective-permute-done.4), channel_id=1, source_target_pairs={{2,0},{4,2},{6,4},{7,6},{5,7},{3,5},{1,3},{0,1},{10,8},{12,10},{14... | collective-permute-start | bytes 3145736 | tf_op jit(solution)/shard_map/ppermute | solution.py:95
  63.4 21.6 %collective-permute-start.8 = (bf16[2048,256]{1,0:T(8,128)(2,1)S(1)}, bf16[2048,256]{1,0:T(8,128)(2,1)}, u32[]{:S(2)}, u32[]{:S(2)}) collective-permute-start(bf16[2048,256]{1,0:T(8,128)(2,1)S(1)} %get-tuple-element.106), channel_id=1, source_target_pairs={{0,16},{8,24},{16,0},{24,8},{1,17},{9,25},{17,1},{25,9},{2,18},{10... | collective-permute-start | bytes 3145736 | tf_op jit(solution)/shard_map/ppermute | solution.py:23
  85.0 16.3 %collective-permute-start.13 = (bf16[2048,256]{1,0:T(8,128)(2,1)}, bf16[2048,256]{1,0:T(8,128)(2,1)}, u32[]{:S(2)}, u32[]{:S(2)}) collective-permute-start(bf16[2048,256]{1,0:T(8,128)(2,1)} %collective-permute-done.2.refs_2_), channel_id=1, source_target_pairs={{0,8},{8,0},{16,24},{24,16},{1,9},{9,1},{17,25},{25,17},{2,10},{10... | collective-permute-start | bytes 3145736 | tf_op jit(solution)/shard_map/ppermute | solution.py:23
  85.1 16.3 %collective-permute-start.12 = (bf16[2048,256]{1,0:T(8,128)(2,1)}, bf16[2048,256]{1,0:T(8,128)(2,1)}, u32[]{:S(2)}, u32[]{:S(2)}) collective-permute-start(bf16[2048,256]{1,0:T(8,128)(2,1)} %copy_bitcast_fusion.refs_0_), channel_id=1, source_target_pairs={{0,8},{8,0},{16,24},{24,16},{1,9},{9,1},{17,25},{25,17},{2,10},{10... | collective-permute-start | bytes 3145736 | tf_op jit(solution)/shard_map/ppermute | solution.py:23
  85.6 13.9 %collective-permute-start.10 = (bf16[256,1024]{1,0:T(8,128)(2,1)S(1)}, bf16[256,1024]{1,0:T(8,128)(2,1)S(1)}, u32[]{:S(2)}, u32[]{:S(2)}) collective-permute-start(bf16[256,1024]{1,0:T(8,128)(2,1)S(1)} %slice.89), channel_id=1, source_target_pairs={{2,0},{4,2},{6,4},{7,6},{5,7},{3,5},{1,3},{0,1},{10,8},{12,10},{14... | collective-permute-start | bytes 1572872 | tf_op jit(solution)/shard_map/ppermute | solution.py:95
  87.1 13.9 %collective-permute-start.9 = (bf16[256,1024]{1,0:T(8,128)(2,1)S(1)}, bf16[256,1024]{1,0:T(8,128)(2,1)S(1)}, u32[]{:S(2)}, u32[]{:S(2)}) collective-permute-start(bf16[256,1024]{1,0:T(8,128)(2,1)S(1)} %slice.88), channel_id=1, source_target_pairs={{0,2},{2,4},{4,6},{6,7},{7,5},{5,3},{3,1},{1,0},{8,10},{10,12},{12... | collective-permute-start | bytes 1572872 | tf_op jit(solution)/shard_map/ppermute | solution.py:95
  87.9 13.5 %collective-permute-start.11 = (bf16[2048,128]{1,0:T(8,128)(2,1)S(1)}, bf16[2048,128]{1,0:T(8,128)(2,1)}, u32[]{:S(2)}, u32[]{:S(2)}) collective-permute-start(bf16[2048,128]{1,0:T(8,128)(2,1)S(1)} %get-tuple-element.114), channel_id=1, source_target_pairs={{0,16},{8,24},{16,0},{24,8},{1,17},{9,25},{17,1},{25,9},{2,18},{10... | collective-permute-start | bytes 1572872 | tf_op jit(solution)/shard_map/ppermute | solution.py:23
  101.4 13.1 %collective-permute-start.15 = (bf16[2048,1024]{1,0:T(8,128)(2,1)}, bf16[2048,1024]{1,0:T(8,128)(2,1)}, u32[]{:S(2)}, u32[]{:S(2)}) collective-permute-start(bf16[2048,1024]{1,0:T(8,128)(2,1)} %refs_0_.2), channel_id=1, source_target_pairs={{0,8},{8,0},{16,24},{24,16},{1,9},{9,1},{17,25},{25,17},{2,10},{10... | collective-permute-start | bytes 12582920 | tf_op jit(solution)/shard_map/ppermute | solution.py:23
  102.0 31.1 %collective-permute-start.19 = (bf16[2048,256]{1,0:T(8,128)(2,1)S(1)}, bf16[2048,256]{1,0:T(8,128)(2,1)}, u32[]{:S(2)}, u32[]{:S(2)}) collective-permute-start(bf16[2048,256]{1,0:T(8,128)(2,1)S(1)} %get-tuple-element.135), channel_id=1, source_target_pairs={{0,16},{8,24},{16,0},{24,8},{1,17},{9,25},{17,1},{25,9},{2,18},{10... | collective-permute-start | bytes 3145736 | tf_op jit(solution)/shard_map/ppermute | solution.py:23
  113.1 20.0 %collective-permute-start.14 = (bf16[512,256]{1,0:T(8,128)(2,1)}, bf16[512,256]{1,0:T(8,128)(2,1)S(1)}, u32[]{:S(2)}, u32[]{:S(2)}) collective-permute-start(bf16[512,256]{1,0:T(8,128)(2,1)} %shard_map.65.refs_1_), channel_id=1, source_target_pairs={{0,16},{8,24},{16,0},{24,8},{1,17},{9,25},{17,1},{25,9},{2,18},{10... | collective-permute-start | bytes 786440 | tf_op jit(solution)/shard_map/ppermute | solution.py:23
  114.4 18.7 %collective-permute-start.18 = (bf16[512,256]{1,0:T(8,128)(2,1)}, bf16[512,256]{1,0:T(8,128)(2,1)S(1)}, u32[]{:S(2)}, u32[]{:S(2)}) collective-permute-start(bf16[512,256]{1,0:T(8,128)(2,1)} %shard_map.65.refs_1_), channel_id=1, source_target_pairs={{0,8},{8,0},{16,24},{24,16},{1,9},{9,1},{17,25},{25,17},{2,10},{10... | collective-permute-start | bytes 786440 | tf_op jit(solution)/shard_map/ppermute | solution.py:23
  133.1 13.1 %collective-permute-start.25 = (bf16[2048,256]{1,0:T(8,128)(2,1)}, bf16[2048,256]{1,0:T(8,128)(2,1)S(1)}, u32[]{:S(2)}, u32[]{:S(2)}) collective-permute-start(bf16[2048,256]{1,0:T(8,128)(2,1)} %collective-permute-done.19.refs_3_), channel_id=1, source_target_pairs={{0,8},{8,0},{16,24},{24,16},{1,9},{9,1},{17,25},{25,17},{2,10},{10... | collective-permute-start | bytes 3145736 | tf_op jit(solution)/shard_map/ppermute | solution.py:23
  133.8 25.3 %collective-permute-start.23 = (bf16[2048,128]{1,0:T(8,128)(2,1)}, bf16[2048,128]{1,0:T(8,128)(2,1)}, u32[]{:S(2)}, u32[]{:S(2)}) collective-permute-start(bf16[2048,128]{1,0:T(8,128)(2,1)} %get-tuple-element.140), channel_id=1, source_target_pairs={{0,16},{8,24},{16,0},{24,8},{1,17},{9,25},{17,1},{25,9},{2,18},{10... | collective-permute-start | bytes 1572872 | tf_op jit(solution)/shard_map/ppermute | solution.py:23
  143.3 15.8 %collective-permute-start.21 = (bf16[512,512]{1,0:T(8,128)(2,1)S(1)}, bf16[512,512]{1,0:T(8,128)(2,1)S(1)}, u32[]{:S(2)}, u32[]{:S(2)}) collective-permute-start(bf16[512,512]{1,0:T(8,128)(2,1)S(1)} %shard_map.67), channel_id=1, source_target_pairs={{0,2},{2,4},{4,6},{6,7},{7,5},{5,3},{3,1},{1,0},{8,10},{10,12},{12... | collective-permute-start | bytes 1572872 | tf_op jit(solution)/shard_map/ppermute | solution.py:95
  144.9 15.0 %collective-permute-start.22 = (bf16[512,512]{1,0:T(8,128)(2,1)S(1)}, bf16[512,512]{1,0:T(8,128)(2,1)}, u32[]{:S(2)}, u32[]{:S(2)}) collective-permute-start(bf16[512,512]{1,0:T(8,128)(2,1)S(1)} %shard_map.67), channel_id=1, source_target_pairs={{2,0},{4,2},{6,4},{7,6},{5,7},{3,5},{1,3},{0,1},{10,8},{12,10},{14... | collective-permute-start | bytes 1572872 | tf_op jit(solution)/shard_map/ppermute | solution.py:95
  161.0 14.7 %collective-permute-start.26 = (bf16[512,512]{1,0:T(8,128)(2,1)}, bf16[512,512]{1,0:T(8,128)(2,1)S(1)}, u32[]{:S(2)}, u32[]{:S(2)}) collective-permute-start(bf16[512,512]{1,0:T(8,128)(2,1)} %copy-done.15), channel_id=1, source_target_pairs={{0,2},{2,4},{4,6},{6,7},{7,5},{5,3},{3,1},{1,0},{8,10},{10,12},{12... | collective-permute-start | bytes 1572872 | tf_op jit(solution)/shard_map/ppermute | solution.py:95
  162.6 13.8 %collective-permute-start.27 = (bf16[512,512]{1,0:T(8,128)(2,1)}, bf16[512,512]{1,0:T(8,128)(2,1)S(1)}, u32[]{:S(2)}, u32[]{:S(2)}) collective-permute-start(bf16[512,512]{1,0:T(8,128)(2,1)} %collective-permute-done.22), channel_id=1, source_target_pairs={{2,0},{4,2},{6,4},{7,6},{5,7},{3,5},{1,3},{0,1},{10,8},{12,10},{14... | collective-permute-start | bytes 1572872 | tf_op jit(solution)/shard_map/ppermute | solution.py:95
  176.4 15.7 %collective-permute-start.31 = (bf16[2048,1024]{1,0:T(8,128)(2,1)}, bf16[2048,1024]{1,0:T(8,128)(2,1)S(1)}, u32[]{:S(2)}, u32[]{:S(2)}) collective-permute-start(bf16[2048,1024]{1,0:T(8,128)(2,1)} %refs_2_), channel_id=1, source_target_pairs={{0,8},{8,0},{16,24},{24,16},{1,9},{9,1},{17,25},{25,17},{2,10},{10... | collective-permute-start | bytes 12582920 | tf_op jit(solution)/shard_map/ppermute | solution.py:23
  176.4 14.3 %collective-permute-start.29 = (bf16[512,512]{1,0:T(8,128)(2,1)S(1)}, bf16[512,512]{1,0:T(8,128)(2,1)S(1)}, u32[]{:S(2)}, u32[]{:S(2)}) collective-permute-start(bf16[512,512]{1,0:T(8,128)(2,1)S(1)} %collective-permute-done.26), channel_id=1, source_target_pairs={{0,2},{2,4},{4,6},{6,7},{7,5},{5,3},{3,1},{1,0},{8,10},{10,12},{12... | collective-permute-start | bytes 1572872 | tf_op jit(solution)/shard_map/ppermute | solution.py:95
  177.9 14.1 %collective-permute-start.30 = (bf16[512,512]{1,0:T(8,128)(2,1)S(1)}, bf16[512,512]{1,0:T(8,128)(2,1)S(1)}, u32[]{:S(2)}, u32[]{:S(2)}) collective-permute-start(bf16[512,512]{1,0:T(8,128)(2,1)S(1)} %collective-permute-done.27), channel_id=1, source_target_pairs={{2,0},{4,2},{6,4},{7,6},{5,7},{3,5},{1,3},{0,1},{10,8},{12,10},{14... | collective-permute-start | bytes 1572872 | tf_op jit(solution)/shard_map/ppermute | solution.py:95
  192.0 20.2 %collective-permute-start.34 = (bf16[512,512]{1,0:T(8,128)(2,1)S(1)}, bf16[512,512]{1,0:T(8,128)(2,1)S(1)}, u32[]{:S(2)}, u32[]{:S(2)}) collective-permute-start(bf16[512,512]{1,0:T(8,128)(2,1)S(1)} %shard_map.72), channel_id=1, source_target_pairs={{0,2},{2,4},{4,6},{6,7},{7,5},{5,3},{3,1},{1,0},{8,10},{10,12},{12... | collective-permute-start | bytes 1572872 | tf_op jit(solution)/shard_map/ppermute | solution.py:95
  193.5 18.7 %collective-permute-start.35 = (bf16[512,512]{1,0:T(8,128)(2,1)S(1)}, bf16[512,512]{1,0:T(8,128)(2,1)S(1)}, u32[]{:S(2)}, u32[]{:S(2)}) collective-permute-start(bf16[512,512]{1,0:T(8,128)(2,1)S(1)} %shard_map.72), channel_id=1, source_target_pairs={{2,0},{4,2},{6,4},{7,6},{5,7},{3,5},{1,3},{0,1},{10,8},{12,10},{14... | collective-permute-start | bytes 1572872 | tf_op jit(solution)/shard_map/ppermute | solution.py:95
  194.9 16.0 %collective-permute-start.32 = (bf16[256,512]{1,0:T(8,128)(2,1)S(1)}, bf16[256,512]{1,0:T(8,128)(2,1)S(1)}, u32[]{:S(2)}, u32[]{:S(2)}) collective-permute-start(bf16[256,512]{1,0:T(8,128)(2,1)S(1)} %slice.96), channel_id=1, source_target_pairs={{0,2},{2,4},{4,6},{6,7},{7,5},{5,3},{3,1},{1,0},{8,10},{10,12},{12... | collective-permute-start | bytes 786440 | tf_op jit(solution)/shard_map/ppermute | solution.py:95
  196.5 15.7 %collective-permute-start.33 = (bf16[256,512]{1,0:T(8,128)(2,1)S(1)}, bf16[256,512]{1,0:T(8,128)(2,1)S(1)}, u32[]{:S(2)}, u32[]{:S(2)}) collective-permute-start(bf16[256,512]{1,0:T(8,128)(2,1)S(1)} %slice.97), channel_id=1, source_target_pairs={{2,0},{4,2},{6,4},{7,6},{5,7},{3,5},{1,3},{0,1},{10,8},{12,10},{14... | collective-permute-start | bytes 786440 | tf_op jit(solution)/shard_map/ppermute | solution.py:95
  (28 other events, 273.6 us)
Sparse Core Ops, SparseCore 0:
  133.2 107.0 all-gather.2
